TPU v7x, 128 devices: a whole 4x4x4 slice. The times are simulated.
128 devices in a mesh: seq: 16 (over x_lo, z, core), head: 8 (over x_hi, y).
Axes of the slice: x: 4 (x_hi: 2, x_lo: 2; x = x_hi * 2 + x_lo), y: 4, z: 4, core: 2. Of those that a mesh axis runs over, the one named last changes fastest.
Arguments:
- tokens: bfloat16 [8192, 5120], P('seq'), may hold values from -6 to 6
- shift_vector: float32 [5120], replicated, may hold values from -3 to 3
- scale_vector: float32 [5120], replicated, may hold values from -3 to 3
- query_weight: bfloat16 [5120, 3072], P(None, 'head'), may hold values from -0.078125 to 0.078125
- key_weight: bfloat16 [5120, 3072], P(None, 'head'), may hold values from -0.078125 to 0.078125
- value_weight: bfloat16 [5120, 3072], P(None, 'head'), may hold values from -0.078125 to 0.078125
- query_gain: float32 [3072], P('head'), may hold values from 0.8 to 1.8
- key_gain: float32 [3072], P('head'), may hold values from 0.8 to 1.8
- out_weight: bfloat16 [3072, 5120], P('head'), may hold values from -1.75 to 1.75
Outputs:
- attn_out: bfloat16 [8192, 5120], P('seq', 'head')
All inputs are finite; a program needn't handle non-finite values.
Results may differ from a plain program's by a relative error of at most 0.02.
Values may be sent and summed in bfloat16 or wider, within the bound.
No kernel may reach another device: no remote copies, remote signals or barrier semaphores. Data moves between devices by JAX's collectives and lax.ppermute only.
A program may use at most 128 MiB of HBM per device.

v0:
```python
import math

import jax
import jax.numpy as jnp
from jax import lax
from jax.sharding import PartitionSpec as P

HD = 128


softcap = 10.0
epsilon = 1e-06


def modulate(tokens, shift_vector, scale_vector):
    values = tokens.astype(jnp.float32)
    center = jnp.mean(values, axis=-1, keepdims=True)
    spread = jnp.mean(jnp.square(values - center), axis=-1, keepdims=True)
    normed = (values - center) * lax.rsqrt(spread + epsilon)
    return (normed * (1.0 + scale_vector) + shift_vector).astype(jnp.bfloat16)


def head_norm(projected, gain_vector):
    shaped = projected.reshape(projected.shape[0], -1, HD)
    mean_sq = jnp.mean(jnp.square(shaped), axis=-1, keepdims=True)
    gain_rows = gain_vector.reshape(-1, HD)
    return (shaped * lax.rsqrt(mean_sq + epsilon) * gain_rows).astype(jnp.bfloat16)


def capped_weights(scores):
    return jnp.exp(softcap * jnp.tanh(scores / (math.sqrt(HD) * softcap)) - softcap)


def attend(queries, key_block, value_block):
    scores = jnp.einsum("qhd,khd->hqk", queries, key_block, preferred_element_type=jnp.float32)
    weights = capped_weights(scores)
    totals = jnp.sum(weights, axis=-1)
    mixture = jnp.einsum(
        "hqk,khd->qhd",
        weights.astype(jnp.bfloat16),
        value_block,
        preferred_element_type=jnp.float32,
    )
    return (mixture, totals)


def attend_blocks(queries, key_block, value_block):
    length = key_block.shape[0]
    span_len = math.gcd(length, 2048)
    pieces = length // span_len
    key_split = key_block.reshape(pieces, span_len, key_block.shape[1], key_block.shape[2])
    value_split = value_block.reshape(pieces, span_len, value_block.shape[1], value_block.shape[2])

    def advance(carry, pair):
        mixture, totals = attend(queries, pair[0], pair[1])
        return ((carry[0] + mixture, carry[1] + totals), None)

    start_sum = jnp.zeros((queries.shape[0], queries.shape[1], queries.shape[2]), jnp.float32)
    start_tot = jnp.zeros((queries.shape[1], queries.shape[0]), jnp.float32)
    outcome, unused = lax.scan(advance, (start_sum, start_tot), (key_split, value_split))
    return outcome


def shards(
    tokens,
    shift_vector,
    scale_vector,
    query_weight,
    key_weight,
    value_weight,
    query_gain,
    key_gain,
    out_weight,
):
    tok_rows = tokens.shape[0]
    normed = modulate(tokens, shift_vector, scale_vector)
    queries = head_norm(
        jnp.dot(normed, query_weight, preferred_element_type=jnp.float32), query_gain
    )
    key_local = head_norm(jnp.dot(normed, key_weight, preferred_element_type=jnp.float32), key_gain)
    value_local = jnp.dot(normed, value_weight, preferred_element_type=jnp.float32).astype(
        jnp.bfloat16
    )
    value_local = value_local.reshape(tok_rows, -1, HD)
    key_whole, value_whole = (
        lax.all_gather(key_local, "seq", axis=0, tiled=True),
        lax.all_gather(value_local, "seq", axis=0, tiled=True),
    )
    mixture, totals = attend_blocks(queries, key_whole, value_whole)
    attended = (
        (mixture / jnp.transpose(totals)[:, :, None]).astype(jnp.bfloat16).reshape(tok_rows, -1)
    )
    partial_out = jnp.dot(attended, out_weight, preferred_element_type=jnp.float32)
    return lax.psum_scatter(
        partial_out.astype(jnp.bfloat16), "head", scatter_dimension=1, tiled=True
    )


def solution(mesh):
    in_specs = (
        P("seq", None),
        P(),
        P(),
        P(None, "head"),
        P(None, "head"),
        P(None, "head"),
        P("head"),
        P("head"),
        P("head", None),
    )
    out_specs = P("seq", "head")
    return jax.shard_map(shards, mesh=mesh, in_specs=in_specs, out_specs=out_specs, check_vma=False)
```

profile of v0, /device:TPU:0, one launch (start us, length us, event | category | flops | bytes accessed | tf_op | source)
XLA Modules:
  0.0 284.9 jit_solution(10960913866544359934)
XLA Ops:
  6.5 0.0 all-gather.5.cloned.1.call-start
  6.5 0.0 copy-start
  6.5 0.0 copy-start.3
  6.5 0.0 copy-start.2
  6.5 3.4 %convert_reduce_fusion = f32[512]{0:T(512)S(1)} fusion(bf16[512,5120]{1,0:T(8,128)(2,1)} %param.11), kind=kLoop, calls=%fused_computation.18 | loop fusion | flops 5242368 | bytes 5244928 | tf_op jit(solution)/shard_map/reduce_sum | solution.py:17
  10.0 0.6 copy-done
  10.6 1.5 fusion.19
  12.1 0.0 copy-start.6
  12.1 0.0 copy-done.3
  12.1 0.0 copy-done.2
  12.1 3.0 %fusion.22 = bf16[512,5120]{1,0:T(8,128)(2,1)S(1)} fusion(bf16[512,5120]{1,0:T(8,128)(2,1)S(1)} %copy-done, f32[5120]{0:T(1024)S(1)} %copy-done.2, f32[5120]{0:T(1024)S(1)} %broadcast_add_fusion, f32[512]{0:T(512)S(1)} %add_rsqrt_fusion.2, f32[512]{0:T(512)S(1)} %broadcast_multiply_fusion), kind=kLoop, calls=%fused_computation.24 | loop fusion | flops 15728640 | bytes 10530816 | tf_op jit(solution)/shard_map/convert_element_type | solution.py:20
  15.2 0.0 copy-done.6
  15.2 0.0 copy-start.1
  15.2 0.0 copy-start.4
  15.2 2.2 fusion.23
  17.4 0.0 copy-done.1
  17.5 0.3 copy.20
  17.7 0.1 multiply_reduce_fusion.1
  17.9 0.0 copy-done.4
  17.9 1.0 multiply_convert_fusion.1
  18.9 0.0 all-gather.5.cloned.1.call-update
  18.9 0.0 all-gather.3.cloned.1.call-start
  19.0 5.9 %convolution_convert_fusion.1 = bf16[512,384]{0,1:T(8,128)(2,1)S(1)} fusion(bf16[512,5120]{1,0:T(8,128)(2,1)} %copy-done.1, bf16[5120,384]{1,0:T(8,128)(2,1)} %param.16), kind=kOutput, calls=%fused_computation.26 | convolution fusion | flops 2013462528 | bytes 9568256 | tf_op jit(solution)/shard_map/dot_general | solution.py:81
  24.9 0.9 copy.19
  25.8 0.0 all-gather.3.cloned.1.call-update
  25.8 0.2 reduce-scatter.4.cloned.1.call-start
  26.1 0.0 copy-start.5
  26.1 5.9 %fusion.24 = f32[512,384]{0,1:T(8,128)S(1)} fusion(bf16[512,5120]{1,0:T(8,128)(2,1)} %copy-done.1, bf16[5120,384]{1,0:T(8,128)(2,1)} %param.14), kind=kOutput, calls=%fused_computation.38 | convolution fusion | flops 2013265920 | bytes 9961472 | tf_op jit(solution)/shard_map/dot_general | solution.py:78
  32.0 0.3 copy.21
  32.3 0.1 multiply_reduce_fusion
  32.4 0.0 copy-done.5
  32.4 0.3 multiply_convert_fusion
  32.7 31.3 %all-gather.5.cloned.1.call-done = bf16[8192,3,128]{2,0,1:T(8,128)(2,1)} async-done(((bf16[512,3,128]{2,0,1:T(8,128)(2,1)}), bf16[8192,3,128]{2,0,1:T(8,128)(2,1)}) %all-gather.5.cloned.1.call-update) | async-done | bytes 6291472 | tf_op jit(solution)/shard_map/all_gather | solution.py:86
  64.0 45.0 %all-gather.3.cloned.1.call-done = bf16[8192,3,128]{2,0,1:T(8,128)(2,1)} async-done(((bf16[512,3,128]{2,0,1:T(8,128)(2,1)}), bf16[8192,3,128]{2,0,1:T(8,128)(2,1)}) %all-gather.3.cloned.1.call-update) | async-done | bytes 6291472 | tf_op jit(solution)/shard_map/all_gather | solution.py:87
  108.9 60.4 %while.15 = (s32[]{:T(128)}, f32[512,3,128]{0,2,1:T(8,128)S(1)}, f32[3,512]{1,0:T(4,128)S(1)}, bf16[4,2048,3,128]{3,1,0,2:T(8,128)(2,1)}, bf16[4,2048,3,128]{3,1...) while((s32[]{:T(128)}, f32[512,3,128]{0,2,1:T(8,128)S(1)}, ...), condition=%wide.region_6.7_spmd.clone, body=%wide.region_4.6_spmd.clone.sunk | while | flops 1636173312 | bytes 30303328 | solution.py:60
  108.9 7.9 %bitcast_reduce_fusion.2 = (f32[3,512]{1,0:T(4,128)S(1)}, f32[3,2048,512]{2,1,0:T(8,128)}) fusion(bf16[512,3,128]{2,0,1:T(8,128)(2,1)S(1)} %get-tuple-element.194, bf16[4,2048,3,128]{3,1,0,2:T(8,128)(2,1)} %get-tuple-element.193, s32[]{:T(128)} %get-tuple-element.181), kind=kOutput, calls=%fused_computation.clone.1 | convolution fusion | flops 817887744 | bytes 14555648 | tf_op jit(solution)/shard_map/while/body/eval_jaxpr/qhd,khd->hqk/dot_general | solution.py:35
  116.8 7.2 %fusion.39 = f32[512,3,128]{0,2,1:T(8,128)S(1)} fusion(f32[3,2048,512]{2,1,0:T(8,128)} %get-tuple-element.171, bf16[4,2048,3,128]{3,1,0,2:T(8,128)(2,1)} %get-tuple-element.192, s32[]{:T(128)} %get-tuple-element.181, f32[512,3,128]{0,2,1:T(8,128)S(1)} %get-tuple-element.182, pred[]{:T(512)S(6)} %compare.3), kind=kOutput, calls=%fused_computation.10.clone.1 | convolution fusion | flops 818282496 | bytes 15729153 | tf_op jit(solution)/shard_map/while/body/eval_jaxpr/hqk,khd->qhd/dot_general | solution.py:38
  124.0 7.9 %bitcast_reduce_fusion.2 = (f32[3,512]{1,0:T(4,128)S(1)}, f32[3,2048,512]{2,1,0:T(8,128)}) fusion(bf16[512,3,128]{2,0,1:T(8,128)(2,1)S(1)} %get-tuple-element.194, bf16[4,2048,3,128]{3,1,0,2:T(8,128)(2,1)} %get-tuple-element.193, s32[]{:T(128)} %get-tuple-element.181), kind=kOutput, calls=%fused_computation.clone.1 | convolution fusion | flops 817887744 | bytes 14555648 | tf_op jit(solution)/shard_map/while/body/eval_jaxpr/qhd,khd->hqk/dot_general | solution.py:35
  131.9 7.2 %fusion.39 = f32[512,3,128]{0,2,1:T(8,128)S(1)} fusion(f32[3,2048,512]{2,1,0:T(8,128)} %get-tuple-element.171, bf16[4,2048,3,128]{3,1,0,2:T(8,128)(2,1)} %get-tuple-element.192, s32[]{:T(128)} %get-tuple-element.181, f32[512,3,128]{0,2,1:T(8,128)S(1)} %get-tuple-element.182, pred[]{:T(512)S(6)} %compare.3), kind=kOutput, calls=%fused_computation.10.clone.1 | convolution fusion | flops 818282496 | bytes 15729153 | tf_op jit(solution)/shard_map/while/body/eval_jaxpr/hqk,khd->qhd/dot_general | solution.py:38
  139.1 7.9 %bitcast_reduce_fusion.2 = (f32[3,512]{1,0:T(4,128)S(1)}, f32[3,2048,512]{2,1,0:T(8,128)}) fusion(bf16[512,3,128]{2,0,1:T(8,128)(2,1)S(1)} %get-tuple-element.194, bf16[4,2048,3,128]{3,1,0,2:T(8,128)(2,1)} %get-tuple-element.193, s32[]{:T(128)} %get-tuple-element.181), kind=kOutput, calls=%fused_computation.clone.1 | convolution fusion | flops 817887744 | bytes 14555648 | tf_op jit(solution)/shard_map/while/body/eval_jaxpr/qhd,khd->hqk/dot_general | solution.py:35
  147.0 7.2 %fusion.39 = f32[512,3,128]{0,2,1:T(8,128)S(1)} fusion(f32[3,2048,512]{2,1,0:T(8,128)} %get-tuple-element.171, bf16[4,2048,3,128]{3,1,0,2:T(8,128)(2,1)} %get-tuple-element.192, s32[]{:T(128)} %get-tuple-element.181, f32[512,3,128]{0,2,1:T(8,128)S(1)} %get-tuple-element.182, pred[]{:T(512)S(6)} %compare.3), kind=kOutput, calls=%fused_computation.10.clone.1 | convolution fusion | flops 818282496 | bytes 15729153 | tf_op jit(solution)/shard_map/while/body/eval_jaxpr/hqk,khd->qhd/dot_general | solution.py:38
  154.2 7.9 %bitcast_reduce_fusion.2 = (f32[3,512]{1,0:T(4,128)S(1)}, f32[3,2048,512]{2,1,0:T(8,128)}) fusion(bf16[512,3,128]{2,0,1:T(8,128)(2,1)S(1)} %get-tuple-element.194, bf16[4,2048,3,128]{3,1,0,2:T(8,128)(2,1)} %get-tuple-element.193, s32[]{:T(128)} %get-tuple-element.181), kind=kOutput, calls=%fused_computation.clone.1 | convolution fusion | flops 817887744 | bytes 14555648 | tf_op jit(solution)/shard_map/while/body/eval_jaxpr/qhd,khd->hqk/dot_general | solution.py:35
  162.1 7.2 %fusion.39 = f32[512,3,128]{0,2,1:T(8,128)S(1)} fusion(f32[3,2048,512]{2,1,0:T(8,128)} %get-tuple-element.171, bf16[4,2048,3,128]{3,1,0,2:T(8,128)(2,1)} %get-tuple-element.192, s32[]{:T(128)} %get-tuple-element.181, f32[512,3,128]{0,2,1:T(8,128)S(1)} %get-tuple-element.182, pred[]{:T(512)S(6)} %compare.3), kind=kOutput, calls=%fused_computation.10.clone.1 | convolution fusion | flops 818282496 | bytes 15729153 | tf_op jit(solution)/shard_map/while/body/eval_jaxpr/hqk,khd->qhd/dot_general | solution.py:38
  169.3 0.1 divide_convert_fusion
  169.4 6.8 %convolution_convert_fusion = bf16[512,5120]{1,0:T(8,128)(2,1)} fusion(bf16[512,384]{0,1:T(8,128)(2,1)S(1)} %bitcast.64, bf16[384,5120]{1,0:T(8,128)(2,1)} %param.19), kind=kOutput, calls=%fused_computation.25 | convolution fusion | flops 2015887360 | bytes 9568256 | tf_op jit(solution)/shard_map/dot_general | solution.py:93
  176.2 7.9 %copy.25 = bf16[512,5120]{0,1:T(8,128)(2,1)} copy(bf16[512,5120]{1,0:T(8,128)(2,1)} %convolution_convert_fusion) | data formatting | bytes 10485760
  184.2 0.0 reduce-scatter.4.cloned.1.call-update
  184.2 92.0 %reduce-scatter.4.cloned.1.call-done = bf16[640,512]{1,0:T(8,128)(2,1)} async-done(((bf16[5120,512]{1,0:T(8,128)(2,1)}), bf16[640,512]{1,0:T(8,128)(2,1)}) %reduce-scatter.4.cloned.1.call-update) | async-done | bytes 655376
  276.2 2.2 copy.26
  (11 shorter events, 0.1 us)
Async XLA Ops:
  6.5 57.4 %all-gather.5.cloned.1.call-start = ((), (), s32[]{:S(2)}) async-start(), calls=%async_computation.2 | async-start | bytes 6684672 | tf_op jit(solution)/shard_map/all_gather | solution.py:86
  6.5 4.0 %copy-start = (bf16[512,5120]{1,0:T(8,128)(2,1)S(1)}, bf16[512,5120]{1,0:T(8,128)(2,1)}, u32[]{:S(2)}) copy-start(bf16[512,5120]{1,0:T(8,128)(2,1)} %param.11) | copy-start | bytes 15728644
  6.5 5.6 %copy-start.3 = (f32[5120]{0:T(1024)S(1)}, f32[5120]{0:T(1024)}, u32[]{:S(2)}) copy-start(f32[5120]{0:T(1024)} %param.13) | copy-start | bytes 61444
  6.5 5.6 %copy-start.2 = (f32[5120]{0:T(1024)S(1)}, f32[5120]{0:T(1024)}, u32[]{:S(2)}) copy-start(f32[5120]{0:T(1024)} %param.12) | copy-start | bytes 61444
  12.1 3.1 %copy-start.6 = (bf16[5120,384]{1,0:T(8,128)(2,1)S(1)}, bf16[5120,384]{1,0:T(8,128)(2,1)}, u32[]{:S(2)}) copy-start(bf16[5120,384]{1,0:T(8,128)(2,1)} %param.15) | copy-start | bytes 11796484
  15.2 2.3 copy-start.1
  15.2 2.7 copy-start.4
  18.9 90.0 %all-gather.3.cloned.1.call-start = ((), (), s32[]{:S(2)}) async-start(), calls=%async_computation.1 | async-start | bytes 6684672 | tf_op jit(solution)/shard_map/all_gather | solution.py:87
  25.8 250.3 %reduce-scatter.4.cloned.1.call-start = ((), (), s32[]{:S(2)}) async-start(), calls=%async_computation.3 | async-start | bytes 5898240
  26.1 6.3 %copy-start.5 = (f32[384]{0:T(512)S(1)}, f32[384]{0:T(512)}, u32[]{:S(2)}) copy-start(f32[384]{0:T(512)} %param.17) | copy-start | bytes 4612
Sparse Core Ops, SparseCore 0:
  19.0 44.8 all-gather.4
  65.6 43.2 all-gather.2
  184.3 91.8 reduce-scatter.3
where the time goes:
time: 285 us
  waiting for transfers between devices  168 us (59%)
  matrix products  81.1 us (28%)
  between operations  13.3 us (5%)
  local copies, waits for them, and re-layouts  12.2 us (4%)
  other arithmetic  9.59 us (3%)
    unnamed x4, waiting for transfers between devices  92 us
    all_gather x1, waiting for transfers between devices, shards(): lax.all_gather(value_local, 'seq', axis=0, tiled=True)  45 us
    dot_general x4, matrix products, attend(): jnp.einsum('qhd,khd->hqk', queries, key_block, preferred_element_type=jnp...  31.6 us
    all_gather x1, waiting for transfers between devices, shards(): lax.all_gather(key_local, 'seq', axis=0, tiled=True)  31.3 us
    dot_general x4, matrix products, attend(): jnp.einsum('hqk,khd->qhd', weights.astype(jnp.bfloat16), value_block, pre...  28.7 us
    unnamed x16, local copies, waits for them, and re-layouts  10.8 us
    dot_general x1, matrix products, shards(): jnp.dot(attended, out_weight, preferred_element_type=jnp.float32)  6.82 us
    dot_general x1, matrix products, shards(): jnp.dot(normed, value_weight, preferred_element_type=jnp.float32)  5.92 us
  transfers between devices with their start and end apart: 3, of which 3 were waited for; matrix products, arithmetic and copies ran while one was open for 5% of the time, Pallas kernels for 0%

commit v1 on v0

v1 whole, which is shorter than its diff:
```python
import functools
import math

import jax
import jax.numpy as jnp
from jax import lax
from jax.experimental import pallas as pl
from jax.experimental.pallas import tpu as pltpu
from jax.sharding import PartitionSpec as P

HD = 128
SOFTCAP = 10.0
EPSILON = 1e-06
GROUP_HEADS = 3
WIDE = GROUP_HEADS * HD
ROWS = 512
D = 5120
OUT_COLS = 640
BK = 512
EXP_SCALE = SOFTCAP * math.log2(math.e)
SCORE_SCALE = 1.0 / (SOFTCAP * math.sqrt(HD))
VMEM = 56 * 2**20

BF16 = jnp.bfloat16
F32 = jnp.float32


def seq_perm(move):
    pairs = []
    for i in range(16):
        x, z, c = move(i // 8, (i // 2) % 4, i % 2)
        pairs.append((i, x * 8 + (z % 4) * 2 + c))
    return pairs


def head_perm(move):
    pairs = []
    for i in range(8):
        x, y = move(i // 4, i % 4)
        pairs.append((i, x * 4 + (y % 4)))
    return pairs


SWAP_CORE = seq_perm(lambda x, z, c: (x, z, 1 - c))
SWAP_X = seq_perm(lambda x, z, c: (1 - x, z, c))
Z_UP = seq_perm(lambda x, z, c: (x, z + 1, c))
Z_DOWN = seq_perm(lambda x, z, c: (x, z - 1, c))
SWAP_XHI = head_perm(lambda x, y: (1 - x, y))
Y_STEP = [None] + [head_perm(lambda x, y, r=r: (x, y + r)) for r in (1, 2, 3)]


def params(flops=0):
    return pltpu.CompilerParams(vmem_limit_bytes=VMEM)


def cost(flops, nbytes, trans=0):
    return pl.CostEstimate(flops=int(flops), bytes_accessed=int(nbytes), transcendentals=int(trans))


def qkv_kernel(tok, shift, scale, wq, wk, wv, gq, gk, q_o, kv0, kv1, kv2, mean_s, rstd_s, n_s, aq, ak, av):
    j = pl.program_id(0)
    nk = pl.num_programs(0)

    def normalise(block, slot):
        cols = pl.ds(pl.multiple_of(block * BK, BK), BK)
        xb = tok[:, cols].astype(F32)
        m = jnp.concatenate([mean_s[...]] * (BK // 128), axis=1)
        r = jnp.concatenate([rstd_s[...]] * (BK // 128), axis=1)
        y = (xb - m) * r
        n_s[slot] = (y * (1.0 + scale[:, cols]) + shift[:, cols]).astype(BF16)

    @pl.when(j == 0)
    def _():
        def stats(i, carry):
            rows = pl.ds(pl.multiple_of(i * 32, 32), 32)
            x = tok[rows, :].astype(F32)
            mean = jnp.sum(x, axis=1, keepdims=True) * (1.0 / D)
            cen = x - mean
            var = jnp.sum(cen * cen, axis=1, keepdims=True) * (1.0 / D)
            mean_s[rows, :] = jnp.broadcast_to(mean, (32, 128))
            rstd_s[rows, :] = jnp.broadcast_to(lax.rsqrt(var + EPSILON), (32, 128))
            return carry

        lax.fori_loop(0, ROWS // 32, stats, 0, unroll=4)
        normalise(0, 0)
        aq[...] = jnp.zeros_like(aq)
        ak[...] = jnp.zeros_like(ak)
        av[...] = jnp.zeros_like(av)

    n = n_s[j % 2]
    aq[...] += jnp.dot(n, wq[...], preferred_element_type=F32)
    ak[...] += jnp.dot(n, wk[...], preferred_element_type=F32)
    av[...] += jnp.dot(n, wv[...], preferred_element_type=F32)
    normalise(jnp.minimum(j + 1, nk - 1), (j + 1) % 2)

    @pl.when(j == nk - 1)
    def _():
        for h, kv in enumerate((kv0, kv1, kv2)):
            cols = slice(h * HD, (h + 1) * HD)

            def unit(a):
                return a * lax.rsqrt(jnp.mean(a * a, axis=1, keepdims=True) + EPSILON)

            q_o[:, cols] = (unit(aq[:, cols]) * (gq[:, cols] * SCORE_SCALE)).astype(BF16)
            kv[:, :HD] = (unit(ak[:, cols]) * gk[:, cols]).astype(BF16)
            kv[:, HD:] = av[:, cols].astype(BF16)


def project(tokens, shift, scale, wq, wk, wv, gq, gk):
    nk = D // BK
    whole = lambda shape: pl.BlockSpec(shape, lambda j: (0, 0))
    wspec = pl.BlockSpec((BK, WIDE), lambda j: (j, 0))
    return pl.pallas_call(
        qkv_kernel,
        grid=(nk,),
        in_specs=[whole((ROWS, D)), whole((1, D)), whole((1, D)), wspec, wspec, wspec,
                  whole((1, WIDE)), whole((1, WIDE))],
        out_specs=[whole((ROWS, WIDE))] + [whole((ROWS, 2 * HD))] * 3,
        out_shape=[jax.ShapeDtypeStruct((ROWS, WIDE), BF16)]
        + [jax.ShapeDtypeStruct((ROWS, 2 * HD), BF16)] * 3,
        scratch_shapes=[
            pltpu.VMEM((ROWS, 128), F32),
            pltpu.VMEM((ROWS, 128), F32),
            pltpu.VMEM((2, ROWS, BK), BF16),
            pltpu.VMEM((ROWS, WIDE), F32),
            pltpu.VMEM((ROWS, WIDE), F32),
            pltpu.VMEM((ROWS, WIDE), F32),
        ],
        compiler_params=params(),
        cost_estimate=cost(2 * ROWS * D * WIDE * 3, 18e6),
        name="qkv",
    )(tokens, shift.reshape(1, D), scale.reshape(1, D), wq, wk, wv, gq.reshape(1, WIDE), gk.reshape(1, WIDE))


def attend_kernel(q0, q1, q2, q3, k0, k1, k2, k3, k4, keep, send):
    chunks = []
    for kv in (k0, k1, k2, k3, k4):
        for s in range(0, kv.shape[0], 256):
            chunks.append((kv, s))
    for q, out, base in ((q0, keep, 0), (q1, send, 0), (q2, keep, ROWS), (q3, send, ROWS)):
        qq = q[...]
        acc = None
        for kv, s in chunks:
            k = kv[s : s + 256, :HD]
            v = kv[s : s + 256, HD:]
            x = lax.dot_general(qq, k, (((1,), (1,)), ((), ())), preferred_element_type=F32)
            p = jnp.exp2(EXP_SCALE * jnp.tanh(x)).astype(BF16)
            d = jnp.dot(p, jnp.concatenate([v, jnp.ones_like(v)], axis=1), preferred_element_type=F32)
            acc = d if acc is None else acc + d
        out[base : base + ROWS, :] = acc.astype(BF16)


def attend(qs, kvs, h):
    whole = lambda shape: pl.BlockSpec(shape, lambda i: (0, 0))
    return pl.pallas_call(
        attend_kernel,
        grid=(1,),
        in_specs=[pl.BlockSpec((ROWS, HD), lambda i: (0, h))] * 4 + [whole(kv.shape) for kv in kvs],
        out_specs=[whole((2 * ROWS, 2 * HD))] * 2,
        out_shape=[jax.ShapeDtypeStruct((2 * ROWS, 2 * HD), BF16)] * 2,
        compiler_params=params(),
        cost_estimate=cost(4 * 2048 * 2048 * 256, 3e6, 2 * 2048 * 2048),
        name="attend",
    )(*qs, *kvs)


def combine_core_kernel(keep, recv, mine, away):
    a = keep[:ROWS, :].astype(F32) + recv[:ROWS, :].astype(F32)
    mine[...] = a
    b = keep[ROWS:, :].astype(F32) + recv[ROWS:, :].astype(F32)
    away[:ROWS, :] = b[:, :HD].astype(BF16)
    for p in range(ROWS // 128):
        t = jnp.transpose(b[p * 128 : (p + 1) * 128, HD:])
        away[ROWS + 16 * p : ROWS + 16 * (p + 1), :] = t[:16].astype(BF16)


def combine_core(keep, recv):
    return pl.pallas_call(
        combine_core_kernel,
        out_shape=[jax.ShapeDtypeStruct((ROWS, 2 * HD), F32), jax.ShapeDtypeStruct((ROWS + 64, HD), BF16)],
        compiler_params=params(),
        cost_estimate=cost(1e6, 2e6),
        name="combine_core",
    )(keep, recv)


def combine_x_kernel(mine, recv, out):
    for p in range(ROWS // 128):
        rows = slice(p * 128, (p + 1) * 128)
        t = recv[ROWS + 16 * p : ROWS + 16 * (p + 1), :].astype(F32)[:1]
        total = mine[rows, HD:] + jnp.transpose(jnp.broadcast_to(t, (128, 128)))
        out[rows, :] = ((mine[rows, :HD] + recv[rows, :].astype(F32)) / total).astype(BF16)


def combine_x(mine, recv):
    return pl.pallas_call(
        combine_x_kernel,
        out_shape=jax.ShapeDtypeStruct((ROWS, HD), BF16),
        compiler_params=params(),
        cost_estimate=cost(1e6, 1e6),
        name="combine_x",
    )(mine, recv)


def out_kernel(core, *refs):
    a = refs[:12]
    first = refs[12:16]
    second = refs[16:20]
    keep, send = refs[20:]
    acc = None
    for r in range(4):
        w = jnp.concatenate([first[r][...], second[r][...]], axis=1)
        for h in range(3):
            d = jnp.dot(a[3 * r + h][...], w[h * HD : (h + 1) * HD], preferred_element_type=F32)
            acc = d if acc is None else acc + d
    lead = core[0] == 0
    keep[...] = jnp.where(lead, acc[:, :128], acc[:, 128:])
    send[...] = jnp.where(lead, acc[:, 128:], acc[:, :128]).astype(BF16)


def out_project(core, attended, first, second):
    whole = pl.BlockSpec((ROWS, HD), lambda j: (0, 0))
    wspec = pl.BlockSpec((WIDE, 128), lambda j: (0, j))
    ospec = pl.BlockSpec((ROWS, 128), lambda j: (0, j))
    return pl.pallas_call(
        out_kernel,
        grid=(OUT_COLS // 128,),
        in_specs=[pl.BlockSpec(memory_space=pltpu.SMEM)] + [whole] * 12 + [wspec] * 8,
        out_specs=[ospec, ospec],
        out_shape=[jax.ShapeDtypeStruct((ROWS, OUT_COLS), F32), jax.ShapeDtypeStruct((ROWS, OUT_COLS), BF16)],
        compiler_params=params(),
        cost_estimate=cost(2 * ROWS * 1536 * 1280, 8e6),
        name="out_project",
    )(core.reshape(1), *attended, *first, *second)


def shards(tokens, shift, scale, wq, wk, wv, gq, gk, wo):
    seq = lax.axis_index("seq")
    head = lax.axis_index("head")
    core = seq % 2
    x_hi, y = head // 4, head % 4

    def columns(side, r):
        col = ((x_hi + side) % 2) * 4 + (y + r) % 4
        return lax.dynamic_slice(wo, (0, col * OUT_COLS), (WIDE, OUT_COLS))

    first = [columns(core, 0)]
    for r in (1, 2, 3):
        first.append(lax.ppermute(columns(core, r), "head", Y_STEP[r]))
    second = [columns(1 - core, 0)]
    for r in (1, 2, 3):
        second.append(lax.ppermute(first[r], "seq", SWAP_CORE))

    q, *kvs = project(tokens, shift, scale, wq, wk, wv, gq, gk)
    q_core = lax.ppermute(q, "seq", SWAP_CORE)
    q_x = lax.ppermute(q, "seq", SWAP_X)
    q_xc = lax.ppermute(q_x, "seq", SWAP_CORE)
    qs = (q, q_core, q_x, q_xc)

    gathered = [[], [], [], []]
    for h in range(GROUP_HEADS):
        kv = kvs[h]
        below = lax.ppermute(kv, "seq", Z_UP)
        above = lax.ppermute(kv, "seq", Z_DOWN)
        far_a = lax.ppermute(below[:256], "seq", Z_UP)
        far_b = lax.ppermute(above[256:], "seq", Z_DOWN)
        keep, send = attend(qs, (kv, below, above, far_a, far_b), h)
        mine, away = combine_core(keep, lax.ppermute(send, "seq", SWAP_CORE))
        att = combine_x(mine, lax.ppermute(away, "seq", SWAP_X))
        gathered[0].append(att)
        for r in (1, 2, 3):
            gathered[r].append(lax.ppermute(att, "head", Y_STEP[r]))
    keep, send = out_project(core, [a for rel in gathered for a in rel], first, second)
    other = lax.ppermute(send, "head", SWAP_XHI)
    return (keep + other.astype(F32)).astype(BF16)


def solution(mesh):
    in_specs = (
        P("seq", None),
        P(),
        P(),
        P(None, "head"),
        P(None, "head"),
        P(None, "head"),
        P("head"),
        P("head"),
        P("head", None),
    )
    out_specs = P("seq", "head")
    return jax.shard_map(shards, mesh=mesh, in_specs=in_specs, out_specs=out_specs, check_vma=False)
```

time: 285 us -> 151 us (0.53)
  waiting for transfers between devices: 168 us -> 34.2 us
  matrix products: 81.1 us -> 0 us
  Pallas kernels: 0 us -> 60.5 us
  starting transfers between devices: 0.27 us -> 44.1 us
  between operations: 13.3 us -> 0.36 us
  other arithmetic: 9.59 us -> 2.31 us
  local copies, waits for them, and re-layouts: 12.2 us -> 9.02 us
    unnamed x4 -> x0, waiting for transfers between devices: 92 us -> none
    dot_general x12 -> x0, matrix products: 81.1 us -> none  [the longest x4 31.6 us: attend(): jnp.einsum('qhd,khd->hqk', queries, key_block, preferred_element_type=jnp...]
    all_gather x2 -> x0, waiting for transfers between devices: 76.2 us -> none  [the longest x1 45 us: shards(): lax.all_gather(value_local, 'seq', axis=0, tiled=True)]
    pallas_call x0 -> x11, Pallas kernels: none -> 60.5 us  [the longest x3 21 us: attend(): pl.pallas_call(attend_kernel, grid=(1,), in_specs=[pl.BlockSpec((ROWS, HD...]
    ppermute x0 -> x37, starting transfers between devices: none -> 44.1 us  [the longest x9 11 us: shards(): gathered[r].append(lax.ppermute(att, 'head', Y_STEP[r]))]
    ppermute x0 -> x37, waiting for transfers between devices: none -> 34.2 us  [the longest x1 14 us: shards(): other = lax.ppermute(send, 'head', SWAP_XHI)]
    unnamed x16 -> x74, local copies, waits for them, and re-layouts: 10.8 us -> 3.61 us
    reduce_sum x4 -> x0, other arithmetic: 5.07 us -> none  [the longest x1 3.4 us: modulate(): center = jnp.mean(values, axis=-1, keepdims=True)]
  transfers between devices with their start and end apart: 3 -> 37, of which waited for: 3 -> 10; matrix products, arithmetic and copies ran while one was open for 5% -> 2% of each run, Pallas kernels for 0% -> 22%
where the time goes in v1:
time: 151 us; the launch traced here: 150 us
  Pallas kernels  60.5 us (40%)
  starting transfers between devices  44.1 us (29%)
  waiting for transfers between devices  34.2 us (23%)
  local copies, waits for them, and re-layouts  9.02 us (6%)
  other arithmetic  2.31 us (2%)
    pallas_call x3, Pallas kernels, attend(): pl.pallas_call(attend_kernel, grid=(1,), in_specs=[pl.BlockSpec((ROWS, HD...  21 us
    pallas_call x1, Pallas kernels, project(): pl.pallas_call(qkv_kernel, grid=(nk,), in_specs=[whole((ROWS, D)), whole(...  19.2 us
    ppermute x1, waiting for transfers between devices, shards(): other = lax.ppermute(send, 'head', SWAP_XHI)  14 us
    ppermute x9, starting transfers between devices, shards(): gathered[r].append(lax.ppermute(att, 'head', Y_STEP[r]))  11 us
    pallas_call x1, Pallas kernels, out_project(): pl.pallas_call(out_kernel, grid=(OUT_COLS // 128,), in_specs=[pl.BlockSpe...  8.25 us
    ppermute x3, starting transfers between devices, shards(): above = lax.ppermute(kv, 'seq', Z_DOWN)  8.02 us
    ppermute x9, waiting for transfers between devices, shards(): gathered[r].append(lax.ppermute(att, 'head', Y_STEP[r]))  7.55 us
    ppermute x3, starting transfers between devices, shards(): far_b = lax.ppermute(above[256:], 'seq', Z_DOWN)  7.09 us
  transfers between devices with their start and end apart: 37, of which 10 were waited for; matrix products, arithmetic and copies ran while one was open for 2% of the time, Pallas kernels for 22%

profile of v1, /device:TPU:0, one launch (start us, length us, event | category | flops | bytes accessed | tf_op | source)
XLA Modules:
  0.0 150.5 jit_solution(16639013184835192517)
XLA Ops:
  0.0 1.3 reshape.18.gq
  1.3 1.3 reshape.19.gk
  2.5 19.2 %qkv.1 = (bf16[512,384]{1,0:T(8,128)(2,1)}, bf16[512,256]{1,0:T(8,128)(2,1)}, bf16[512,256]{1,0:T(8,128)(2,1)}, bf16[512,256]{1,0:T(8,128)(2,1)}) custom-call(bf16[512,5120]{1,0:T(8,128)(2,1)} %tok.1, f32[1,5120]{1,0:T(1,128)} %bitcast.3, f32[1,5120]{1,0:T(1,128)} %bitcast.4, bf16[5120,384]{1,0:T(8,128)(2,1)} %wq.1, bf16[5120,384]{1,0:T(8,128)(2,1)} %wk.1, ...), custom_call_target="tpu_custom_call" | custom-call | flops 6039797760 | bytes 18000000 | tf_op jit(solution)/shard_map/qkv/pallas_call | solution.py:113
  21.8 1.6 %collective-permute-start.1 = (bf16[512,384]{1,0:T(8,128)(2,1)}, bf16[512,384]{1,0:T(8,128)(2,1)S(1)}, u32[]{:S(2)}, u32[]{:S(2)}) collective-permute-start(bf16[512,384]{1,0:T(8,128)(2,1)} %get-tuple-element.23.q0), channel_id=1, source_target_pairs={{0,64},{8,72},{16,80},{24,88},{32,96},{40,104},{48,112},{56,120},{... | collective-permute-start | bytes 1179656 | tf_op jit(solution)/shard_map/ppermute | solution.py:256
  23.3 4.0 %collective-permute-start.4 = (bf16[512,256]{1,0:T(8,128)(2,1)}, bf16[512,256]{1,0:T(8,128)(2,1)S(1)}, u32[]{:S(2)}, u32[]{:S(2)}) collective-permute-start(bf16[512,256]{1,0:T(8,128)(2,1)} %get-tuple-element.24.k0), channel_id=1, source_target_pairs={{0,48},{8,56},{16,0},{24,8},{32,16},{40,24},{48,32},{56,40},{64,11... | collective-permute-start | bytes 786440 | tf_op jit(solution)/shard_map/ppermute | solution.py:264
  27.4 0.4 collective-permute-start.10
  27.8 1.6 %collective-permute-start.9 = (bf16[512,256]{1,0:T(8,128)(2,1)}, bf16[512,256]{1,0:T(8,128)(2,1)S(1)}, u32[]{:S(2)}, u32[]{:S(2)}) collective-permute-start(bf16[512,256]{1,0:T(8,128)(2,1)} %get-tuple-element.29.k0), channel_id=1, source_target_pairs={{0,16},{8,24},{16,32},{24,40},{32,48},{40,56},{48,0},{56,8},{64,80... | collective-permute-start | bytes 786440 | tf_op jit(solution)/shard_map/ppermute | solution.py:263
  29.4 5.0 %collective-permute-done.4.k2 = bf16[512,256]{1,0:T(8,128)(2,1)S(1)} collective-permute-done((bf16[512,256]{1,0:T(8,128)(2,1)}, bf16[512,256]{1,0:T(8,128)(2,1)S(1)}, u32[]{:S(2)}, u32[]{:S(2)}) %collective-permute-start.4) | collective-permute-done | bytes 262176 | tf_op jit(solution)/shard_map/ppermute | solution.py:264
  34.4 3.6 %collective-permute-start.16 = (bf16[512,256]{1,0:T(8,128)(2,1)}, bf16[512,256]{1,0:T(8,128)(2,1)S(1)}, u32[]{:S(2)}, u32[]{:S(2)}) collective-permute-start(bf16[512,256]{1,0:T(8,128)(2,1)} %get-tuple-element.34.k0), channel_id=1, source_target_pairs={{0,48},{8,56},{16,0},{24,8},{32,16},{40,24},{48,32},{56,40},{64,11... | collective-permute-start | bytes 786440 | tf_op jit(solution)/shard_map/ppermute | solution.py:264
  38.0 2.0 %collective-permute-done.10.k2 = bf16[512,256]{1,0:T(8,128)(2,1)S(1)} collective-permute-done((bf16[512,256]{1,0:T(8,128)(2,1)}, bf16[512,256]{1,0:T(8,128)(2,1)S(1)}, u32[]{:S(2)}, u32[]{:S(2)}) %collective-permute-start.10) | collective-permute-done | bytes 262176 | tf_op jit(solution)/shard_map/ppermute | solution.py:264
  40.1 0.5 collective-permute-start.2
  40.6 0.2 collective-permute-start.15
  40.8 1.2 collective-permute-done.3.k1
  42.0 2.4 %collective-permute-start.12 = (bf16[256,256]{1,0:T(8,128)(2,1)S(1)}, bf16[256,256]{1,0:T(8,128)(2,1)S(1)}, u32[]{:S(2)}, u32[]{:S(2)}) collective-permute-start(bf16[256,256]{1,0:T(8,128)(2,1)S(1)} %slice.27), channel_id=1, source_target_pairs={{0,48},{8,56},{16,0},{24,8},{32,16},{40,24},{48,32},{56,40},{64,11... | collective-permute-start | bytes 393224 | tf_op jit(solution)/shard_map/ppermute | solution.py:266
  44.4 0.2 collective-permute-start.11
  44.6 2.8 %constant_dynamic-slice_fusion = (bf16[384,640]{1,0:T(8,128)(2,1)}, bf16[384,640]{1,0:T(8,128)(2,1)S(1)}, bf16[384,640]{1,0:T(8,128)(2,1)S(1)}, bf16[384,640]{1,0:T(8,128)(2,1)}, bf16[384,640]{1,0:T(8,128)(2,1)S(1)}) fusion(bf16[384,5120]{1,0:T(8,128)(2,1)} %param.17, s32[]{:T(128)S(6)} %select_n.75, s32[]{:T(128)S(6)} %select_n.71, s32[]{:T(128)S(6)} %select_n.69, ...), kind=kLoop, calls=%fused_computation.1 | loop fusion | bytes 4915220 | tf_op jit(solution)/shard_map/dynamic_slice | solution.py:245
  47.5 4.0 %collective-permute-done.15.k1 = bf16[512,256]{1,0:T(8,128)(2,1)S(1)} collective-permute-done((bf16[512,256]{1,0:T(8,128)(2,1)}, bf16[512,256]{1,0:T(8,128)(2,1)S(1)}, u32[]{:S(2)}, u32[]{:S(2)}) %collective-permute-start.15) | collective-permute-done | bytes 262176 | tf_op jit(solution)/shard_map/ppermute | solution.py:263
  51.5 3.2 %collective-permute-start.31 = (bf16[384,640]{1,0:T(8,128)(2,1)S(1)}, bf16[384,640]{1,0:T(8,128)(2,1)S(1)}, u32[]{:S(2)}, u32[]{:S(2)}) collective-permute-start(bf16[384,640]{1,0:T(8,128)(2,1)S(1)} %get-tuple-element.42), channel_id=1, source_target_pairs={{0,2},{1,3},{2,0},{3,1},{4,6},{5,7},{6,4},{7,5},{8,10},{9,11},{10,... | collective-permute-start | bytes 1474568 | tf_op jit(solution)/shard_map/ppermute | solution.py:249
  54.7 0.7 collective-permute-start.30
  55.4 2.6 %collective-permute-start.32 = (bf16[384,640]{1,0:T(8,128)(2,1)S(1)}, bf16[384,640]{1,0:T(8,128)(2,1)S(1)}, u32[]{:S(2)}, u32[]{:S(2)}) collective-permute-start(bf16[384,640]{1,0:T(8,128)(2,1)S(1)} %get-tuple-element.45), channel_id=1, source_target_pairs={{0,3},{1,0},{2,1},{3,2},{4,7},{5,4},{6,5},{7,6},{8,11},{9,8},{10,9... | collective-permute-start | bytes 1474568 | tf_op jit(solution)/shard_map/ppermute | solution.py:249
  58.0 2.1 %collective-permute-start.6 = (bf16[256,256]{1,0:T(8,128)(2,1)S(1)}, bf16[256,256]{1,0:T(8,128)(2,1)S(1)}, u32[]{:S(2)}, u32[]{:S(2)}) collective-permute-start(bf16[256,256]{1,0:T(8,128)(2,1)S(1)} %slice.25), channel_id=1, source_target_pairs={{0,48},{8,56},{16,0},{24,8},{32,16},{40,24},{48,32},{56,40},{64,11... | collective-permute-start | bytes 393224 | tf_op jit(solution)/shard_map/ppermute | solution.py:266
  60.1 0.7 copy-done.21
  60.8 7.0 %attend.4 = (bf16[1024,256]{1,0:T(8,128)(2,1)}, bf16[1024,256]{1,0:T(8,128)(2,1)}) custom-call(bf16[512,384]{1,0:T(8,128)(2,1)} %get-tuple-element.23.q0, bf16[512,384]{1,0:T(8,128)(2,1)} %copy-done.20, bf16[512,384]{1,0:T(8,128)(2,1)} %copy-done.19, bf16[512,384]{1,0:T(8,128)(2,1)} %copy-done.21, bf16[512,256]{1,0:T(8,128)(2,1)} %get-tuple-element.29.k0, ...), custom_call_target="tpu_custom_call" | custom-call | flops 4294967296 | bytes 3000000 | tf_op jit(solution)/shard_map/attend/pallas_call | solution.py:155
  67.9 2.6 %collective-permute-start.18 = (bf16[256,256]{1,0:T(8,128)(2,1)S(1)}, bf16[256,256]{1,0:T(8,128)(2,1)S(1)}, u32[]{:S(2)}, u32[]{:S(2)}) collective-permute-start(bf16[256,256]{1,0:T(8,128)(2,1)S(1)} %slice.29), channel_id=1, source_target_pairs={{0,48},{8,56},{16,0},{24,8},{32,16},{40,24},{48,32},{56,40},{64,11... | collective-permute-start | bytes 393224 | tf_op jit(solution)/shard_map/ppermute | solution.py:266
  70.5 0.6 copy-done.36
  71.1 7.0 %attend.3 = (bf16[1024,256]{1,0:T(8,128)(2,1)}, bf16[1024,256]{1,0:T(8,128)(2,1)}) custom-call(bf16[512,384]{1,0:T(8,128)(2,1)} %get-tuple-element.23.q0, bf16[512,384]{1,0:T(8,128)(2,1)} %copy-done.20, bf16[512,384]{1,0:T(8,128)(2,1)} %copy-done.19, bf16[512,384]{1,0:T(8,128)(2,1)} %copy-done.21, bf16[512,256]{1,0:T(8,128)(2,1)} %get-tuple-element.24.k0, ...), custom_call_target="tpu_custom_call" | custom-call | flops 4294967296 | bytes 3000000 | tf_op jit(solution)/shard_map/attend/pallas_call | solution.py:155
  78.2 0.5 collective-permute-start.7
  78.7 0.1 copy-done.35
  78.9 7.0 %attend.5 = (bf16[1024,256]{1,0:T(8,128)(2,1)}, bf16[1024,256]{1,0:T(8,128)(2,1)}) custom-call(bf16[512,384]{1,0:T(8,128)(2,1)} %get-tuple-element.23.q0, bf16[512,384]{1,0:T(8,128)(2,1)} %copy-done.20, bf16[512,384]{1,0:T(8,128)(2,1)} %copy-done.19, bf16[512,384]{1,0:T(8,128)(2,1)} %copy-done.21, bf16[512,256]{1,0:T(8,128)(2,1)} %get-tuple-element.34.k0, ...), custom_call_target="tpu_custom_call" | custom-call | flops 4294967296 | bytes 3000000 | tf_op jit(solution)/shard_map/attend/pallas_call | solution.py:155
  85.9 0.6 collective-permute-start.19
  86.5 0.1 collective-permute-start.34
  86.6 0.4 collective-permute-start.33
  87.0 0.1 collective-permute-start.35
  87.1 0.7 copy-done.1
  87.8 2.2 %combine_core.4 = (f32[512,256]{1,0:T(8,128)}, bf16[576,128]{1,0:T(8,128)(2,1)}) custom-call(bf16[1024,256]{1,0:T(8,128)(2,1)} %get-tuple-element.30.keep, bf16[1024,256]{1,0:T(8,128)(2,1)} %copy-done.1), custom_call_target="tpu_custom_call" | custom-call | flops 1000000 | bytes 2000000 | tf_op jit(solution)/shard_map/combine_core/pallas_call | solution.py:178
  90.0 0.6 collective-permute-start.14
  90.6 0.2 copy-done
  90.8 2.1 %combine_core.3 = (f32[512,256]{1,0:T(8,128)}, bf16[576,128]{1,0:T(8,128)(2,1)}) custom-call(bf16[1024,256]{1,0:T(8,128)(2,1)} %get-tuple-element.25.keep, bf16[1024,256]{1,0:T(8,128)(2,1)} %copy-done), custom_call_target="tpu_custom_call" | custom-call | flops 1000000 | bytes 2000000 | tf_op jit(solution)/shard_map/combine_core/pallas_call | solution.py:178
  92.9 1.4 collective-permute-start.8
  94.3 2.2 %combine_core.5 = (f32[512,256]{1,0:T(8,128)}, bf16[576,128]{1,0:T(8,128)(2,1)}) custom-call(bf16[1024,256]{1,0:T(8,128)(2,1)} %get-tuple-element.35.keep, bf16[1024,256]{1,0:T(8,128)(2,1)} %copy-done.2), custom_call_target="tpu_custom_call" | custom-call | flops 1000000 | bytes 2000000 | tf_op jit(solution)/shard_map/combine_core/pallas_call | solution.py:178
  96.5 0.8 collective-permute-start.20
  97.3 1.9 %combine_x.4.refs_1_ = bf16[512,128]{1,0:T(8,128)(2,1)} custom-call(f32[512,256]{1,0:T(8,128)} %get-tuple-element.32.mine, bf16[576,128]{1,0:T(8,128)(2,1)} %copy-done.4), custom_call_target="tpu_custom_call" | custom-call | flops 1000000 | bytes 1000000 | tf_op jit(solution)/shard_map/combine_x/pallas_call | solution.py:196
  99.1 0.5 collective-permute-done.8.recv
  99.6 0.1 collective-permute-start.28
  99.7 0.6 copy-done.5
  100.3 1.9 %combine_x.3.refs_0_ = bf16[512,128]{1,0:T(8,128)(2,1)} custom-call(f32[512,256]{1,0:T(8,128)} %get-tuple-element.27.mine, bf16[576,128]{1,0:T(8,128)(2,1)} %copy-done.5), custom_call_target="tpu_custom_call" | custom-call | flops 1000000 | bytes 1000000 | tf_op jit(solution)/shard_map/combine_x/pallas_call | solution.py:196
  102.2 0.9 collective-permute-start.25
  103.0 0.6 collective-permute-start.22
  103.6 2.7 %collective-permute-start.27 = (bf16[512,128]{1,0:T(8,128)(2,1)}, bf16[512,128]{1,0:T(8,128)(2,1)S(1)}, u32[]{:S(2)}, u32[]{:S(2)}) collective-permute-start(bf16[512,128]{1,0:T(8,128)(2,1)} %combine_x.3.refs_0_), channel_id=1, source_target_pairs={{0,3},{1,0},{2,1},{3,2},{4,7},{5,4},{6,5},{7,6},{8,11},{9,8},{10,9... | collective-permute-start | bytes 393224 | tf_op jit(solution)/shard_map/ppermute | solution.py:272
  106.3 1.9 %combine_x.5.refs_2_ = bf16[512,128]{1,0:T(8,128)(2,1)} custom-call(f32[512,256]{1,0:T(8,128)} %get-tuple-element.37.mine, bf16[576,128]{1,0:T(8,128)(2,1)} %copy-done.3), custom_call_target="tpu_custom_call" | custom-call | flops 1000000 | bytes 1000000 | tf_op jit(solution)/shard_map/combine_x/pallas_call | solution.py:196
  108.2 2.0 %collective-permute-start.24 = (bf16[512,128]{1,0:T(8,128)(2,1)}, bf16[512,128]{1,0:T(8,128)(2,1)S(1)}, u32[]{:S(2)}, u32[]{:S(2)}) collective-permute-start(bf16[512,128]{1,0:T(8,128)(2,1)} %combine_x.3.refs_0_), channel_id=1, source_target_pairs={{0,2},{1,3},{2,0},{3,1},{4,6},{5,7},{6,4},{7,5},{8,10},{9,11},{10,... | collective-permute-start | bytes 393224 | tf_op jit(solution)/shard_map/ppermute | solution.py:272
  110.2 0.8 collective-permute-start.21
  111.0 2.5 %collective-permute-start.29 = (bf16[512,128]{1,0:T(8,128)(2,1)}, bf16[512,128]{1,0:T(8,128)(2,1)S(1)}, u32[]{:S(2)}, u32[]{:S(2)}) collective-permute-start(bf16[512,128]{1,0:T(8,128)(2,1)} %combine_x.5.refs_2_), channel_id=1, source_target_pairs={{0,3},{1,0},{2,1},{3,2},{4,7},{5,4},{6,5},{7,6},{8,11},{9,8},{10,9... | collective-permute-start | bytes 393224 | tf_op jit(solution)/shard_map/ppermute | solution.py:272
  113.5 0.3 collective-permute-start.26
  113.7 1.3 collective-permute-start.23
  115.0 0.7 collective-permute-done.24.refs_6_
  115.8 5.0 %collective-permute-done.21.refs_3_ = bf16[512,128]{1,0:T(8,128)(2,1)S(1)} collective-permute-done((bf16[512,128]{1,0:T(8,128)(2,1)}, bf16[512,128]{1,0:T(8,128)(2,1)S(1)}, u32[]{:S(2)}, u32[]{:S(2)}) %collective-permute-start.21) | collective-permute-done | bytes 131104 | tf_op jit(solution)/shard_map/ppermute | solution.py:272
  120.7 0.5 collective-permute-done.26.refs_8_
  121.2 1.4 collective-permute-done.23.refs_5_
  122.7 0.5 copy-done.33
  123.2 8.3 %out_project.1 = (f32[512,640]{1,0:T(8,128)}, bf16[512,640]{1,0:T(8,128)(2,1)}) custom-call(s32[1]{0:T(128)} %bitcast.core, bf16[512,128]{1,0:T(8,128)(2,1)} %combine_x.3.refs_0_, bf16[512,128]{1,0:T(8,128)(2,1)} %combine_x.4.refs_1_, bf16[512,128]{1,0:T(8,128)(2,1)} %combine_x.5.refs_2_, bf16[512,128]{1,0:T(8,128)(2,1)} %copy-done.29, ...), custom_call_target="tpu_custom_call" | custom-call | flops 2013265920 | bytes 8000000 | tf_op jit(solution)/shard_map/out_project/pallas_call | solution.py:225
  131.5 2.7 %collective-permute-start.36 = (bf16[512,640]{1,0:T(8,128)(2,1)}, bf16[512,640]{1,0:T(8,128)(2,1)S(1)}, u32[]{:S(2)}, u32[]{:S(2)}) collective-permute-start(bf16[512,640]{1,0:T(8,128)(2,1)} %get-tuple-element.40), channel_id=1, source_target_pairs={{0,4},{1,5},{2,6},{3,7},{4,0},{5,1},{6,2},{7,3},{8,12},{9,13},{10,... | collective-permute-start | bytes 1966088 | tf_op jit(solution)/shard_map/ppermute | solution.py:274
  134.2 14.0 %collective-permute-done.36 = bf16[512,640]{1,0:T(8,128)(2,1)S(1)} collective-permute-done((bf16[512,640]{1,0:T(8,128)(2,1)}, bf16[512,640]{1,0:T(8,128)(2,1)S(1)}, u32[]{:S(2)}, u32[]{:S(2)}) %collective-permute-start.36) | collective-permute-done | bytes 655392 | tf_op jit(solution)/shard_map/ppermute | solution.py:274
  148.2 2.3 %add_convert_fusion = bf16[512,640]{1,0:T(8,128)(2,1)} fusion(f32[512,640]{1,0:T(8,128)} %get-tuple-element.39, bf16[512,640]{1,0:T(8,128)(2,1)S(1)} %collective-permute-done.36), kind=kLoop, calls=%fused_computation | loop fusion | flops 983040 | bytes 2621440 | tf_op jit(solution)/shard_map/convert_element_type | solution.py:275
  (105 shorter events, 0.4 us)
Async XLA Ops:
  21.8 18.3 %collective-permute-start.1 = (bf16[512,384]{1,0:T(8,128)(2,1)}, bf16[512,384]{1,0:T(8,128)(2,1)S(1)}, u32[]{:S(2)}, u32[]{:S(2)}) collective-permute-start(bf16[512,384]{1,0:T(8,128)(2,1)} %get-tuple-element.23.q0), channel_id=1, source_target_pairs={{0,64},{8,72},{16,80},{24,88},{32,96},{40,104},{48,112},{56,120},{... | collective-permute-start | bytes 1179656 | tf_op jit(solution)/shard_map/ppermute | solution.py:256
  23.3 11.1 %collective-permute-start.4 = (bf16[512,256]{1,0:T(8,128)(2,1)}, bf16[512,256]{1,0:T(8,128)(2,1)S(1)}, u32[]{:S(2)}, u32[]{:S(2)}) collective-permute-start(bf16[512,256]{1,0:T(8,128)(2,1)} %get-tuple-element.24.k0), channel_id=1, source_target_pairs={{0,48},{8,56},{16,0},{24,8},{32,16},{40,24},{48,32},{56,40},{64,11... | collective-permute-start | bytes 786440 | tf_op jit(solution)/shard_map/ppermute | solution.py:264
  27.4 12.7 %collective-permute-start.10 = (bf16[512,256]{1,0:T(8,128)(2,1)}, bf16[512,256]{1,0:T(8,128)(2,1)S(1)}, u32[]{:S(2)}, u32[]{:S(2)}) collective-permute-start(bf16[512,256]{1,0:T(8,128)(2,1)} %get-tuple-element.29.k0), channel_id=1, source_target_pairs={{0,48},{8,56},{16,0},{24,8},{32,16},{40,24},{48,32},{56,40},{64,11... | collective-permute-start | bytes 786440 | tf_op jit(solution)/shard_map/ppermute | solution.py:264
  27.8 12.8 %collective-permute-start.9 = (bf16[512,256]{1,0:T(8,128)(2,1)}, bf16[512,256]{1,0:T(8,128)(2,1)S(1)}, u32[]{:S(2)}, u32[]{:S(2)}) collective-permute-start(bf16[512,256]{1,0:T(8,128)(2,1)} %get-tuple-element.29.k0), channel_id=1, source_target_pairs={{0,16},{8,24},{16,32},{24,40},{32,48},{40,56},{48,0},{56,8},{64,80... | collective-permute-start | bytes 786440 | tf_op jit(solution)/shard_map/ppermute | solution.py:263
  29.4 12.6 %collective-permute-start.3 = (bf16[512,256]{1,0:T(8,128)(2,1)}, bf16[512,256]{1,0:T(8,128)(2,1)S(1)}, u32[]{:S(2)}, u32[]{:S(2)}) collective-permute-start(bf16[512,256]{1,0:T(8,128)(2,1)} %get-tuple-element.24.k0), channel_id=1, source_target_pairs={{0,16},{8,24},{16,32},{24,40},{32,48},{40,56},{48,0},{56,8},{64,80... | collective-permute-start | bytes 786440 | tf_op jit(solution)/shard_map/ppermute | solution.py:263
  34.4 33.4 %copy-start.7 = (bf16[512,256]{1,0:T(8,128)(2,1)}, bf16[512,256]{1,0:T(8,128)(2,1)S(1)}, u32[]{:S(2)}) copy-start(bf16[512,256]{1,0:T(8,128)(2,1)S(1)} %collective-permute-done.4.k2) | copy-start | bytes 786436
  34.4 10.0 %collective-permute-start.16 = (bf16[512,256]{1,0:T(8,128)(2,1)}, bf16[512,256]{1,0:T(8,128)(2,1)S(1)}, u32[]{:S(2)}, u32[]{:S(2)}) collective-permute-start(bf16[512,256]{1,0:T(8,128)(2,1)} %get-tuple-element.34.k0), channel_id=1, source_target_pairs={{0,48},{8,56},{16,0},{24,8},{32,16},{40,24},{48,32},{56,40},{64,11... | collective-permute-start | bytes 786440 | tf_op jit(solution)/shard_map/ppermute | solution.py:264
  40.0 20.0 %copy-start.10 = (bf16[512,256]{1,0:T(8,128)(2,1)}, bf16[512,256]{1,0:T(8,128)(2,1)S(1)}, u32[]{:S(2)}) copy-start(bf16[512,256]{1,0:T(8,128)(2,1)S(1)} %collective-permute-done.10.k2) | copy-start | bytes 786436
  40.0 18.0 %collective-permute-start = (bf16[512,384]{1,0:T(8,128)(2,1)}, bf16[512,384]{1,0:T(8,128)(2,1)S(1)}, u32[]{:S(2)}, u32[]{:S(2)}) collective-permute-start(bf16[512,384]{1,0:T(8,128)(2,1)} %get-tuple-element.23.q0), channel_id=1, source_target_pairs={{0,8},{8,0},{16,24},{24,16},{32,40},{40,32},{48,56},{56,48},{64,72... | collective-permute-start | bytes 1179656 | tf_op jit(solution)/shard_map/ppermute | solution.py:255
  40.1 20.0 %copy-start.19 = (bf16[512,384]{1,0:T(8,128)(2,1)}, bf16[512,384]{1,0:T(8,128)(2,1)S(1)}, u32[]{:S(2)}) copy-start(bf16[512,384]{1,0:T(8,128)(2,1)S(1)} %collective-permute-done.1.q2) | copy-start | bytes 1179652
  40.1 20.0 %collective-permute-start.2 = (bf16[512,384]{1,0:T(8,128)(2,1)S(1)}, bf16[512,384]{1,0:T(8,128)(2,1)S(1)}, u32[]{:S(2)}, u32[]{:S(2)}) collective-permute-start(bf16[512,384]{1,0:T(8,128)(2,1)S(1)} %collective-permute-done.1.q2), channel_id=1, source_target_pairs={{0,8},{8,0},{16,24},{24,16},{32,40},{40,32},{48,56},{56,48},{64,72... | collective-permute-start | bytes 1179656 | tf_op jit(solution)/shard_map/ppermute | solution.py:257
  40.6 19.5 %copy-start.11 = (bf16[512,256]{1,0:T(8,128)(2,1)}, bf16[512,256]{1,0:T(8,128)(2,1)S(1)}, u32[]{:S(2)}) copy-start(bf16[512,256]{1,0:T(8,128)(2,1)S(1)} %collective-permute-done.9.k1) | copy-start | bytes 786436
  40.6 10.9 %collective-permute-start.15 = (bf16[512,256]{1,0:T(8,128)(2,1)}, bf16[512,256]{1,0:T(8,128)(2,1)S(1)}, u32[]{:S(2)}, u32[]{:S(2)}) collective-permute-start(bf16[512,256]{1,0:T(8,128)(2,1)} %get-tuple-element.34.k0), channel_id=1, source_target_pairs={{0,16},{8,24},{16,32},{24,40},{32,48},{40,56},{48,0},{56,8},{64,80... | collective-permute-start | bytes 786440 | tf_op jit(solution)/shard_map/ppermute | solution.py:263
  42.0 25.8 %copy-start.8 = (bf16[512,256]{1,0:T(8,128)(2,1)}, bf16[512,256]{1,0:T(8,128)(2,1)S(1)}, u32[]{:S(2)}) copy-start(bf16[512,256]{1,0:T(8,128)(2,1)S(1)} %collective-permute-done.3.k1) | copy-start | bytes 786436
  42.0 12.7 %collective-permute-start.12 = (bf16[256,256]{1,0:T(8,128)(2,1)S(1)}, bf16[256,256]{1,0:T(8,128)(2,1)S(1)}, u32[]{:S(2)}, u32[]{:S(2)}) collective-permute-start(bf16[256,256]{1,0:T(8,128)(2,1)S(1)} %slice.27), channel_id=1, source_target_pairs={{0,48},{8,56},{16,0},{24,8},{32,16},{40,24},{48,32},{56,40},{64,11... | collective-permute-start | bytes 393224 | tf_op jit(solution)/shard_map/ppermute | solution.py:266
  44.4 23.4 %copy-start.6 = (bf16[512,256]{1,0:T(8,128)(2,1)}, bf16[512,256]{1,0:T(8,128)(2,1)S(1)}, u32[]{:S(2)}) copy-start(bf16[512,256]{1,0:T(8,128)(2,1)S(1)} %collective-permute-done.16.k2) | copy-start | bytes 786436
  44.4 11.0 %collective-permute-start.11 = (bf16[256,256]{1,0:T(8,128)(2,1)S(1)}, bf16[256,256]{1,0:T(8,128)(2,1)S(1)}, u32[]{:S(2)}, u32[]{:S(2)}) collective-permute-start(bf16[256,256]{1,0:T(8,128)(2,1)S(1)} %slice.26), channel_id=1, source_target_pairs={{0,16},{8,24},{16,32},{24,40},{32,48},{40,56},{48,0},{56,8},{64,80... | collective-permute-start | bytes 393224 | tf_op jit(solution)/shard_map/ppermute | solution.py:265
  51.5 16.4 %copy-start.9 = (bf16[512,256]{1,0:T(8,128)(2,1)}, bf16[512,256]{1,0:T(8,128)(2,1)S(1)}, u32[]{:S(2)}) copy-start(bf16[512,256]{1,0:T(8,128)(2,1)S(1)} %collective-permute-done.15.k1) | copy-start | bytes 786436
  51.5 34.4 %collective-permute-start.31 = (bf16[384,640]{1,0:T(8,128)(2,1)S(1)}, bf16[384,640]{1,0:T(8,128)(2,1)S(1)}, u32[]{:S(2)}, u32[]{:S(2)}) collective-permute-start(bf16[384,640]{1,0:T(8,128)(2,1)S(1)} %get-tuple-element.42), channel_id=1, source_target_pairs={{0,2},{1,3},{2,0},{3,1},{4,6},{5,7},{6,4},{7,5},{8,10},{9,11},{10,... | collective-permute-start | bytes 1474568 | tf_op jit(solution)/shard_map/ppermute | solution.py:249
  54.7 5.4 %copy-start.26 = (bf16[256,256]{1,0:T(8,128)(2,1)}, bf16[256,256]{1,0:T(8,128)(2,1)S(1)}, u32[]{:S(2)}) copy-start(bf16[256,256]{1,0:T(8,128)(2,1)S(1)} %collective-permute-done.12.k4) | copy-start | bytes 393220
  54.7 31.8 %collective-permute-start.30 = (bf16[384,640]{1,0:T(8,128)(2,1)S(1)}, bf16[384,640]{1,0:T(8,128)(2,1)S(1)}, u32[]{:S(2)}, u32[]{:S(2)}) collective-permute-start(bf16[384,640]{1,0:T(8,128)(2,1)S(1)} %get-tuple-element.43), channel_id=1, source_target_pairs={{0,1},{1,2},{2,3},{3,0},{4,5},{5,6},{6,7},{7,4},{8,9},{9,10},{10,1... | collective-permute-start | bytes 1474568 | tf_op jit(solution)/shard_map/ppermute | solution.py:249
  55.4 4.7 %copy-start.28 = (bf16[256,256]{1,0:T(8,128)(2,1)}, bf16[256,256]{1,0:T(8,128)(2,1)S(1)}, u32[]{:S(2)}) copy-start(bf16[256,256]{1,0:T(8,128)(2,1)S(1)} %collective-permute-done.11.k3) | copy-start | bytes 393220
  55.4 31.1 %collective-permute-start.32 = (bf16[384,640]{1,0:T(8,128)(2,1)S(1)}, bf16[384,640]{1,0:T(8,128)(2,1)S(1)}, u32[]{:S(2)}, u32[]{:S(2)}) collective-permute-start(bf16[384,640]{1,0:T(8,128)(2,1)S(1)} %get-tuple-element.45), channel_id=1, source_target_pairs={{0,3},{1,0},{2,1},{3,2},{4,7},{5,4},{6,5},{7,6},{8,11},{9,8},{10,9... | collective-permute-start | bytes 1474568 | tf_op jit(solution)/shard_map/ppermute | solution.py:249
  58.0 2.1 %copy-start.20 = (bf16[512,384]{1,0:T(8,128)(2,1)}, bf16[512,384]{1,0:T(8,128)(2,1)S(1)}, u32[]{:S(2)}) copy-start(bf16[512,384]{1,0:T(8,128)(2,1)S(1)} %collective-permute-done.q1) | copy-start | bytes 1179652
  58.0 9.9 %collective-permute-start.6 = (bf16[256,256]{1,0:T(8,128)(2,1)S(1)}, bf16[256,256]{1,0:T(8,128)(2,1)S(1)}, u32[]{:S(2)}, u32[]{:S(2)}) collective-permute-start(bf16[256,256]{1,0:T(8,128)(2,1)S(1)} %slice.25), channel_id=1, source_target_pairs={{0,48},{8,56},{16,0},{24,8},{32,16},{40,24},{48,32},{56,40},{64,11... | collective-permute-start | bytes 393224 | tf_op jit(solution)/shard_map/ppermute | solution.py:266
  60.1 10.4 %collective-permute-start.5 = (bf16[256,256]{1,0:T(8,128)(2,1)S(1)}, bf16[256,256]{1,0:T(8,128)(2,1)S(1)}, u32[]{:S(2)}, u32[]{:S(2)}) collective-permute-start(bf16[256,256]{1,0:T(8,128)(2,1)S(1)} %slice.24), channel_id=1, source_target_pairs={{0,16},{8,24},{16,32},{24,40},{32,48},{40,56},{48,0},{56,8},{64,80... | collective-permute-start | bytes 393224 | tf_op jit(solution)/shard_map/ppermute | solution.py:265
  67.9 10.3 %copy-start.12 = (bf16[1024,256]{1,0:T(8,128)(2,1)S(1)}, bf16[1024,256]{1,0:T(8,128)(2,1)}, u32[]{:S(2)}) copy-start(bf16[1024,256]{1,0:T(8,128)(2,1)} %get-tuple-element.31) | copy-start | bytes 1572868
  67.9 2.6 %copy-start.34 = (bf16[256,256]{1,0:T(8,128)(2,1)}, bf16[256,256]{1,0:T(8,128)(2,1)S(1)}, u32[]{:S(2)}) copy-start(bf16[256,256]{1,0:T(8,128)(2,1)S(1)} %collective-permute-done.6.k4) | copy-start | bytes 393220
  67.9 10.2 %collective-permute-start.18 = (bf16[256,256]{1,0:T(8,128)(2,1)S(1)}, bf16[256,256]{1,0:T(8,128)(2,1)S(1)}, u32[]{:S(2)}, u32[]{:S(2)}) collective-permute-start(bf16[256,256]{1,0:T(8,128)(2,1)S(1)} %slice.29), channel_id=1, source_target_pairs={{0,48},{8,56},{16,0},{24,8},{32,16},{40,24},{48,32},{56,40},{64,11... | collective-permute-start | bytes 393224 | tf_op jit(solution)/shard_map/ppermute | solution.py:266
  70.5 7.7 %collective-permute-start.17 = (bf16[256,256]{1,0:T(8,128)(2,1)S(1)}, bf16[256,256]{1,0:T(8,128)(2,1)S(1)}, u32[]{:S(2)}, u32[]{:S(2)}) collective-permute-start(bf16[256,256]{1,0:T(8,128)(2,1)S(1)} %slice.28), channel_id=1, source_target_pairs={{0,16},{8,24},{16,32},{24,40},{32,48},{40,56},{48,0},{56,8},{64,80... | collective-permute-start | bytes 393224 | tf_op jit(solution)/shard_map/ppermute | solution.py:265
  78.1 8.8 %collective-permute-start.13 = (bf16[1024,256]{1,0:T(8,128)(2,1)S(1)}, bf16[1024,256]{1,0:T(8,128)(2,1)S(1)}, u32[]{:S(2)}, u32[]{:S(2)}) collective-permute-start(bf16[1024,256]{1,0:T(8,128)(2,1)S(1)} %copy-done.12), channel_id=1, source_target_pairs={{0,8},{8,0},{16,24},{24,16},{32,40},{40,32},{48,56},{56,48},{64,72... | collective-permute-start | bytes 1572872 | tf_op jit(solution)/shard_map/ppermute | solution.py:268
  78.2 11.7 %collective-permute-start.7 = (bf16[1024,256]{1,0:T(8,128)(2,1)}, bf16[1024,256]{1,0:T(8,128)(2,1)S(1)}, u32[]{:S(2)}, u32[]{:S(2)}) collective-permute-start(bf16[1024,256]{1,0:T(8,128)(2,1)} %get-tuple-element.26), channel_id=1, source_target_pairs={{0,8},{8,0},{16,24},{24,16},{32,40},{40,32},{48,56},{56,48},{64,72... | collective-permute-start | bytes 1572872 | tf_op jit(solution)/shard_map/ppermute | solution.py:268
  85.9 36.7 %copy-start.13 = (bf16[384,640]{1,0:T(8,128)(2,1)}, bf16[384,640]{1,0:T(8,128)(2,1)S(1)}, u32[]{:S(2)}) copy-start(bf16[384,640]{1,0:T(8,128)(2,1)S(1)} %collective-permute-done.31.refs_14_) | copy-start | bytes 1474564
  85.9 7.0 %collective-permute-start.19 = (bf16[1024,256]{1,0:T(8,128)(2,1)}, bf16[1024,256]{1,0:T(8,128)(2,1)S(1)}, u32[]{:S(2)}, u32[]{:S(2)}) collective-permute-start(bf16[1024,256]{1,0:T(8,128)(2,1)} %get-tuple-element.36), channel_id=1, source_target_pairs={{0,8},{8,0},{16,24},{24,16},{32,40},{40,32},{48,56},{56,48},{64,72... | collective-permute-start | bytes 1572872 | tf_op jit(solution)/shard_map/ppermute | solution.py:268
  86.5 36.1 %copy-start.14 = (bf16[384,640]{1,0:T(8,128)(2,1)}, bf16[384,640]{1,0:T(8,128)(2,1)S(1)}, u32[]{:S(2)}) copy-start(bf16[384,640]{1,0:T(8,128)(2,1)S(1)} %collective-permute-done.30.refs_13_) | copy-start | bytes 1474564
  86.5 15.7 %collective-permute-start.34 = (bf16[384,640]{1,0:T(8,128)(2,1)S(1)}, bf16[384,640]{1,0:T(8,128)(2,1)S(1)}, u32[]{:S(2)}, u32[]{:S(2)}) collective-permute-start(bf16[384,640]{1,0:T(8,128)(2,1)S(1)} %collective-permute-done.31.refs_14_), channel_id=1, source_target_pairs={{0,8},{8,0},{16,24},{24,16},{32,40},{40,32},{48,56},{56,48},{64,72... | collective-permute-start | bytes 1474568 | tf_op jit(solution)/shard_map/ppermute | solution.py:252
  86.6 36.0 %copy-start.15 = (bf16[384,640]{1,0:T(8,128)(2,1)}, bf16[384,640]{1,0:T(8,128)(2,1)S(1)}, u32[]{:S(2)}) copy-start(bf16[384,640]{1,0:T(8,128)(2,1)S(1)} %collective-permute-done.32.refs_15_) | copy-start | bytes 1474564
  86.6 16.5 %collective-permute-start.33 = (bf16[384,640]{1,0:T(8,128)(2,1)S(1)}, bf16[384,640]{1,0:T(8,128)(2,1)S(1)}, u32[]{:S(2)}, u32[]{:S(2)}) collective-permute-start(bf16[384,640]{1,0:T(8,128)(2,1)S(1)} %collective-permute-done.30.refs_13_), channel_id=1, source_target_pairs={{0,8},{8,0},{16,24},{24,16},{32,40},{40,32},{48,56},{56,48},{64,72... | collective-permute-start | bytes 1474568 | tf_op jit(solution)/shard_map/ppermute | solution.py:252
  87.0 21.2 %collective-permute-start.35 = (bf16[384,640]{1,0:T(8,128)(2,1)S(1)}, bf16[384,640]{1,0:T(8,128)(2,1)S(1)}, u32[]{:S(2)}, u32[]{:S(2)}) collective-permute-start(bf16[384,640]{1,0:T(8,128)(2,1)S(1)} %collective-permute-done.32.refs_15_), channel_id=1, source_target_pairs={{0,8},{8,0},{16,24},{24,16},{32,40},{40,32},{48,56},{56,48},{64,72... | collective-permute-start | bytes 1474568 | tf_op jit(solution)/shard_map/ppermute | solution.py:252
  90.0 6.5 %collective-permute-start.14 = (bf16[576,128]{1,0:T(8,128)(2,1)}, bf16[576,128]{1,0:T(8,128)(2,1)S(1)}, u32[]{:S(2)}, u32[]{:S(2)}) collective-permute-start(bf16[576,128]{1,0:T(8,128)(2,1)} %get-tuple-element.33), channel_id=1, source_target_pairs={{0,64},{8,72},{16,80},{24,88},{32,96},{40,104},{48,112},{56,120},{... | collective-permute-start | bytes 442376 | tf_op jit(solution)/shard_map/ppermute | solution.py:269
  92.9 6.7 %collective-permute-start.8 = (bf16[576,128]{1,0:T(8,128)(2,1)}, bf16[576,128]{1,0:T(8,128)(2,1)S(1)}, u32[]{:S(2)}, u32[]{:S(2)}) collective-permute-start(bf16[576,128]{1,0:T(8,128)(2,1)} %get-tuple-element.28), channel_id=1, source_target_pairs={{0,64},{8,72},{16,80},{24,88},{32,96},{40,104},{48,112},{56,120},{... | collective-permute-start | bytes 442376 | tf_op jit(solution)/shard_map/ppermute | solution.py:269
  96.5 7.2 %collective-permute-start.20 = (bf16[576,128]{1,0:T(8,128)(2,1)}, bf16[576,128]{1,0:T(8,128)(2,1)S(1)}, u32[]{:S(2)}, u32[]{:S(2)}) collective-permute-start(bf16[576,128]{1,0:T(8,128)(2,1)} %get-tuple-element.38), channel_id=1, source_target_pairs={{0,64},{8,72},{16,80},{24,88},{32,96},{40,104},{48,112},{56,120},{... | collective-permute-start | bytes 442376 | tf_op jit(solution)/shard_map/ppermute | solution.py:269
  99.6 10.6 %collective-permute-start.28 = (bf16[512,128]{1,0:T(8,128)(2,1)}, bf16[512,128]{1,0:T(8,128)(2,1)S(1)}, u32[]{:S(2)}, u32[]{:S(2)}) collective-permute-start(bf16[512,128]{1,0:T(8,128)(2,1)} %combine_x.4.refs_1_), channel_id=1, source_target_pairs={{0,3},{1,0},{2,1},{3,2},{4,7},{5,4},{6,5},{7,6},{8,11},{9,8},{10,9... | collective-permute-start | bytes 393224 | tf_op jit(solution)/shard_map/ppermute | solution.py:272
  102.2 20.4 %copy-start.16 = (bf16[384,640]{1,0:T(8,128)(2,1)}, bf16[384,640]{1,0:T(8,128)(2,1)S(1)}, u32[]{:S(2)}) copy-start(bf16[384,640]{1,0:T(8,128)(2,1)S(1)} %collective-permute-done.34.refs_18_) | copy-start | bytes 1474564
  102.2 8.8 %collective-permute-start.25 = (bf16[512,128]{1,0:T(8,128)(2,1)}, bf16[512,128]{1,0:T(8,128)(2,1)S(1)}, u32[]{:S(2)}, u32[]{:S(2)}) collective-permute-start(bf16[512,128]{1,0:T(8,128)(2,1)} %combine_x.4.refs_1_), channel_id=1, source_target_pairs={{0,2},{1,3},{2,0},{3,1},{4,6},{5,7},{6,4},{7,5},{8,10},{9,11},{10,... | collective-permute-start | bytes 393224 | tf_op jit(solution)/shard_map/ppermute | solution.py:272
  103.0 19.6 %copy-start.17 = (bf16[384,640]{1,0:T(8,128)(2,1)}, bf16[384,640]{1,0:T(8,128)(2,1)S(1)}, u32[]{:S(2)}) copy-start(bf16[384,640]{1,0:T(8,128)(2,1)S(1)} %collective-permute-done.33.refs_17_) | copy-start | bytes 1474564
  103.0 10.4 %collective-permute-start.22 = (bf16[512,128]{1,0:T(8,128)(2,1)}, bf16[512,128]{1,0:T(8,128)(2,1)S(1)}, u32[]{:S(2)}, u32[]{:S(2)}) collective-permute-start(bf16[512,128]{1,0:T(8,128)(2,1)} %combine_x.4.refs_1_), channel_id=1, source_target_pairs={{0,1},{1,2},{2,3},{3,0},{4,5},{5,6},{6,7},{7,4},{8,9},{9,10},{10,1... | collective-permute-start | bytes 393224 | tf_op jit(solution)/shard_map/ppermute | solution.py:272
  103.6 2.7 %copy-start.3 = (bf16[576,128]{1,0:T(8,128)(2,1)}, bf16[576,128]{1,0:T(8,128)(2,1)S(1)}, u32[]{:S(2)}) copy-start(bf16[576,128]{1,0:T(8,128)(2,1)S(1)} %collective-permute-done.20.recv) | copy-start | bytes 442372
  103.6 10.1 %collective-permute-start.27 = (bf16[512,128]{1,0:T(8,128)(2,1)}, bf16[512,128]{1,0:T(8,128)(2,1)S(1)}, u32[]{:S(2)}, u32[]{:S(2)}) collective-permute-start(bf16[512,128]{1,0:T(8,128)(2,1)} %combine_x.3.refs_0_), channel_id=1, source_target_pairs={{0,3},{1,0},{2,1},{3,2},{4,7},{5,4},{6,5},{7,6},{8,11},{9,8},{10,9... | collective-permute-start | bytes 393224 | tf_op jit(solution)/shard_map/ppermute | solution.py:272
  108.2 14.4 %copy-start.18 = (bf16[384,640]{1,0:T(8,128)(2,1)}, bf16[384,640]{1,0:T(8,128)(2,1)S(1)}, u32[]{:S(2)}) copy-start(bf16[384,640]{1,0:T(8,128)(2,1)S(1)} %collective-permute-done.35.refs_19_) | copy-start | bytes 1474564
  108.2 7.6 %collective-permute-start.24 = (bf16[512,128]{1,0:T(8,128)(2,1)}, bf16[512,128]{1,0:T(8,128)(2,1)S(1)}, u32[]{:S(2)}, u32[]{:S(2)}) collective-permute-start(bf16[512,128]{1,0:T(8,128)(2,1)} %combine_x.3.refs_0_), channel_id=1, source_target_pairs={{0,2},{1,3},{2,0},{3,1},{4,6},{5,7},{6,4},{7,5},{8,10},{9,11},{10,... | collective-permute-start | bytes 393224 | tf_op jit(solution)/shard_map/ppermute | solution.py:272
  110.2 12.4 %copy-start.22 = (bf16[512,128]{1,0:T(8,128)(2,1)}, bf16[512,128]{1,0:T(8,128)(2,1)S(1)}, u32[]{:S(2)}) copy-start(bf16[512,128]{1,0:T(8,128)(2,1)S(1)} %collective-permute-done.28.refs_10_) | copy-start | bytes 393220
  110.2 10.5 %collective-permute-start.21 = (bf16[512,128]{1,0:T(8,128)(2,1)}, bf16[512,128]{1,0:T(8,128)(2,1)S(1)}, u32[]{:S(2)}, u32[]{:S(2)}) collective-permute-start(bf16[512,128]{1,0:T(8,128)(2,1)} %combine_x.3.refs_0_), channel_id=1, source_target_pairs={{0,1},{1,2},{2,3},{3,0},{4,5},{5,6},{6,7},{7,4},{8,9},{9,10},{10,1... | collective-permute-start | bytes 393224 | tf_op jit(solution)/shard_map/ppermute | solution.py:272
  111.0 11.6 %copy-start.23 = (bf16[512,128]{1,0:T(8,128)(2,1)}, bf16[512,128]{1,0:T(8,128)(2,1)S(1)}, u32[]{:S(2)}) copy-start(bf16[512,128]{1,0:T(8,128)(2,1)S(1)} %collective-permute-done.25.refs_7_) | copy-start | bytes 393220
  111.0 9.7 %collective-permute-start.29 = (bf16[512,128]{1,0:T(8,128)(2,1)}, bf16[512,128]{1,0:T(8,128)(2,1)S(1)}, u32[]{:S(2)}, u32[]{:S(2)}) collective-permute-start(bf16[512,128]{1,0:T(8,128)(2,1)} %combine_x.5.refs_2_), channel_id=1, source_target_pairs={{0,3},{1,0},{2,1},{3,2},{4,7},{5,4},{6,5},{7,6},{8,11},{9,8},{10,9... | collective-permute-start | bytes 393224 | tf_op jit(solution)/shard_map/ppermute | solution.py:272
  113.4 9.2 %copy-start.24 = (bf16[512,128]{1,0:T(8,128)(2,1)}, bf16[512,128]{1,0:T(8,128)(2,1)S(1)}, u32[]{:S(2)}) copy-start(bf16[512,128]{1,0:T(8,128)(2,1)S(1)} %collective-permute-done.22.refs_4_) | copy-start | bytes 393220
  113.5 7.8 %collective-permute-start.26 = (bf16[512,128]{1,0:T(8,128)(2,1)}, bf16[512,128]{1,0:T(8,128)(2,1)S(1)}, u32[]{:S(2)}, u32[]{:S(2)}) collective-permute-start(bf16[512,128]{1,0:T(8,128)(2,1)} %combine_x.5.refs_2_), channel_id=1, source_target_pairs={{0,2},{1,3},{2,0},{3,1},{4,6},{5,7},{6,4},{7,5},{8,10},{9,11},{10,... | collective-permute-start | bytes 393224 | tf_op jit(solution)/shard_map/ppermute | solution.py:272
  113.7 8.9 %copy-start.25 = (bf16[512,128]{1,0:T(8,128)(2,1)}, bf16[512,128]{1,0:T(8,128)(2,1)S(1)}, u32[]{:S(2)}) copy-start(bf16[512,128]{1,0:T(8,128)(2,1)S(1)} %collective-permute-done.27.refs_9_) | copy-start | bytes 393220
  113.7 8.8 %collective-permute-start.23 = (bf16[512,128]{1,0:T(8,128)(2,1)}, bf16[512,128]{1,0:T(8,128)(2,1)S(1)}, u32[]{:S(2)}, u32[]{:S(2)}) collective-permute-start(bf16[512,128]{1,0:T(8,128)(2,1)} %combine_x.5.refs_2_), channel_id=1, source_target_pairs={{0,1},{1,2},{2,3},{3,0},{4,5},{5,6},{6,7},{7,4},{8,9},{9,10},{10,1... | collective-permute-start | bytes 393224 | tf_op jit(solution)/shard_map/ppermute | solution.py:272
  115.8 6.9 %copy-start.27 = (bf16[512,128]{1,0:T(8,128)(2,1)}, bf16[512,128]{1,0:T(8,128)(2,1)S(1)}, u32[]{:S(2)}) copy-start(bf16[512,128]{1,0:T(8,128)(2,1)S(1)} %collective-permute-done.24.refs_6_) | copy-start | bytes 393220
  120.7 1.9 %copy-start.29 = (bf16[512,128]{1,0:T(8,128)(2,1)}, bf16[512,128]{1,0:T(8,128)(2,1)S(1)}, u32[]{:S(2)}) copy-start(bf16[512,128]{1,0:T(8,128)(2,1)S(1)} %collective-permute-done.21.refs_3_) | copy-start | bytes 393220
  120.7 2.0 %copy-start.30 = (bf16[512,128]{1,0:T(8,128)(2,1)}, bf16[512,128]{1,0:T(8,128)(2,1)S(1)}, u32[]{:S(2)}) copy-start(bf16[512,128]{1,0:T(8,128)(2,1)S(1)} %collective-permute-done.29.refs_11_) | copy-start | bytes 393220
  121.2 1.5 copy-start.31
  131.5 16.7 %collective-permute-start.36 = (bf16[512,640]{1,0:T(8,128)(2,1)}, bf16[512,640]{1,0:T(8,128)(2,1)S(1)}, u32[]{:S(2)}, u32[]{:S(2)}) collective-permute-start(bf16[512,640]{1,0:T(8,128)(2,1)} %get-tuple-element.40), channel_id=1, source_target_pairs={{0,4},{1,5},{2,6},{3,7},{4,0},{5,1},{6,2},{7,3},{8,12},{9,13},{10,... | collective-permute-start | bytes 1966088 | tf_op jit(solution)/shard_map/ppermute | solution.py:274
  (10 other events, 7.8 us)

commit v2 on v1

v2 whole, which is shorter than its diff:
```python
import functools
import math

import jax
import jax.numpy as jnp
from jax import lax
from jax.experimental import pallas as pl
from jax.experimental.pallas import tpu as pltpu
from jax.sharding import PartitionSpec as P

HD = 128
SOFTCAP = 10.0
EPSILON = 1e-06
GROUP_HEADS = 3
WIDE = GROUP_HEADS * HD
ROWS = 512
D = 5120
OUT_COLS = 640
TOK_PARTS = 4
HALF = ROWS // 2
PACK = HALF + HALF // 8
EXP_SCALE = SOFTCAP * math.log2(math.e)
SCORE_SCALE = 1.0 / (SOFTCAP * math.sqrt(HD))

BF16 = jnp.bfloat16
F32 = jnp.float32


def seq_perm(move):
    pairs = []
    for i in range(16):
        x, z, c = move(i // 8, (i // 2) % 4, i % 2)
        pairs.append((i, x * 8 + (z % 4) * 2 + c))
    return pairs


def head_perm(move):
    pairs = []
    for i in range(8):
        x, y = move(i // 4, i % 4)
        pairs.append((i, x * 4 + (y % 4)))
    return pairs


SWAP_CORE = seq_perm(lambda x, z, c: (x, z, 1 - c))
SWAP_X = seq_perm(lambda x, z, c: (1 - x, z, c))
Z_UP = seq_perm(lambda x, z, c: (x, z + 1, c))
Z_DOWN = seq_perm(lambda x, z, c: (x, z - 1, c))
SWAP_XHI = head_perm(lambda x, y: (1 - x, y))
Y_STEP = [None] + [head_perm(lambda x, y, r=r: (x, y + r)) for r in (1, 2, 3)]


def params(mib=8):
    return pltpu.CompilerParams(vmem_limit_bytes=mib * 2**20)


def cost(flops, nbytes, trans=0):
    return pl.CostEstimate(flops=int(flops), bytes_accessed=int(nbytes), transcendentals=int(trans))


def unit(a):
    return a * lax.rsqrt(jnp.mean(a * a, axis=1, keepdims=True) + EPSILON)


def kv_kernel(tok, shift_h, scale_h, wk, wv, gk_h, kv_o, n_o, tok_v, n_s, wk_v, wv_v, shift, scale, gk, tsem, wsem, nsem, vsem):
    tiles = D // 128
    part = ROWS // TOK_PARTS

    def rows_of(i):
        return pl.ds(i * part, part)

    tok_in = [pltpu.make_async_copy(tok.at[rows_of(i)], tok_v.at[rows_of(i)], tsem.at[i]) for i in range(TOK_PARTS)]
    n_out = [pltpu.make_async_copy(n_s.at[rows_of(i)], n_o.at[rows_of(i)], nsem.at[i]) for i in range(TOK_PARTS)]
    w_in = [pltpu.make_async_copy(w, dst, wsem.at[i]) for i, (w, dst) in enumerate(((wk, wk_v), (wv, wv_v)))]
    vec_in = [
        pltpu.make_async_copy(src, dst, vsem.at[i])
        for i, (src, dst) in enumerate(((shift_h, shift), (scale_h, scale), (gk_h, gk)))
    ]
    for c in vec_in + tok_in:
        c.start()
    for c in vec_in:
        c.wait()

    for p in range(TOK_PARTS):
        tok_in[p].wait()
        if p == TOK_PARTS - 2:
            for c in w_in:
                c.start()

        def stats(i, carry, p=p):
            rows = pl.ds(pl.multiple_of(p * part + i * 32, 32), 32)
            base = tok_v[rows, :128].astype(F32)
            s1 = jnp.zeros((32, 128), F32)
            s2 = jnp.zeros((32, 128), F32)
            for t in range(1, tiles):
                d = tok_v[rows, t * 128 : (t + 1) * 128].astype(F32) - base
                s1 = s1 + d
                s2 = s2 + d * d
            low = s1 * (1.0 / tiles)
            lane_mean = base + low
            mean = jnp.sum(lane_mean, axis=1, keepdims=True) * (1.0 / 128)
            off = lane_mean - mean
            var = jnp.sum(s2 - s1 * low + tiles * (off * off), axis=1, keepdims=True) * (1.0 / D)
            m = jnp.broadcast_to(mean, (32, 128))
            r = jnp.broadcast_to(lax.rsqrt(var + EPSILON), (32, 128))
            for t in range(tiles):
                cols = slice(t * 128, (t + 1) * 128)
                y = (tok_v[rows, cols].astype(F32) - m) * r
                n_s[rows, cols] = (y * (1.0 + scale[:, cols]) + shift[:, cols]).astype(BF16)
            return carry

        lax.fori_loop(0, part // 32, stats, 0, unroll=2)
        n_out[p].start()
    for c in w_in:
        c.wait()
    for h in range(GROUP_HEADS):
        cols = slice(h * HD, (h + 1) * HD)
        w = jnp.concatenate([wk_v[:, cols], wv_v[:, cols]], axis=1)
        d = jnp.dot(n_s[...], w, preferred_element_type=F32)
        at = 2 * h * HD
        kv_o[:, at : at + HD] = (unit(d[:, :HD]) * gk[cols].reshape(1, HD)).astype(BF16)
        kv_o[:, at + HD : at + 2 * HD] = d[:, HD:].astype(BF16)
    for c in n_out:
        c.wait()


def project_kv(tokens, shift, scale, wk, wv, gk):
    hbm = pl.BlockSpec(memory_space=pltpu.HBM)
    vmem = pl.BlockSpec(memory_space=pltpu.VMEM)
    return pl.pallas_call(
        kv_kernel,
        in_specs=[hbm] * 6,
        out_specs=[vmem, hbm],
        out_shape=[jax.ShapeDtypeStruct((ROWS, 2 * WIDE), BF16), jax.ShapeDtypeStruct((ROWS, D), BF16)],
        scratch_shapes=[
            pltpu.VMEM((ROWS, D), BF16),
            pltpu.VMEM((ROWS, D), BF16),
            pltpu.VMEM((D, WIDE), BF16),
            pltpu.VMEM((D, WIDE), BF16),
            pltpu.VMEM((1, D), F32),
            pltpu.VMEM((1, D), F32),
            pltpu.VMEM((WIDE,), F32),
            pltpu.SemaphoreType.DMA((TOK_PARTS,)),
            pltpu.SemaphoreType.DMA((2,)),
            pltpu.SemaphoreType.DMA((TOK_PARTS,)),
            pltpu.SemaphoreType.DMA((3,)),
        ],
        compiler_params=params(56),
        cost_estimate=cost(2 * ROWS * D * WIDE * 2, 18e6),
        name="project_kv",
    )(tokens, shift.reshape(1, D), scale.reshape(1, D), wk, wv, gk)


def q_kernel(cols, n_h, wq_h, gq_h, wo, q_o, o0, o1, o2, o3, o4, n, wq, gq, blocks, isem, bsem, osem):
    halves = [pl.ds(i * HALF, HALF) for i in range(2)]
    gain_in = pltpu.make_async_copy(gq_h, gq, isem.at[0])
    w_in = pltpu.make_async_copy(wq_h, wq, isem.at[1])
    n_in = [pltpu.make_async_copy(n_h.at[rows], n.at[rows], isem.at[2 + i]) for i, rows in enumerate(halves)]
    outs = (o0, o1, o2, o3, o4)
    block_in = [
        pltpu.make_async_copy(wo.at[:, pl.ds(pl.multiple_of(cols[i] * 128, 128), OUT_COLS)], blocks.at[i], bsem.at[i])
        for i in range(5)
    ]
    block_out = [pltpu.make_async_copy(blocks.at[i], outs[i], osem.at[i]) for i in range(5)]
    for c in [gain_in, w_in] + n_in + block_in:
        c.start()
    gain_in.wait()
    w_in.wait()
    for i in range(2):
        n_in[i].wait()
        rows = slice(i * HALF, (i + 1) * HALF)
        d = jnp.dot(n[rows, :], wq[...], preferred_element_type=F32)
        for h in range(GROUP_HEADS):
            at = slice(h * HD, (h + 1) * HD)
            q_o[rows, at] = (unit(d[:, at]) * (gq[at] * SCORE_SCALE).reshape(1, HD)).astype(BF16)
        for j in range(5):
            if i == 0:
                block_in[j].wait()
                block_out[j].start()
    for c in block_out:
        c.wait()


def project_q(cols, n, wq, gq, wo):
    hbm = pl.BlockSpec(memory_space=pltpu.HBM)
    return pl.pallas_call(
        q_kernel,
        in_specs=[pl.BlockSpec(memory_space=pltpu.SMEM)] + [hbm] * 4,
        out_specs=[pl.BlockSpec(memory_space=pltpu.VMEM)] + [hbm] * 5,
        out_shape=[jax.ShapeDtypeStruct((ROWS, WIDE), BF16)] + [jax.ShapeDtypeStruct((WIDE, OUT_COLS), BF16)] * 5,
        scratch_shapes=[
            pltpu.VMEM((ROWS, D), BF16),
            pltpu.VMEM((D, WIDE), BF16),
            pltpu.VMEM((WIDE,), F32),
            pltpu.VMEM((5, WIDE, OUT_COLS), BF16),
            pltpu.SemaphoreType.DMA((4,)),
            pltpu.SemaphoreType.DMA((5,)),
            pltpu.SemaphoreType.DMA((5,)),
        ],
        compiler_params=params(60),
        cost_estimate=cost(2 * ROWS * D * WIDE, 14e6),
        name="project_q",
    )(cols, n, wq, gq, wo)


def mix(qq, kvs, chunk):
    acc = None
    for kv in kvs:
        for s in range(0, kv.shape[0], chunk):
            k = kv[s : s + chunk, :HD]
            v = kv[s : s + chunk, HD:]
            x = lax.dot_general(qq, k, (((1,), (1,)), ((), ())), preferred_element_type=F32)
            p = jnp.exp2(EXP_SCALE * jnp.tanh(x)).astype(BF16)
            d = jnp.dot(p, jnp.concatenate([v, jnp.ones_like(v)], axis=1), preferred_element_type=F32)
            acc = d if acc is None else acc + d
    return acc


def first_kernel(q0, q1, q2, k0, k1, k2, part0, part1):
    for i, q in enumerate((q0, q1, q2)):
        acc = mix(q[...], (k0, k1, k2), 256)
        for half, part in enumerate((part0, part1)):
            rows = acc[half * HALF : (half + 1) * HALF]
            at = i * PACK
            part[at : at + HALF, :] = rows[:, :HD].astype(BF16)
            for p in range(HALF // 128):
                t = jnp.transpose(rows[p * 128 : (p + 1) * 128, HD:])
                to = at + HALF + 16 * p
                part[to : to + 16, :] = t[:16].astype(BF16)


def attend_first(qs, kvs):
    head = lambda rows, cols: pl.BlockSpec((rows, cols), lambda h: (0, h))
    return pl.pallas_call(
        first_kernel,
        grid=(GROUP_HEADS,),
        in_specs=[head(ROWS, HD)] * 3 + [head(ROWS, 2 * HD)] * 3,
        out_specs=[head(3 * PACK, HD)] * 2,
        out_shape=[jax.ShapeDtypeStruct((3 * PACK, WIDE), BF16)] * 2,
        compiler_params=params(24),
        cost_estimate=cost(3 * 4 * 1536 * 1536 * 256, 6e6, 3 * 2 * 1536 * 1536),
        name="attend_first",
    )(*qs, *kvs)


def last_kernel(q0, q1, q2, q3, n0, n1, n2, k0, k1, part, keep, send):
    for h in range(GROUP_HEADS):
        col = slice(h * HD, (h + 1) * HD)
        wide = slice(2 * h * HD, 2 * (h + 1) * HD)
        for i, (q, out, base) in enumerate(((q0, keep, 0), (q1, send, 0), (q2, keep, PACK), (q3, send, PACK))):
            far = (k0[:, wide], k1[:, wide])
            if i == 3:
                acc = mix(q[:, col], (n0[:, wide], n1[:, wide], n2[:, wide]) + far, 256)
                mixture, totals = acc[:, :HD], None
            else:
                acc = mix(q[:, col], far, 256)
                old = part[i * PACK : (i + 1) * PACK, col].astype(F32)
                mixture, totals = acc[:, :HD] + old[:HALF], old[HALF:]
            out[base : base + HALF, col] = mixture.astype(BF16)
            for p in range(HALF // 128):
                t = jnp.transpose(acc[p * 128 : (p + 1) * 128, HD:])[:16]
                if totals is not None:
                    t = t + totals[16 * p : 16 * (p + 1)]
                at = base + HALF + 16 * p
                out[at : at + 16, col] = t.astype(BF16)


def attend_last(half, qs, kvs, part):
    whole = lambda shape: pl.BlockSpec(shape, lambda j: (0, 0))
    return pl.pallas_call(
        last_kernel,
        grid=(1,),
        in_specs=[pl.BlockSpec((HALF, WIDE), lambda j: (half, 0))] * 4
        + [whole((ROWS, 2 * WIDE))] * 3
        + [whole((256, 2 * WIDE))] * 2
        + [whole((3 * PACK, WIDE))],
        out_specs=[whole((2 * PACK, WIDE))] * 2,
        out_shape=[jax.ShapeDtypeStruct((2 * PACK, WIDE), BF16)] * 2,
        compiler_params=params(24),
        cost_estimate=cost(3 * 4 * 1024 * 1024 * 256, 4e6, 3 * 2 * 1024 * 1024),
        name="attend_last",
    )(*qs, *kvs, part)


def combine_core_kernel(keep, recv, mine, away):
    total = keep[...].astype(F32) + recv[...].astype(F32)
    mine[...] = total[:PACK].astype(BF16)
    away[...] = total[PACK:].astype(BF16)


def combine_core(keep, recv):
    return pl.pallas_call(
        combine_core_kernel,
        out_shape=[jax.ShapeDtypeStruct((PACK, WIDE), BF16)] * 2,
        compiler_params=params(),
        cost_estimate=cost(1e6, 2e6),
        name="combine_core",
    )(keep, recv)


def combine_x_kernel(mine, recv, out):
    total = mine[...].astype(F32) + recv[...].astype(F32)
    for h in range(GROUP_HEADS):
        cols = slice(h * HD, (h + 1) * HD)
        for p in range(HALF // 128):
            rows = slice(p * 128, (p + 1) * 128)
            t = total[HALF + 16 * p : HALF + 16 * p + 1, cols]
            out[rows, cols] = (total[rows, cols] / jnp.transpose(jnp.broadcast_to(t, (128, 128)))).astype(BF16)


def combine_x(mine, recv):
    return pl.pallas_call(
        combine_x_kernel,
        out_shape=jax.ShapeDtypeStruct((HALF, WIDE), BF16),
        compiler_params=params(),
        cost_estimate=cost(1e6, 1e6),
        name="combine_x",
    )(mine, recv)


def out_kernel(core, *refs):
    a = refs[:4]
    first = refs[4:8]
    second = refs[8:12]
    keep, send = refs[12:]
    rows = jnp.concatenate([piece[...] for piece in a], axis=1)
    lead = core[0] == 0
    for t in range(OUT_COLS // 128):
        col = slice(t * 128, (t + 1) * 128)
        w = jnp.concatenate(
            [jnp.concatenate([first[r][:, col], second[r][:, col]], axis=1) for r in range(4)], axis=0
        )
        acc = jnp.dot(rows, w, preferred_element_type=F32)
        keep[:, col] = jnp.where(lead, acc[:, :128], acc[:, 128:]).astype(BF16)
        send[:, col] = jnp.where(lead, acc[:, 128:], acc[:, :128]).astype(BF16)


def out_project(core, attended, first, second):
    vmem = pl.BlockSpec(memory_space=pltpu.VMEM)
    return pl.pallas_call(
        out_kernel,
        in_specs=[pl.BlockSpec(memory_space=pltpu.SMEM)] + [vmem] * 12,
        out_specs=[vmem, vmem],
        out_shape=[jax.ShapeDtypeStruct((HALF, OUT_COLS), BF16)] * 2,
        compiler_params=params(16),
        cost_estimate=cost(2 * HALF * 1536 * 1280, 6e6),
        name="out_project",
    )(core.reshape(1), *attended, *first, *second)


def final_kernel(keep, recv, *rest):
    rest[-1][...] = (keep[...].astype(F32) + recv[...].astype(F32)).astype(BF16)


def finish(half, keep, recv, out=None):
    whole = pl.BlockSpec((HALF, OUT_COLS), lambda j: (0, 0))
    return pl.pallas_call(
        final_kernel,
        grid=(1,),
        in_specs=[whole] * 2 + ([] if out is None else [pl.BlockSpec(memory_space=pl.ANY)]),
        out_specs=pl.BlockSpec((HALF, OUT_COLS), lambda j: (half, 0)),
        out_shape=jax.ShapeDtypeStruct((ROWS, OUT_COLS), BF16),
        input_output_aliases={} if out is None else {2: 0},
        compiler_params=params(8),
        cost_estimate=cost(1e6, 1e6),
        name="finish",
    )(*([keep, recv] if out is None else [keep, recv, out]))


def shards(tokens, shift, scale, wq, wk, wv, gq, gk, wo):
    seq = lax.axis_index("seq")
    head = lax.axis_index("head")
    core = seq % 2
    x_hi, y = head // 4, head % 4

    kv, normed = project_kv(tokens, shift, scale, wk, wv, gk)
    below = lax.ppermute(kv, "seq", Z_UP)
    above = lax.ppermute(kv, "seq", Z_DOWN)

    def column(side, r):
        return (((x_hi + side) % 2) * 4 + (y + r) % 4) * (OUT_COLS // 128)

    cols = jnp.stack([column(core, r) for r in range(4)] + [column(1 - core, 0)])
    q, *blocks = project_q(cols, normed, wq, gq, wo)
    q_core = lax.ppermute(q, "seq", SWAP_CORE)
    q_x = lax.ppermute(q, "seq", SWAP_X)
    first = [blocks[0]] + [lax.ppermute(blocks[r], "head", Y_STEP[r]) for r in (1, 2, 3)]
    q_xc = lax.ppermute(q_x, "seq", SWAP_CORE)
    far_a = lax.ppermute(below[:256], "seq", Z_UP)
    far_b = lax.ppermute(above[256:], "seq", Z_DOWN)
    qs = (q, q_core, q_x, q_xc)
    parts = attend_first(qs[:3], (kv, below, above))
    part, *first[1:] = lax.optimization_barrier((parts[0], *first[1:]))
    parts = [part, parts[1]]
    second = [blocks[4]] + [lax.ppermute(first[r], "seq", SWAP_CORE) for r in (1, 2, 3)]

    out = None
    for half in range(2):
        keep, send = attend_last(half, qs, (kv, below, above, far_a, far_b), parts[half])
        mine, away = combine_core(keep, lax.ppermute(send, "seq", SWAP_CORE))
        if half == 0:
            away, parts[1], *second[1:] = lax.optimization_barrier((away, parts[1], *second[1:]))
        recv = lax.ppermute(away, "seq", SWAP_X)
        att = combine_x(mine, recv)
        attended = [att] + [lax.ppermute(att, "head", Y_STEP[r]) for r in (1, 2, 3)]
        kept, sent = out_project(core, attended, first, second)
        out = finish(half, kept, lax.ppermute(sent, "head", SWAP_XHI), out)
    return out


def solution(mesh):
    in_specs = (
        P("seq", None),
        P(),
        P(),
        P(None, "head"),
        P(None, "head"),
        P(None, "head"),
        P("head"),
        P("head"),
        P("head", None),
    )
    out_specs = P("seq", "head")
    return jax.shard_map(shards, mesh=mesh, in_specs=in_specs, out_specs=out_specs, check_vma=False)
```

time: 151 us -> 115 us (0.76)
  Pallas kernels: 60.5 us -> 43 us
  starting transfers between devices: 44.1 us -> 34.3 us
  local copies, waits for them, and re-layouts: 9.02 us -> 1.74 us
  other arithmetic: 2.31 us -> 0 us
    pallas_call x11 -> x13, Pallas kernels: 60.5 us -> 43 us  [the longest x1 14.1 us: project_kv(): pl.pallas_call(kv_kernel, in_specs=[hbm] * 6, out_specs=[vmem, hbm], out_...]
    ppermute x19 -> x16, waiting for transfers between devices: 22 us -> 27.6 us  [the longest x6 9.35 us: shards(): attended = [att] + [lax.ppermute(att, 'head', Y_STEP[r]) for r in (1, 2, 3)]]
    ppermute x3 -> x1, waiting for transfers between devices: 5.14 us -> 0.01 us  [shards(): below = lax.ppermute(kv, 'seq', Z_UP)]
    ppermute x3 -> x1, starting transfers between devices: 7.09 us -> 3.02 us  [shards(): far_b = lax.ppermute(above[256:], 'seq', Z_DOWN)]
    ppermute x3 -> x1, starting transfers between devices: 8.02 us -> 4.19 us  [shards(): above = lax.ppermute(kv, 'seq', Z_DOWN)]
    dynamic_slice x1 -> x0, local copies, waits for them, and re-layouts: 2.82 us -> none  [columns(): return lax.dynamic_slice(wo, (0, col * OUT_COLS), (WIDE, OUT_COLS))]
    unnamed x74 -> x10, local copies, waits for them, and re-layouts: 3.61 us -> 1.01 us
    reshape x2 -> x0, local copies, waits for them, and re-layouts: 2.53 us -> none  [the longest x1 1.28 us: project(): gq.reshape(1, WIDE)]
  transfers between devices with their start and end apart: 37 -> 25, of which waited for: 10 -> 10; matrix products, arithmetic and copies ran while one was open for 2% -> 1% of each run, Pallas kernels for 22% -> 22%
where the time goes in v2:
time: 115 us; the launch traced here: 114 us
  Pallas kernels  43 us (37%)
  waiting for transfers between devices  34.9 us (30%)
  starting transfers between devices  34.3 us (30%)
  local copies, waits for them, and re-layouts  1.74 us (2%)
    pallas_call x1, Pallas kernels, project_kv(): pl.pallas_call(kv_kernel, in_specs=[hbm] * 6, out_specs=[vmem, hbm], out_...  14.1 us
    ppermute x6, waiting for transfers between devices, shards(): attended = [att] + [lax.ppermute(att, 'head', Y_STEP[r]) for r in (1, 2, 3)]  9.35 us
    pallas_call x1, Pallas kernels, attend_first(): pl.pallas_call(first_kernel, grid=(GROUP_HEADS,), in_specs=[head(ROWS, HD...  9.32 us
    ppermute x6, starting transfers between devices, shards(): attended = [att] + [lax.ppermute(att, 'head', Y_STEP[r]) for r in (1, 2, 3)]  8.55 us
    pallas_call x1, Pallas kernels, project_q(): pl.pallas_call(q_kernel, in_specs=[pl.BlockSpec(memory_space=pltpu.SMEM)]...  8.41 us
    ppermute x2, waiting for transfers between devices, shards(): out = finish(half, kept, lax.ppermute(sent, 'head', SWAP_XHI), out)  7.77 us
    ppermute x3, starting transfers between devices, shards(): lax.ppermute(blocks[r], 'head', Y_STEP[r])  6.65 us
    pallas_call x2, Pallas kernels, attend_last(): pl.pallas_call(last_kernel, grid=(1,), in_specs=[pl.BlockSpec((HALF, WIDE...  6.57 us
  transfers between devices with their start and end apart: 25, of which 10 were waited for; matrix products, arithmetic and copies ran while one was open for 1% of the time, Pallas kernels for 22%

profile of v2, /device:TPU:0, one launch (start us, length us, event | category | flops | bytes accessed | tf_op | source)
XLA Modules:
  0.0 114.1 jit_solution(1800684677492001368)
XLA Ops:
  0.0 14.1 %project_kv.1 = (bf16[512,768]{1,0:T(8,128)(2,1)}, bf16[512,5120]{1,0:T(8,128)(2,1)}) custom-call(bf16[512,5120]{1,0:T(8,128)(2,1)} %tok.1, f32[1,5120]{1,0:T(1,128)} %bitcast.8, f32[1,5120]{1,0:T(1,128)} %bitcast.9, bf16[5120,384]{1,0:T(8,128)(2,1)} %wk.1, bf16[5120,384]{1,0:T(8,128)(2,1)} %wv.1, f32[384]{0:T(512)} %gk_h.1), custom_call_target="tpu_custom_call" | custom-call | flops 4026531840 | bytes 18000000 | tf_op jit(solution)/shard_map/project_kv/pallas_call | solution.py:130
  14.1 4.2 %collective-permute-start.4 = (bf16[512,768]{1,0:T(8,128)(2,1)}, bf16[512,768]{1,0:T(8,128)(2,1)S(1)}, u32[]{:S(2)}, u32[]{:S(2)}) collective-permute-start(bf16[512,768]{1,0:T(8,128)(2,1)} %get-tuple-element.38.k0.n0), channel_id=1, source_target_pairs={{0,48},{8,56},{16,0},{24,8},{32,16},{40,24},{48,32},{56,40},{64,11... | collective-permute-start | bytes 2359304 | tf_op jit(solution)/shard_map/ppermute | solution.py:378
  18.3 0.0 collective-permute-start.3
  18.3 0.7 stack.23.cols
  19.0 8.4 %project_q.1 = (bf16[512,384]{1,0:T(8,128)(2,1)}, bf16[384,640]{1,0:T(8,128)(2,1)}, bf16[384,640]{1,0:T(8,128)(2,1)}, bf16[384,640]{1,0:T(8,128)(2,1)}, bf16[384...) custom-call(s32[5]{0:T(128)} %stack.23.cols, bf16[512,5120]{1,0:T(8,128)(2,1)} %get-tuple-element.36.n_h, ...), custom_call_target="tpu_custom_call" | custom-call | flops 2013265920 | bytes 14000000 | tf_op jit(solution)/shard_map/project_q/pallas_call | solution.py:186
  27.4 1.6 %collective-permute-start.7 = (bf16[384,640]{1,0:T(8,128)(2,1)}, bf16[384,640]{1,0:T(8,128)(2,1)S(1)}, u32[]{:S(2)}, u32[]{:S(2)}) collective-permute-start(bf16[384,640]{1,0:T(8,128)(2,1)} %get-tuple-element.40), channel_id=1, source_target_pairs={{0,1},{1,2},{2,3},{3,0},{4,5},{5,6},{6,7},{7,4},{8,9},{9,10},{10,1... | collective-permute-start | bytes 1474568 | tf_op jit(solution)/shard_map/ppermute | solution.py:387
  29.0 1.5 %collective-permute-start.1 = (bf16[512,384]{1,0:T(8,128)(2,1)}, bf16[512,384]{1,0:T(8,128)(2,1)S(1)}, u32[]{:S(2)}, u32[]{:S(2)}) collective-permute-start(bf16[512,384]{1,0:T(8,128)(2,1)} %get-tuple-element.37.q0), channel_id=1, source_target_pairs={{0,64},{8,72},{16,80},{24,88},{32,96},{40,104},{48,112},{56,120},{... | collective-permute-start | bytes 1179656 | tf_op jit(solution)/shard_map/ppermute | solution.py:386
  30.5 0.0 collective-permute-start
  30.5 4.9 %collective-permute-done.4.k2.n2 = bf16[512,768]{1,0:T(8,128)(2,1)S(1)} collective-permute-done((bf16[512,768]{1,0:T(8,128)(2,1)}, bf16[512,768]{1,0:T(8,128)(2,1)S(1)}, u32[]{:S(2)}, u32[]{:S(2)}) %collective-permute-start.4) | collective-permute-done | bytes 786464 | tf_op jit(solution)/shard_map/ppermute | solution.py:378
  35.4 3.2 %collective-permute-start.8 = (bf16[384,640]{1,0:T(8,128)(2,1)}, bf16[384,640]{1,0:T(8,128)(2,1)S(1)}, u32[]{:S(2)}, u32[]{:S(2)}) collective-permute-start(bf16[384,640]{1,0:T(8,128)(2,1)} %get-tuple-element.41), channel_id=1, source_target_pairs={{0,2},{1,3},{2,0},{3,1},{4,6},{5,7},{6,4},{7,5},{8,10},{9,11},{10,... | collective-permute-start | bytes 1474568 | tf_op jit(solution)/shard_map/ppermute | solution.py:387
  38.6 0.9 collective-permute-done.1.q2
  39.5 1.8 %collective-permute-start.9 = (bf16[384,640]{1,0:T(8,128)(2,1)}, bf16[384,640]{1,0:T(8,128)(2,1)S(1)}, u32[]{:S(2)}, u32[]{:S(2)}) collective-permute-start(bf16[384,640]{1,0:T(8,128)(2,1)} %get-tuple-element.42), channel_id=1, source_target_pairs={{0,3},{1,0},{2,1},{3,2},{4,7},{5,4},{6,5},{7,6},{8,11},{9,8},{10,9... | collective-permute-start | bytes 1474568 | tf_op jit(solution)/shard_map/ppermute | solution.py:387
  41.4 0.0 collective-permute-done.3.k1.n1
  41.4 0.0 collective-permute-start.2
  41.4 0.0 collective-permute-done.q1
  41.4 3.0 %collective-permute-start.6 = (bf16[256,768]{1,0:T(8,128)(2,1)S(1)}, bf16[256,768]{1,0:T(8,128)(2,1)S(1)}, u32[]{:S(2)}, u32[]{:S(2)}) collective-permute-start(bf16[256,768]{1,0:T(8,128)(2,1)S(1)} %slice.9), channel_id=1, source_target_pairs={{0,48},{8,56},{16,0},{24,8},{32,16},{40,24},{48,32},{56,40},{64,11... | collective-permute-start | bytes 1179656 | tf_op jit(solution)/shard_map/ppermute | solution.py:390
  44.4 0.0 collective-permute-done.7.refs_5_
  44.4 0.0 collective-permute-start.5
  44.5 1.0 copy-done.3
  45.4 9.3 %attend_first.1 = (bf16[864,384]{1,0:T(8,128)(2,1)S(1)}, bf16[864,384]{1,0:T(8,128)(2,1)S(1)}) custom-call(bf16[512,384]{1,0:T(8,128)(2,1)S(1)} %copy-done.3, bf16[512,384]{1,0:T(8,128)(2,1)S(1)} %collective-permute-done.q1, bf16[512,384]{1,0:T(8,128)(2,1)S(1)} %collective-permute-done.1.q2, bf16[512,768]{1,0:T(8,128)(2,1)S(1)} %copy-done.2, ...), custom_call_target="tpu_custom_call" | custom-call | flops 7247757312 | bytes 6000000 | tf_op jit(solution)/shard_map/attend_first/pallas_call | solution.py:234
  54.8 0.0 collective-permute-done.8.refs_6_
  54.8 5.3 %collective-permute-done.9.refs_7_ = bf16[384,640]{1,0:T(8,128)(2,1)S(1)} collective-permute-done((bf16[384,640]{1,0:T(8,128)(2,1)}, bf16[384,640]{1,0:T(8,128)(2,1)S(1)}, u32[]{:S(2)}, u32[]{:S(2)}) %collective-permute-start.9) | collective-permute-done | bytes 491552 | tf_op jit(solution)/shard_map/ppermute | solution.py:387
  60.1 0.0 collective-permute-start.11
  60.1 0.5 collective-permute-start.12
  60.6 0.0 collective-permute-done.2.q3
  60.6 0.0 collective-permute-start.13
  60.6 0.0 collective-permute-done.6.k1
  60.6 0.0 collective-permute-done.5.k0
  60.7 3.3 %attend_last.2 = (bf16[576,384]{1,0:T(8,128)(2,1)S(1)}, bf16[576,384]{1,0:T(8,128)(2,1)S(1)}) custom-call(bf16[512,384]{1,0:T(8,128)(2,1)S(1)} %copy-done.4, bf16[512,384]{1,0:T(8,128)(2,1)S(1)} %collective-permute-done.q1, bf16[512,384]{1,0:T(8,128)(2,1)S(1)} %collective-permute-done.1.q2, bf16[512,384]{1,0:T(8,128)(2,1)S(1)} %collective-permute-done.2.q3, ...), custom_call_target="tpu_custom_call" | custom-call | flops 3221225472 | bytes 4000000 | tf_op jit(solution)/shard_map/attend_last/pallas_call | solution.py:270
  64.0 0.5 collective-permute-start.10
  64.5 1.4 %collective-permute-done.10.recv = bf16[576,384]{1,0:T(8,128)(2,1)S(1)} collective-permute-done((bf16[576,384]{1,0:T(8,128)(2,1)S(1)}, bf16[576,384]{1,0:T(8,128)(2,1)S(1)}, u32[]{:S(2)}, u32[]{:S(2)}) %collective-permute-start.10) | collective-permute-done | bytes 442400 | tf_op jit(solution)/shard_map/ppermute | solution.py:400
  65.9 0.1 combine_core.2
  66.0 0.0 collective-permute-done.11.refs_9_
  66.1 0.0 collective-permute-done.13.refs_11_
  66.1 0.0 copy-start
  66.1 3.3 %attend_last.3 = (bf16[576,384]{1,0:T(8,128)(2,1)S(1)}, bf16[576,384]{1,0:T(8,128)(2,1)S(1)}) custom-call(bf16[512,384]{1,0:T(8,128)(2,1)S(1)} %copy-done.4, bf16[512,384]{1,0:T(8,128)(2,1)S(1)} %collective-permute-done.q1, bf16[512,384]{1,0:T(8,128)(2,1)S(1)} %collective-permute-done.1.q2, bf16[512,384]{1,0:T(8,128)(2,1)S(1)} %collective-permute-done.2.q3, ...), custom_call_target="tpu_custom_call" | custom-call | flops 3221225472 | bytes 4000000 | tf_op jit(solution)/shard_map/attend_last/pallas_call | solution.py:270
  69.4 0.4 collective-permute-start.14
  69.8 1.5 %collective-permute-start.20 = (bf16[288,384]{1,0:T(8,128)(2,1)S(1)}, bf16[288,384]{1,0:T(8,128)(2,1)S(1)}, u32[]{:S(2)}, u32[]{:S(2)}) collective-permute-start(bf16[288,384]{1,0:T(8,128)(2,1)S(1)} %get-tuple-element.64), channel_id=1, source_target_pairs={{0,64},{8,72},{16,80},{24,88},{32,96},{40,104},{48,112},{56,120},{... | collective-permute-start | bytes 663560 | tf_op jit(solution)/shard_map/ppermute | solution.py:403
  71.3 0.1 combine_core.3
  71.4 1.5 %collective-permute-start.15 = (bf16[288,384]{1,0:T(8,128)(2,1)S(1)}, bf16[288,384]{1,0:T(8,128)(2,1)S(1)}, u32[]{:S(2)}, u32[]{:S(2)}) collective-permute-start(bf16[288,384]{1,0:T(8,128)(2,1)S(1)} %get-tuple-element.55), channel_id=1, source_target_pairs={{0,64},{8,72},{16,80},{24,88},{32,96},{40,104},{48,112},{56,120},{... | collective-permute-start | bytes 663560 | tf_op jit(solution)/shard_map/ppermute | solution.py:403
  72.9 5.2 %collective-permute-done.20.recv = bf16[288,384]{1,0:T(8,128)(2,1)S(1)} collective-permute-done((bf16[288,384]{1,0:T(8,128)(2,1)S(1)}, bf16[288,384]{1,0:T(8,128)(2,1)S(1)}, u32[]{:S(2)}, u32[]{:S(2)}) %collective-permute-start.20) | collective-permute-done | bytes 221216 | tf_op jit(solution)/shard_map/ppermute | solution.py:403
  78.1 0.2 combine_x.3.refs_0_
  78.3 2.9 %collective-permute-start.23 = (bf16[256,384]{1,0:T(8,128)(2,1)S(1)}, bf16[256,384]{1,0:T(8,128)(2,1)S(1)}, u32[]{:S(2)}, u32[]{:S(2)}) collective-permute-start(bf16[256,384]{1,0:T(8,128)(2,1)S(1)} %combine_x.3.refs_0_), channel_id=1, source_target_pairs={{0,3},{1,0},{2,1},{3,2},{4,7},{5,4},{6,5},{7,6},{8,11},{9,8},{10,9... | collective-permute-start | bytes 589832 | tf_op jit(solution)/shard_map/ppermute | solution.py:405
  81.2 1.8 %collective-permute-start.22 = (bf16[256,384]{1,0:T(8,128)(2,1)S(1)}, bf16[256,384]{1,0:T(8,128)(2,1)S(1)}, u32[]{:S(2)}, u32[]{:S(2)}) collective-permute-start(bf16[256,384]{1,0:T(8,128)(2,1)S(1)} %combine_x.3.refs_0_), channel_id=1, source_target_pairs={{0,2},{1,3},{2,0},{3,1},{4,6},{5,7},{6,4},{7,5},{8,10},{9,11},{10,... | collective-permute-start | bytes 589832 | tf_op jit(solution)/shard_map/ppermute | solution.py:405
  83.0 1.3 %collective-permute-start.21 = (bf16[256,384]{1,0:T(8,128)(2,1)S(1)}, bf16[256,384]{1,0:T(8,128)(2,1)S(1)}, u32[]{:S(2)}, u32[]{:S(2)}) collective-permute-start(bf16[256,384]{1,0:T(8,128)(2,1)S(1)} %combine_x.3.refs_0_), channel_id=1, source_target_pairs={{0,1},{1,2},{2,3},{3,0},{4,5},{5,6},{6,7},{7,4},{8,9},{9,10},{10,1... | collective-permute-start | bytes 589832 | tf_op jit(solution)/shard_map/ppermute | solution.py:405
  84.3 0.0 collective-permute-done.15.recv
  84.3 0.2 combine_x.2.refs_0_
  84.5 2.0 %collective-permute-start.18 = (bf16[256,384]{1,0:T(8,128)(2,1)S(1)}, bf16[256,384]{1,0:T(8,128)(2,1)S(1)}, u32[]{:S(2)}, u32[]{:S(2)}) collective-permute-start(bf16[256,384]{1,0:T(8,128)(2,1)S(1)} %combine_x.2.refs_0_), channel_id=1, source_target_pairs={{0,3},{1,0},{2,1},{3,2},{4,7},{5,4},{6,5},{7,6},{8,11},{9,8},{10,9... | collective-permute-start | bytes 589832 | tf_op jit(solution)/shard_map/ppermute | solution.py:405
  86.5 0.5 collective-permute-start.17
  87.0 2.2 %collective-permute-done.23.refs_3_ = bf16[256,384]{1,0:T(8,128)(2,1)S(1)} collective-permute-done((bf16[256,384]{1,0:T(8,128)(2,1)S(1)}, bf16[256,384]{1,0:T(8,128)(2,1)S(1)}, u32[]{:S(2)}, u32[]{:S(2)}) %collective-permute-start.23) | collective-permute-done | bytes 196640 | tf_op jit(solution)/shard_map/ppermute | solution.py:405
  89.2 0.0 collective-permute-start.16
  89.2 1.4 %collective-permute-done.22.refs_2_ = bf16[256,384]{1,0:T(8,128)(2,1)S(1)} collective-permute-done((bf16[256,384]{1,0:T(8,128)(2,1)S(1)}, bf16[256,384]{1,0:T(8,128)(2,1)S(1)}, u32[]{:S(2)}, u32[]{:S(2)}) %collective-permute-start.22) | collective-permute-done | bytes 196640 | tf_op jit(solution)/shard_map/ppermute | solution.py:405
  90.6 5.8 %collective-permute-done.21.refs_1_ = bf16[256,384]{1,0:T(8,128)(2,1)S(1)} collective-permute-done((bf16[256,384]{1,0:T(8,128)(2,1)S(1)}, bf16[256,384]{1,0:T(8,128)(2,1)S(1)}, u32[]{:S(2)}, u32[]{:S(2)}) %collective-permute-start.21) | collective-permute-done | bytes 196640 | tf_op jit(solution)/shard_map/ppermute | solution.py:405
  96.3 1.2 %out_project.3 = (bf16[256,640]{1,0:T(8,128)(2,1)S(1)}, bf16[256,640]{1,0:T(8,128)(2,1)S(1)}) custom-call(s32[1]{0:T(128)} %bitcast.core, bf16[256,384]{1,0:T(8,128)(2,1)S(1)} %combine_x.3.refs_0_, bf16[256,384]{1,0:T(8,128)(2,1)S(1)} %collective-permute-done.21.refs_1_, bf16[256,384]{1,0:T(8,128)(2,1)S(1)} %collective-permute-done.22.refs_2_, ...), custom_call_target="tpu_custom_call" | custom-call | flops 1006632960 | bytes 6000000 | tf_op jit(solution)/shard_map/out_project/pallas_call | solution.py:340
  97.6 3.1 %collective-permute-start.24 = (bf16[256,640]{1,0:T(8,128)(2,1)S(1)}, bf16[256,640]{1,0:T(8,128)(2,1)S(1)}, u32[]{:S(2)}, u32[]{:S(2)}) collective-permute-start(bf16[256,640]{1,0:T(8,128)(2,1)S(1)} %get-tuple-element.66), channel_id=1, source_target_pairs={{0,4},{1,5},{2,6},{3,7},{4,0},{5,1},{6,2},{7,3},{8,12},{9,13},{10,... | collective-permute-start | bytes 983048 | tf_op jit(solution)/shard_map/ppermute | solution.py:407
  100.7 0.0 collective-permute-done.18.refs_3_
  100.7 0.0 collective-permute-done.17.refs_2_
  100.7 0.0 collective-permute-done.16.refs_1_
  100.7 1.2 %out_project.2 = (bf16[256,640]{1,0:T(8,128)(2,1)S(1)}, bf16[256,640]{1,0:T(8,128)(2,1)S(1)}) custom-call(s32[1]{0:T(128)} %bitcast.core, bf16[256,384]{1,0:T(8,128)(2,1)S(1)} %combine_x.2.refs_0_, bf16[256,384]{1,0:T(8,128)(2,1)S(1)} %collective-permute-done.16.refs_1_, bf16[256,384]{1,0:T(8,128)(2,1)S(1)} %collective-permute-done.17.refs_2_, ...), custom_call_target="tpu_custom_call" | custom-call | flops 1006632960 | bytes 6000000 | tf_op jit(solution)/shard_map/out_project/pallas_call | solution.py:340
  101.9 2.8 %collective-permute-start.19 = (bf16[256,640]{1,0:T(8,128)(2,1)S(1)}, bf16[256,640]{1,0:T(8,128)(2,1)S(1)}, u32[]{:S(2)}, u32[]{:S(2)}) collective-permute-start(bf16[256,640]{1,0:T(8,128)(2,1)S(1)} %get-tuple-element.62), channel_id=1, source_target_pairs={{0,4},{1,5},{2,6},{3,7},{4,0},{5,1},{6,2},{7,3},{8,12},{9,13},{10,... | collective-permute-start | bytes 983048 | tf_op jit(solution)/shard_map/ppermute | solution.py:407
  104.7 3.4 %collective-permute-done.24.recv = bf16[256,640]{1,0:T(8,128)(2,1)S(1)} collective-permute-done((bf16[256,640]{1,0:T(8,128)(2,1)S(1)}, bf16[256,640]{1,0:T(8,128)(2,1)S(1)}, u32[]{:S(2)}, u32[]{:S(2)}) %collective-permute-start.24) | collective-permute-done | bytes 327712 | tf_op jit(solution)/shard_map/ppermute | solution.py:407
  108.1 0.8 finish.2.rest_0_
  108.9 4.4 %collective-permute-done.19.recv = bf16[256,640]{1,0:T(8,128)(2,1)S(1)} collective-permute-done((bf16[256,640]{1,0:T(8,128)(2,1)S(1)}, bf16[256,640]{1,0:T(8,128)(2,1)S(1)}, u32[]{:S(2)}, u32[]{:S(2)}) %collective-permute-start.19) | collective-permute-done | bytes 327712 | tf_op jit(solution)/shard_map/ppermute | solution.py:407
  113.3 0.8 finish.3
  (12 shorter events, 0.1 us)
Async XLA Ops:
  14.1 21.3 %collective-permute-start.4 = (bf16[512,768]{1,0:T(8,128)(2,1)}, bf16[512,768]{1,0:T(8,128)(2,1)S(1)}, u32[]{:S(2)}, u32[]{:S(2)}) collective-permute-start(bf16[512,768]{1,0:T(8,128)(2,1)} %get-tuple-element.38.k0.n0), channel_id=1, source_target_pairs={{0,48},{8,56},{16,0},{24,8},{32,16},{40,24},{48,32},{56,40},{64,11... | collective-permute-start | bytes 2359304 | tf_op jit(solution)/shard_map/ppermute | solution.py:378
  18.3 23.1 %collective-permute-start.3 = (bf16[512,768]{1,0:T(8,128)(2,1)}, bf16[512,768]{1,0:T(8,128)(2,1)S(1)}, u32[]{:S(2)}, u32[]{:S(2)}) collective-permute-start(bf16[512,768]{1,0:T(8,128)(2,1)} %get-tuple-element.38.k0.n0), channel_id=1, source_target_pairs={{0,16},{8,24},{16,32},{24,40},{32,48},{40,56},{48,0},{56,8},{64,80... | collective-permute-start | bytes 2359304 | tf_op jit(solution)/shard_map/ppermute | solution.py:377
  19.0 25.5 %copy-start.2 = (bf16[512,768]{1,0:T(8,128)(2,1)S(1)}, bf16[512,768]{1,0:T(8,128)(2,1)}, u32[]{:S(2)}) copy-start(bf16[512,768]{1,0:T(8,128)(2,1)} %get-tuple-element.38.k0.n0) | copy-start | bytes 2359300
  27.4 17.0 %collective-permute-start.7 = (bf16[384,640]{1,0:T(8,128)(2,1)}, bf16[384,640]{1,0:T(8,128)(2,1)S(1)}, u32[]{:S(2)}, u32[]{:S(2)}) collective-permute-start(bf16[384,640]{1,0:T(8,128)(2,1)} %get-tuple-element.40), channel_id=1, source_target_pairs={{0,1},{1,2},{2,3},{3,0},{4,5},{5,6},{6,7},{7,4},{8,9},{9,10},{10,1... | collective-permute-start | bytes 1474568 | tf_op jit(solution)/shard_map/ppermute | solution.py:387
  29.0 10.5 %collective-permute-start.1 = (bf16[512,384]{1,0:T(8,128)(2,1)}, bf16[512,384]{1,0:T(8,128)(2,1)S(1)}, u32[]{:S(2)}, u32[]{:S(2)}) collective-permute-start(bf16[512,384]{1,0:T(8,128)(2,1)} %get-tuple-element.37.q0), channel_id=1, source_target_pairs={{0,64},{8,72},{16,80},{24,88},{32,96},{40,104},{48,112},{56,120},{... | collective-permute-start | bytes 1179656 | tf_op jit(solution)/shard_map/ppermute | solution.py:386
  30.5 10.9 %collective-permute-start = (bf16[512,384]{1,0:T(8,128)(2,1)}, bf16[512,384]{1,0:T(8,128)(2,1)S(1)}, u32[]{:S(2)}, u32[]{:S(2)}) collective-permute-start(bf16[512,384]{1,0:T(8,128)(2,1)} %get-tuple-element.37.q0), channel_id=1, source_target_pairs={{0,8},{8,0},{16,24},{24,16},{32,40},{40,32},{48,56},{56,48},{64,72... | collective-permute-start | bytes 1179656 | tf_op jit(solution)/shard_map/ppermute | solution.py:385
  35.4 19.4 %collective-permute-start.8 = (bf16[384,640]{1,0:T(8,128)(2,1)}, bf16[384,640]{1,0:T(8,128)(2,1)S(1)}, u32[]{:S(2)}, u32[]{:S(2)}) collective-permute-start(bf16[384,640]{1,0:T(8,128)(2,1)} %get-tuple-element.41), channel_id=1, source_target_pairs={{0,2},{1,3},{2,0},{3,1},{4,6},{5,7},{6,4},{7,5},{8,10},{9,11},{10,... | collective-permute-start | bytes 1474568 | tf_op jit(solution)/shard_map/ppermute | solution.py:387
  39.5 20.6 %collective-permute-start.9 = (bf16[384,640]{1,0:T(8,128)(2,1)}, bf16[384,640]{1,0:T(8,128)(2,1)S(1)}, u32[]{:S(2)}, u32[]{:S(2)}) collective-permute-start(bf16[384,640]{1,0:T(8,128)(2,1)} %get-tuple-element.42), channel_id=1, source_target_pairs={{0,3},{1,0},{2,1},{3,2},{4,7},{5,4},{6,5},{7,6},{8,11},{9,8},{10,9... | collective-permute-start | bytes 1474568 | tf_op jit(solution)/shard_map/ppermute | solution.py:387
  41.4 19.3 %collective-permute-start.2 = (bf16[512,384]{1,0:T(8,128)(2,1)S(1)}, bf16[512,384]{1,0:T(8,128)(2,1)S(1)}, u32[]{:S(2)}, u32[]{:S(2)}) collective-permute-start(bf16[512,384]{1,0:T(8,128)(2,1)S(1)} %collective-permute-done.1.q2), channel_id=1, source_target_pairs={{0,8},{8,0},{16,24},{24,16},{32,40},{40,32},{48,56},{56,48},{64,72... | collective-permute-start | bytes 1179656 | tf_op jit(solution)/shard_map/ppermute | solution.py:388
  41.4 19.3 %copy-start.4 = (bf16[512,384]{1,0:T(8,128)(2,1)S(1)}, bf16[512,384]{1,0:T(8,128)(2,1)}, u32[]{:S(2)}) copy-start(bf16[512,384]{1,0:T(8,128)(2,1)} %get-tuple-element.37.q0) | copy-start | bytes 1179652
  41.4 19.2 %collective-permute-start.6 = (bf16[256,768]{1,0:T(8,128)(2,1)S(1)}, bf16[256,768]{1,0:T(8,128)(2,1)S(1)}, u32[]{:S(2)}, u32[]{:S(2)}) collective-permute-start(bf16[256,768]{1,0:T(8,128)(2,1)S(1)} %slice.9), channel_id=1, source_target_pairs={{0,48},{8,56},{16,0},{24,8},{32,16},{40,24},{48,32},{56,40},{64,11... | collective-permute-start | bytes 1179656 | tf_op jit(solution)/shard_map/ppermute | solution.py:390
  44.4 16.2 %collective-permute-start.5 = (bf16[256,768]{1,0:T(8,128)(2,1)S(1)}, bf16[256,768]{1,0:T(8,128)(2,1)S(1)}, u32[]{:S(2)}, u32[]{:S(2)}) collective-permute-start(bf16[256,768]{1,0:T(8,128)(2,1)S(1)} %slice.8), channel_id=1, source_target_pairs={{0,16},{8,24},{16,32},{24,40},{32,48},{40,56},{48,0},{56,8},{64,80... | collective-permute-start | bytes 1179656 | tf_op jit(solution)/shard_map/ppermute | solution.py:389
  44.4 1.0 copy-start.3
  60.1 5.9 %collective-permute-start.11 = (bf16[384,640]{1,0:T(8,128)(2,1)S(1)}, bf16[384,640]{1,0:T(8,128)(2,1)S(1)}, u32[]{:S(2)}, u32[]{:S(2)}) collective-permute-start(bf16[384,640]{1,0:T(8,128)(2,1)S(1)} %collective-permute-done.7.refs_5_), channel_id=1, source_target_pairs={{0,8},{8,0},{16,24},{24,16},{32,40},{40,32},{48,56},{56,48},{64,72... | collective-permute-start | bytes 1474568 | tf_op jit(solution)/shard_map/ppermute | solution.py:395
  60.1 5.9 %collective-permute-start.12 = (bf16[384,640]{1,0:T(8,128)(2,1)S(1)}, bf16[384,640]{1,0:T(8,128)(2,1)S(1)}, u32[]{:S(2)}, u32[]{:S(2)}) collective-permute-start(bf16[384,640]{1,0:T(8,128)(2,1)S(1)} %collective-permute-done.8.refs_6_), channel_id=1, source_target_pairs={{0,8},{8,0},{16,24},{24,16},{32,40},{40,32},{48,56},{56,48},{64,72... | collective-permute-start | bytes 1474568 | tf_op jit(solution)/shard_map/ppermute | solution.py:395
  60.6 5.4 %collective-permute-start.13 = (bf16[384,640]{1,0:T(8,128)(2,1)S(1)}, bf16[384,640]{1,0:T(8,128)(2,1)S(1)}, u32[]{:S(2)}, u32[]{:S(2)}) collective-permute-start(bf16[384,640]{1,0:T(8,128)(2,1)S(1)} %collective-permute-done.9.refs_7_), channel_id=1, source_target_pairs={{0,8},{8,0},{16,24},{24,16},{32,40},{40,32},{48,56},{56,48},{64,72... | collective-permute-start | bytes 1474568 | tf_op jit(solution)/shard_map/ppermute | solution.py:395
  64.0 2.0 %collective-permute-start.10 = (bf16[576,384]{1,0:T(8,128)(2,1)S(1)}, bf16[576,384]{1,0:T(8,128)(2,1)S(1)}, u32[]{:S(2)}, u32[]{:S(2)}) collective-permute-start(bf16[576,384]{1,0:T(8,128)(2,1)S(1)} %get-tuple-element.45), channel_id=1, source_target_pairs={{0,8},{8,0},{16,24},{24,16},{32,40},{40,32},{48,56},{56,48},{64,72... | collective-permute-start | bytes 1327112 | tf_op jit(solution)/shard_map/ppermute | solution.py:400
  66.1 30.3 %copy-start = (bf16[384,640]{1,0:T(8,128)(2,1)S(1)}, bf16[384,640]{1,0:T(8,128)(2,1)}, u32[]{:S(2)}) copy-start(bf16[384,640]{1,0:T(8,128)(2,1)} %get-tuple-element.56.refs_4_) | copy-start | bytes 1474564
  66.1 30.3 %copy-start.1 = (bf16[384,640]{1,0:T(8,128)(2,1)S(1)}, bf16[384,640]{1,0:T(8,128)(2,1)}, u32[]{:S(2)}) copy-start(bf16[384,640]{1,0:T(8,128)(2,1)} %get-tuple-element.57.refs_8_) | copy-start | bytes 1474564
  69.4 1.9 %collective-permute-start.14 = (bf16[576,384]{1,0:T(8,128)(2,1)S(1)}, bf16[576,384]{1,0:T(8,128)(2,1)S(1)}, u32[]{:S(2)}, u32[]{:S(2)}) collective-permute-start(bf16[576,384]{1,0:T(8,128)(2,1)S(1)} %get-tuple-element.53), channel_id=1, source_target_pairs={{0,8},{8,0},{16,24},{24,16},{32,40},{40,32},{48,56},{56,48},{64,72... | collective-permute-start | bytes 1327112 | tf_op jit(solution)/shard_map/ppermute | solution.py:400
  69.8 8.3 %collective-permute-start.20 = (bf16[288,384]{1,0:T(8,128)(2,1)S(1)}, bf16[288,384]{1,0:T(8,128)(2,1)S(1)}, u32[]{:S(2)}, u32[]{:S(2)}) collective-permute-start(bf16[288,384]{1,0:T(8,128)(2,1)S(1)} %get-tuple-element.64), channel_id=1, source_target_pairs={{0,64},{8,72},{16,80},{24,88},{32,96},{40,104},{48,112},{56,120},{... | collective-permute-start | bytes 663560 | tf_op jit(solution)/shard_map/ppermute | solution.py:403
  71.4 12.9 %collective-permute-start.15 = (bf16[288,384]{1,0:T(8,128)(2,1)S(1)}, bf16[288,384]{1,0:T(8,128)(2,1)S(1)}, u32[]{:S(2)}, u32[]{:S(2)}) collective-permute-start(bf16[288,384]{1,0:T(8,128)(2,1)S(1)} %get-tuple-element.55), channel_id=1, source_target_pairs={{0,64},{8,72},{16,80},{24,88},{32,96},{40,104},{48,112},{56,120},{... | collective-permute-start | bytes 663560 | tf_op jit(solution)/shard_map/ppermute | solution.py:403
  78.3 10.9 %collective-permute-start.23 = (bf16[256,384]{1,0:T(8,128)(2,1)S(1)}, bf16[256,384]{1,0:T(8,128)(2,1)S(1)}, u32[]{:S(2)}, u32[]{:S(2)}) collective-permute-start(bf16[256,384]{1,0:T(8,128)(2,1)S(1)} %combine_x.3.refs_0_), channel_id=1, source_target_pairs={{0,3},{1,0},{2,1},{3,2},{4,7},{5,4},{6,5},{7,6},{8,11},{9,8},{10,9... | collective-permute-start | bytes 589832 | tf_op jit(solution)/shard_map/ppermute | solution.py:405
  81.2 9.4 %collective-permute-start.22 = (bf16[256,384]{1,0:T(8,128)(2,1)S(1)}, bf16[256,384]{1,0:T(8,128)(2,1)S(1)}, u32[]{:S(2)}, u32[]{:S(2)}) collective-permute-start(bf16[256,384]{1,0:T(8,128)(2,1)S(1)} %combine_x.3.refs_0_), channel_id=1, source_target_pairs={{0,2},{1,3},{2,0},{3,1},{4,6},{5,7},{6,4},{7,5},{8,10},{9,11},{10,... | collective-permute-start | bytes 589832 | tf_op jit(solution)/shard_map/ppermute | solution.py:405
  83.0 13.3 %collective-permute-start.21 = (bf16[256,384]{1,0:T(8,128)(2,1)S(1)}, bf16[256,384]{1,0:T(8,128)(2,1)S(1)}, u32[]{:S(2)}, u32[]{:S(2)}) collective-permute-start(bf16[256,384]{1,0:T(8,128)(2,1)S(1)} %combine_x.3.refs_0_), channel_id=1, source_target_pairs={{0,1},{1,2},{2,3},{3,0},{4,5},{5,6},{6,7},{7,4},{8,9},{9,10},{10,1... | collective-permute-start | bytes 589832 | tf_op jit(solution)/shard_map/ppermute | solution.py:405
  84.5 16.1 %collective-permute-start.18 = (bf16[256,384]{1,0:T(8,128)(2,1)S(1)}, bf16[256,384]{1,0:T(8,128)(2,1)S(1)}, u32[]{:S(2)}, u32[]{:S(2)}) collective-permute-start(bf16[256,384]{1,0:T(8,128)(2,1)S(1)} %combine_x.2.refs_0_), channel_id=1, source_target_pairs={{0,3},{1,0},{2,1},{3,2},{4,7},{5,4},{6,5},{7,6},{8,11},{9,8},{10,9... | collective-permute-start | bytes 589832 | tf_op jit(solution)/shard_map/ppermute | solution.py:405
  86.5 14.2 %collective-permute-start.17 = (bf16[256,384]{1,0:T(8,128)(2,1)S(1)}, bf16[256,384]{1,0:T(8,128)(2,1)S(1)}, u32[]{:S(2)}, u32[]{:S(2)}) collective-permute-start(bf16[256,384]{1,0:T(8,128)(2,1)S(1)} %combine_x.2.refs_0_), channel_id=1, source_target_pairs={{0,2},{1,3},{2,0},{3,1},{4,6},{5,7},{6,4},{7,5},{8,10},{9,11},{10,... | collective-permute-start | bytes 589832 | tf_op jit(solution)/shard_map/ppermute | solution.py:405
  89.2 11.5 %collective-permute-start.16 = (bf16[256,384]{1,0:T(8,128)(2,1)S(1)}, bf16[256,384]{1,0:T(8,128)(2,1)S(1)}, u32[]{:S(2)}, u32[]{:S(2)}) collective-permute-start(bf16[256,384]{1,0:T(8,128)(2,1)S(1)} %combine_x.2.refs_0_), channel_id=1, source_target_pairs={{0,1},{1,2},{2,3},{3,0},{4,5},{5,6},{6,7},{7,4},{8,9},{9,10},{10,1... | collective-permute-start | bytes 589832 | tf_op jit(solution)/shard_map/ppermute | solution.py:405
  97.6 10.5 %collective-permute-start.24 = (bf16[256,640]{1,0:T(8,128)(2,1)S(1)}, bf16[256,640]{1,0:T(8,128)(2,1)S(1)}, u32[]{:S(2)}, u32[]{:S(2)}) collective-permute-start(bf16[256,640]{1,0:T(8,128)(2,1)S(1)} %get-tuple-element.66), channel_id=1, source_target_pairs={{0,4},{1,5},{2,6},{3,7},{4,0},{5,1},{6,2},{7,3},{8,12},{9,13},{10,... | collective-permute-start | bytes 983048 | tf_op jit(solution)/shard_map/ppermute | solution.py:407
  101.9 11.3 %collective-permute-start.19 = (bf16[256,640]{1,0:T(8,128)(2,1)S(1)}, bf16[256,640]{1,0:T(8,128)(2,1)S(1)}, u32[]{:S(2)}, u32[]{:S(2)}) collective-permute-start(bf16[256,640]{1,0:T(8,128)(2,1)S(1)} %get-tuple-element.62), channel_id=1, source_target_pairs={{0,4},{1,5},{2,6},{3,7},{4,0},{5,1},{6,2},{7,3},{8,12},{9,13},{10,... | collective-permute-start | bytes 983048 | tf_op jit(solution)/shard_map/ppermute | solution.py:407

commit v3 on v2

--- a/solution.py
+++ b/solution.py
@@ -16,7 +16,7 @@
 ROWS = 512
 D = 5120
 OUT_COLS = 640
-TOK_PARTS = 4
+TOK_PARTS = 2
 HALF = ROWS // 2
 PACK = HALF + HALF // 8
 EXP_SCALE = SOFTCAP * math.log2(math.e)
@@ -62,7 +62,7 @@
     return a * lax.rsqrt(jnp.mean(a * a, axis=1, keepdims=True) + EPSILON)
 
 
-def kv_kernel(tok, shift_h, scale_h, wk, wv, gk_h, kv_o, n_o, tok_v, n_s, wk_v, wv_v, shift, scale, gk, tsem, wsem, nsem, vsem):
+def qkv_kernel(tok, shift_h, scale_h, wq, wk, wv, gq_h, gk_h, q_o, kv_o, tok_v, n_s, wq_v, wk_v, wv_v, shift, scale, gq, gk, tsem, wsem, vsem):
     tiles = D // 128
     part = ROWS // TOK_PARTS
 
@@ -70,11 +70,10 @@
         return pl.ds(i * part, part)
 
     tok_in = [pltpu.make_async_copy(tok.at[rows_of(i)], tok_v.at[rows_of(i)], tsem.at[i]) for i in range(TOK_PARTS)]
-    n_out = [pltpu.make_async_copy(n_s.at[rows_of(i)], n_o.at[rows_of(i)], nsem.at[i]) for i in range(TOK_PARTS)]
-    w_in = [pltpu.make_async_copy(w, dst, wsem.at[i]) for i, (w, dst) in enumerate(((wk, wk_v), (wv, wv_v)))]
+    w_in = [pltpu.make_async_copy(w, dst, wsem.at[i]) for i, (w, dst) in enumerate(((wk, wk_v), (wv, wv_v), (wq, wq_v)))]
     vec_in = [
         pltpu.make_async_copy(src, dst, vsem.at[i])
-        for i, (src, dst) in enumerate(((shift_h, shift), (scale_h, scale), (gk_h, gk)))
+        for i, (src, dst) in enumerate(((shift_h, shift), (scale_h, scale), (gq_h, gq), (gk_h, gk)))
     ]
     for c in vec_in + tok_in:
         c.start()
@@ -83,7 +82,7 @@
 
     for p in range(TOK_PARTS):
         tok_in[p].wait()
-        if p == TOK_PARTS - 2:
+        if p == 0:
             for c in w_in:
                 c.start()
 
@@ -110,8 +109,7 @@
             return carry
 
         lax.fori_loop(0, part // 32, stats, 0, unroll=2)
-        n_out[p].start()
-    for c in w_in:
+    for c in w_in[:2]:
         c.wait()
     for h in range(GROUP_HEADS):
         cols = slice(h * HD, (h + 1) * HD)
@@ -120,87 +118,74 @@
         at = 2 * h * HD
         kv_o[:, at : at + HD] = (unit(d[:, :HD]) * gk[cols].reshape(1, HD)).astype(BF16)
         kv_o[:, at + HD : at + 2 * HD] = d[:, HD:].astype(BF16)
-    for c in n_out:
-        c.wait()
-
-
-def project_kv(tokens, shift, scale, wk, wv, gk):
+    w_in[2].wait()
+    d = jnp.dot(n_s[...], wq_v[...], preferred_element_type=F32)
+    for h in range(GROUP_HEADS):
+        cols = slice(h * HD, (h + 1) * HD)
+        q_o[:, cols] = (unit(d[:, cols]) * (gq[cols] * SCORE_SCALE).reshape(1, HD)).astype(BF16)
+
+
+def project(tokens, shift, scale, wq, wk, wv, gq, gk):
     hbm = pl.BlockSpec(memory_space=pltpu.HBM)
     vmem = pl.BlockSpec(memory_space=pltpu.VMEM)
     return pl.pallas_call(
-        kv_kernel,
-        in_specs=[hbm] * 6,
-        out_specs=[vmem, hbm],
-        out_shape=[jax.ShapeDtypeStruct((ROWS, 2 * WIDE), BF16), jax.ShapeDtypeStruct((ROWS, D), BF16)],
+        qkv_kernel,
+        in_specs=[hbm] * 8,
+        out_specs=[vmem, vmem],
+        out_shape=[jax.ShapeDtypeStruct((ROWS, WIDE), BF16), jax.ShapeDtypeStruct((ROWS, 2 * WIDE), BF16)],
         scratch_shapes=[
             pltpu.VMEM((ROWS, D), BF16),
             pltpu.VMEM((ROWS, D), BF16),
             pltpu.VMEM((D, WIDE), BF16),
             pltpu.VMEM((D, WIDE), BF16),
+            pltpu.VMEM((D, WIDE), BF16),
             pltpu.VMEM((1, D), F32),
             pltpu.VMEM((1, D), F32),
             pltpu.VMEM((WIDE,), F32),
-            pltpu.SemaphoreType.DMA((TOK_PARTS,)),
-            pltpu.SemaphoreType.DMA((2,)),
+            pltpu.VMEM((WIDE,), F32),
             pltpu.SemaphoreType.DMA((TOK_PARTS,)),
             pltpu.SemaphoreType.DMA((3,)),
-        ],
-        compiler_params=params(56),
-        cost_estimate=cost(2 * ROWS * D * WIDE * 2, 18e6),
-        name="project_kv",
-    )(tokens, shift.reshape(1, D), scale.reshape(1, D), wk, wv, gk)
-
-
-def q_kernel(cols, n_h, wq_h, gq_h, wo, q_o, o0, o1, o2, o3, o4, n, wq, gq, blocks, isem, bsem, osem):
-    halves = [pl.ds(i * HALF, HALF) for i in range(2)]
-    gain_in = pltpu.make_async_copy(gq_h, gq, isem.at[0])
-    w_in = pltpu.make_async_copy(wq_h, wq, isem.at[1])
-    n_in = [pltpu.make_async_copy(n_h.at[rows], n.at[rows], isem.at[2 + i]) for i, rows in enumerate(halves)]
-    outs = (o0, o1, o2, o3, o4)
-    block_in = [
-        pltpu.make_async_copy(wo.at[:, pl.ds(pl.multiple_of(cols[i] * 128, 128), OUT_COLS)], blocks.at[i], bsem.at[i])
-        for i in range(5)
-    ]
-    block_out = [pltpu.make_async_copy(blocks.at[i], outs[i], osem.at[i]) for i in range(5)]
-    for c in [gain_in, w_in] + n_in + block_in:
-        c.start()
-    gain_in.wait()
-    w_in.wait()
-    for i in range(2):
-        n_in[i].wait()
-        rows = slice(i * HALF, (i + 1) * HALF)
-        d = jnp.dot(n[rows, :], wq[...], preferred_element_type=F32)
-        for h in range(GROUP_HEADS):
-            at = slice(h * HD, (h + 1) * HD)
-            q_o[rows, at] = (unit(d[:, at]) * (gq[at] * SCORE_SCALE).reshape(1, HD)).astype(BF16)
-        for j in range(5):
-            if i == 0:
-                block_in[j].wait()
-                block_out[j].start()
-    for c in block_out:
-        c.wait()
-
-
-def project_q(cols, n, wq, gq, wo):
-    hbm = pl.BlockSpec(memory_space=pltpu.HBM)
-    return pl.pallas_call(
-        q_kernel,
-        in_specs=[pl.BlockSpec(memory_space=pltpu.SMEM)] + [hbm] * 4,
-        out_specs=[pl.BlockSpec(memory_space=pltpu.VMEM)] + [hbm] * 5,
-        out_shape=[jax.ShapeDtypeStruct((ROWS, WIDE), BF16)] + [jax.ShapeDtypeStruct((WIDE, OUT_COLS), BF16)] * 5,
-        scratch_shapes=[
-            pltpu.VMEM((ROWS, D), BF16),
-            pltpu.VMEM((D, WIDE), BF16),
-            pltpu.VMEM((WIDE,), F32),
-            pltpu.VMEM((5, WIDE, OUT_COLS), BF16),
             pltpu.SemaphoreType.DMA((4,)),
-            pltpu.SemaphoreType.DMA((5,)),
-            pltpu.SemaphoreType.DMA((5,)),
         ],
         compiler_params=params(60),
-        cost_estimate=cost(2 * ROWS * D * WIDE, 14e6),
-        name="project_q",
-    )(cols, n, wq, gq, wo)
+        cost_estimate=cost(2 * ROWS * D * WIDE * 3, 18e6),
+        name="project",
+    )(tokens, shift.reshape(1, D), scale.reshape(1, D), wq, wk, wv, gq, gk)
+
+
+def blocks_kernel(cols, wo, own, up, down, other, sem):
+    mid = WIDE // 2
+
+    def block(i, rows, dst, j):
+        src = wo.at[rows, pl.ds(pl.multiple_of(cols[i] * 128, 128), OUT_COLS)]
+        return pltpu.make_async_copy(src, dst, sem.at[j])
+
+    every = pl.ds(0, WIDE)
+    copies = [
+        block(1, every, up.at[every], 0),
+        block(2, pl.ds(0, mid), up.at[pl.ds(WIDE, mid)], 1),
+        block(3, every, down.at[every], 2),
+        block(2, pl.ds(mid, mid), down.at[pl.ds(WIDE, mid)], 3),
+        block(0, every, own, 4),
+        block(4, every, other, 5),
+    ]
+    for c in copies:
+        c.start()
+    for c in copies:
+        c.wait()
+
+
+def take_blocks(cols, wo):
+    return pl.pallas_call(
+        blocks_kernel,
+        in_specs=[pl.BlockSpec(memory_space=pltpu.SMEM), pl.BlockSpec(memory_space=pltpu.HBM)],
+        out_specs=[pl.BlockSpec(memory_space=pltpu.VMEM)] * 4,
+        out_shape=[jax.ShapeDtypeStruct((rows, OUT_COLS), BF16) for rows in (WIDE, WIDE * 3 // 2, WIDE * 3 // 2, WIDE)],
+        scratch_shapes=[pltpu.SemaphoreType.DMA((6,))],
+        compiler_params=params(60),
+        cost_estimate=cost(1e6, 6e6),
+        name="take_blocks",
+    )(cols, wo)
 
 
 def mix(qq, kvs, chunk):
@@ -318,18 +303,21 @@
     )(mine, recv)
 
 
-def out_kernel(core, *refs):
-    a = refs[:4]
-    first = refs[4:8]
-    second = refs[8:12]
-    keep, send = refs[12:]
-    rows = jnp.concatenate([piece[...] for piece in a], axis=1)
+def out_kernel(core, a0, a1, a2, a3, *refs):
+    first = refs[:5]
+    second = refs[5:10]
+    keep, send = refs[10:]
+    rows = jnp.concatenate([a0[...], a1[...], a2[...], a3[...]], axis=1)
     lead = core[0] == 0
+
+    def stacked(refs, col):
+        own, up, far_up, far_down, down = refs
+        pieces = [own[:, col], up[:WIDE, col], far_up[:, col], far_down[:, col], down[:WIDE, col]]
+        return jnp.concatenate(pieces, axis=0)
+
     for t in range(OUT_COLS // 128):
         col = slice(t * 128, (t + 1) * 128)
-        w = jnp.concatenate(
-            [jnp.concatenate([first[r][:, col], second[r][:, col]], axis=1) for r in range(4)], axis=0
-        )
+        w = jnp.concatenate([stacked(first, col), stacked(second, col)], axis=1)
         acc = jnp.dot(rows, w, preferred_element_type=F32)
         keep[:, col] = jnp.where(lead, acc[:, :128], acc[:, 128:]).astype(BF16)
         send[:, col] = jnp.where(lead, acc[:, 128:], acc[:, :128]).astype(BF16)
@@ -339,7 +327,7 @@
     vmem = pl.BlockSpec(memory_space=pltpu.VMEM)
     return pl.pallas_call(
         out_kernel,
-        in_specs=[pl.BlockSpec(memory_space=pltpu.SMEM)] + [vmem] * 12,
+        in_specs=[pl.BlockSpec(memory_space=pltpu.SMEM)] + [vmem] * 14,
         out_specs=[vmem, vmem],
         out_shape=[jax.ShapeDtypeStruct((HALF, OUT_COLS), BF16)] * 2,
         compiler_params=params(16),
@@ -373,7 +361,7 @@
     core = seq % 2
     x_hi, y = head // 4, head % 4
 
-    kv, normed = project_kv(tokens, shift, scale, wk, wv, gk)
+    q, kv = project(tokens, shift, scale, wq, wk, wv, gq, gk)
     below = lax.ppermute(kv, "seq", Z_UP)
     above = lax.ppermute(kv, "seq", Z_DOWN)
 
@@ -381,29 +369,37 @@
         return (((x_hi + side) % 2) * 4 + (y + r) % 4) * (OUT_COLS // 128)
 
     cols = jnp.stack([column(core, r) for r in range(4)] + [column(1 - core, 0)])
-    q, *blocks = project_q(cols, normed, wq, gq, wo)
     q_core = lax.ppermute(q, "seq", SWAP_CORE)
     q_x = lax.ppermute(q, "seq", SWAP_X)
-    first = [blocks[0]] + [lax.ppermute(blocks[r], "head", Y_STEP[r]) for r in (1, 2, 3)]
+    q_core, cols = lax.optimization_barrier((q_core, cols))
+    own, up, down, other = take_blocks(cols, wo)
+    up = lax.ppermute(up, "head", Y_STEP[1])
+    down = lax.ppermute(down, "head", Y_STEP[3])
     q_xc = lax.ppermute(q_x, "seq", SWAP_CORE)
     far_a = lax.ppermute(below[:256], "seq", Z_UP)
     far_b = lax.ppermute(above[256:], "seq", Z_DOWN)
     qs = (q, q_core, q_x, q_xc)
     parts = attend_first(qs[:3], (kv, below, above))
-    part, *first[1:] = lax.optimization_barrier((parts[0], *first[1:]))
+    part, up, down = lax.optimization_barrier((parts[0], up, down))
     parts = [part, parts[1]]
-    second = [blocks[4]] + [lax.ppermute(first[r], "seq", SWAP_CORE) for r in (1, 2, 3)]
+    second = [lax.ppermute(w, "seq", SWAP_CORE) for w in (up, down)]
+    far = [lax.ppermute(up[WIDE:], "head", Y_STEP[1]), lax.ppermute(down[WIDE:], "head", Y_STEP[3])]
 
     out = None
     for half in range(2):
         keep, send = attend_last(half, qs, (kv, below, above, far_a, far_b), parts[half])
         mine, away = combine_core(keep, lax.ppermute(send, "seq", SWAP_CORE))
         if half == 0:
-            away, parts[1], *second[1:] = lax.optimization_barrier((away, parts[1], *second[1:]))
+            away, parts[1] = lax.optimization_barrier((away, parts[1]))
         recv = lax.ppermute(away, "seq", SWAP_X)
+        if half == 0:
+            recv, *far = lax.optimization_barrier((recv, *far))
+            far_core = [lax.ppermute(w, "seq", SWAP_CORE) for w in far]
         att = combine_x(mine, recv)
         attended = [att] + [lax.ppermute(att, "head", Y_STEP[r]) for r in (1, 2, 3)]
-        kept, sent = out_project(core, attended, first, second)
+        first_w = (own, up, *far, down)
+        second_w = (other, second[0], *far_core, second[1])
+        kept, sent = out_project(core, attended, first_w, second_w)
         out = finish(half, kept, lax.ppermute(sent, "head", SWAP_XHI), out)
     return out
 

time: 115 us -> 105 us (0.913); the launches traced: 114 us -> 105 us
  Pallas kernels: 43 us -> 38.6 us
  starting transfers between devices: 34.3 us -> 32.5 us
  waiting for transfers between devices: 34.9 us -> 33.3 us
    ppermute x1, waiting for transfers between devices: 0.01 us -> 5.92 us  [shards(): below = lax.ppermute(kv, 'seq', Z_UP)]
    ppermute x1, waiting for transfers between devices: 4.87 us -> 0.01 us  [shards(): above = lax.ppermute(kv, 'seq', Z_DOWN)]
    ppermute x2, waiting for transfers between devices: 5.16 us -> 0.66 us  [shards(): recv = lax.ppermute(away, 'seq', SWAP_X)]
    pallas_call x2, Pallas kernels: 22.5 us -> 18.1 us  [the longest x1 14.3 us: project(): pl.pallas_call(qkv_kernel, in_specs=[hbm] * 8, out_specs=[vmem, vmem], ou...]
    ppermute x1, starting transfers between devices: 0.01 us -> 2.07 us  [shards(): below = lax.ppermute(kv, 'seq', Z_UP)]
    ppermute x1, starting transfers between devices: 4.19 us -> 2.2 us  [shards(): above = lax.ppermute(kv, 'seq', Z_DOWN)]
    ppermute x1, waiting for transfers between devices: 0.91 us -> 2.48 us  [shards(): q_x = lax.ppermute(q, 'seq', SWAP_X)]
    ppermute x2, waiting for transfers between devices: 7.77 us -> 9.03 us  [shards(): out = finish(half, kept, lax.ppermute(sent, 'head', SWAP_XHI), out)]
  transfers between devices with their start and end apart: 25 -> 27, of which waited for: 10 -> 12; matrix products, arithmetic and copies ran while one was open for 1% -> 1% of each run, Pallas kernels for 22% -> 19%
where the time goes in v3:
time: 105 us
  Pallas kernels  38.6 us (37%)
  waiting for transfers between devices  33.3 us (32%)
  starting transfers between devices  32.5 us (31%)
    pallas_call x1, Pallas kernels, project(): pl.pallas_call(qkv_kernel, in_specs=[hbm] * 8, out_specs=[vmem, vmem], ou...  14.3 us
    ppermute x6, waiting for transfers between devices, shards(): attended = [att] + [lax.ppermute(att, 'head', Y_STEP[r]) for r in (1, 2, 3)]  9.46 us
    pallas_call x1, Pallas kernels, attend_first(): pl.pallas_call(first_kernel, grid=(GROUP_HEADS,), in_specs=[head(ROWS, HD...  9.31 us
    ppermute x2, waiting for transfers between devices, shards(): out = finish(half, kept, lax.ppermute(sent, 'head', SWAP_XHI), out)  9.03 us
    ppermute x6, starting transfers between devices, shards(): attended = [att] + [lax.ppermute(att, 'head', Y_STEP[r]) for r in (1, 2, 3)]  7.87 us
    pallas_call x2, Pallas kernels, attend_last(): pl.pallas_call(last_kernel, grid=(1,), in_specs=[pl.BlockSpec((HALF, WIDE...  6.57 us
    ppermute x1, waiting for transfers between devices, shards(): below = lax.ppermute(kv, 'seq', Z_UP)  5.92 us
    ppermute x2, starting transfers between devices, shards(): out = finish(half, kept, lax.ppermute(sent, 'head', SWAP_XHI), out)  4.78 us
  transfers between devices with their start and end apart: 27, of which 12 were waited for; matrix products, arithmetic and copies ran while one was open for 1% of the time, Pallas kernels for 19%

profile of v3, /device:TPU:0, one launch (start us, length us, event | category | flops | bytes accessed | tf_op | source)
XLA Modules:
  0.0 105.3 jit_solution(16147190131371323371)
XLA Ops:
  0.0 14.3 %project.1 = (bf16[512,384]{1,0:T(8,128)(2,1)}, bf16[512,768]{1,0:T(8,128)(2,1)}) custom-call(bf16[512,5120]{1,0:T(8,128)(2,1)} %tok.1, f32[1,5120]{1,0:T(1,128)} %bitcast.8, f32[1,5120]{1,0:T(1,128)} %bitcast.9, bf16[5120,384]{1,0:T(8,128)(2,1)} %wq.1, bf16[5120,384]{1,0:T(8,128)(2,1)} %wk.1, bf16[5120,384]{1,0:T(8,128)(2,1)} %wv.1, f32[384]{0:T(512)} %gq_h.1, ...), custom_call_target="tpu_custom_call" | custom-call | flops 6039797760 | bytes 18000000 | tf_op jit(solution)/shard_map/project/pallas_call | solution.py:131
  14.3 2.1 %collective-permute-start.3 = (bf16[512,768]{1,0:T(8,128)(2,1)}, bf16[512,768]{1,0:T(8,128)(2,1)S(1)}, u32[]{:S(2)}, u32[]{:S(2)}) collective-permute-start(bf16[512,768]{1,0:T(8,128)(2,1)} %get-tuple-element.37.k0.n0), channel_id=1, source_target_pairs={{0,16},{8,24},{16,32},{24,40},{32,48},{40,56},{48,0},{56,8},{64,80... | collective-permute-start | bytes 2359304 | tf_op jit(solution)/shard_map/ppermute | solution.py:365
  16.4 2.2 %collective-permute-start.4 = (bf16[512,768]{1,0:T(8,128)(2,1)}, bf16[512,768]{1,0:T(8,128)(2,1)S(1)}, u32[]{:S(2)}, u32[]{:S(2)}) collective-permute-start(bf16[512,768]{1,0:T(8,128)(2,1)} %get-tuple-element.37.k0.n0), channel_id=1, source_target_pairs={{0,48},{8,56},{16,0},{24,8},{32,16},{40,24},{48,32},{56,40},{64,11... | collective-permute-start | bytes 2359304 | tf_op jit(solution)/shard_map/ppermute | solution.py:366
  18.6 0.0 collective-permute-start
  18.6 1.5 %collective-permute-start.1 = (bf16[512,384]{1,0:T(8,128)(2,1)}, bf16[512,384]{1,0:T(8,128)(2,1)S(1)}, u32[]{:S(2)}, u32[]{:S(2)}) collective-permute-start(bf16[512,384]{1,0:T(8,128)(2,1)} %get-tuple-element.35.q0), channel_id=1, source_target_pairs={{0,64},{8,72},{16,80},{24,88},{32,96},{40,104},{48,112},{56,120},{... | collective-permute-start | bytes 1179656 | tf_op jit(solution)/shard_map/ppermute | solution.py:373
  20.1 0.6 stack.23.cols
  20.7 0.0 collective-permute-done.q1
  20.7 3.8 %take_blocks.1 = (bf16[384,640]{1,0:T(8,128)(2,1)}, bf16[576,640]{1,0:T(8,128)(2,1)}, bf16[576,640]{1,0:T(8,128)(2,1)}, bf16[384,640]{1,0:T(8,128)(2,1)}) custom-call(s32[5]{0:T(128)} %stack.23.cols, bf16[384,5120]{1,0:T(8,128)(2,1)} %wo.1), custom_call_target="tpu_custom_call" | custom-call | flops 1000000 | bytes 6000000 | tf_op jit(solution)/shard_map/take_blocks/pallas_call | solution.py:179
  24.5 1.6 %collective-permute-start.7 = (bf16[576,640]{1,0:T(8,128)(2,1)}, bf16[576,640]{1,0:T(8,128)(2,1)S(1)}, u32[]{:S(2)}, u32[]{:S(2)}) collective-permute-start(bf16[576,640]{1,0:T(8,128)(2,1)} %get-tuple-element.40), channel_id=1, source_target_pairs={{0,1},{1,2},{2,3},{3,0},{4,5},{5,6},{6,7},{7,4},{8,9},{9,10},{10,1... | collective-permute-start | bytes 2211848 | tf_op jit(solution)/shard_map/ppermute | solution.py:376
  26.2 1.7 %collective-permute-start.8 = (bf16[576,640]{1,0:T(8,128)(2,1)}, bf16[576,640]{1,0:T(8,128)(2,1)S(1)}, u32[]{:S(2)}, u32[]{:S(2)}) collective-permute-start(bf16[576,640]{1,0:T(8,128)(2,1)} %get-tuple-element.41), channel_id=1, source_target_pairs={{0,3},{1,0},{2,1},{3,2},{4,7},{5,4},{6,5},{7,6},{8,11},{9,8},{10,9... | collective-permute-start | bytes 2211848 | tf_op jit(solution)/shard_map/ppermute | solution.py:377
  27.9 2.5 %collective-permute-done.1.q2 = bf16[512,384]{1,0:T(8,128)(2,1)S(1)} collective-permute-done((bf16[512,384]{1,0:T(8,128)(2,1)}, bf16[512,384]{1,0:T(8,128)(2,1)S(1)}, u32[]{:S(2)}, u32[]{:S(2)}) %collective-permute-start.1) | collective-permute-done | bytes 393248 | tf_op jit(solution)/shard_map/ppermute | solution.py:373
  30.3 0.0 collective-permute-start.2
  30.3 5.9 %collective-permute-done.3.k1.n1 = bf16[512,768]{1,0:T(8,128)(2,1)S(1)} collective-permute-done((bf16[512,768]{1,0:T(8,128)(2,1)}, bf16[512,768]{1,0:T(8,128)(2,1)S(1)}, u32[]{:S(2)}, u32[]{:S(2)}) %collective-permute-start.3) | collective-permute-done | bytes 786464 | tf_op jit(solution)/shard_map/ppermute | solution.py:365
  36.3 0.1 collective-permute-start.5
  36.4 0.0 collective-permute-done.4.k2.n2
  36.4 3.5 %collective-permute-start.6 = (bf16[256,768]{1,0:T(8,128)(2,1)S(1)}, bf16[256,768]{1,0:T(8,128)(2,1)S(1)}, u32[]{:S(2)}, u32[]{:S(2)}) collective-permute-start(bf16[256,768]{1,0:T(8,128)(2,1)S(1)} %slice.17), channel_id=1, source_target_pairs={{0,48},{8,56},{16,0},{24,8},{32,16},{40,24},{48,32},{56,40},{64,11... | collective-permute-start | bytes 1179656 | tf_op jit(solution)/shard_map/ppermute | solution.py:380
  39.9 9.3 %attend_first.1 = (bf16[864,384]{1,0:T(8,128)(2,1)S(1)}, bf16[864,384]{1,0:T(8,128)(2,1)S(1)}) custom-call(bf16[512,384]{1,0:T(8,128)(2,1)S(1)} %copy-done.3, bf16[512,384]{1,0:T(8,128)(2,1)S(1)} %collective-permute-done.q1, bf16[512,384]{1,0:T(8,128)(2,1)S(1)} %collective-permute-done.1.q2, bf16[512,768]{1,0:T(8,128)(2,1)S(1)} %copy-done.2, ...), custom_call_target="tpu_custom_call" | custom-call | flops 7247757312 | bytes 6000000 | tf_op jit(solution)/shard_map/attend_first/pallas_call | solution.py:219
  49.2 0.0 collective-permute-done.7.refs_1_
  49.2 0.0 collective-permute-done.8.refs_4_
  49.2 0.0 collective-permute-done.2.q3
  49.3 3.3 %attend_last.2 = (bf16[576,384]{1,0:T(8,128)(2,1)S(1)}, bf16[576,384]{1,0:T(8,128)(2,1)S(1)}) custom-call(bf16[512,384]{1,0:T(8,128)(2,1)S(1)} %copy-done.3, bf16[512,384]{1,0:T(8,128)(2,1)S(1)} %collective-permute-done.q1, bf16[512,384]{1,0:T(8,128)(2,1)S(1)} %collective-permute-done.1.q2, bf16[512,384]{1,0:T(8,128)(2,1)S(1)} %collective-permute-done.2.q3, ...), custom_call_target="tpu_custom_call" | custom-call | flops 3221225472 | bytes 4000000 | tf_op jit(solution)/shard_map/attend_last/pallas_call | solution.py:255
  52.5 0.1 collective-permute-start.9
  52.6 0.5 collective-permute-start.18
  53.1 0.1 collective-permute-start.21
  53.2 1.2 %collective-permute-done.9.recv = bf16[576,384]{1,0:T(8,128)(2,1)S(1)} collective-permute-done((bf16[576,384]{1,0:T(8,128)(2,1)S(1)}, bf16[576,384]{1,0:T(8,128)(2,1)S(1)}, u32[]{:S(2)}, u32[]{:S(2)}) %collective-permute-start.9) | collective-permute-done | bytes 442400 | tf_op jit(solution)/shard_map/ppermute | solution.py:391
  54.4 0.1 combine_core.2
  54.5 0.0 copy-start
  54.5 3.3 %attend_last.3 = (bf16[576,384]{1,0:T(8,128)(2,1)S(1)}, bf16[576,384]{1,0:T(8,128)(2,1)S(1)}) custom-call(bf16[512,384]{1,0:T(8,128)(2,1)S(1)} %copy-done.3, bf16[512,384]{1,0:T(8,128)(2,1)S(1)} %collective-permute-done.q1, bf16[512,384]{1,0:T(8,128)(2,1)S(1)} %collective-permute-done.1.q2, bf16[512,384]{1,0:T(8,128)(2,1)S(1)} %collective-permute-done.2.q3, ...), custom_call_target="tpu_custom_call" | custom-call | flops 3221225472 | bytes 4000000 | tf_op jit(solution)/shard_map/attend_last/pallas_call | solution.py:255
  57.8 0.2 collective-permute-start.10
  58.0 1.7 %collective-permute-start.16 = (bf16[192,640]{1,0:T(8,128)(2,1)S(1)}, bf16[192,640]{1,0:T(8,128)(2,1)S(1)}, u32[]{:S(2)}, u32[]{:S(2)}) collective-permute-start(bf16[192,640]{1,0:T(8,128)(2,1)S(1)} %slice.14), channel_id=1, source_target_pairs={{0,1},{1,2},{2,3},{3,0},{4,5},{5,6},{6,7},{7,4},{8,9},{9,10},{10,1... | collective-permute-start | bytes 737288 | tf_op jit(solution)/shard_map/ppermute | solution.py:386
  59.7 1.7 %collective-permute-start.17 = (bf16[192,640]{1,0:T(8,128)(2,1)S(1)}, bf16[192,640]{1,0:T(8,128)(2,1)S(1)}, u32[]{:S(2)}, u32[]{:S(2)}) collective-permute-start(bf16[192,640]{1,0:T(8,128)(2,1)S(1)} %slice.15), channel_id=1, source_target_pairs={{0,3},{1,0},{2,1},{3,2},{4,7},{5,4},{6,5},{7,6},{8,11},{9,8},{10,9... | collective-permute-start | bytes 737288 | tf_op jit(solution)/shard_map/ppermute | solution.py:386
  61.4 0.0 collective-permute-done.10.recv
  61.4 1.5 %collective-permute-start.15 = (bf16[288,384]{1,0:T(8,128)(2,1)S(1)}, bf16[288,384]{1,0:T(8,128)(2,1)S(1)}, u32[]{:S(2)}, u32[]{:S(2)}) collective-permute-start(bf16[288,384]{1,0:T(8,128)(2,1)S(1)} %get-tuple-element.54), channel_id=1, source_target_pairs={{0,64},{8,72},{16,80},{24,88},{32,96},{40,104},{48,112},{56,120},{... | collective-permute-start | bytes 663560 | tf_op jit(solution)/shard_map/ppermute | solution.py:394
  62.9 0.1 combine_core.3
  63.0 4.6 %collective-permute-done.16.refs_2_ = bf16[192,640]{1,0:T(8,128)(2,1)S(1)} collective-permute-done((bf16[192,640]{1,0:T(8,128)(2,1)S(1)}, bf16[192,640]{1,0:T(8,128)(2,1)S(1)}, u32[]{:S(2)}, u32[]{:S(2)}) %collective-permute-start.16) | collective-permute-done | bytes 245792 | tf_op jit(solution)/shard_map/ppermute | solution.py:386
  67.6 1.5 %collective-permute-start.11 = (bf16[288,384]{1,0:T(8,128)(2,1)S(1)}, bf16[288,384]{1,0:T(8,128)(2,1)S(1)}, u32[]{:S(2)}, u32[]{:S(2)}) collective-permute-start(bf16[288,384]{1,0:T(8,128)(2,1)S(1)} %get-tuple-element.51), channel_id=1, source_target_pairs={{0,64},{8,72},{16,80},{24,88},{32,96},{40,104},{48,112},{56,120},{... | collective-permute-start | bytes 663560 | tf_op jit(solution)/shard_map/ppermute | solution.py:394
  69.1 0.2 combine_x.3.a0
  69.3 0.4 collective-permute-start.23
  69.7 2.9 %collective-permute-start.24 = (bf16[256,384]{1,0:T(8,128)(2,1)S(1)}, bf16[256,384]{1,0:T(8,128)(2,1)S(1)}, u32[]{:S(2)}, u32[]{:S(2)}) collective-permute-start(bf16[256,384]{1,0:T(8,128)(2,1)S(1)} %combine_x.3.a0), channel_id=1, source_target_pairs={{0,2},{1,3},{2,0},{3,1},{4,6},{5,7},{6,4},{7,5},{8,10},{9,11},{10,... | collective-permute-start | bytes 589832 | tf_op jit(solution)/shard_map/ppermute | solution.py:399
  72.6 1.3 %collective-permute-start.25 = (bf16[256,384]{1,0:T(8,128)(2,1)S(1)}, bf16[256,384]{1,0:T(8,128)(2,1)S(1)}, u32[]{:S(2)}, u32[]{:S(2)}) collective-permute-start(bf16[256,384]{1,0:T(8,128)(2,1)S(1)} %combine_x.3.a0), channel_id=1, source_target_pairs={{0,3},{1,0},{2,1},{3,2},{4,7},{5,4},{6,5},{7,6},{8,11},{9,8},{10,9... | collective-permute-start | bytes 589832 | tf_op jit(solution)/shard_map/ppermute | solution.py:399
  73.9 0.0 collective-permute-done.21.refs_9_
  73.9 0.0 collective-permute-start.19
  73.9 0.7 collective-permute-done.11.recv
  74.6 0.0 collective-permute-start.20
  74.6 0.2 combine_x.2.a0
  74.8 4.5 %collective-permute-done.23.a1 = bf16[256,384]{1,0:T(8,128)(2,1)S(1)} collective-permute-done((bf16[256,384]{1,0:T(8,128)(2,1)S(1)}, bf16[256,384]{1,0:T(8,128)(2,1)S(1)}, u32[]{:S(2)}, u32[]{:S(2)}) %collective-permute-start.23) | collective-permute-done | bytes 196640 | tf_op jit(solution)/shard_map/ppermute | solution.py:399
  79.3 0.0 collective-permute-start.12
  79.3 3.3 %collective-permute-done.24.a2 = bf16[256,384]{1,0:T(8,128)(2,1)S(1)} collective-permute-done((bf16[256,384]{1,0:T(8,128)(2,1)S(1)}, bf16[256,384]{1,0:T(8,128)(2,1)S(1)}, u32[]{:S(2)}, u32[]{:S(2)}) %collective-permute-start.24) | collective-permute-done | bytes 196640 | tf_op jit(solution)/shard_map/ppermute | solution.py:399
  82.6 0.6 collective-permute-start.13
  83.2 0.1 collective-permute-done.25.a3
  83.2 2.7 %collective-permute-start.14 = (bf16[256,384]{1,0:T(8,128)(2,1)S(1)}, bf16[256,384]{1,0:T(8,128)(2,1)S(1)}, u32[]{:S(2)}, u32[]{:S(2)}) collective-permute-start(bf16[256,384]{1,0:T(8,128)(2,1)S(1)} %combine_x.2.a0), channel_id=1, source_target_pairs={{0,3},{1,0},{2,1},{3,2},{4,7},{5,4},{6,5},{7,6},{8,11},{9,8},{10,9... | collective-permute-start | bytes 589832 | tf_op jit(solution)/shard_map/ppermute | solution.py:399
  85.9 0.0 collective-permute-done.19.refs_7_
  85.9 0.0 collective-permute-done.20.refs_8_
  85.9 1.2 %out_project.3 = (bf16[256,640]{1,0:T(8,128)(2,1)S(1)}, bf16[256,640]{1,0:T(8,128)(2,1)S(1)}) custom-call(s32[1]{0:T(128)} %bitcast.core, bf16[256,384]{1,0:T(8,128)(2,1)S(1)} %combine_x.3.a0, bf16[256,384]{1,0:T(8,128)(2,1)S(1)} %collective-permute-done.23.a1, bf16[256,384]{1,0:T(8,128)(2,1)S(1)} %collective-permute-done.24.a2, ...), custom_call_target="tpu_custom_call" | custom-call | flops 1006632960 | bytes 6000000 | tf_op jit(solution)/shard_map/out_project/pallas_call | solution.py:328
  87.1 2.5 %collective-permute-start.26 = (bf16[256,640]{1,0:T(8,128)(2,1)S(1)}, bf16[256,640]{1,0:T(8,128)(2,1)S(1)}, u32[]{:S(2)}, u32[]{:S(2)}) collective-permute-start(bf16[256,640]{1,0:T(8,128)(2,1)S(1)} %get-tuple-element.64), channel_id=1, source_target_pairs={{0,4},{1,5},{2,6},{3,7},{4,0},{5,1},{6,2},{7,3},{8,12},{9,13},{10,... | collective-permute-start | bytes 983048 | tf_op jit(solution)/shard_map/ppermute | solution.py:403
  89.6 0.4 collective-permute-done.12.a1
  90.0 0.0 collective-permute-done.13.a2
  90.0 1.2 %collective-permute-done.14.a3 = bf16[256,384]{1,0:T(8,128)(2,1)S(1)} collective-permute-done((bf16[256,384]{1,0:T(8,128)(2,1)S(1)}, bf16[256,384]{1,0:T(8,128)(2,1)S(1)}, u32[]{:S(2)}, u32[]{:S(2)}) %collective-permute-start.14) | collective-permute-done | bytes 196640 | tf_op jit(solution)/shard_map/ppermute | solution.py:399
  91.2 1.2 %out_project.2 = (bf16[256,640]{1,0:T(8,128)(2,1)S(1)}, bf16[256,640]{1,0:T(8,128)(2,1)S(1)}) custom-call(s32[1]{0:T(128)} %bitcast.core, bf16[256,384]{1,0:T(8,128)(2,1)S(1)} %combine_x.2.a0, bf16[256,384]{1,0:T(8,128)(2,1)S(1)} %collective-permute-done.12.a1, bf16[256,384]{1,0:T(8,128)(2,1)S(1)} %collective-permute-done.13.a2, ...), custom_call_target="tpu_custom_call" | custom-call | flops 1006632960 | bytes 6000000 | tf_op jit(solution)/shard_map/out_project/pallas_call | solution.py:328
  92.4 2.3 %collective-permute-start.22 = (bf16[256,640]{1,0:T(8,128)(2,1)S(1)}, bf16[256,640]{1,0:T(8,128)(2,1)S(1)}, u32[]{:S(2)}, u32[]{:S(2)}) collective-permute-start(bf16[256,640]{1,0:T(8,128)(2,1)S(1)} %get-tuple-element.60), channel_id=1, source_target_pairs={{0,4},{1,5},{2,6},{3,7},{4,0},{5,1},{6,2},{7,3},{8,12},{9,13},{10,... | collective-permute-start | bytes 983048 | tf_op jit(solution)/shard_map/ppermute | solution.py:403
  94.7 4.6 %collective-permute-done.26.recv = bf16[256,640]{1,0:T(8,128)(2,1)S(1)} collective-permute-done((bf16[256,640]{1,0:T(8,128)(2,1)S(1)}, bf16[256,640]{1,0:T(8,128)(2,1)S(1)}, u32[]{:S(2)}, u32[]{:S(2)}) %collective-permute-start.26) | collective-permute-done | bytes 327712 | tf_op jit(solution)/shard_map/ppermute | solution.py:403
  99.2 0.8 finish.2.rest_0_
  100.0 4.5 %collective-permute-done.22.recv = bf16[256,640]{1,0:T(8,128)(2,1)S(1)} collective-permute-done((bf16[256,640]{1,0:T(8,128)(2,1)S(1)}, bf16[256,640]{1,0:T(8,128)(2,1)S(1)}, u32[]{:S(2)}, u32[]{:S(2)}) %collective-permute-start.22) | collective-permute-done | bytes 327712 | tf_op jit(solution)/shard_map/ppermute | solution.py:403
  104.5 0.8 finish.3
  (16 shorter events, 0.1 us)
Async XLA Ops:
  14.3 25.6 %copy-start.2 = (bf16[512,768]{1,0:T(8,128)(2,1)S(1)}, bf16[512,768]{1,0:T(8,128)(2,1)}, u32[]{:S(2)}) copy-start(bf16[512,768]{1,0:T(8,128)(2,1)} %get-tuple-element.37.k0.n0) | copy-start | bytes 2359300
  14.3 25.6 %copy-start.3 = (bf16[512,384]{1,0:T(8,128)(2,1)S(1)}, bf16[512,384]{1,0:T(8,128)(2,1)}, u32[]{:S(2)}) copy-start(bf16[512,384]{1,0:T(8,128)(2,1)} %get-tuple-element.35.q0) | copy-start | bytes 1179652
  14.3 21.9 %collective-permute-start.3 = (bf16[512,768]{1,0:T(8,128)(2,1)}, bf16[512,768]{1,0:T(8,128)(2,1)S(1)}, u32[]{:S(2)}, u32[]{:S(2)}) collective-permute-start(bf16[512,768]{1,0:T(8,128)(2,1)} %get-tuple-element.37.k0.n0), channel_id=1, source_target_pairs={{0,16},{8,24},{16,32},{24,40},{32,48},{40,56},{48,0},{56,8},{64,80... | collective-permute-start | bytes 2359304 | tf_op jit(solution)/shard_map/ppermute | solution.py:365
  16.4 20.0 %collective-permute-start.4 = (bf16[512,768]{1,0:T(8,128)(2,1)}, bf16[512,768]{1,0:T(8,128)(2,1)S(1)}, u32[]{:S(2)}, u32[]{:S(2)}) collective-permute-start(bf16[512,768]{1,0:T(8,128)(2,1)} %get-tuple-element.37.k0.n0), channel_id=1, source_target_pairs={{0,48},{8,56},{16,0},{24,8},{32,16},{40,24},{48,32},{56,40},{64,11... | collective-permute-start | bytes 2359304 | tf_op jit(solution)/shard_map/ppermute | solution.py:366
  18.6 2.1 %collective-permute-start = (bf16[512,384]{1,0:T(8,128)(2,1)}, bf16[512,384]{1,0:T(8,128)(2,1)S(1)}, u32[]{:S(2)}, u32[]{:S(2)}) collective-permute-start(bf16[512,384]{1,0:T(8,128)(2,1)} %get-tuple-element.35.q0), channel_id=1, source_target_pairs={{0,8},{8,0},{16,24},{24,16},{32,40},{40,32},{48,56},{56,48},{64,72... | collective-permute-start | bytes 1179656 | tf_op jit(solution)/shard_map/ppermute | solution.py:372
  18.6 11.7 %collective-permute-start.1 = (bf16[512,384]{1,0:T(8,128)(2,1)}, bf16[512,384]{1,0:T(8,128)(2,1)S(1)}, u32[]{:S(2)}, u32[]{:S(2)}) collective-permute-start(bf16[512,384]{1,0:T(8,128)(2,1)} %get-tuple-element.35.q0), channel_id=1, source_target_pairs={{0,64},{8,72},{16,80},{24,88},{32,96},{40,104},{48,112},{56,120},{... | collective-permute-start | bytes 1179656 | tf_op jit(solution)/shard_map/ppermute | solution.py:373
  24.5 24.7 %collective-permute-start.7 = (bf16[576,640]{1,0:T(8,128)(2,1)}, bf16[576,640]{1,0:T(8,128)(2,1)S(1)}, u32[]{:S(2)}, u32[]{:S(2)}) collective-permute-start(bf16[576,640]{1,0:T(8,128)(2,1)} %get-tuple-element.40), channel_id=1, source_target_pairs={{0,1},{1,2},{2,3},{3,0},{4,5},{5,6},{6,7},{7,4},{8,9},{9,10},{10,1... | collective-permute-start | bytes 2211848 | tf_op jit(solution)/shard_map/ppermute | solution.py:376
  26.2 23.0 %collective-permute-start.8 = (bf16[576,640]{1,0:T(8,128)(2,1)}, bf16[576,640]{1,0:T(8,128)(2,1)S(1)}, u32[]{:S(2)}, u32[]{:S(2)}) collective-permute-start(bf16[576,640]{1,0:T(8,128)(2,1)} %get-tuple-element.41), channel_id=1, source_target_pairs={{0,3},{1,0},{2,1},{3,2},{4,7},{5,4},{6,5},{7,6},{8,11},{9,8},{10,9... | collective-permute-start | bytes 2211848 | tf_op jit(solution)/shard_map/ppermute | solution.py:377
  30.3 18.9 %collective-permute-start.2 = (bf16[512,384]{1,0:T(8,128)(2,1)S(1)}, bf16[512,384]{1,0:T(8,128)(2,1)S(1)}, u32[]{:S(2)}, u32[]{:S(2)}) collective-permute-start(bf16[512,384]{1,0:T(8,128)(2,1)S(1)} %collective-permute-done.1.q2), channel_id=1, source_target_pairs={{0,8},{8,0},{16,24},{24,16},{32,40},{40,32},{48,56},{56,48},{64,72... | collective-permute-start | bytes 1179656 | tf_op jit(solution)/shard_map/ppermute | solution.py:378
  36.3 13.0 %collective-permute-start.5 = (bf16[256,768]{1,0:T(8,128)(2,1)S(1)}, bf16[256,768]{1,0:T(8,128)(2,1)S(1)}, u32[]{:S(2)}, u32[]{:S(2)}) collective-permute-start(bf16[256,768]{1,0:T(8,128)(2,1)S(1)} %slice.16), channel_id=1, source_target_pairs={{0,16},{8,24},{16,32},{24,40},{32,48},{40,56},{48,0},{56,8},{64,80... | collective-permute-start | bytes 1179656 | tf_op jit(solution)/shard_map/ppermute | solution.py:379
  36.4 12.8 %collective-permute-start.6 = (bf16[256,768]{1,0:T(8,128)(2,1)S(1)}, bf16[256,768]{1,0:T(8,128)(2,1)S(1)}, u32[]{:S(2)}, u32[]{:S(2)}) collective-permute-start(bf16[256,768]{1,0:T(8,128)(2,1)S(1)} %slice.17), channel_id=1, source_target_pairs={{0,48},{8,56},{16,0},{24,8},{32,16},{40,24},{48,32},{56,40},{64,11... | collective-permute-start | bytes 1179656 | tf_op jit(solution)/shard_map/ppermute | solution.py:380
  52.5 1.8 %collective-permute-start.9 = (bf16[576,384]{1,0:T(8,128)(2,1)S(1)}, bf16[576,384]{1,0:T(8,128)(2,1)S(1)}, u32[]{:S(2)}, u32[]{:S(2)}) collective-permute-start(bf16[576,384]{1,0:T(8,128)(2,1)S(1)} %get-tuple-element.44), channel_id=1, source_target_pairs={{0,8},{8,0},{16,24},{24,16},{32,40},{40,32},{48,56},{56,48},{64,72... | collective-permute-start | bytes 1327112 | tf_op jit(solution)/shard_map/ppermute | solution.py:391
  52.6 19.9 %collective-permute-start.18 = (bf16[576,640]{1,0:T(8,128)(2,1)S(1)}, bf16[576,640]{1,0:T(8,128)(2,1)S(1)}, u32[]{:S(2)}, u32[]{:S(2)}) collective-permute-start(bf16[576,640]{1,0:T(8,128)(2,1)S(1)} %collective-permute-done.7.refs_1_), channel_id=1, source_target_pairs={{0,8},{8,0},{16,24},{24,16},{32,40},{40,32},{48,56},{56,48},{64,72... | collective-permute-start | bytes 2211848 | tf_op jit(solution)/shard_map/ppermute | solution.py:385
  53.1 20.8 %collective-permute-start.21 = (bf16[576,640]{1,0:T(8,128)(2,1)S(1)}, bf16[576,640]{1,0:T(8,128)(2,1)S(1)}, u32[]{:S(2)}, u32[]{:S(2)}) collective-permute-start(bf16[576,640]{1,0:T(8,128)(2,1)S(1)} %collective-permute-done.8.refs_4_), channel_id=1, source_target_pairs={{0,8},{8,0},{16,24},{24,16},{32,40},{40,32},{48,56},{56,48},{64,72... | collective-permute-start | bytes 2211848 | tf_op jit(solution)/shard_map/ppermute | solution.py:385
  54.5 31.4 %copy-start = (bf16[384,640]{1,0:T(8,128)(2,1)S(1)}, bf16[384,640]{1,0:T(8,128)(2,1)}, u32[]{:S(2)}) copy-start(bf16[384,640]{1,0:T(8,128)(2,1)} %get-tuple-element.52.refs_0_) | copy-start | bytes 1474564
  54.5 31.4 %copy-start.1 = (bf16[384,640]{1,0:T(8,128)(2,1)S(1)}, bf16[384,640]{1,0:T(8,128)(2,1)}, u32[]{:S(2)}) copy-start(bf16[384,640]{1,0:T(8,128)(2,1)} %get-tuple-element.58.refs_5_) | copy-start | bytes 1474564
  57.8 3.6 %collective-permute-start.10 = (bf16[576,384]{1,0:T(8,128)(2,1)S(1)}, bf16[576,384]{1,0:T(8,128)(2,1)S(1)}, u32[]{:S(2)}, u32[]{:S(2)}) collective-permute-start(bf16[576,384]{1,0:T(8,128)(2,1)S(1)} %get-tuple-element.49), channel_id=1, source_target_pairs={{0,8},{8,0},{16,24},{24,16},{32,40},{40,32},{48,56},{56,48},{64,72... | collective-permute-start | bytes 1327112 | tf_op jit(solution)/shard_map/ppermute | solution.py:391
  58.0 9.6 %collective-permute-start.16 = (bf16[192,640]{1,0:T(8,128)(2,1)S(1)}, bf16[192,640]{1,0:T(8,128)(2,1)S(1)}, u32[]{:S(2)}, u32[]{:S(2)}) collective-permute-start(bf16[192,640]{1,0:T(8,128)(2,1)S(1)} %slice.14), channel_id=1, source_target_pairs={{0,1},{1,2},{2,3},{3,0},{4,5},{5,6},{6,7},{7,4},{8,9},{9,10},{10,1... | collective-permute-start | bytes 737288 | tf_op jit(solution)/shard_map/ppermute | solution.py:386
  59.7 9.4 %collective-permute-start.17 = (bf16[192,640]{1,0:T(8,128)(2,1)S(1)}, bf16[192,640]{1,0:T(8,128)(2,1)S(1)}, u32[]{:S(2)}, u32[]{:S(2)}) collective-permute-start(bf16[192,640]{1,0:T(8,128)(2,1)S(1)} %slice.15), channel_id=1, source_target_pairs={{0,3},{1,0},{2,1},{3,2},{4,7},{5,4},{6,5},{7,6},{8,11},{9,8},{10,9... | collective-permute-start | bytes 737288 | tf_op jit(solution)/shard_map/ppermute | solution.py:386
  61.4 7.7 %collective-permute-start.15 = (bf16[288,384]{1,0:T(8,128)(2,1)S(1)}, bf16[288,384]{1,0:T(8,128)(2,1)S(1)}, u32[]{:S(2)}, u32[]{:S(2)}) collective-permute-start(bf16[288,384]{1,0:T(8,128)(2,1)S(1)} %get-tuple-element.54), channel_id=1, source_target_pairs={{0,64},{8,72},{16,80},{24,88},{32,96},{40,104},{48,112},{56,120},{... | collective-permute-start | bytes 663560 | tf_op jit(solution)/shard_map/ppermute | solution.py:394
  67.6 7.0 %collective-permute-start.11 = (bf16[288,384]{1,0:T(8,128)(2,1)S(1)}, bf16[288,384]{1,0:T(8,128)(2,1)S(1)}, u32[]{:S(2)}, u32[]{:S(2)}) collective-permute-start(bf16[288,384]{1,0:T(8,128)(2,1)S(1)} %get-tuple-element.51), channel_id=1, source_target_pairs={{0,64},{8,72},{16,80},{24,88},{32,96},{40,104},{48,112},{56,120},{... | collective-permute-start | bytes 663560 | tf_op jit(solution)/shard_map/ppermute | solution.py:394
  69.3 10.0 %collective-permute-start.23 = (bf16[256,384]{1,0:T(8,128)(2,1)S(1)}, bf16[256,384]{1,0:T(8,128)(2,1)S(1)}, u32[]{:S(2)}, u32[]{:S(2)}) collective-permute-start(bf16[256,384]{1,0:T(8,128)(2,1)S(1)} %combine_x.3.a0), channel_id=1, source_target_pairs={{0,1},{1,2},{2,3},{3,0},{4,5},{5,6},{6,7},{7,4},{8,9},{9,10},{10,1... | collective-permute-start | bytes 589832 | tf_op jit(solution)/shard_map/ppermute | solution.py:399
  69.7 12.9 %collective-permute-start.24 = (bf16[256,384]{1,0:T(8,128)(2,1)S(1)}, bf16[256,384]{1,0:T(8,128)(2,1)S(1)}, u32[]{:S(2)}, u32[]{:S(2)}) collective-permute-start(bf16[256,384]{1,0:T(8,128)(2,1)S(1)} %combine_x.3.a0), channel_id=1, source_target_pairs={{0,2},{1,3},{2,0},{3,1},{4,6},{5,7},{6,4},{7,5},{8,10},{9,11},{10,... | collective-permute-start | bytes 589832 | tf_op jit(solution)/shard_map/ppermute | solution.py:399
  72.6 10.7 %collective-permute-start.25 = (bf16[256,384]{1,0:T(8,128)(2,1)S(1)}, bf16[256,384]{1,0:T(8,128)(2,1)S(1)}, u32[]{:S(2)}, u32[]{:S(2)}) collective-permute-start(bf16[256,384]{1,0:T(8,128)(2,1)S(1)} %combine_x.3.a0), channel_id=1, source_target_pairs={{0,3},{1,0},{2,1},{3,2},{4,7},{5,4},{6,5},{7,6},{8,11},{9,8},{10,9... | collective-permute-start | bytes 589832 | tf_op jit(solution)/shard_map/ppermute | solution.py:399
  73.9 12.0 %collective-permute-start.19 = (bf16[192,640]{1,0:T(8,128)(2,1)S(1)}, bf16[192,640]{1,0:T(8,128)(2,1)S(1)}, u32[]{:S(2)}, u32[]{:S(2)}) collective-permute-start(bf16[192,640]{1,0:T(8,128)(2,1)S(1)} %collective-permute-done.16.refs_2_), channel_id=1, source_target_pairs={{0,8},{8,0},{16,24},{24,16},{32,40},{40,32},{48,56},{56,48},{64,72... | collective-permute-start | bytes 737288 | tf_op jit(solution)/shard_map/ppermute | solution.py:397
  74.6 11.3 %collective-permute-start.20 = (bf16[192,640]{1,0:T(8,128)(2,1)S(1)}, bf16[192,640]{1,0:T(8,128)(2,1)S(1)}, u32[]{:S(2)}, u32[]{:S(2)}) collective-permute-start(bf16[192,640]{1,0:T(8,128)(2,1)S(1)} %collective-permute-done.17.refs_3_), channel_id=1, source_target_pairs={{0,8},{8,0},{16,24},{24,16},{32,40},{40,32},{48,56},{56,48},{64,72... | collective-permute-start | bytes 737288 | tf_op jit(solution)/shard_map/ppermute | solution.py:397
  79.3 10.7 %collective-permute-start.12 = (bf16[256,384]{1,0:T(8,128)(2,1)S(1)}, bf16[256,384]{1,0:T(8,128)(2,1)S(1)}, u32[]{:S(2)}, u32[]{:S(2)}) collective-permute-start(bf16[256,384]{1,0:T(8,128)(2,1)S(1)} %combine_x.2.a0), channel_id=1, source_target_pairs={{0,1},{1,2},{2,3},{3,0},{4,5},{5,6},{6,7},{7,4},{8,9},{9,10},{10,1... | collective-permute-start | bytes 589832 | tf_op jit(solution)/shard_map/ppermute | solution.py:399
  82.6 7.4 %collective-permute-start.13 = (bf16[256,384]{1,0:T(8,128)(2,1)S(1)}, bf16[256,384]{1,0:T(8,128)(2,1)S(1)}, u32[]{:S(2)}, u32[]{:S(2)}) collective-permute-start(bf16[256,384]{1,0:T(8,128)(2,1)S(1)} %combine_x.2.a0), channel_id=1, source_target_pairs={{0,2},{1,3},{2,0},{3,1},{4,6},{5,7},{6,4},{7,5},{8,10},{9,11},{10,... | collective-permute-start | bytes 589832 | tf_op jit(solution)/shard_map/ppermute | solution.py:399
  83.2 8.0 %collective-permute-start.14 = (bf16[256,384]{1,0:T(8,128)(2,1)S(1)}, bf16[256,384]{1,0:T(8,128)(2,1)S(1)}, u32[]{:S(2)}, u32[]{:S(2)}) collective-permute-start(bf16[256,384]{1,0:T(8,128)(2,1)S(1)} %combine_x.2.a0), channel_id=1, source_target_pairs={{0,3},{1,0},{2,1},{3,2},{4,7},{5,4},{6,5},{7,6},{8,11},{9,8},{10,9... | collective-permute-start | bytes 589832 | tf_op jit(solution)/shard_map/ppermute | solution.py:399
  87.1 12.1 %collective-permute-start.26 = (bf16[256,640]{1,0:T(8,128)(2,1)S(1)}, bf16[256,640]{1,0:T(8,128)(2,1)S(1)}, u32[]{:S(2)}, u32[]{:S(2)}) collective-permute-start(bf16[256,640]{1,0:T(8,128)(2,1)S(1)} %get-tuple-element.64), channel_id=1, source_target_pairs={{0,4},{1,5},{2,6},{3,7},{4,0},{5,1},{6,2},{7,3},{8,12},{9,13},{10,... | collective-permute-start | bytes 983048 | tf_op jit(solution)/shard_map/ppermute | solution.py:403
  92.4 12.1 %collective-permute-start.22 = (bf16[256,640]{1,0:T(8,128)(2,1)S(1)}, bf16[256,640]{1,0:T(8,128)(2,1)S(1)}, u32[]{:S(2)}, u32[]{:S(2)}) collective-permute-start(bf16[256,640]{1,0:T(8,128)(2,1)S(1)} %get-tuple-element.60), channel_id=1, source_target_pairs={{0,4},{1,5},{2,6},{3,7},{4,0},{5,1},{6,2},{7,3},{8,12},{9,13},{10,... | collective-permute-start | bytes 983048 | tf_op jit(solution)/shard_map/ppermute | solution.py:403

commit v4 on v3

--- a/solution.py
+++ b/solution.py
@@ -228,56 +228,56 @@
     )(*qs, *kvs)
 
 
-def last_kernel(q0, q1, q2, q3, n0, n1, n2, k0, k1, part, keep, send):
+def last_kernel(q0, q1, q2, q3, n0, n1, n2, k0, k1, part0, part1, keep, send):
     for h in range(GROUP_HEADS):
         col = slice(h * HD, (h + 1) * HD)
         wide = slice(2 * h * HD, 2 * (h + 1) * HD)
-        for i, (q, out, base) in enumerate(((q0, keep, 0), (q1, send, 0), (q2, keep, PACK), (q3, send, PACK))):
-            far = (k0[:, wide], k1[:, wide])
+        for i, (q, out) in enumerate(((q0, keep), (q1, send), (q2, keep), (q3, send))):
+            kvs = (k0[:, wide], k1[:, wide])
             if i == 3:
-                acc = mix(q[:, col], (n0[:, wide], n1[:, wide], n2[:, wide]) + far, 256)
-                mixture, totals = acc[:, :HD], None
-            else:
-                acc = mix(q[:, col], far, 256)
-                old = part[i * PACK : (i + 1) * PACK, col].astype(F32)
-                mixture, totals = acc[:, :HD] + old[:HALF], old[HALF:]
-            out[base : base + HALF, col] = mixture.astype(BF16)
-            for p in range(HALF // 128):
-                t = jnp.transpose(acc[p * 128 : (p + 1) * 128, HD:])[:16]
-                if totals is not None:
-                    t = t + totals[16 * p : 16 * (p + 1)]
-                at = base + HALF + 16 * p
-                out[at : at + 16, col] = t.astype(BF16)
-
-
-def attend_last(half, qs, kvs, part):
+                kvs = (n0[:, wide], n1[:, wide], n2[:, wide]) + kvs
+            acc = mix(q[:, col], kvs, 256)
+            for half, part in enumerate((part0, part1)):
+                rows = acc[half * HALF : (half + 1) * HALF]
+                base = (2 * half + i // 2) * PACK
+                mixture, old = rows[:, :HD], None
+                if i < 3:
+                    old = part[i * PACK : (i + 1) * PACK, col].astype(F32)
+                    mixture = mixture + old[:HALF]
+                out[base : base + HALF, col] = mixture.astype(BF16)
+                for p in range(HALF // 128):
+                    t = jnp.transpose(rows[p * 128 : (p + 1) * 128, HD:])[:16]
+                    at = HALF + 16 * p
+                    if i < 3:
+                        t = t + old[at : at + 16]
+                    out[base + at : base + at + 16, col] = t.astype(BF16)
+
+
+def attend_last(qs, kvs, parts):
     whole = lambda shape: pl.BlockSpec(shape, lambda j: (0, 0))
     return pl.pallas_call(
         last_kernel,
         grid=(1,),
-        in_specs=[pl.BlockSpec((HALF, WIDE), lambda j: (half, 0))] * 4
-        + [whole((ROWS, 2 * WIDE))] * 3
-        + [whole((256, 2 * WIDE))] * 2
-        + [whole((3 * PACK, WIDE))],
-        out_specs=[whole((2 * PACK, WIDE))] * 2,
-        out_shape=[jax.ShapeDtypeStruct((2 * PACK, WIDE), BF16)] * 2,
-        compiler_params=params(24),
-        cost_estimate=cost(3 * 4 * 1024 * 1024 * 256, 4e6, 3 * 2 * 1024 * 1024),
+        in_specs=[whole(a.shape) for a in (*qs, *kvs, *parts)],
+        out_specs=[whole((4 * PACK, WIDE))] * 2,
+        out_shape=[jax.ShapeDtypeStruct((4 * PACK, WIDE), BF16)] * 2,
+        compiler_params=params(32),
+        cost_estimate=cost(3 * 4 * 2048 * 1024 * 256, 8e6, 3 * 2 * 2048 * 1024),
         name="attend_last",
-    )(*qs, *kvs, part)
-
-
-def combine_core_kernel(keep, recv, mine, away):
+    )(*qs, *kvs, *parts)
+
+
+def combine_core_kernel(keep, recv, *outs):
     total = keep[...].astype(F32) + recv[...].astype(F32)
-    mine[...] = total[:PACK].astype(BF16)
-    away[...] = total[PACK:].astype(BF16)
+    for i, out in enumerate(outs):
+        out[...] = total[i * PACK : (i + 1) * PACK].astype(BF16)
 
 
 def combine_core(keep, recv):
     return pl.pallas_call(
         combine_core_kernel,
-        out_shape=[jax.ShapeDtypeStruct((PACK, WIDE), BF16)] * 2,
-        compiler_params=params(),
+        out_shape=[jax.ShapeDtypeStruct((PACK, WIDE), BF16)] * 4,
+        compiler_params=params(12),
         cost_estimate=cost(1e6, 2e6),
         name="combine_core",
     )(keep, recv)
@@ -385,20 +385,19 @@
     second = [lax.ppermute(w, "seq", SWAP_CORE) for w in (up, down)]
     far = [lax.ppermute(up[WIDE:], "head", Y_STEP[1]), lax.ppermute(down[WIDE:], "head", Y_STEP[3])]
 
+    keep, send = attend_last(qs, (kv, below, above, far_a, far_b), parts)
+    recv, *second = lax.optimization_barrier((lax.ppermute(send, "seq", SWAP_CORE), *second))
+    mine0, away0, mine1, away1 = combine_core(keep, recv)
+    recv0 = lax.ppermute(away0, "seq", SWAP_X)
+    recv1 = lax.ppermute(away1, "seq", SWAP_X)
+    recv1, *far = lax.optimization_barrier((recv1, *far))
+    far_core = [lax.ppermute(w, "seq", SWAP_CORE) for w in far]
+    first_w = (own, up, *far, down)
+    second_w = (other, second[0], *far_core, second[1])
     out = None
-    for half in range(2):
-        keep, send = attend_last(half, qs, (kv, below, above, far_a, far_b), parts[half])
-        mine, away = combine_core(keep, lax.ppermute(send, "seq", SWAP_CORE))
-        if half == 0:
-            away, parts[1] = lax.optimization_barrier((away, parts[1]))
-        recv = lax.ppermute(away, "seq", SWAP_X)
-        if half == 0:
-            recv, *far = lax.optimization_barrier((recv, *far))
-            far_core = [lax.ppermute(w, "seq", SWAP_CORE) for w in far]
+    for half, (mine, recv) in enumerate(((mine0, recv0), (mine1, recv1))):
         att = combine_x(mine, recv)
         attended = [att] + [lax.ppermute(att, "head", Y_STEP[r]) for r in (1, 2, 3)]
-        first_w = (own, up, *far, down)
-        second_w = (other, second[0], *far_core, second[1])
         kept, sent = out_project(core, attended, first_w, second_w)
         out = finish(half, kept, lax.ppermute(sent, "head", SWAP_XHI), out)
     return out

time: 105 us -> 105 us (level)
  starting transfers between devices: 32.5 us -> 36.6 us
  waiting for transfers between devices: 33.3 us -> 29.2 us
    ppermute x1, waiting for transfers between devices: 5.92 us -> 0.01 us  [shards(): below = lax.ppermute(kv, 'seq', Z_UP)]
    ppermute x1, waiting for transfers between devices: 0.01 us -> 5.37 us  [shards(): above = lax.ppermute(kv, 'seq', Z_DOWN)]
    ppermute x1, waiting for transfers between devices: 4.56 us -> 0.01 us  [shards(): lax.ppermute(up[WIDE:], 'head', Y_STEP[1])]
    ppermute x2, waiting for transfers between devices: 9.03 us -> 5.5 us  [shards(): out = finish(half, kept, lax.ppermute(sent, 'head', SWAP_XHI), out)]
    ppermute x4 -> x3, waiting for transfers between devices: 1.85 us -> 4.58 us  [the longest x1 4.57 us: shards(): recv0 = lax.ppermute(away0, 'seq', SWAP_X)]
    ppermute x1, starting transfers between devices: 2.07 us -> 0.01 us  [shards(): below = lax.ppermute(kv, 'seq', Z_UP)]
    ppermute x1, starting transfers between devices: 2.2 us -> 4.19 us  [shards(): above = lax.ppermute(kv, 'seq', Z_DOWN)]
    ppermute x6, starting transfers between devices: 7.87 us -> 9.46 us  [shards(): attended = [att] + [lax.ppermute(att, 'head', Y_STEP[r]) for r in (1, 2, 3)]]
  transfers between devices with their start and end apart: 27 -> 26, of which waited for: 12 -> 10; matrix products, arithmetic and copies ran while one was open for 1% -> 1% of each run, Pallas kernels for 19% -> 16%
where the time goes in v4:
time: 105 us
  Pallas kernels  38.2 us (36%)
  starting transfers between devices  36.6 us (35%)
  waiting for transfers between devices  29.2 us (28%)
    pallas_call x1, Pallas kernels, project(): pl.pallas_call(qkv_kernel, in_specs=[hbm] * 8, out_specs=[vmem, vmem], ou...  14.3 us
    ppermute x6, starting transfers between devices, shards(): attended = [att] + [lax.ppermute(att, 'head', Y_STEP[r]) for r in (1, 2, 3)]  9.46 us
    pallas_call x1, Pallas kernels, attend_first(): pl.pallas_call(first_kernel, grid=(GROUP_HEADS,), in_specs=[head(ROWS, HD...  9.33 us
    ppermute x6, waiting for transfers between devices, shards(): attended = [att] + [lax.ppermute(att, 'head', Y_STEP[r]) for r in (1, 2, 3)]  8.89 us
    ppermute x2, starting transfers between devices, shards(): out = finish(half, kept, lax.ppermute(sent, 'head', SWAP_XHI), out)  6.21 us
    pallas_call x1, Pallas kernels, attend_last(): pl.pallas_call(last_kernel, grid=(1,), in_specs=[whole(a.shape) for a in...  6.18 us
    ppermute x2, waiting for transfers between devices, shards(): out = finish(half, kept, lax.ppermute(sent, 'head', SWAP_XHI), out)  5.5 us
    ppermute x1, waiting for transfers between devices, shards(): above = lax.ppermute(kv, 'seq', Z_DOWN)  5.37 us
  transfers between devices with their start and end apart: 26, of which 10 were waited for; matrix products, arithmetic and copies ran while one was open for 1% of the time, Pallas kernels for 16%

profile of v4, /device:TPU:0, one launch (start us, length us, event | category | flops | bytes accessed | tf_op | source)
XLA Modules:
  0.0 104.9 jit_solution(13322143541014849761)
XLA Ops:
  0.0 14.3 %project.1 = (bf16[512,384]{1,0:T(8,128)(2,1)}, bf16[512,768]{1,0:T(8,128)(2,1)}) custom-call(bf16[512,5120]{1,0:T(8,128)(2,1)} %tok.1, f32[1,5120]{1,0:T(1,128)} %bitcast.8, f32[1,5120]{1,0:T(1,128)} %bitcast.9, bf16[5120,384]{1,0:T(8,128)(2,1)} %wq.1, bf16[5120,384]{1,0:T(8,128)(2,1)} %wk.1, bf16[5120,384]{1,0:T(8,128)(2,1)} %wv.1, f32[384]{0:T(512)} %gq_h.1, ...), custom_call_target="tpu_custom_call" | custom-call | flops 6039797760 | bytes 18000000 | tf_op jit(solution)/shard_map/project/pallas_call | solution.py:131
  14.3 4.2 %collective-permute-start.4 = (bf16[512,768]{1,0:T(8,128)(2,1)}, bf16[512,768]{1,0:T(8,128)(2,1)S(1)}, u32[]{:S(2)}, u32[]{:S(2)}) collective-permute-start(bf16[512,768]{1,0:T(8,128)(2,1)} %get-tuple-element.36.k0.n0), channel_id=1, source_target_pairs={{0,48},{8,56},{16,0},{24,8},{32,16},{40,24},{48,32},{56,40},{64,11... | collective-permute-start | bytes 2359304 | tf_op jit(solution)/shard_map/ppermute | solution.py:366
  18.5 0.0 collective-permute-start.3
  18.5 0.0 collective-permute-start
  18.5 1.5 %collective-permute-start.1 = (bf16[512,384]{1,0:T(8,128)(2,1)}, bf16[512,384]{1,0:T(8,128)(2,1)S(1)}, u32[]{:S(2)}, u32[]{:S(2)}) collective-permute-start(bf16[512,384]{1,0:T(8,128)(2,1)} %get-tuple-element.34.q0), channel_id=1, source_target_pairs={{0,64},{8,72},{16,80},{24,88},{32,96},{40,104},{48,112},{56,120},{... | collective-permute-start | bytes 1179656 | tf_op jit(solution)/shard_map/ppermute | solution.py:373
  20.0 0.6 stack.23.cols
  20.6 0.0 collective-permute-done.q1
  20.6 3.8 %take_blocks.1 = (bf16[384,640]{1,0:T(8,128)(2,1)}, bf16[576,640]{1,0:T(8,128)(2,1)}, bf16[576,640]{1,0:T(8,128)(2,1)}, bf16[384,640]{1,0:T(8,128)(2,1)}) custom-call(s32[5]{0:T(128)} %stack.23.cols, bf16[384,5120]{1,0:T(8,128)(2,1)} %wo.1), custom_call_target="tpu_custom_call" | custom-call | flops 1000000 | bytes 6000000 | tf_op jit(solution)/shard_map/take_blocks/pallas_call | solution.py:179
  24.4 1.6 %collective-permute-start.7 = (bf16[576,640]{1,0:T(8,128)(2,1)}, bf16[576,640]{1,0:T(8,128)(2,1)S(1)}, u32[]{:S(2)}, u32[]{:S(2)}) collective-permute-start(bf16[576,640]{1,0:T(8,128)(2,1)} %get-tuple-element.39), channel_id=1, source_target_pairs={{0,1},{1,2},{2,3},{3,0},{4,5},{5,6},{6,7},{7,4},{8,9},{9,10},{10,1... | collective-permute-start | bytes 2211848 | tf_op jit(solution)/shard_map/ppermute | solution.py:376
  26.1 1.7 %collective-permute-start.8 = (bf16[576,640]{1,0:T(8,128)(2,1)}, bf16[576,640]{1,0:T(8,128)(2,1)S(1)}, u32[]{:S(2)}, u32[]{:S(2)}) collective-permute-start(bf16[576,640]{1,0:T(8,128)(2,1)} %get-tuple-element.40), channel_id=1, source_target_pairs={{0,3},{1,0},{2,1},{3,2},{4,7},{5,4},{6,5},{7,6},{8,11},{9,8},{10,9... | collective-permute-start | bytes 2211848 | tf_op jit(solution)/shard_map/ppermute | solution.py:377
  27.7 2.5 %collective-permute-done.1.q2 = bf16[512,384]{1,0:T(8,128)(2,1)S(1)} collective-permute-done((bf16[512,384]{1,0:T(8,128)(2,1)}, bf16[512,384]{1,0:T(8,128)(2,1)S(1)}, u32[]{:S(2)}, u32[]{:S(2)}) %collective-permute-start.1) | collective-permute-done | bytes 393248 | tf_op jit(solution)/shard_map/ppermute | solution.py:373
  30.3 0.0 collective-permute-start.2
  30.3 5.4 %collective-permute-done.4.k2.n2 = bf16[512,768]{1,0:T(8,128)(2,1)S(1)} collective-permute-done((bf16[512,768]{1,0:T(8,128)(2,1)}, bf16[512,768]{1,0:T(8,128)(2,1)S(1)}, u32[]{:S(2)}, u32[]{:S(2)}) %collective-permute-start.4) | collective-permute-done | bytes 786464 | tf_op jit(solution)/shard_map/ppermute | solution.py:366
  35.7 3.7 %collective-permute-start.6 = (bf16[256,768]{1,0:T(8,128)(2,1)S(1)}, bf16[256,768]{1,0:T(8,128)(2,1)S(1)}, u32[]{:S(2)}, u32[]{:S(2)}) collective-permute-start(bf16[256,768]{1,0:T(8,128)(2,1)S(1)} %slice.17), channel_id=1, source_target_pairs={{0,48},{8,56},{16,0},{24,8},{32,16},{40,24},{48,32},{56,40},{64,11... | collective-permute-start | bytes 1179656 | tf_op jit(solution)/shard_map/ppermute | solution.py:380
  39.3 0.0 collective-permute-done.3.k1.n1
  39.3 0.3 collective-permute-start.5
  39.6 9.3 %attend_first.1 = (bf16[864,384]{1,0:T(8,128)(2,1)S(1)}, bf16[864,384]{1,0:T(8,128)(2,1)S(1)}) custom-call(bf16[512,384]{1,0:T(8,128)(2,1)S(1)} %copy-done.3, bf16[512,384]{1,0:T(8,128)(2,1)S(1)} %collective-permute-done.q1, bf16[512,384]{1,0:T(8,128)(2,1)S(1)} %collective-permute-done.1.q2, bf16[512,768]{1,0:T(8,128)(2,1)S(1)} %copy-done.2, ...), custom_call_target="tpu_custom_call" | custom-call | flops 7247757312 | bytes 6000000 | tf_op jit(solution)/shard_map/attend_first/pallas_call | solution.py:219
  49.0 0.0 collective-permute-done.7.refs_1_
  49.0 0.0 collective-permute-done.8.refs_4_
  49.0 0.0 collective-permute-done.2.q3
  49.0 0.0 collective-permute-done.6.k1
  49.0 1.5 %collective-permute-done.5.k0 = bf16[256,768]{1,0:T(8,128)(2,1)S(1)} collective-permute-done((bf16[256,768]{1,0:T(8,128)(2,1)S(1)}, bf16[256,768]{1,0:T(8,128)(2,1)S(1)}, u32[]{:S(2)}, u32[]{:S(2)}) %collective-permute-start.5) | collective-permute-done | bytes 393248 | tf_op jit(solution)/shard_map/ppermute | solution.py:379
  50.5 6.2 %attend_last.1 = (bf16[1152,384]{1,0:T(8,128)(2,1)S(1)}, bf16[1152,384]{1,0:T(8,128)(2,1)S(1)}) custom-call(bf16[512,384]{1,0:T(8,128)(2,1)S(1)} %copy-done.3, bf16[512,384]{1,0:T(8,128)(2,1)S(1)} %collective-permute-done.q1, bf16[512,384]{1,0:T(8,128)(2,1)S(1)} %collective-permute-done.1.q2, bf16[512,384]{1,0:T(8,128)(2,1)S(1)} %collective-permute-done.2.q3, ...), custom_call_target="tpu_custom_call" | custom-call | flops 6442450944 | bytes 8000000 | tf_op jit(solution)/shard_map/attend_last/pallas_call | solution.py:258
  56.7 0.1 collective-permute-start.9
  56.8 0.5 collective-permute-start.10
  57.3 0.1 collective-permute-start.11
  57.4 3.1 %collective-permute-start.14 = (bf16[192,640]{1,0:T(8,128)(2,1)S(1)}, bf16[192,640]{1,0:T(8,128)(2,1)S(1)}, u32[]{:S(2)}, u32[]{:S(2)}) collective-permute-start(bf16[192,640]{1,0:T(8,128)(2,1)S(1)} %slice.15), channel_id=1, source_target_pairs={{0,3},{1,0},{2,1},{3,2},{4,7},{5,4},{6,5},{7,6},{8,11},{9,8},{10,9... | collective-permute-start | bytes 737288 | tf_op jit(solution)/shard_map/ppermute | solution.py:386
  60.5 0.0 collective-permute-done.10.refs_6_
  60.5 0.8 collective-permute-done.11.refs_9_
  61.3 0.0 collective-permute-done.9.recv
  61.3 0.2 combine_core.1
  61.5 1.6 %collective-permute-start.21 = (bf16[288,384]{1,0:T(8,128)(2,1)S(1)}, bf16[288,384]{1,0:T(8,128)(2,1)S(1)}, u32[]{:S(2)}, u32[]{:S(2)}) collective-permute-start(bf16[288,384]{1,0:T(8,128)(2,1)S(1)} %get-tuple-element.60), channel_id=1, source_target_pairs={{0,64},{8,72},{16,80},{24,88},{32,96},{40,104},{48,112},{56,120},{... | collective-permute-start | bytes 663560 | tf_op jit(solution)/shard_map/ppermute | solution.py:391
  63.1 1.6 %collective-permute-start.13 = (bf16[192,640]{1,0:T(8,128)(2,1)S(1)}, bf16[192,640]{1,0:T(8,128)(2,1)S(1)}, u32[]{:S(2)}, u32[]{:S(2)}) collective-permute-start(bf16[192,640]{1,0:T(8,128)(2,1)S(1)} %slice.14), channel_id=1, source_target_pairs={{0,1},{1,2},{2,3},{3,0},{4,5},{5,6},{6,7},{7,4},{8,9},{9,10},{10,1... | collective-permute-start | bytes 737288 | tf_op jit(solution)/shard_map/ppermute | solution.py:386
  64.8 0.5 collective-permute-start.12
  65.3 4.6 %collective-permute-done.21.recv = bf16[288,384]{1,0:T(8,128)(2,1)S(1)} collective-permute-done((bf16[288,384]{1,0:T(8,128)(2,1)S(1)}, bf16[288,384]{1,0:T(8,128)(2,1)S(1)}, u32[]{:S(2)}, u32[]{:S(2)}) %collective-permute-start.21) | collective-permute-done | bytes 221216 | tf_op jit(solution)/shard_map/ppermute | solution.py:391
  69.9 0.2 combine_x.3.a0
  70.1 3.3 %collective-permute-start.24 = (bf16[256,384]{1,0:T(8,128)(2,1)S(1)}, bf16[256,384]{1,0:T(8,128)(2,1)S(1)}, u32[]{:S(2)}, u32[]{:S(2)}) collective-permute-start(bf16[256,384]{1,0:T(8,128)(2,1)S(1)} %combine_x.3.a0), channel_id=1, source_target_pairs={{0,3},{1,0},{2,1},{3,2},{4,7},{5,4},{6,5},{7,6},{8,11},{9,8},{10,9... | collective-permute-start | bytes 589832 | tf_op jit(solution)/shard_map/ppermute | solution.py:400
  73.4 0.6 collective-permute-start.23
  74.0 0.0 collective-permute-done.14.refs_3_
  74.0 1.0 collective-permute-start.22
  75.0 0.0 collective-permute-done.13.refs_2_
  75.0 0.0 collective-permute-done.12.recv
  75.0 0.0 collective-permute-start.18
  75.0 0.5 collective-permute-start.19
  75.5 0.2 combine_x.2.a0
  75.7 4.7 %collective-permute-done.24.a3 = bf16[256,384]{1,0:T(8,128)(2,1)S(1)} collective-permute-done((bf16[256,384]{1,0:T(8,128)(2,1)S(1)}, bf16[256,384]{1,0:T(8,128)(2,1)S(1)}, u32[]{:S(2)}, u32[]{:S(2)}) %collective-permute-start.24) | collective-permute-done | bytes 196640 | tf_op jit(solution)/shard_map/ppermute | solution.py:400
  80.4 3.7 %collective-permute-start.17 = (bf16[256,384]{1,0:T(8,128)(2,1)S(1)}, bf16[256,384]{1,0:T(8,128)(2,1)S(1)}, u32[]{:S(2)}, u32[]{:S(2)}) collective-permute-start(bf16[256,384]{1,0:T(8,128)(2,1)S(1)} %combine_x.2.a0), channel_id=1, source_target_pairs={{0,3},{1,0},{2,1},{3,2},{4,7},{5,4},{6,5},{7,6},{8,11},{9,8},{10,9... | collective-permute-start | bytes 589832 | tf_op jit(solution)/shard_map/ppermute | solution.py:400
  84.1 0.0 collective-permute-done.23.a2
  84.1 0.0 collective-permute-start.16
  84.1 0.0 collective-permute-done.22.a1
  84.1 0.9 collective-permute-start.15
  85.0 0.0 collective-permute-done.18.refs_7_
  85.0 0.0 collective-permute-done.19.refs_8_
  85.0 1.2 %out_project.3 = (bf16[256,640]{1,0:T(8,128)(2,1)S(1)}, bf16[256,640]{1,0:T(8,128)(2,1)S(1)}) custom-call(s32[1]{0:T(128)} %bitcast.core, bf16[256,384]{1,0:T(8,128)(2,1)S(1)} %combine_x.3.a0, bf16[256,384]{1,0:T(8,128)(2,1)S(1)} %collective-permute-done.22.a1, bf16[256,384]{1,0:T(8,128)(2,1)S(1)} %collective-permute-done.23.a2, ...), custom_call_target="tpu_custom_call" | custom-call | flops 1006632960 | bytes 6000000 | tf_op jit(solution)/shard_map/out_project/pallas_call | solution.py:328
  86.2 3.1 %collective-permute-start.25 = (bf16[256,640]{1,0:T(8,128)(2,1)S(1)}, bf16[256,640]{1,0:T(8,128)(2,1)S(1)}, u32[]{:S(2)}, u32[]{:S(2)}) collective-permute-start(bf16[256,640]{1,0:T(8,128)(2,1)S(1)} %get-tuple-element.62), channel_id=1, source_target_pairs={{0,4},{1,5},{2,6},{3,7},{4,0},{5,1},{6,2},{7,3},{8,12},{9,13},{10,... | collective-permute-start | bytes 983048 | tf_op jit(solution)/shard_map/ppermute | solution.py:402
  89.3 0.1 collective-permute-done.17.a3
  89.4 2.0 %collective-permute-done.16.a2 = bf16[256,384]{1,0:T(8,128)(2,1)S(1)} collective-permute-done((bf16[256,384]{1,0:T(8,128)(2,1)S(1)}, bf16[256,384]{1,0:T(8,128)(2,1)S(1)}, u32[]{:S(2)}, u32[]{:S(2)}) %collective-permute-start.16) | collective-permute-done | bytes 196640 | tf_op jit(solution)/shard_map/ppermute | solution.py:400
  91.4 2.1 %collective-permute-done.15.a1 = bf16[256,384]{1,0:T(8,128)(2,1)S(1)} collective-permute-done((bf16[256,384]{1,0:T(8,128)(2,1)S(1)}, bf16[256,384]{1,0:T(8,128)(2,1)S(1)}, u32[]{:S(2)}, u32[]{:S(2)}) %collective-permute-start.15) | collective-permute-done | bytes 196640 | tf_op jit(solution)/shard_map/ppermute | solution.py:400
  93.5 1.2 %out_project.2 = (bf16[256,640]{1,0:T(8,128)(2,1)S(1)}, bf16[256,640]{1,0:T(8,128)(2,1)S(1)}) custom-call(s32[1]{0:T(128)} %bitcast.core, bf16[256,384]{1,0:T(8,128)(2,1)S(1)} %combine_x.2.a0, bf16[256,384]{1,0:T(8,128)(2,1)S(1)} %collective-permute-done.15.a1, bf16[256,384]{1,0:T(8,128)(2,1)S(1)} %collective-permute-done.16.a2, ...), custom_call_target="tpu_custom_call" | custom-call | flops 1006632960 | bytes 6000000 | tf_op jit(solution)/shard_map/out_project/pallas_call | solution.py:328
  94.6 3.1 %collective-permute-start.20 = (bf16[256,640]{1,0:T(8,128)(2,1)S(1)}, bf16[256,640]{1,0:T(8,128)(2,1)S(1)}, u32[]{:S(2)}, u32[]{:S(2)}) collective-permute-start(bf16[256,640]{1,0:T(8,128)(2,1)S(1)} %get-tuple-element.58), channel_id=1, source_target_pairs={{0,4},{1,5},{2,6},{3,7},{4,0},{5,1},{6,2},{7,3},{8,12},{9,13},{10,... | collective-permute-start | bytes 983048 | tf_op jit(solution)/shard_map/ppermute | solution.py:402
  97.8 0.0 collective-permute-done.25.recv
  97.8 0.8 finish.2.rest_0_
  98.6 5.5 %collective-permute-done.20.recv = bf16[256,640]{1,0:T(8,128)(2,1)S(1)} collective-permute-done((bf16[256,640]{1,0:T(8,128)(2,1)S(1)}, bf16[256,640]{1,0:T(8,128)(2,1)S(1)}, u32[]{:S(2)}, u32[]{:S(2)}) %collective-permute-start.20) | collective-permute-done | bytes 327712 | tf_op jit(solution)/shard_map/ppermute | solution.py:402
  104.1 0.8 finish.3
  (12 shorter events, 0.1 us)
Async XLA Ops:
  14.3 25.3 %copy-start.2 = (bf16[512,768]{1,0:T(8,128)(2,1)S(1)}, bf16[512,768]{1,0:T(8,128)(2,1)}, u32[]{:S(2)}) copy-start(bf16[512,768]{1,0:T(8,128)(2,1)} %get-tuple-element.36.k0.n0) | copy-start | bytes 2359300
  14.3 25.3 %copy-start.3 = (bf16[512,384]{1,0:T(8,128)(2,1)S(1)}, bf16[512,384]{1,0:T(8,128)(2,1)}, u32[]{:S(2)}) copy-start(bf16[512,384]{1,0:T(8,128)(2,1)} %get-tuple-element.34.q0) | copy-start | bytes 1179652
  14.3 21.3 %collective-permute-start.4 = (bf16[512,768]{1,0:T(8,128)(2,1)}, bf16[512,768]{1,0:T(8,128)(2,1)S(1)}, u32[]{:S(2)}, u32[]{:S(2)}) collective-permute-start(bf16[512,768]{1,0:T(8,128)(2,1)} %get-tuple-element.36.k0.n0), channel_id=1, source_target_pairs={{0,48},{8,56},{16,0},{24,8},{32,16},{40,24},{48,32},{56,40},{64,11... | collective-permute-start | bytes 2359304 | tf_op jit(solution)/shard_map/ppermute | solution.py:366
  18.5 20.8 %collective-permute-start.3 = (bf16[512,768]{1,0:T(8,128)(2,1)}, bf16[512,768]{1,0:T(8,128)(2,1)S(1)}, u32[]{:S(2)}, u32[]{:S(2)}) collective-permute-start(bf16[512,768]{1,0:T(8,128)(2,1)} %get-tuple-element.36.k0.n0), channel_id=1, source_target_pairs={{0,16},{8,24},{16,32},{24,40},{32,48},{40,56},{48,0},{56,8},{64,80... | collective-permute-start | bytes 2359304 | tf_op jit(solution)/shard_map/ppermute | solution.py:365
  18.5 2.1 %collective-permute-start = (bf16[512,384]{1,0:T(8,128)(2,1)}, bf16[512,384]{1,0:T(8,128)(2,1)S(1)}, u32[]{:S(2)}, u32[]{:S(2)}) collective-permute-start(bf16[512,384]{1,0:T(8,128)(2,1)} %get-tuple-element.34.q0), channel_id=1, source_target_pairs={{0,8},{8,0},{16,24},{24,16},{32,40},{40,32},{48,56},{56,48},{64,72... | collective-permute-start | bytes 1179656 | tf_op jit(solution)/shard_map/ppermute | solution.py:372
  18.5 11.7 %collective-permute-start.1 = (bf16[512,384]{1,0:T(8,128)(2,1)}, bf16[512,384]{1,0:T(8,128)(2,1)S(1)}, u32[]{:S(2)}, u32[]{:S(2)}) collective-permute-start(bf16[512,384]{1,0:T(8,128)(2,1)} %get-tuple-element.34.q0), channel_id=1, source_target_pairs={{0,64},{8,72},{16,80},{24,88},{32,96},{40,104},{48,112},{56,120},{... | collective-permute-start | bytes 1179656 | tf_op jit(solution)/shard_map/ppermute | solution.py:373
  24.4 24.5 %collective-permute-start.7 = (bf16[576,640]{1,0:T(8,128)(2,1)}, bf16[576,640]{1,0:T(8,128)(2,1)S(1)}, u32[]{:S(2)}, u32[]{:S(2)}) collective-permute-start(bf16[576,640]{1,0:T(8,128)(2,1)} %get-tuple-element.39), channel_id=1, source_target_pairs={{0,1},{1,2},{2,3},{3,0},{4,5},{5,6},{6,7},{7,4},{8,9},{9,10},{10,1... | collective-permute-start | bytes 2211848 | tf_op jit(solution)/shard_map/ppermute | solution.py:376
  26.1 22.9 %collective-permute-start.8 = (bf16[576,640]{1,0:T(8,128)(2,1)}, bf16[576,640]{1,0:T(8,128)(2,1)S(1)}, u32[]{:S(2)}, u32[]{:S(2)}) collective-permute-start(bf16[576,640]{1,0:T(8,128)(2,1)} %get-tuple-element.40), channel_id=1, source_target_pairs={{0,3},{1,0},{2,1},{3,2},{4,7},{5,4},{6,5},{7,6},{8,11},{9,8},{10,9... | collective-permute-start | bytes 2211848 | tf_op jit(solution)/shard_map/ppermute | solution.py:377
  30.3 18.7 %collective-permute-start.2 = (bf16[512,384]{1,0:T(8,128)(2,1)S(1)}, bf16[512,384]{1,0:T(8,128)(2,1)S(1)}, u32[]{:S(2)}, u32[]{:S(2)}) collective-permute-start(bf16[512,384]{1,0:T(8,128)(2,1)S(1)} %collective-permute-done.1.q2), channel_id=1, source_target_pairs={{0,8},{8,0},{16,24},{24,16},{32,40},{40,32},{48,56},{56,48},{64,72... | collective-permute-start | bytes 1179656 | tf_op jit(solution)/shard_map/ppermute | solution.py:378
  35.7 13.3 %collective-permute-start.6 = (bf16[256,768]{1,0:T(8,128)(2,1)S(1)}, bf16[256,768]{1,0:T(8,128)(2,1)S(1)}, u32[]{:S(2)}, u32[]{:S(2)}) collective-permute-start(bf16[256,768]{1,0:T(8,128)(2,1)S(1)} %slice.17), channel_id=1, source_target_pairs={{0,48},{8,56},{16,0},{24,8},{32,16},{40,24},{48,32},{56,40},{64,11... | collective-permute-start | bytes 1179656 | tf_op jit(solution)/shard_map/ppermute | solution.py:380
  39.3 11.2 %collective-permute-start.5 = (bf16[256,768]{1,0:T(8,128)(2,1)S(1)}, bf16[256,768]{1,0:T(8,128)(2,1)S(1)}, u32[]{:S(2)}, u32[]{:S(2)}) collective-permute-start(bf16[256,768]{1,0:T(8,128)(2,1)S(1)} %slice.16), channel_id=1, source_target_pairs={{0,16},{8,24},{16,32},{24,40},{32,48},{40,56},{48,0},{56,8},{64,80... | collective-permute-start | bytes 1179656 | tf_op jit(solution)/shard_map/ppermute | solution.py:379
  56.7 28.3 %copy-start = (bf16[384,640]{1,0:T(8,128)(2,1)S(1)}, bf16[384,640]{1,0:T(8,128)(2,1)}, u32[]{:S(2)}) copy-start(bf16[384,640]{1,0:T(8,128)(2,1)} %get-tuple-element.51.refs_0_) | copy-start | bytes 1474564
  56.7 28.3 %copy-start.1 = (bf16[384,640]{1,0:T(8,128)(2,1)S(1)}, bf16[384,640]{1,0:T(8,128)(2,1)}, u32[]{:S(2)}) copy-start(bf16[384,640]{1,0:T(8,128)(2,1)} %get-tuple-element.54.refs_5_) | copy-start | bytes 1474564
  56.7 4.6 %collective-permute-start.9 = (bf16[1152,384]{1,0:T(8,128)(2,1)S(1)}, bf16[1152,384]{1,0:T(8,128)(2,1)S(1)}, u32[]{:S(2)}, u32[]{:S(2)}) collective-permute-start(bf16[1152,384]{1,0:T(8,128)(2,1)S(1)} %get-tuple-element.44), channel_id=1, source_target_pairs={{0,8},{8,0},{16,24},{24,16},{32,40},{40,32},{48,56},{56,48},{64,72... | collective-permute-start | bytes 2654216 | tf_op jit(solution)/shard_map/ppermute | solution.py:389
  56.8 3.7 %collective-permute-start.10 = (bf16[576,640]{1,0:T(8,128)(2,1)S(1)}, bf16[576,640]{1,0:T(8,128)(2,1)S(1)}, u32[]{:S(2)}, u32[]{:S(2)}) collective-permute-start(bf16[576,640]{1,0:T(8,128)(2,1)S(1)} %collective-permute-done.7.refs_1_), channel_id=1, source_target_pairs={{0,8},{8,0},{16,24},{24,16},{32,40},{40,32},{48,56},{56,48},{64,72... | collective-permute-start | bytes 2211848 | tf_op jit(solution)/shard_map/ppermute | solution.py:385
  57.3 4.0 %collective-permute-start.11 = (bf16[576,640]{1,0:T(8,128)(2,1)S(1)}, bf16[576,640]{1,0:T(8,128)(2,1)S(1)}, u32[]{:S(2)}, u32[]{:S(2)}) collective-permute-start(bf16[576,640]{1,0:T(8,128)(2,1)S(1)} %collective-permute-done.8.refs_4_), channel_id=1, source_target_pairs={{0,8},{8,0},{16,24},{24,16},{32,40},{40,32},{48,56},{56,48},{64,72... | collective-permute-start | bytes 2211848 | tf_op jit(solution)/shard_map/ppermute | solution.py:385
  57.4 16.6 %collective-permute-start.14 = (bf16[192,640]{1,0:T(8,128)(2,1)S(1)}, bf16[192,640]{1,0:T(8,128)(2,1)S(1)}, u32[]{:S(2)}, u32[]{:S(2)}) collective-permute-start(bf16[192,640]{1,0:T(8,128)(2,1)S(1)} %slice.15), channel_id=1, source_target_pairs={{0,3},{1,0},{2,1},{3,2},{4,7},{5,4},{6,5},{7,6},{8,11},{9,8},{10,9... | collective-permute-start | bytes 737288 | tf_op jit(solution)/shard_map/ppermute | solution.py:386
  61.5 8.3 %collective-permute-start.21 = (bf16[288,384]{1,0:T(8,128)(2,1)S(1)}, bf16[288,384]{1,0:T(8,128)(2,1)S(1)}, u32[]{:S(2)}, u32[]{:S(2)}) collective-permute-start(bf16[288,384]{1,0:T(8,128)(2,1)S(1)} %get-tuple-element.60), channel_id=1, source_target_pairs={{0,64},{8,72},{16,80},{24,88},{32,96},{40,104},{48,112},{56,120},{... | collective-permute-start | bytes 663560 | tf_op jit(solution)/shard_map/ppermute | solution.py:391
  63.1 11.9 %collective-permute-start.13 = (bf16[192,640]{1,0:T(8,128)(2,1)S(1)}, bf16[192,640]{1,0:T(8,128)(2,1)S(1)}, u32[]{:S(2)}, u32[]{:S(2)}) collective-permute-start(bf16[192,640]{1,0:T(8,128)(2,1)S(1)} %slice.14), channel_id=1, source_target_pairs={{0,1},{1,2},{2,3},{3,0},{4,5},{5,6},{6,7},{7,4},{8,9},{9,10},{10,1... | collective-permute-start | bytes 737288 | tf_op jit(solution)/shard_map/ppermute | solution.py:386
  64.8 10.2 %collective-permute-start.12 = (bf16[288,384]{1,0:T(8,128)(2,1)S(1)}, bf16[288,384]{1,0:T(8,128)(2,1)S(1)}, u32[]{:S(2)}, u32[]{:S(2)}) collective-permute-start(bf16[288,384]{1,0:T(8,128)(2,1)S(1)} %get-tuple-element.49), channel_id=1, source_target_pairs={{0,64},{8,72},{16,80},{24,88},{32,96},{40,104},{48,112},{56,120},{... | collective-permute-start | bytes 663560 | tf_op jit(solution)/shard_map/ppermute | solution.py:392
  70.1 10.3 %collective-permute-start.24 = (bf16[256,384]{1,0:T(8,128)(2,1)S(1)}, bf16[256,384]{1,0:T(8,128)(2,1)S(1)}, u32[]{:S(2)}, u32[]{:S(2)}) collective-permute-start(bf16[256,384]{1,0:T(8,128)(2,1)S(1)} %combine_x.3.a0), channel_id=1, source_target_pairs={{0,3},{1,0},{2,1},{3,2},{4,7},{5,4},{6,5},{7,6},{8,11},{9,8},{10,9... | collective-permute-start | bytes 589832 | tf_op jit(solution)/shard_map/ppermute | solution.py:400
  73.4 10.7 %collective-permute-start.23 = (bf16[256,384]{1,0:T(8,128)(2,1)S(1)}, bf16[256,384]{1,0:T(8,128)(2,1)S(1)}, u32[]{:S(2)}, u32[]{:S(2)}) collective-permute-start(bf16[256,384]{1,0:T(8,128)(2,1)S(1)} %combine_x.3.a0), channel_id=1, source_target_pairs={{0,2},{1,3},{2,0},{3,1},{4,6},{5,7},{6,4},{7,5},{8,10},{9,11},{10,... | collective-permute-start | bytes 589832 | tf_op jit(solution)/shard_map/ppermute | solution.py:400
  74.0 10.1 %collective-permute-start.22 = (bf16[256,384]{1,0:T(8,128)(2,1)S(1)}, bf16[256,384]{1,0:T(8,128)(2,1)S(1)}, u32[]{:S(2)}, u32[]{:S(2)}) collective-permute-start(bf16[256,384]{1,0:T(8,128)(2,1)S(1)} %combine_x.3.a0), channel_id=1, source_target_pairs={{0,1},{1,2},{2,3},{3,0},{4,5},{5,6},{6,7},{7,4},{8,9},{9,10},{10,1... | collective-permute-start | bytes 589832 | tf_op jit(solution)/shard_map/ppermute | solution.py:400
  75.0 10.0 %collective-permute-start.18 = (bf16[192,640]{1,0:T(8,128)(2,1)S(1)}, bf16[192,640]{1,0:T(8,128)(2,1)S(1)}, u32[]{:S(2)}, u32[]{:S(2)}) collective-permute-start(bf16[192,640]{1,0:T(8,128)(2,1)S(1)} %collective-permute-done.13.refs_2_), channel_id=1, source_target_pairs={{0,8},{8,0},{16,24},{24,16},{32,40},{40,32},{48,56},{56,48},{64,72... | collective-permute-start | bytes 737288 | tf_op jit(solution)/shard_map/ppermute | solution.py:394
  75.0 10.0 %collective-permute-start.19 = (bf16[192,640]{1,0:T(8,128)(2,1)S(1)}, bf16[192,640]{1,0:T(8,128)(2,1)S(1)}, u32[]{:S(2)}, u32[]{:S(2)}) collective-permute-start(bf16[192,640]{1,0:T(8,128)(2,1)S(1)} %collective-permute-done.14.refs_3_), channel_id=1, source_target_pairs={{0,8},{8,0},{16,24},{24,16},{32,40},{40,32},{48,56},{56,48},{64,72... | collective-permute-start | bytes 737288 | tf_op jit(solution)/shard_map/ppermute | solution.py:394
  80.4 9.0 %collective-permute-start.17 = (bf16[256,384]{1,0:T(8,128)(2,1)S(1)}, bf16[256,384]{1,0:T(8,128)(2,1)S(1)}, u32[]{:S(2)}, u32[]{:S(2)}) collective-permute-start(bf16[256,384]{1,0:T(8,128)(2,1)S(1)} %combine_x.2.a0), channel_id=1, source_target_pairs={{0,3},{1,0},{2,1},{3,2},{4,7},{5,4},{6,5},{7,6},{8,11},{9,8},{10,9... | collective-permute-start | bytes 589832 | tf_op jit(solution)/shard_map/ppermute | solution.py:400
  84.1 7.3 %collective-permute-start.16 = (bf16[256,384]{1,0:T(8,128)(2,1)S(1)}, bf16[256,384]{1,0:T(8,128)(2,1)S(1)}, u32[]{:S(2)}, u32[]{:S(2)}) collective-permute-start(bf16[256,384]{1,0:T(8,128)(2,1)S(1)} %combine_x.2.a0), channel_id=1, source_target_pairs={{0,2},{1,3},{2,0},{3,1},{4,6},{5,7},{6,4},{7,5},{8,10},{9,11},{10,... | collective-permute-start | bytes 589832 | tf_op jit(solution)/shard_map/ppermute | solution.py:400
  84.1 9.3 %collective-permute-start.15 = (bf16[256,384]{1,0:T(8,128)(2,1)S(1)}, bf16[256,384]{1,0:T(8,128)(2,1)S(1)}, u32[]{:S(2)}, u32[]{:S(2)}) collective-permute-start(bf16[256,384]{1,0:T(8,128)(2,1)S(1)} %combine_x.2.a0), channel_id=1, source_target_pairs={{0,1},{1,2},{2,3},{3,0},{4,5},{5,6},{6,7},{7,4},{8,9},{9,10},{10,1... | collective-permute-start | bytes 589832 | tf_op jit(solution)/shard_map/ppermute | solution.py:400
  86.2 11.6 %collective-permute-start.25 = (bf16[256,640]{1,0:T(8,128)(2,1)S(1)}, bf16[256,640]{1,0:T(8,128)(2,1)S(1)}, u32[]{:S(2)}, u32[]{:S(2)}) collective-permute-start(bf16[256,640]{1,0:T(8,128)(2,1)S(1)} %get-tuple-element.62), channel_id=1, source_target_pairs={{0,4},{1,5},{2,6},{3,7},{4,0},{5,1},{6,2},{7,3},{8,12},{9,13},{10,... | collective-permute-start | bytes 983048 | tf_op jit(solution)/shard_map/ppermute | solution.py:402
  94.6 9.4 %collective-permute-start.20 = (bf16[256,640]{1,0:T(8,128)(2,1)S(1)}, bf16[256,640]{1,0:T(8,128)(2,1)S(1)}, u32[]{:S(2)}, u32[]{:S(2)}) collective-permute-start(bf16[256,640]{1,0:T(8,128)(2,1)S(1)} %get-tuple-element.58), channel_id=1, source_target_pairs={{0,4},{1,5},{2,6},{3,7},{4,0},{5,1},{6,2},{7,3},{8,12},{9,13},{10,... | collective-permute-start | bytes 983048 | tf_op jit(solution)/shard_map/ppermute | solution.py:402

commit v5 on v4

--- a/solution.py
+++ b/solution.py
@@ -201,10 +201,12 @@
     return acc
 
 
-def first_kernel(q0, q1, q2, k0, k1, k2, part0, part1):
-    for i, q in enumerate((q0, q1, q2)):
-        acc = mix(q[...], (k0, k1, k2), 256)
-        for half, part in enumerate((part0, part1)):
+def part_kernel(n_q, n_kv, *refs):
+    qs, kvs = refs[:n_q], refs[n_q : n_q + n_kv]
+    parts = refs[n_q + n_kv :]
+    for i, q in enumerate(qs):
+        acc = mix(q[...], kvs, 256)
+        for half, part in enumerate(parts):
             rows = acc[half * HALF : (half + 1) * HALF]
             at = i * PACK
             part[at : at + HALF, :] = rows[:, :HD].astype(BF16)
@@ -214,43 +216,40 @@
                 part[to : to + 16, :] = t[:16].astype(BF16)
 
 
-def attend_first(qs, kvs):
+def attend_part(qs, kvs):
     head = lambda rows, cols: pl.BlockSpec((rows, cols), lambda h: (0, h))
-    return pl.pallas_call(
-        first_kernel,
+    pairs = len(qs) * len(kvs)
+    return pl.pallas_call(
+        functools.partial(part_kernel, len(qs), len(kvs)),
         grid=(GROUP_HEADS,),
-        in_specs=[head(ROWS, HD)] * 3 + [head(ROWS, 2 * HD)] * 3,
-        out_specs=[head(3 * PACK, HD)] * 2,
-        out_shape=[jax.ShapeDtypeStruct((3 * PACK, WIDE), BF16)] * 2,
+        in_specs=[head(ROWS, HD)] * len(qs) + [head(ROWS, 2 * HD)] * len(kvs),
+        out_specs=[head(len(qs) * PACK, HD)] * 2,
+        out_shape=[jax.ShapeDtypeStruct((len(qs) * PACK, WIDE), BF16)] * 2,
         compiler_params=params(24),
-        cost_estimate=cost(3 * 4 * 1536 * 1536 * 256, 6e6, 3 * 2 * 1536 * 1536),
-        name="attend_first",
+        cost_estimate=cost(pairs * 3 * ROWS * ROWS * 256, 1e6, 0),
+        name="attend_part",
     )(*qs, *kvs)
 
 
-def last_kernel(q0, q1, q2, q3, n0, n1, n2, k0, k1, part0, part1, keep, send):
+def last_kernel(q0, q1, q2, q3, k0, k1, own0, own1, near0, near1, cross0, cross1, keep, send):
     for h in range(GROUP_HEADS):
         col = slice(h * HD, (h + 1) * HD)
         wide = slice(2 * h * HD, 2 * (h + 1) * HD)
         for i, (q, out) in enumerate(((q0, keep), (q1, send), (q2, keep), (q3, send))):
-            kvs = (k0[:, wide], k1[:, wide])
-            if i == 3:
-                kvs = (n0[:, wide], n1[:, wide], n2[:, wide]) + kvs
-            acc = mix(q[:, col], kvs, 256)
-            for half, part in enumerate((part0, part1)):
+            acc = mix(q[:, col], (k0[:, wide], k1[:, wide]), 256)
+            for half, (own, near, cross) in enumerate(((own0, near0, cross0), (own1, near1, cross1))):
                 rows = acc[half * HALF : (half + 1) * HALF]
                 base = (2 * half + i // 2) * PACK
-                mixture, old = rows[:, :HD], None
+                quarter = slice(i * PACK, (i + 1) * PACK)
                 if i < 3:
-                    old = part[i * PACK : (i + 1) * PACK, col].astype(F32)
-                    mixture = mixture + old[:HALF]
-                out[base : base + HALF, col] = mixture.astype(BF16)
+                    old = own[quarter, col].astype(F32) + near[quarter, col].astype(F32)
+                else:
+                    old = cross[:, col].astype(F32)
+                out[base : base + HALF, col] = (rows[:, :HD] + old[:HALF]).astype(BF16)
                 for p in range(HALF // 128):
                     t = jnp.transpose(rows[p * 128 : (p + 1) * 128, HD:])[:16]
                     at = HALF + 16 * p
-                    if i < 3:
-                        t = t + old[at : at + 16]
-                    out[base + at : base + at + 16, col] = t.astype(BF16)
+                    out[base + at : base + at + 16, col] = (t + old[at : at + 16]).astype(BF16)
 
 
 def attend_last(qs, kvs, parts):
@@ -262,7 +261,7 @@
         out_specs=[whole((4 * PACK, WIDE))] * 2,
         out_shape=[jax.ShapeDtypeStruct((4 * PACK, WIDE), BF16)] * 2,
         compiler_params=params(32),
-        cost_estimate=cost(3 * 4 * 2048 * 1024 * 256, 8e6, 3 * 2 * 2048 * 1024),
+        cost_estimate=cost(3 * 4 * 2048 * 512 * 256, 8e6, 0),
         name="attend_last",
     )(*qs, *kvs, *parts)
 
@@ -376,16 +375,19 @@
     up = lax.ppermute(up, "head", Y_STEP[1])
     down = lax.ppermute(down, "head", Y_STEP[3])
     q_xc = lax.ppermute(q_x, "seq", SWAP_CORE)
+    parts_own = attend_part((q, q_core, q_x), (kv,))
+    below, above, *parts_own = lax.optimization_barrier((below, above, *parts_own))
     far_a = lax.ppermute(below[:256], "seq", Z_UP)
     far_b = lax.ppermute(above[256:], "seq", Z_DOWN)
     qs = (q, q_core, q_x, q_xc)
-    parts = attend_first(qs[:3], (kv, below, above))
-    part, up, down = lax.optimization_barrier((parts[0], up, down))
-    parts = [part, parts[1]]
+    parts_near = attend_part(qs[:3], (below, above))
+    parts_cross = attend_part(qs[3:], (kv, below, above))
+    part, up, down = lax.optimization_barrier((parts_near[0], up, down))
+    parts = (*parts_own, part, parts_near[1], *parts_cross)
     second = [lax.ppermute(w, "seq", SWAP_CORE) for w in (up, down)]
     far = [lax.ppermute(up[WIDE:], "head", Y_STEP[1]), lax.ppermute(down[WIDE:], "head", Y_STEP[3])]
 
-    keep, send = attend_last(qs, (kv, below, above, far_a, far_b), parts)
+    keep, send = attend_last(qs, (far_a, far_b), parts)
     recv, *second = lax.optimization_barrier((lax.ppermute(send, "seq", SWAP_CORE), *second))
     mine0, away0, mine1, away1 = combine_core(keep, recv)
     recv0 = lax.ppermute(away0, "seq", SWAP_X)

time: 105 us -> 104 us (level)
  Pallas kernels: 38.2 us -> 41.7 us
  waiting for transfers between devices: 29.2 us -> 26.6 us
  starting transfers between devices: 36.6 us -> 34.5 us
    pallas_call x1 -> x3, Pallas kernels: 9.33 us -> 15.3 us  [attend_part(): pl.pallas_call(functools.partial(part_kernel, len(qs), len(kvs)), grid=(G...]
    ppermute x1, waiting for transfers between devices: 5.37 us -> 1.04 us  [shards(): above = lax.ppermute(kv, 'seq', Z_DOWN)]
    ppermute x1, waiting for transfers between devices: 0.01 us -> 3.31 us  [shards(): below = lax.ppermute(kv, 'seq', Z_UP)]
    ppermute x1, starting transfers between devices: 3.66 us -> 0.35 us  [shards(): far_b = lax.ppermute(above[256:], 'seq', Z_DOWN)]
    pallas_call x1, Pallas kernels: 6.18 us -> 3.74 us  [attend_last(): pl.pallas_call(last_kernel, grid=(1,), in_specs=[whole(a.shape) for a in...]
    ppermute x1, waiting for transfers between devices: 1.5 us -> 0.01 us  [shards(): far_a = lax.ppermute(below[:256], 'seq', Z_UP)]
    ppermute x1, starting transfers between devices: 0.26 us -> 1.74 us  [shards(): far_a = lax.ppermute(below[:256], 'seq', Z_UP)]
  transfers between devices with their start and end apart: 26 -> 26, of which waited for: 10 -> 10; matrix products, arithmetic and copies ran while one was open for 1% -> 1% of each run, Pallas kernels for 16% -> 22%
where the time goes in v5:
time: 104 us
  Pallas kernels  41.7 us (40%)
  starting transfers between devices  34.5 us (33%)
  waiting for transfers between devices  26.6 us (26%)
    pallas_call x3, Pallas kernels, attend_part(): pl.pallas_call(functools.partial(part_kernel, len(qs), len(kvs)), grid=(G...  15.3 us
    pallas_call x1, Pallas kernels, project(): pl.pallas_call(qkv_kernel, in_specs=[hbm] * 8, out_specs=[vmem, vmem], ou...  14.3 us
    ppermute x6, starting transfers between devices, shards(): attended = [att] + [lax.ppermute(att, 'head', Y_STEP[r]) for r in (1, 2, 3)]  9.23 us
    ppermute x6, waiting for transfers between devices, shards(): attended = [att] + [lax.ppermute(att, 'head', Y_STEP[r]) for r in (1, 2, 3)]  8.9 us
    ppermute x2, starting transfers between devices, shards(): out = finish(half, kept, lax.ppermute(sent, 'head', SWAP_XHI), out)  6.2 us
    ppermute x2, waiting for transfers between devices, shards(): out = finish(half, kept, lax.ppermute(sent, 'head', SWAP_XHI), out)  5.51 us
    ppermute x1, waiting for transfers between devices, shards(): recv0 = lax.ppermute(away0, 'seq', SWAP_X)  4.57 us
    ppermute x1, starting transfers between devices, shards(): above = lax.ppermute(kv, 'seq', Z_DOWN)  4.19 us
  transfers between devices with their start and end apart: 26, of which 10 were waited for; matrix products, arithmetic and copies ran while one was open for 1% of the time, Pallas kernels for 22%

profile of v5, /device:TPU:0, one launch (start us, length us, event | category | flops | bytes accessed | tf_op | source)
XLA Modules:
  0.0 103.8 jit_solution(15350041109233765169)
XLA Ops:
  0.0 14.3 %project.1 = (bf16[512,384]{1,0:T(8,128)(2,1)}, bf16[512,768]{1,0:T(8,128)(2,1)}) custom-call(bf16[512,5120]{1,0:T(8,128)(2,1)} %tok.1, f32[1,5120]{1,0:T(1,128)} %bitcast.8, f32[1,5120]{1,0:T(1,128)} %bitcast.9, bf16[5120,384]{1,0:T(8,128)(2,1)} %wq.1, bf16[5120,384]{1,0:T(8,128)(2,1)} %wk.1, bf16[5120,384]{1,0:T(8,128)(2,1)} %wv.1, f32[384]{0:T(512)} %gq_h.1, ...), custom_call_target="tpu_custom_call" | custom-call | flops 6039797760 | bytes 18000000 | tf_op jit(solution)/shard_map/project/pallas_call | solution.py:131
  14.3 4.2 %collective-permute-start.4 = (bf16[512,768]{1,0:T(8,128)(2,1)}, bf16[512,768]{1,0:T(8,128)(2,1)S(1)}, u32[]{:S(2)}, u32[]{:S(2)}) collective-permute-start(bf16[512,768]{1,0:T(8,128)(2,1)} %get-tuple-element.44.refs_3_.refs_1_), channel_id=1, source_target_pairs={{0,48},{8,56},{16,0},{24,8},{32,16},{40,24},{48,32},{56,40},{64,11... | collective-permute-start | bytes 2359304 | tf_op jit(solution)/shard_map/ppermute | solution.py:365
  18.5 0.0 collective-permute-start.3
  18.5 0.0 collective-permute-start
  18.5 1.5 %collective-permute-start.1 = (bf16[512,384]{1,0:T(8,128)(2,1)}, bf16[512,384]{1,0:T(8,128)(2,1)S(1)}, u32[]{:S(2)}, u32[]{:S(2)}) collective-permute-start(bf16[512,384]{1,0:T(8,128)(2,1)} %get-tuple-element.42.refs_0_.q0), channel_id=1, source_target_pairs={{0,64},{8,72},{16,80},{24,88},{32,96},{40,104},{48,112},{56,120},{... | collective-permute-start | bytes 1179656 | tf_op jit(solution)/shard_map/ppermute | solution.py:372
  20.0 0.7 stack.23.cols
  20.7 0.0 collective-permute-done.refs_1_.q1
  20.7 3.8 %take_blocks.1 = (bf16[384,640]{1,0:T(8,128)(2,1)}, bf16[576,640]{1,0:T(8,128)(2,1)}, bf16[576,640]{1,0:T(8,128)(2,1)}, bf16[384,640]{1,0:T(8,128)(2,1)}) custom-call(s32[5]{0:T(128)} %stack.23.cols, bf16[384,5120]{1,0:T(8,128)(2,1)} %wo.1), custom_call_target="tpu_custom_call" | custom-call | flops 1000000 | bytes 6000000 | tf_op jit(solution)/shard_map/take_blocks/pallas_call | solution.py:179
  24.5 1.6 %collective-permute-start.7 = (bf16[576,640]{1,0:T(8,128)(2,1)}, bf16[576,640]{1,0:T(8,128)(2,1)S(1)}, u32[]{:S(2)}, u32[]{:S(2)}) collective-permute-start(bf16[576,640]{1,0:T(8,128)(2,1)} %get-tuple-element.53), channel_id=1, source_target_pairs={{0,1},{1,2},{2,3},{3,0},{4,5},{5,6},{6,7},{7,4},{8,9},{9,10},{10,1... | collective-permute-start | bytes 2211848 | tf_op jit(solution)/shard_map/ppermute | solution.py:375
  26.2 1.7 %collective-permute-start.8 = (bf16[576,640]{1,0:T(8,128)(2,1)}, bf16[576,640]{1,0:T(8,128)(2,1)S(1)}, u32[]{:S(2)}, u32[]{:S(2)}) collective-permute-start(bf16[576,640]{1,0:T(8,128)(2,1)} %get-tuple-element.54), channel_id=1, source_target_pairs={{0,3},{1,0},{2,1},{3,2},{4,7},{5,4},{6,5},{7,6},{8,11},{9,8},{10,9... | collective-permute-start | bytes 2211848 | tf_op jit(solution)/shard_map/ppermute | solution.py:376
  27.8 2.4 %collective-permute-done.1.refs_2_.q2 = bf16[512,384]{1,0:T(8,128)(2,1)S(1)} collective-permute-done((bf16[512,384]{1,0:T(8,128)(2,1)}, bf16[512,384]{1,0:T(8,128)(2,1)S(1)}, u32[]{:S(2)}, u32[]{:S(2)}) %collective-permute-start.1) | collective-permute-done | bytes 393248 | tf_op jit(solution)/shard_map/ppermute | solution.py:372
  30.3 0.0 collective-permute-start.2
  30.3 4.3 %attend_part.3 = (bf16[864,384]{1,0:T(8,128)(2,1)S(1)}, bf16[864,384]{1,0:T(8,128)(2,1)S(1)}) custom-call(bf16[512,384]{1,0:T(8,128)(2,1)S(1)} %copy-done.3, bf16[512,384]{1,0:T(8,128)(2,1)S(1)} %collective-permute-done.refs_1_.q1, bf16[512,384]{1,0:T(8,128)(2,1)S(1)} %collective-permute-done.1.refs_2_.q2, bf16[512,768]{1,0:T(8,128)(2,1)S(1)} %copy-done.2), custom_call_target="tpu_custom_call" | custom-call | flops 603979776 | bytes 1000000 | tf_op jit(solution)/shard_map/attend_part/pallas_call | solution.py:222
  34.6 1.0 %collective-permute-done.4.refs_4_.refs_3_ = bf16[512,768]{1,0:T(8,128)(2,1)S(1)} collective-permute-done((bf16[512,768]{1,0:T(8,128)(2,1)}, bf16[512,768]{1,0:T(8,128)(2,1)S(1)}, u32[]{:S(2)}, u32[]{:S(2)}) %collective-permute-start.4) | collective-permute-done | bytes 786464 | tf_op jit(solution)/shard_map/ppermute | solution.py:365
  35.6 3.3 %collective-permute-done.3.refs_3_.refs_2_ = bf16[512,768]{1,0:T(8,128)(2,1)S(1)} collective-permute-done((bf16[512,768]{1,0:T(8,128)(2,1)}, bf16[512,768]{1,0:T(8,128)(2,1)S(1)}, u32[]{:S(2)}, u32[]{:S(2)}) %collective-permute-start.3) | collective-permute-done | bytes 786464 | tf_op jit(solution)/shard_map/ppermute | solution.py:364
  39.0 0.4 collective-permute-start.6
  39.4 1.7 %collective-permute-start.5 = (bf16[256,768]{1,0:T(8,128)(2,1)S(1)}, bf16[256,768]{1,0:T(8,128)(2,1)S(1)}, u32[]{:S(2)}, u32[]{:S(2)}) collective-permute-start(bf16[256,768]{1,0:T(8,128)(2,1)S(1)} %slice.12), channel_id=1, source_target_pairs={{0,16},{8,24},{16,32},{24,40},{32,48},{40,56},{48,0},{56,8},{64,80... | collective-permute-start | bytes 1179656 | tf_op jit(solution)/shard_map/ppermute | solution.py:380
  41.1 0.0 collective-permute-done.2.refs_0_.q3
  41.1 4.2 %attend_part.5 = (bf16[288,384]{1,0:T(8,128)(2,1)S(1)}, bf16[288,384]{1,0:T(8,128)(2,1)S(1)}) custom-call(bf16[512,384]{1,0:T(8,128)(2,1)S(1)} %collective-permute-done.2.refs_0_.q3, bf16[512,768]{1,0:T(8,128)(2,1)S(1)} %copy-done.2, bf16[512,768]{1,0:T(8,128)(2,1)S(1)} %collective-permute-done.3.refs_3_.refs_2_, ...), custom_call_target="tpu_custom_call" | custom-call | flops 603979776 | bytes 1000000 | tf_op jit(solution)/shard_map/attend_part/pallas_call | solution.py:222
  45.3 6.8 %attend_part.4 = (bf16[864,384]{1,0:T(8,128)(2,1)S(1)}, bf16[864,384]{1,0:T(8,128)(2,1)S(1)}) custom-call(bf16[512,384]{1,0:T(8,128)(2,1)S(1)} %copy-done.3, bf16[512,384]{1,0:T(8,128)(2,1)S(1)} %collective-permute-done.refs_1_.q1, bf16[512,384]{1,0:T(8,128)(2,1)S(1)} %collective-permute-done.1.refs_2_.q2, ...), custom_call_target="tpu_custom_call" | custom-call | flops 1207959552 | bytes 1000000 | tf_op jit(solution)/shard_map/attend_part/pallas_call | solution.py:222
  52.1 0.0 collective-permute-done.7.refs_1_
  52.1 0.0 collective-permute-done.8.refs_4_
  52.1 0.0 collective-permute-done.6.k1
  52.2 3.7 %attend_last.1 = (bf16[1152,384]{1,0:T(8,128)(2,1)S(1)}, bf16[1152,384]{1,0:T(8,128)(2,1)S(1)}) custom-call(bf16[512,384]{1,0:T(8,128)(2,1)S(1)} %copy-done.3, bf16[512,384]{1,0:T(8,128)(2,1)S(1)} %collective-permute-done.refs_1_.q1, bf16[512,384]{1,0:T(8,128)(2,1)S(1)} %collective-permute-done.1.refs_2_.q2, ...), custom_call_target="tpu_custom_call" | custom-call | flops 3221225472 | bytes 8000000 | tf_op jit(solution)/shard_map/attend_last/pallas_call | solution.py:257
  55.9 0.1 collective-permute-start.9
  56.0 0.5 collective-permute-start.10
  56.5 0.1 collective-permute-start.11
  56.6 3.1 %collective-permute-start.14 = (bf16[192,640]{1,0:T(8,128)(2,1)S(1)}, bf16[192,640]{1,0:T(8,128)(2,1)S(1)}, u32[]{:S(2)}, u32[]{:S(2)}) collective-permute-start(bf16[192,640]{1,0:T(8,128)(2,1)S(1)} %slice.15), channel_id=1, source_target_pairs={{0,3},{1,0},{2,1},{3,2},{4,7},{5,4},{6,5},{7,6},{8,11},{9,8},{10,9... | collective-permute-start | bytes 737288 | tf_op jit(solution)/shard_map/ppermute | solution.py:388
  59.7 0.0 collective-permute-done.10.refs_6_
  59.7 0.8 collective-permute-done.11.refs_9_
  60.5 0.2 combine_core.1
  60.7 1.6 %collective-permute-start.21 = (bf16[288,384]{1,0:T(8,128)(2,1)S(1)}, bf16[288,384]{1,0:T(8,128)(2,1)S(1)}, u32[]{:S(2)}, u32[]{:S(2)}) collective-permute-start(bf16[288,384]{1,0:T(8,128)(2,1)S(1)} %get-tuple-element.76), channel_id=1, source_target_pairs={{0,64},{8,72},{16,80},{24,88},{32,96},{40,104},{48,112},{56,120},{... | collective-permute-start | bytes 663560 | tf_op jit(solution)/shard_map/ppermute | solution.py:393
  62.3 1.6 %collective-permute-start.13 = (bf16[192,640]{1,0:T(8,128)(2,1)S(1)}, bf16[192,640]{1,0:T(8,128)(2,1)S(1)}, u32[]{:S(2)}, u32[]{:S(2)}) collective-permute-start(bf16[192,640]{1,0:T(8,128)(2,1)S(1)} %slice.14), channel_id=1, source_target_pairs={{0,1},{1,2},{2,3},{3,0},{4,5},{5,6},{6,7},{7,4},{8,9},{9,10},{10,1... | collective-permute-start | bytes 737288 | tf_op jit(solution)/shard_map/ppermute | solution.py:388
  64.0 0.5 collective-permute-start.12
  64.5 4.6 %collective-permute-done.21.recv = bf16[288,384]{1,0:T(8,128)(2,1)S(1)} collective-permute-done((bf16[288,384]{1,0:T(8,128)(2,1)S(1)}, bf16[288,384]{1,0:T(8,128)(2,1)S(1)}, u32[]{:S(2)}, u32[]{:S(2)}) %collective-permute-start.21) | collective-permute-done | bytes 221216 | tf_op jit(solution)/shard_map/ppermute | solution.py:393
  69.1 0.2 combine_x.3.a0
  69.3 3.1 %collective-permute-start.24 = (bf16[256,384]{1,0:T(8,128)(2,1)S(1)}, bf16[256,384]{1,0:T(8,128)(2,1)S(1)}, u32[]{:S(2)}, u32[]{:S(2)}) collective-permute-start(bf16[256,384]{1,0:T(8,128)(2,1)S(1)} %combine_x.3.a0), channel_id=1, source_target_pairs={{0,3},{1,0},{2,1},{3,2},{4,7},{5,4},{6,5},{7,6},{8,11},{9,8},{10,9... | collective-permute-start | bytes 589832 | tf_op jit(solution)/shard_map/ppermute | solution.py:402
  72.3 0.6 collective-permute-start.23
  73.0 0.0 collective-permute-done.14.refs_3_
  73.0 1.0 collective-permute-start.22
  73.9 0.0 collective-permute-done.13.refs_2_
  74.0 0.0 collective-permute-done.12.recv
  74.0 0.0 collective-permute-start.18
  74.0 0.5 collective-permute-start.19
  74.5 0.2 combine_x.2.a0
  74.7 4.7 %collective-permute-done.24.a3 = bf16[256,384]{1,0:T(8,128)(2,1)S(1)} collective-permute-done((bf16[256,384]{1,0:T(8,128)(2,1)S(1)}, bf16[256,384]{1,0:T(8,128)(2,1)S(1)}, u32[]{:S(2)}, u32[]{:S(2)}) %collective-permute-start.24) | collective-permute-done | bytes 196640 | tf_op jit(solution)/shard_map/ppermute | solution.py:402
  79.4 3.7 %collective-permute-start.17 = (bf16[256,384]{1,0:T(8,128)(2,1)S(1)}, bf16[256,384]{1,0:T(8,128)(2,1)S(1)}, u32[]{:S(2)}, u32[]{:S(2)}) collective-permute-start(bf16[256,384]{1,0:T(8,128)(2,1)S(1)} %combine_x.2.a0), channel_id=1, source_target_pairs={{0,3},{1,0},{2,1},{3,2},{4,7},{5,4},{6,5},{7,6},{8,11},{9,8},{10,9... | collective-permute-start | bytes 589832 | tf_op jit(solution)/shard_map/ppermute | solution.py:402
  83.1 0.0 collective-permute-done.23.a2
  83.1 0.0 collective-permute-start.16
  83.1 0.0 collective-permute-done.22.a1
  83.1 0.9 collective-permute-start.15
  84.0 0.0 collective-permute-done.18.refs_7_
  84.0 0.0 collective-permute-done.19.refs_8_
  84.0 1.2 %out_project.3 = (bf16[256,640]{1,0:T(8,128)(2,1)S(1)}, bf16[256,640]{1,0:T(8,128)(2,1)S(1)}) custom-call(s32[1]{0:T(128)} %bitcast.core, bf16[256,384]{1,0:T(8,128)(2,1)S(1)} %combine_x.3.a0, bf16[256,384]{1,0:T(8,128)(2,1)S(1)} %collective-permute-done.22.a1, bf16[256,384]{1,0:T(8,128)(2,1)S(1)} %collective-permute-done.23.a2, ...), custom_call_target="tpu_custom_call" | custom-call | flops 1006632960 | bytes 6000000 | tf_op jit(solution)/shard_map/out_project/pallas_call | solution.py:327
  85.2 3.1 %collective-permute-start.25 = (bf16[256,640]{1,0:T(8,128)(2,1)S(1)}, bf16[256,640]{1,0:T(8,128)(2,1)S(1)}, u32[]{:S(2)}, u32[]{:S(2)}) collective-permute-start(bf16[256,640]{1,0:T(8,128)(2,1)S(1)} %get-tuple-element.78), channel_id=1, source_target_pairs={{0,4},{1,5},{2,6},{3,7},{4,0},{5,1},{6,2},{7,3},{8,12},{9,13},{10,... | collective-permute-start | bytes 983048 | tf_op jit(solution)/shard_map/ppermute | solution.py:404
  88.3 0.1 collective-permute-done.17.a3
  88.4 2.0 %collective-permute-done.16.a2 = bf16[256,384]{1,0:T(8,128)(2,1)S(1)} collective-permute-done((bf16[256,384]{1,0:T(8,128)(2,1)S(1)}, bf16[256,384]{1,0:T(8,128)(2,1)S(1)}, u32[]{:S(2)}, u32[]{:S(2)}) %collective-permute-start.16) | collective-permute-done | bytes 196640 | tf_op jit(solution)/shard_map/ppermute | solution.py:402
  90.4 2.1 %collective-permute-done.15.a1 = bf16[256,384]{1,0:T(8,128)(2,1)S(1)} collective-permute-done((bf16[256,384]{1,0:T(8,128)(2,1)S(1)}, bf16[256,384]{1,0:T(8,128)(2,1)S(1)}, u32[]{:S(2)}, u32[]{:S(2)}) %collective-permute-start.15) | collective-permute-done | bytes 196640 | tf_op jit(solution)/shard_map/ppermute | solution.py:402
  92.4 1.2 %out_project.2 = (bf16[256,640]{1,0:T(8,128)(2,1)S(1)}, bf16[256,640]{1,0:T(8,128)(2,1)S(1)}) custom-call(s32[1]{0:T(128)} %bitcast.core, bf16[256,384]{1,0:T(8,128)(2,1)S(1)} %combine_x.2.a0, bf16[256,384]{1,0:T(8,128)(2,1)S(1)} %collective-permute-done.15.a1, bf16[256,384]{1,0:T(8,128)(2,1)S(1)} %collective-permute-done.16.a2, ...), custom_call_target="tpu_custom_call" | custom-call | flops 1006632960 | bytes 6000000 | tf_op jit(solution)/shard_map/out_project/pallas_call | solution.py:327
  93.6 3.1 %collective-permute-start.20 = (bf16[256,640]{1,0:T(8,128)(2,1)S(1)}, bf16[256,640]{1,0:T(8,128)(2,1)S(1)}, u32[]{:S(2)}, u32[]{:S(2)}) collective-permute-start(bf16[256,640]{1,0:T(8,128)(2,1)S(1)} %get-tuple-element.74), channel_id=1, source_target_pairs={{0,4},{1,5},{2,6},{3,7},{4,0},{5,1},{6,2},{7,3},{8,12},{9,13},{10,... | collective-permute-start | bytes 983048 | tf_op jit(solution)/shard_map/ppermute | solution.py:404
  96.7 0.0 collective-permute-done.25.recv
  96.7 0.8 finish.2.rest_0_
  97.5 5.5 %collective-permute-done.20.recv = bf16[256,640]{1,0:T(8,128)(2,1)S(1)} collective-permute-done((bf16[256,640]{1,0:T(8,128)(2,1)S(1)}, bf16[256,640]{1,0:T(8,128)(2,1)S(1)}, u32[]{:S(2)}, u32[]{:S(2)}) %collective-permute-start.20) | collective-permute-done | bytes 327712 | tf_op jit(solution)/shard_map/ppermute | solution.py:404
  103.0 0.8 finish.3
  (14 shorter events, 0.1 us)
Async XLA Ops:
  14.3 16.0 %copy-start.2 = (bf16[512,768]{1,0:T(8,128)(2,1)S(1)}, bf16[512,768]{1,0:T(8,128)(2,1)}, u32[]{:S(2)}) copy-start(bf16[512,768]{1,0:T(8,128)(2,1)} %get-tuple-element.44.refs_3_.refs_1_) | copy-start | bytes 2359300
  14.3 16.0 %copy-start.3 = (bf16[512,384]{1,0:T(8,128)(2,1)S(1)}, bf16[512,384]{1,0:T(8,128)(2,1)}, u32[]{:S(2)}) copy-start(bf16[512,384]{1,0:T(8,128)(2,1)} %get-tuple-element.42.refs_0_.q0) | copy-start | bytes 1179652
  14.3 21.3 %collective-permute-start.4 = (bf16[512,768]{1,0:T(8,128)(2,1)}, bf16[512,768]{1,0:T(8,128)(2,1)S(1)}, u32[]{:S(2)}, u32[]{:S(2)}) collective-permute-start(bf16[512,768]{1,0:T(8,128)(2,1)} %get-tuple-element.44.refs_3_.refs_1_), channel_id=1, source_target_pairs={{0,48},{8,56},{16,0},{24,8},{32,16},{40,24},{48,32},{56,40},{64,11... | collective-permute-start | bytes 2359304 | tf_op jit(solution)/shard_map/ppermute | solution.py:365
  18.5 20.4 %collective-permute-start.3 = (bf16[512,768]{1,0:T(8,128)(2,1)}, bf16[512,768]{1,0:T(8,128)(2,1)S(1)}, u32[]{:S(2)}, u32[]{:S(2)}) collective-permute-start(bf16[512,768]{1,0:T(8,128)(2,1)} %get-tuple-element.44.refs_3_.refs_1_), channel_id=1, source_target_pairs={{0,16},{8,24},{16,32},{24,40},{32,48},{40,56},{48,0},{56,8},{64,80... | collective-permute-start | bytes 2359304 | tf_op jit(solution)/shard_map/ppermute | solution.py:364
  18.5 2.2 %collective-permute-start = (bf16[512,384]{1,0:T(8,128)(2,1)}, bf16[512,384]{1,0:T(8,128)(2,1)S(1)}, u32[]{:S(2)}, u32[]{:S(2)}) collective-permute-start(bf16[512,384]{1,0:T(8,128)(2,1)} %get-tuple-element.42.refs_0_.q0), channel_id=1, source_target_pairs={{0,8},{8,0},{16,24},{24,16},{32,40},{40,32},{48,56},{56,48},{64,72... | collective-permute-start | bytes 1179656 | tf_op jit(solution)/shard_map/ppermute | solution.py:371
  18.5 11.7 %collective-permute-start.1 = (bf16[512,384]{1,0:T(8,128)(2,1)}, bf16[512,384]{1,0:T(8,128)(2,1)S(1)}, u32[]{:S(2)}, u32[]{:S(2)}) collective-permute-start(bf16[512,384]{1,0:T(8,128)(2,1)} %get-tuple-element.42.refs_0_.q0), channel_id=1, source_target_pairs={{0,64},{8,72},{16,80},{24,88},{32,96},{40,104},{48,112},{56,120},{... | collective-permute-start | bytes 1179656 | tf_op jit(solution)/shard_map/ppermute | solution.py:372
  24.5 27.6 %collective-permute-start.7 = (bf16[576,640]{1,0:T(8,128)(2,1)}, bf16[576,640]{1,0:T(8,128)(2,1)S(1)}, u32[]{:S(2)}, u32[]{:S(2)}) collective-permute-start(bf16[576,640]{1,0:T(8,128)(2,1)} %get-tuple-element.53), channel_id=1, source_target_pairs={{0,1},{1,2},{2,3},{3,0},{4,5},{5,6},{6,7},{7,4},{8,9},{9,10},{10,1... | collective-permute-start | bytes 2211848 | tf_op jit(solution)/shard_map/ppermute | solution.py:375
  26.2 26.0 %collective-permute-start.8 = (bf16[576,640]{1,0:T(8,128)(2,1)}, bf16[576,640]{1,0:T(8,128)(2,1)S(1)}, u32[]{:S(2)}, u32[]{:S(2)}) collective-permute-start(bf16[576,640]{1,0:T(8,128)(2,1)} %get-tuple-element.54), channel_id=1, source_target_pairs={{0,3},{1,0},{2,1},{3,2},{4,7},{5,4},{6,5},{7,6},{8,11},{9,8},{10,9... | collective-permute-start | bytes 2211848 | tf_op jit(solution)/shard_map/ppermute | solution.py:376
  30.3 10.8 %collective-permute-start.2 = (bf16[512,384]{1,0:T(8,128)(2,1)S(1)}, bf16[512,384]{1,0:T(8,128)(2,1)S(1)}, u32[]{:S(2)}, u32[]{:S(2)}) collective-permute-start(bf16[512,384]{1,0:T(8,128)(2,1)S(1)} %collective-permute-done.1.refs_2_.q2), channel_id=1, source_target_pairs={{0,8},{8,0},{16,24},{24,16},{32,40},{40,32},{48,56},{56,48},{64,72... | collective-permute-start | bytes 1179656 | tf_op jit(solution)/shard_map/ppermute | solution.py:377
  39.0 13.1 %collective-permute-start.6 = (bf16[256,768]{1,0:T(8,128)(2,1)S(1)}, bf16[256,768]{1,0:T(8,128)(2,1)S(1)}, u32[]{:S(2)}, u32[]{:S(2)}) collective-permute-start(bf16[256,768]{1,0:T(8,128)(2,1)S(1)} %slice.13), channel_id=1, source_target_pairs={{0,48},{8,56},{16,0},{24,8},{32,16},{40,24},{48,32},{56,40},{64,11... | collective-permute-start | bytes 1179656 | tf_op jit(solution)/shard_map/ppermute | solution.py:381
  39.4 12.8 %collective-permute-start.5 = (bf16[256,768]{1,0:T(8,128)(2,1)S(1)}, bf16[256,768]{1,0:T(8,128)(2,1)S(1)}, u32[]{:S(2)}, u32[]{:S(2)}) collective-permute-start(bf16[256,768]{1,0:T(8,128)(2,1)S(1)} %slice.12), channel_id=1, source_target_pairs={{0,16},{8,24},{16,32},{24,40},{32,48},{40,56},{48,0},{56,8},{64,80... | collective-permute-start | bytes 1179656 | tf_op jit(solution)/shard_map/ppermute | solution.py:380
  55.9 28.1 %copy-start = (bf16[384,640]{1,0:T(8,128)(2,1)S(1)}, bf16[384,640]{1,0:T(8,128)(2,1)}, u32[]{:S(2)}) copy-start(bf16[384,640]{1,0:T(8,128)(2,1)} %get-tuple-element.67.refs_0_) | copy-start | bytes 1474564
  55.9 28.1 %copy-start.1 = (bf16[384,640]{1,0:T(8,128)(2,1)S(1)}, bf16[384,640]{1,0:T(8,128)(2,1)}, u32[]{:S(2)}) copy-start(bf16[384,640]{1,0:T(8,128)(2,1)} %get-tuple-element.70.refs_5_) | copy-start | bytes 1474564
  55.9 4.6 %collective-permute-start.9 = (bf16[1152,384]{1,0:T(8,128)(2,1)S(1)}, bf16[1152,384]{1,0:T(8,128)(2,1)S(1)}, u32[]{:S(2)}, u32[]{:S(2)}) collective-permute-start(bf16[1152,384]{1,0:T(8,128)(2,1)S(1)} %get-tuple-element.60), channel_id=1, source_target_pairs={{0,8},{8,0},{16,24},{24,16},{32,40},{40,32},{48,56},{56,48},{64,72... | collective-permute-start | bytes 2654216 | tf_op jit(solution)/shard_map/ppermute | solution.py:391
  56.0 3.7 %collective-permute-start.10 = (bf16[576,640]{1,0:T(8,128)(2,1)S(1)}, bf16[576,640]{1,0:T(8,128)(2,1)S(1)}, u32[]{:S(2)}, u32[]{:S(2)}) collective-permute-start(bf16[576,640]{1,0:T(8,128)(2,1)S(1)} %collective-permute-done.7.refs_1_), channel_id=1, source_target_pairs={{0,8},{8,0},{16,24},{24,16},{32,40},{40,32},{48,56},{56,48},{64,72... | collective-permute-start | bytes 2211848 | tf_op jit(solution)/shard_map/ppermute | solution.py:387
  56.5 4.0 %collective-permute-start.11 = (bf16[576,640]{1,0:T(8,128)(2,1)S(1)}, bf16[576,640]{1,0:T(8,128)(2,1)S(1)}, u32[]{:S(2)}, u32[]{:S(2)}) collective-permute-start(bf16[576,640]{1,0:T(8,128)(2,1)S(1)} %collective-permute-done.8.refs_4_), channel_id=1, source_target_pairs={{0,8},{8,0},{16,24},{24,16},{32,40},{40,32},{48,56},{56,48},{64,72... | collective-permute-start | bytes 2211848 | tf_op jit(solution)/shard_map/ppermute | solution.py:387
  56.6 16.4 %collective-permute-start.14 = (bf16[192,640]{1,0:T(8,128)(2,1)S(1)}, bf16[192,640]{1,0:T(8,128)(2,1)S(1)}, u32[]{:S(2)}, u32[]{:S(2)}) collective-permute-start(bf16[192,640]{1,0:T(8,128)(2,1)S(1)} %slice.15), channel_id=1, source_target_pairs={{0,3},{1,0},{2,1},{3,2},{4,7},{5,4},{6,5},{7,6},{8,11},{9,8},{10,9... | collective-permute-start | bytes 737288 | tf_op jit(solution)/shard_map/ppermute | solution.py:388
  60.7 8.3 %collective-permute-start.21 = (bf16[288,384]{1,0:T(8,128)(2,1)S(1)}, bf16[288,384]{1,0:T(8,128)(2,1)S(1)}, u32[]{:S(2)}, u32[]{:S(2)}) collective-permute-start(bf16[288,384]{1,0:T(8,128)(2,1)S(1)} %get-tuple-element.76), channel_id=1, source_target_pairs={{0,64},{8,72},{16,80},{24,88},{32,96},{40,104},{48,112},{56,120},{... | collective-permute-start | bytes 663560 | tf_op jit(solution)/shard_map/ppermute | solution.py:393
  62.3 11.6 %collective-permute-start.13 = (bf16[192,640]{1,0:T(8,128)(2,1)S(1)}, bf16[192,640]{1,0:T(8,128)(2,1)S(1)}, u32[]{:S(2)}, u32[]{:S(2)}) collective-permute-start(bf16[192,640]{1,0:T(8,128)(2,1)S(1)} %slice.14), channel_id=1, source_target_pairs={{0,1},{1,2},{2,3},{3,0},{4,5},{5,6},{6,7},{7,4},{8,9},{9,10},{10,1... | collective-permute-start | bytes 737288 | tf_op jit(solution)/shard_map/ppermute | solution.py:388
  64.0 10.0 %collective-permute-start.12 = (bf16[288,384]{1,0:T(8,128)(2,1)S(1)}, bf16[288,384]{1,0:T(8,128)(2,1)S(1)}, u32[]{:S(2)}, u32[]{:S(2)}) collective-permute-start(bf16[288,384]{1,0:T(8,128)(2,1)S(1)} %get-tuple-element.65), channel_id=1, source_target_pairs={{0,64},{8,72},{16,80},{24,88},{32,96},{40,104},{48,112},{56,120},{... | collective-permute-start | bytes 663560 | tf_op jit(solution)/shard_map/ppermute | solution.py:394
  69.3 10.1 %collective-permute-start.24 = (bf16[256,384]{1,0:T(8,128)(2,1)S(1)}, bf16[256,384]{1,0:T(8,128)(2,1)S(1)}, u32[]{:S(2)}, u32[]{:S(2)}) collective-permute-start(bf16[256,384]{1,0:T(8,128)(2,1)S(1)} %combine_x.3.a0), channel_id=1, source_target_pairs={{0,3},{1,0},{2,1},{3,2},{4,7},{5,4},{6,5},{7,6},{8,11},{9,8},{10,9... | collective-permute-start | bytes 589832 | tf_op jit(solution)/shard_map/ppermute | solution.py:402
  72.3 10.7 %collective-permute-start.23 = (bf16[256,384]{1,0:T(8,128)(2,1)S(1)}, bf16[256,384]{1,0:T(8,128)(2,1)S(1)}, u32[]{:S(2)}, u32[]{:S(2)}) collective-permute-start(bf16[256,384]{1,0:T(8,128)(2,1)S(1)} %combine_x.3.a0), channel_id=1, source_target_pairs={{0,2},{1,3},{2,0},{3,1},{4,6},{5,7},{6,4},{7,5},{8,10},{9,11},{10,... | collective-permute-start | bytes 589832 | tf_op jit(solution)/shard_map/ppermute | solution.py:402
  73.0 10.1 %collective-permute-start.22 = (bf16[256,384]{1,0:T(8,128)(2,1)S(1)}, bf16[256,384]{1,0:T(8,128)(2,1)S(1)}, u32[]{:S(2)}, u32[]{:S(2)}) collective-permute-start(bf16[256,384]{1,0:T(8,128)(2,1)S(1)} %combine_x.3.a0), channel_id=1, source_target_pairs={{0,1},{1,2},{2,3},{3,0},{4,5},{5,6},{6,7},{7,4},{8,9},{9,10},{10,1... | collective-permute-start | bytes 589832 | tf_op jit(solution)/shard_map/ppermute | solution.py:402
  74.0 10.0 %collective-permute-start.18 = (bf16[192,640]{1,0:T(8,128)(2,1)S(1)}, bf16[192,640]{1,0:T(8,128)(2,1)S(1)}, u32[]{:S(2)}, u32[]{:S(2)}) collective-permute-start(bf16[192,640]{1,0:T(8,128)(2,1)S(1)} %collective-permute-done.13.refs_2_), channel_id=1, source_target_pairs={{0,8},{8,0},{16,24},{24,16},{32,40},{40,32},{48,56},{56,48},{64,72... | collective-permute-start | bytes 737288 | tf_op jit(solution)/shard_map/ppermute | solution.py:396
  74.0 10.0 %collective-permute-start.19 = (bf16[192,640]{1,0:T(8,128)(2,1)S(1)}, bf16[192,640]{1,0:T(8,128)(2,1)S(1)}, u32[]{:S(2)}, u32[]{:S(2)}) collective-permute-start(bf16[192,640]{1,0:T(8,128)(2,1)S(1)} %collective-permute-done.14.refs_3_), channel_id=1, source_target_pairs={{0,8},{8,0},{16,24},{24,16},{32,40},{40,32},{48,56},{56,48},{64,72... | collective-permute-start | bytes 737288 | tf_op jit(solution)/shard_map/ppermute | solution.py:396
  79.4 9.0 %collective-permute-start.17 = (bf16[256,384]{1,0:T(8,128)(2,1)S(1)}, bf16[256,384]{1,0:T(8,128)(2,1)S(1)}, u32[]{:S(2)}, u32[]{:S(2)}) collective-permute-start(bf16[256,384]{1,0:T(8,128)(2,1)S(1)} %combine_x.2.a0), channel_id=1, source_target_pairs={{0,3},{1,0},{2,1},{3,2},{4,7},{5,4},{6,5},{7,6},{8,11},{9,8},{10,9... | collective-permute-start | bytes 589832 | tf_op jit(solution)/shard_map/ppermute | solution.py:402
  83.1 7.3 %collective-permute-start.16 = (bf16[256,384]{1,0:T(8,128)(2,1)S(1)}, bf16[256,384]{1,0:T(8,128)(2,1)S(1)}, u32[]{:S(2)}, u32[]{:S(2)}) collective-permute-start(bf16[256,384]{1,0:T(8,128)(2,1)S(1)} %combine_x.2.a0), channel_id=1, source_target_pairs={{0,2},{1,3},{2,0},{3,1},{4,6},{5,7},{6,4},{7,5},{8,10},{9,11},{10,... | collective-permute-start | bytes 589832 | tf_op jit(solution)/shard_map/ppermute | solution.py:402
  83.1 9.3 %collective-permute-start.15 = (bf16[256,384]{1,0:T(8,128)(2,1)S(1)}, bf16[256,384]{1,0:T(8,128)(2,1)S(1)}, u32[]{:S(2)}, u32[]{:S(2)}) collective-permute-start(bf16[256,384]{1,0:T(8,128)(2,1)S(1)} %combine_x.2.a0), channel_id=1, source_target_pairs={{0,1},{1,2},{2,3},{3,0},{4,5},{5,6},{6,7},{7,4},{8,9},{9,10},{10,1... | collective-permute-start | bytes 589832 | tf_op jit(solution)/shard_map/ppermute | solution.py:402
  85.2 11.6 %collective-permute-start.25 = (bf16[256,640]{1,0:T(8,128)(2,1)S(1)}, bf16[256,640]{1,0:T(8,128)(2,1)S(1)}, u32[]{:S(2)}, u32[]{:S(2)}) collective-permute-start(bf16[256,640]{1,0:T(8,128)(2,1)S(1)} %get-tuple-element.78), channel_id=1, source_target_pairs={{0,4},{1,5},{2,6},{3,7},{4,0},{5,1},{6,2},{7,3},{8,12},{9,13},{10,... | collective-permute-start | bytes 983048 | tf_op jit(solution)/shard_map/ppermute | solution.py:404
  93.6 9.4 %collective-permute-start.20 = (bf16[256,640]{1,0:T(8,128)(2,1)S(1)}, bf16[256,640]{1,0:T(8,128)(2,1)S(1)}, u32[]{:S(2)}, u32[]{:S(2)}) collective-permute-start(bf16[256,640]{1,0:T(8,128)(2,1)S(1)} %get-tuple-element.74), channel_id=1, source_target_pairs={{0,4},{1,5},{2,6},{3,7},{4,0},{5,1},{6,2},{7,3},{8,12},{9,13},{10,... | collective-permute-start | bytes 983048 | tf_op jit(solution)/shard_map/ppermute | solution.py:404

commit v6 on v5

--- a/solution.py
+++ b/solution.py
@@ -392,13 +392,14 @@
     mine0, away0, mine1, away1 = combine_core(keep, recv)
     recv0 = lax.ppermute(away0, "seq", SWAP_X)
     recv1 = lax.ppermute(away1, "seq", SWAP_X)
-    recv1, *far = lax.optimization_barrier((recv1, *far))
     far_core = [lax.ppermute(w, "seq", SWAP_CORE) for w in far]
+    att0 = combine_x(mine0, recv0)
+    att1 = combine_x(mine1, recv1)
+    att1, *far_core = lax.optimization_barrier((att1, *far_core))
     first_w = (own, up, *far, down)
     second_w = (other, second[0], *far_core, second[1])
     out = None
-    for half, (mine, recv) in enumerate(((mine0, recv0), (mine1, recv1))):
-        att = combine_x(mine, recv)
+    for half, att in enumerate((att0, att1)):
         attended = [att] + [lax.ppermute(att, "head", Y_STEP[r]) for r in (1, 2, 3)]
         kept, sent = out_project(core, attended, first_w, second_w)
         out = finish(half, kept, lax.ppermute(sent, "head", SWAP_XHI), out)

time: 104 us -> 104 us (level)
  waiting for transfers between devices: 26.6 us -> 28.4 us
  starting transfers between devices: 34.5 us -> 32.9 us
    ppermute x1, waiting for transfers between devices: 4.57 us -> 0.07 us  [shards(): recv0 = lax.ppermute(away0, 'seq', SWAP_X)]
    ppermute x1, waiting for transfers between devices: 0.01 us -> 3.5 us  [shards(): lax.ppermute(up[WIDE:], 'head', Y_STEP[1])]
    ppermute x1, waiting for transfers between devices: 0.01 us -> 2.66 us  [shards(): lax.ppermute(down[WIDE:], 'head', Y_STEP[3])]
    ppermute x1, starting transfers between devices: 1.65 us -> 0.07 us  [shards(): lax.ppermute(up[WIDE:], 'head', Y_STEP[1])]
    ppermute x2, waiting for transfers between devices: 5.51 us -> 6.59 us  [shards(): out = finish(half, kept, lax.ppermute(sent, 'head', SWAP_XHI), out)]
  transfers between devices with their start and end apart: 26 -> 26, of which waited for: 10 -> 12; matrix products, arithmetic and copies ran while one was open for 1% -> 1% of each run, Pallas kernels for 22% -> 22%
where the time goes in v6:
time: 104 us
  Pallas kernels  41.7 us (40%)
  starting transfers between devices  32.9 us (32%)
  waiting for transfers between devices  28.4 us (27%)
    pallas_call x3, Pallas kernels, attend_part(): pl.pallas_call(functools.partial(part_kernel, len(qs), len(kvs)), grid=(G...  15.3 us
    pallas_call x1, Pallas kernels, project(): pl.pallas_call(qkv_kernel, in_specs=[hbm] * 8, out_specs=[vmem, vmem], ou...  14.3 us
    ppermute x6, starting transfers between devices, shards(): attended = [att] + [lax.ppermute(att, 'head', Y_STEP[r]) for r in (1, 2, 3)]  9.68 us
    ppermute x6, waiting for transfers between devices, shards(): attended = [att] + [lax.ppermute(att, 'head', Y_STEP[r]) for r in (1, 2, 3)]  8.03 us
    ppermute x2, waiting for transfers between devices, shards(): out = finish(half, kept, lax.ppermute(sent, 'head', SWAP_XHI), out)  6.59 us
    ppermute x2, starting transfers between devices, shards(): out = finish(half, kept, lax.ppermute(sent, 'head', SWAP_XHI), out)  6.2 us
    ppermute x1, starting transfers between devices, shards(): above = lax.ppermute(kv, 'seq', Z_DOWN)  4.19 us
    pallas_call x1, Pallas kernels, take_blocks(): pl.pallas_call(blocks_kernel, in_specs=[pl.BlockSpec(memory_space=pltpu.S...  3.83 us
  transfers between devices with their start and end apart: 26, of which 12 were waited for; matrix products, arithmetic and copies ran while one was open for 1% of the time, Pallas kernels for 22%

profile of v6, /device:TPU:0, one launch (start us, length us, event | category | flops | bytes accessed | tf_op | source)
XLA Modules:
  0.0 104.0 jit_solution(16326381673913043331)
XLA Ops:
  0.0 14.3 %project.1 = (bf16[512,384]{1,0:T(8,128)(2,1)}, bf16[512,768]{1,0:T(8,128)(2,1)}) custom-call(bf16[512,5120]{1,0:T(8,128)(2,1)} %tok.1, f32[1,5120]{1,0:T(1,128)} %bitcast.8, f32[1,5120]{1,0:T(1,128)} %bitcast.9, bf16[5120,384]{1,0:T(8,128)(2,1)} %wq.1, bf16[5120,384]{1,0:T(8,128)(2,1)} %wk.1, bf16[5120,384]{1,0:T(8,128)(2,1)} %wv.1, f32[384]{0:T(512)} %gq_h.1, ...), custom_call_target="tpu_custom_call" | custom-call | flops 6039797760 | bytes 18000000 | tf_op jit(solution)/shard_map/project/pallas_call | solution.py:131
  14.3 4.2 %collective-permute-start.4 = (bf16[512,768]{1,0:T(8,128)(2,1)}, bf16[512,768]{1,0:T(8,128)(2,1)S(1)}, u32[]{:S(2)}, u32[]{:S(2)}) collective-permute-start(bf16[512,768]{1,0:T(8,128)(2,1)} %get-tuple-element.44.refs_3_.refs_1_), channel_id=1, source_target_pairs={{0,48},{8,56},{16,0},{24,8},{32,16},{40,24},{48,32},{56,40},{64,11... | collective-permute-start | bytes 2359304 | tf_op jit(solution)/shard_map/ppermute | solution.py:365
  18.5 0.0 collective-permute-start.3
  18.5 0.0 collective-permute-start
  18.5 1.5 %collective-permute-start.1 = (bf16[512,384]{1,0:T(8,128)(2,1)}, bf16[512,384]{1,0:T(8,128)(2,1)S(1)}, u32[]{:S(2)}, u32[]{:S(2)}) collective-permute-start(bf16[512,384]{1,0:T(8,128)(2,1)} %get-tuple-element.42.refs_0_.q0), channel_id=1, source_target_pairs={{0,64},{8,72},{16,80},{24,88},{32,96},{40,104},{48,112},{56,120},{... | collective-permute-start | bytes 1179656 | tf_op jit(solution)/shard_map/ppermute | solution.py:372
  20.0 0.7 stack.23.cols
  20.7 0.0 collective-permute-done.refs_1_.q1
  20.7 3.8 %take_blocks.1 = (bf16[384,640]{1,0:T(8,128)(2,1)}, bf16[576,640]{1,0:T(8,128)(2,1)}, bf16[576,640]{1,0:T(8,128)(2,1)}, bf16[384,640]{1,0:T(8,128)(2,1)}) custom-call(s32[5]{0:T(128)} %stack.23.cols, bf16[384,5120]{1,0:T(8,128)(2,1)} %wo.1), custom_call_target="tpu_custom_call" | custom-call | flops 1000000 | bytes 6000000 | tf_op jit(solution)/shard_map/take_blocks/pallas_call | solution.py:179
  24.5 1.6 %collective-permute-start.7 = (bf16[576,640]{1,0:T(8,128)(2,1)}, bf16[576,640]{1,0:T(8,128)(2,1)S(1)}, u32[]{:S(2)}, u32[]{:S(2)}) collective-permute-start(bf16[576,640]{1,0:T(8,128)(2,1)} %get-tuple-element.53), channel_id=1, source_target_pairs={{0,1},{1,2},{2,3},{3,0},{4,5},{5,6},{6,7},{7,4},{8,9},{9,10},{10,1... | collective-permute-start | bytes 2211848 | tf_op jit(solution)/shard_map/ppermute | solution.py:375
  26.2 1.7 %collective-permute-start.8 = (bf16[576,640]{1,0:T(8,128)(2,1)}, bf16[576,640]{1,0:T(8,128)(2,1)S(1)}, u32[]{:S(2)}, u32[]{:S(2)}) collective-permute-start(bf16[576,640]{1,0:T(8,128)(2,1)} %get-tuple-element.54), channel_id=1, source_target_pairs={{0,3},{1,0},{2,1},{3,2},{4,7},{5,4},{6,5},{7,6},{8,11},{9,8},{10,9... | collective-permute-start | bytes 2211848 | tf_op jit(solution)/shard_map/ppermute | solution.py:376
  27.8 2.4 %collective-permute-done.1.refs_2_.q2 = bf16[512,384]{1,0:T(8,128)(2,1)S(1)} collective-permute-done((bf16[512,384]{1,0:T(8,128)(2,1)}, bf16[512,384]{1,0:T(8,128)(2,1)S(1)}, u32[]{:S(2)}, u32[]{:S(2)}) %collective-permute-start.1) | collective-permute-done | bytes 393248 | tf_op jit(solution)/shard_map/ppermute | solution.py:372
  30.3 0.0 collective-permute-start.2
  30.3 4.3 %attend_part.3 = (bf16[864,384]{1,0:T(8,128)(2,1)S(1)}, bf16[864,384]{1,0:T(8,128)(2,1)S(1)}) custom-call(bf16[512,384]{1,0:T(8,128)(2,1)S(1)} %copy-done.3, bf16[512,384]{1,0:T(8,128)(2,1)S(1)} %collective-permute-done.refs_1_.q1, bf16[512,384]{1,0:T(8,128)(2,1)S(1)} %collective-permute-done.1.refs_2_.q2, bf16[512,768]{1,0:T(8,128)(2,1)S(1)} %copy-done.2), custom_call_target="tpu_custom_call" | custom-call | flops 603979776 | bytes 1000000 | tf_op jit(solution)/shard_map/attend_part/pallas_call | solution.py:222
  34.6 1.0 %collective-permute-done.4.refs_4_.refs_3_ = bf16[512,768]{1,0:T(8,128)(2,1)S(1)} collective-permute-done((bf16[512,768]{1,0:T(8,128)(2,1)}, bf16[512,768]{1,0:T(8,128)(2,1)S(1)}, u32[]{:S(2)}, u32[]{:S(2)}) %collective-permute-start.4) | collective-permute-done | bytes 786464 | tf_op jit(solution)/shard_map/ppermute | solution.py:365
  35.6 3.3 %collective-permute-done.3.refs_3_.refs_2_ = bf16[512,768]{1,0:T(8,128)(2,1)S(1)} collective-permute-done((bf16[512,768]{1,0:T(8,128)(2,1)}, bf16[512,768]{1,0:T(8,128)(2,1)S(1)}, u32[]{:S(2)}, u32[]{:S(2)}) %collective-permute-start.3) | collective-permute-done | bytes 786464 | tf_op jit(solution)/shard_map/ppermute | solution.py:364
  39.0 0.4 collective-permute-start.6
  39.4 1.7 %collective-permute-start.5 = (bf16[256,768]{1,0:T(8,128)(2,1)S(1)}, bf16[256,768]{1,0:T(8,128)(2,1)S(1)}, u32[]{:S(2)}, u32[]{:S(2)}) collective-permute-start(bf16[256,768]{1,0:T(8,128)(2,1)S(1)} %slice.12), channel_id=1, source_target_pairs={{0,16},{8,24},{16,32},{24,40},{32,48},{40,56},{48,0},{56,8},{64,80... | collective-permute-start | bytes 1179656 | tf_op jit(solution)/shard_map/ppermute | solution.py:380
  41.1 0.0 collective-permute-done.2.refs_0_.q3
  41.1 4.2 %attend_part.5 = (bf16[288,384]{1,0:T(8,128)(2,1)S(1)}, bf16[288,384]{1,0:T(8,128)(2,1)S(1)}) custom-call(bf16[512,384]{1,0:T(8,128)(2,1)S(1)} %collective-permute-done.2.refs_0_.q3, bf16[512,768]{1,0:T(8,128)(2,1)S(1)} %copy-done.2, bf16[512,768]{1,0:T(8,128)(2,1)S(1)} %collective-permute-done.3.refs_3_.refs_2_, ...), custom_call_target="tpu_custom_call" | custom-call | flops 603979776 | bytes 1000000 | tf_op jit(solution)/shard_map/attend_part/pallas_call | solution.py:222
  45.3 6.8 %attend_part.4 = (bf16[864,384]{1,0:T(8,128)(2,1)S(1)}, bf16[864,384]{1,0:T(8,128)(2,1)S(1)}) custom-call(bf16[512,384]{1,0:T(8,128)(2,1)S(1)} %copy-done.3, bf16[512,384]{1,0:T(8,128)(2,1)S(1)} %collective-permute-done.refs_1_.q1, bf16[512,384]{1,0:T(8,128)(2,1)S(1)} %collective-permute-done.1.refs_2_.q2, ...), custom_call_target="tpu_custom_call" | custom-call | flops 1207959552 | bytes 1000000 | tf_op jit(solution)/shard_map/attend_part/pallas_call | solution.py:222
  52.1 0.0 collective-permute-done.7.refs_1_
  52.1 0.0 collective-permute-done.8.refs_4_
  52.1 0.0 collective-permute-done.6.k1
  52.1 0.0 collective-permute-done.5.k0
  52.2 3.7 %attend_last.1 = (bf16[1152,384]{1,0:T(8,128)(2,1)S(1)}, bf16[1152,384]{1,0:T(8,128)(2,1)S(1)}) custom-call(bf16[512,384]{1,0:T(8,128)(2,1)S(1)} %copy-done.3, bf16[512,384]{1,0:T(8,128)(2,1)S(1)} %collective-permute-done.refs_1_.q1, bf16[512,384]{1,0:T(8,128)(2,1)S(1)} %collective-permute-done.1.refs_2_.q2, ...), custom_call_target="tpu_custom_call" | custom-call | flops 3221225472 | bytes 8000000 | tf_op jit(solution)/shard_map/attend_last/pallas_call | solution.py:257
  55.9 0.1 collective-permute-start.9
  56.0 0.5 collective-permute-start.10
  56.5 0.1 collective-permute-start.11
  56.6 3.1 %collective-permute-start.15 = (bf16[192,640]{1,0:T(8,128)(2,1)S(1)}, bf16[192,640]{1,0:T(8,128)(2,1)S(1)}, u32[]{:S(2)}, u32[]{:S(2)}) collective-permute-start(bf16[192,640]{1,0:T(8,128)(2,1)S(1)} %slice.15), channel_id=1, source_target_pairs={{0,3},{1,0},{2,1},{3,2},{4,7},{5,4},{6,5},{7,6},{8,11},{9,8},{10,9... | collective-permute-start | bytes 737288 | tf_op jit(solution)/shard_map/ppermute | solution.py:388
  59.7 0.1 collective-permute-start.13
  59.8 0.0 collective-permute-done.10.refs_6_
  59.8 0.7 collective-permute-done.11.refs_9_
  60.5 0.0 collective-permute-done.9.recv
  60.5 0.2 combine_core.1
  60.7 1.6 %collective-permute-start.21 = (bf16[288,384]{1,0:T(8,128)(2,1)S(1)}, bf16[288,384]{1,0:T(8,128)(2,1)S(1)}, u32[]{:S(2)}, u32[]{:S(2)}) collective-permute-start(bf16[288,384]{1,0:T(8,128)(2,1)S(1)} %get-tuple-element.76), channel_id=1, source_target_pairs={{0,64},{8,72},{16,80},{24,88},{32,96},{40,104},{48,112},{56,120},{... | collective-permute-start | bytes 663560 | tf_op jit(solution)/shard_map/ppermute | solution.py:393
  62.3 0.5 collective-permute-start.12
  62.8 2.7 %collective-permute-done.15.refs_3_ = bf16[192,640]{1,0:T(8,128)(2,1)S(1)} collective-permute-done((bf16[192,640]{1,0:T(8,128)(2,1)S(1)}, bf16[192,640]{1,0:T(8,128)(2,1)S(1)}, u32[]{:S(2)}, u32[]{:S(2)}) %collective-permute-start.15) | collective-permute-done | bytes 245792 | tf_op jit(solution)/shard_map/ppermute | solution.py:388
  65.5 0.0 collective-permute-start.16
  65.5 3.5 %collective-permute-done.13.refs_2_ = bf16[192,640]{1,0:T(8,128)(2,1)S(1)} collective-permute-done((bf16[192,640]{1,0:T(8,128)(2,1)S(1)}, bf16[192,640]{1,0:T(8,128)(2,1)S(1)}, u32[]{:S(2)}, u32[]{:S(2)}) %collective-permute-start.13) | collective-permute-done | bytes 245792 | tf_op jit(solution)/shard_map/ppermute | solution.py:388
  69.0 0.1 collective-permute-done.21.recv
  69.1 0.2 combine_x.3.a0
  69.3 3.1 %collective-permute-start.24 = (bf16[256,384]{1,0:T(8,128)(2,1)S(1)}, bf16[256,384]{1,0:T(8,128)(2,1)S(1)}, u32[]{:S(2)}, u32[]{:S(2)}) collective-permute-start(bf16[256,384]{1,0:T(8,128)(2,1)S(1)} %combine_x.3.a0), channel_id=1, source_target_pairs={{0,3},{1,0},{2,1},{3,2},{4,7},{5,4},{6,5},{7,6},{8,11},{9,8},{10,9... | collective-permute-start | bytes 589832 | tf_op jit(solution)/shard_map/ppermute | solution.py:403
  72.3 0.6 collective-permute-start.23
  73.0 0.0 collective-permute-done.12.recv
  73.0 1.6 %collective-permute-start.22 = (bf16[256,384]{1,0:T(8,128)(2,1)S(1)}, bf16[256,384]{1,0:T(8,128)(2,1)S(1)}, u32[]{:S(2)}, u32[]{:S(2)}) collective-permute-start(bf16[256,384]{1,0:T(8,128)(2,1)S(1)} %combine_x.3.a0), channel_id=1, source_target_pairs={{0,1},{1,2},{2,3},{3,0},{4,5},{5,6},{6,7},{7,4},{8,9},{9,10},{10,1... | collective-permute-start | bytes 589832 | tf_op jit(solution)/shard_map/ppermute | solution.py:403
  74.6 0.2 combine_x.2.a0
  74.8 0.0 collective-permute-done.16.refs_8_
  74.8 1.7 %collective-permute-start.19 = (bf16[256,384]{1,0:T(8,128)(2,1)S(1)}, bf16[256,384]{1,0:T(8,128)(2,1)S(1)}, u32[]{:S(2)}, u32[]{:S(2)}) collective-permute-start(bf16[256,384]{1,0:T(8,128)(2,1)S(1)} %combine_x.2.a0), channel_id=1, source_target_pairs={{0,3},{1,0},{2,1},{3,2},{4,7},{5,4},{6,5},{7,6},{8,11},{9,8},{10,9... | collective-permute-start | bytes 589832 | tf_op jit(solution)/shard_map/ppermute | solution.py:403
  76.5 2.0 %collective-permute-start.18 = (bf16[256,384]{1,0:T(8,128)(2,1)S(1)}, bf16[256,384]{1,0:T(8,128)(2,1)S(1)}, u32[]{:S(2)}, u32[]{:S(2)}) collective-permute-start(bf16[256,384]{1,0:T(8,128)(2,1)S(1)} %combine_x.2.a0), channel_id=1, source_target_pairs={{0,2},{1,3},{2,0},{3,1},{4,6},{5,7},{6,4},{7,5},{8,10},{9,11},{10,... | collective-permute-start | bytes 589832 | tf_op jit(solution)/shard_map/ppermute | solution.py:403
  78.5 0.0 collective-permute-done.24.a3
  78.5 0.7 collective-permute-start.17
  79.2 2.4 %collective-permute-done.23.a2 = bf16[256,384]{1,0:T(8,128)(2,1)S(1)} collective-permute-done((bf16[256,384]{1,0:T(8,128)(2,1)S(1)}, bf16[256,384]{1,0:T(8,128)(2,1)S(1)}, u32[]{:S(2)}, u32[]{:S(2)}) %collective-permute-start.23) | collective-permute-done | bytes 196640 | tf_op jit(solution)/shard_map/ppermute | solution.py:403
  81.6 4.7 %collective-permute-done.22.a1 = bf16[256,384]{1,0:T(8,128)(2,1)S(1)} collective-permute-done((bf16[256,384]{1,0:T(8,128)(2,1)S(1)}, bf16[256,384]{1,0:T(8,128)(2,1)S(1)}, u32[]{:S(2)}, u32[]{:S(2)}) %collective-permute-start.22) | collective-permute-done | bytes 196640 | tf_op jit(solution)/shard_map/ppermute | solution.py:403
  86.3 1.2 %out_project.3 = (bf16[256,640]{1,0:T(8,128)(2,1)S(1)}, bf16[256,640]{1,0:T(8,128)(2,1)S(1)}) custom-call(s32[1]{0:T(128)} %bitcast.core, bf16[256,384]{1,0:T(8,128)(2,1)S(1)} %combine_x.3.a0, bf16[256,384]{1,0:T(8,128)(2,1)S(1)} %collective-permute-done.22.a1, bf16[256,384]{1,0:T(8,128)(2,1)S(1)} %collective-permute-done.23.a2, ...), custom_call_target="tpu_custom_call" | custom-call | flops 1006632960 | bytes 6000000 | tf_op jit(solution)/shard_map/out_project/pallas_call | solution.py:327
  87.5 3.1 %collective-permute-start.25 = (bf16[256,640]{1,0:T(8,128)(2,1)S(1)}, bf16[256,640]{1,0:T(8,128)(2,1)S(1)}, u32[]{:S(2)}, u32[]{:S(2)}) collective-permute-start(bf16[256,640]{1,0:T(8,128)(2,1)S(1)} %get-tuple-element.78), channel_id=1, source_target_pairs={{0,4},{1,5},{2,6},{3,7},{4,0},{5,1},{6,2},{7,3},{8,12},{9,13},{10,... | collective-permute-start | bytes 983048 | tf_op jit(solution)/shard_map/ppermute | solution.py:405
  90.6 0.0 collective-permute-done.19.a3
  90.6 0.0 collective-permute-done.18.a2
  90.6 0.9 collective-permute-done.17.a1
  91.5 1.2 %out_project.2 = (bf16[256,640]{1,0:T(8,128)(2,1)S(1)}, bf16[256,640]{1,0:T(8,128)(2,1)S(1)}) custom-call(s32[1]{0:T(128)} %bitcast.core, bf16[256,384]{1,0:T(8,128)(2,1)S(1)} %combine_x.2.a0, bf16[256,384]{1,0:T(8,128)(2,1)S(1)} %collective-permute-done.17.a1, bf16[256,384]{1,0:T(8,128)(2,1)S(1)} %collective-permute-done.18.a2, ...), custom_call_target="tpu_custom_call" | custom-call | flops 1006632960 | bytes 6000000 | tf_op jit(solution)/shard_map/out_project/pallas_call | solution.py:327
  92.7 3.1 %collective-permute-start.20 = (bf16[256,640]{1,0:T(8,128)(2,1)S(1)}, bf16[256,640]{1,0:T(8,128)(2,1)S(1)}, u32[]{:S(2)}, u32[]{:S(2)}) collective-permute-start(bf16[256,640]{1,0:T(8,128)(2,1)S(1)} %get-tuple-element.74), channel_id=1, source_target_pairs={{0,4},{1,5},{2,6},{3,7},{4,0},{5,1},{6,2},{7,3},{8,12},{9,13},{10,... | collective-permute-start | bytes 983048 | tf_op jit(solution)/shard_map/ppermute | solution.py:405
  95.8 0.4 collective-permute-done.25.recv
  96.2 0.8 finish.2.rest_0_
  97.0 6.2 %collective-permute-done.20.recv = bf16[256,640]{1,0:T(8,128)(2,1)S(1)} collective-permute-done((bf16[256,640]{1,0:T(8,128)(2,1)S(1)}, bf16[256,640]{1,0:T(8,128)(2,1)S(1)}, u32[]{:S(2)}, u32[]{:S(2)}) %collective-permute-start.20) | collective-permute-done | bytes 327712 | tf_op jit(solution)/shard_map/ppermute | solution.py:405
  103.2 0.8 finish.3
  (14 shorter events, 0.1 us)
Async XLA Ops:
  14.3 16.0 %copy-start.2 = (bf16[512,768]{1,0:T(8,128)(2,1)S(1)}, bf16[512,768]{1,0:T(8,128)(2,1)}, u32[]{:S(2)}) copy-start(bf16[512,768]{1,0:T(8,128)(2,1)} %get-tuple-element.44.refs_3_.refs_1_) | copy-start | bytes 2359300
  14.3 16.0 %copy-start.3 = (bf16[512,384]{1,0:T(8,128)(2,1)S(1)}, bf16[512,384]{1,0:T(8,128)(2,1)}, u32[]{:S(2)}) copy-start(bf16[512,384]{1,0:T(8,128)(2,1)} %get-tuple-element.42.refs_0_.q0) | copy-start | bytes 1179652
  14.3 21.3 %collective-permute-start.4 = (bf16[512,768]{1,0:T(8,128)(2,1)}, bf16[512,768]{1,0:T(8,128)(2,1)S(1)}, u32[]{:S(2)}, u32[]{:S(2)}) collective-permute-start(bf16[512,768]{1,0:T(8,128)(2,1)} %get-tuple-element.44.refs_3_.refs_1_), channel_id=1, source_target_pairs={{0,48},{8,56},{16,0},{24,8},{32,16},{40,24},{48,32},{56,40},{64,11... | collective-permute-start | bytes 2359304 | tf_op jit(solution)/shard_map/ppermute | solution.py:365
  18.5 20.4 %collective-permute-start.3 = (bf16[512,768]{1,0:T(8,128)(2,1)}, bf16[512,768]{1,0:T(8,128)(2,1)S(1)}, u32[]{:S(2)}, u32[]{:S(2)}) collective-permute-start(bf16[512,768]{1,0:T(8,128)(2,1)} %get-tuple-element.44.refs_3_.refs_1_), channel_id=1, source_target_pairs={{0,16},{8,24},{16,32},{24,40},{32,48},{40,56},{48,0},{56,8},{64,80... | collective-permute-start | bytes 2359304 | tf_op jit(solution)/shard_map/ppermute | solution.py:364
  18.5 2.2 %collective-permute-start = (bf16[512,384]{1,0:T(8,128)(2,1)}, bf16[512,384]{1,0:T(8,128)(2,1)S(1)}, u32[]{:S(2)}, u32[]{:S(2)}) collective-permute-start(bf16[512,384]{1,0:T(8,128)(2,1)} %get-tuple-element.42.refs_0_.q0), channel_id=1, source_target_pairs={{0,8},{8,0},{16,24},{24,16},{32,40},{40,32},{48,56},{56,48},{64,72... | collective-permute-start | bytes 1179656 | tf_op jit(solution)/shard_map/ppermute | solution.py:371
  18.5 11.7 %collective-permute-start.1 = (bf16[512,384]{1,0:T(8,128)(2,1)}, bf16[512,384]{1,0:T(8,128)(2,1)S(1)}, u32[]{:S(2)}, u32[]{:S(2)}) collective-permute-start(bf16[512,384]{1,0:T(8,128)(2,1)} %get-tuple-element.42.refs_0_.q0), channel_id=1, source_target_pairs={{0,64},{8,72},{16,80},{24,88},{32,96},{40,104},{48,112},{56,120},{... | collective-permute-start | bytes 1179656 | tf_op jit(solution)/shard_map/ppermute | solution.py:372
  24.5 27.6 %collective-permute-start.7 = (bf16[576,640]{1,0:T(8,128)(2,1)}, bf16[576,640]{1,0:T(8,128)(2,1)S(1)}, u32[]{:S(2)}, u32[]{:S(2)}) collective-permute-start(bf16[576,640]{1,0:T(8,128)(2,1)} %get-tuple-element.53), channel_id=1, source_target_pairs={{0,1},{1,2},{2,3},{3,0},{4,5},{5,6},{6,7},{7,4},{8,9},{9,10},{10,1... | collective-permute-start | bytes 2211848 | tf_op jit(solution)/shard_map/ppermute | solution.py:375
  26.2 26.0 %collective-permute-start.8 = (bf16[576,640]{1,0:T(8,128)(2,1)}, bf16[576,640]{1,0:T(8,128)(2,1)S(1)}, u32[]{:S(2)}, u32[]{:S(2)}) collective-permute-start(bf16[576,640]{1,0:T(8,128)(2,1)} %get-tuple-element.54), channel_id=1, source_target_pairs={{0,3},{1,0},{2,1},{3,2},{4,7},{5,4},{6,5},{7,6},{8,11},{9,8},{10,9... | collective-permute-start | bytes 2211848 | tf_op jit(solution)/shard_map/ppermute | solution.py:376
  30.3 10.8 %collective-permute-start.2 = (bf16[512,384]{1,0:T(8,128)(2,1)S(1)}, bf16[512,384]{1,0:T(8,128)(2,1)S(1)}, u32[]{:S(2)}, u32[]{:S(2)}) collective-permute-start(bf16[512,384]{1,0:T(8,128)(2,1)S(1)} %collective-permute-done.1.refs_2_.q2), channel_id=1, source_target_pairs={{0,8},{8,0},{16,24},{24,16},{32,40},{40,32},{48,56},{56,48},{64,72... | collective-permute-start | bytes 1179656 | tf_op jit(solution)/shard_map/ppermute | solution.py:377
  39.0 13.1 %collective-permute-start.6 = (bf16[256,768]{1,0:T(8,128)(2,1)S(1)}, bf16[256,768]{1,0:T(8,128)(2,1)S(1)}, u32[]{:S(2)}, u32[]{:S(2)}) collective-permute-start(bf16[256,768]{1,0:T(8,128)(2,1)S(1)} %slice.13), channel_id=1, source_target_pairs={{0,48},{8,56},{16,0},{24,8},{32,16},{40,24},{48,32},{56,40},{64,11... | collective-permute-start | bytes 1179656 | tf_op jit(solution)/shard_map/ppermute | solution.py:381
  39.4 12.8 %collective-permute-start.5 = (bf16[256,768]{1,0:T(8,128)(2,1)S(1)}, bf16[256,768]{1,0:T(8,128)(2,1)S(1)}, u32[]{:S(2)}, u32[]{:S(2)}) collective-permute-start(bf16[256,768]{1,0:T(8,128)(2,1)S(1)} %slice.12), channel_id=1, source_target_pairs={{0,16},{8,24},{16,32},{24,40},{32,48},{40,56},{48,0},{56,8},{64,80... | collective-permute-start | bytes 1179656 | tf_op jit(solution)/shard_map/ppermute | solution.py:380
  55.9 30.4 %copy-start = (bf16[384,640]{1,0:T(8,128)(2,1)S(1)}, bf16[384,640]{1,0:T(8,128)(2,1)}, u32[]{:S(2)}) copy-start(bf16[384,640]{1,0:T(8,128)(2,1)} %get-tuple-element.67.refs_0_) | copy-start | bytes 1474564
  55.9 30.4 %copy-start.1 = (bf16[384,640]{1,0:T(8,128)(2,1)S(1)}, bf16[384,640]{1,0:T(8,128)(2,1)}, u32[]{:S(2)}) copy-start(bf16[384,640]{1,0:T(8,128)(2,1)} %get-tuple-element.68.refs_5_) | copy-start | bytes 1474564
  55.9 4.6 %collective-permute-start.9 = (bf16[1152,384]{1,0:T(8,128)(2,1)S(1)}, bf16[1152,384]{1,0:T(8,128)(2,1)S(1)}, u32[]{:S(2)}, u32[]{:S(2)}) collective-permute-start(bf16[1152,384]{1,0:T(8,128)(2,1)S(1)} %get-tuple-element.60), channel_id=1, source_target_pairs={{0,8},{8,0},{16,24},{24,16},{32,40},{40,32},{48,56},{56,48},{64,72... | collective-permute-start | bytes 2654216 | tf_op jit(solution)/shard_map/ppermute | solution.py:391
  56.0 3.8 %collective-permute-start.10 = (bf16[576,640]{1,0:T(8,128)(2,1)S(1)}, bf16[576,640]{1,0:T(8,128)(2,1)S(1)}, u32[]{:S(2)}, u32[]{:S(2)}) collective-permute-start(bf16[576,640]{1,0:T(8,128)(2,1)S(1)} %collective-permute-done.7.refs_1_), channel_id=1, source_target_pairs={{0,8},{8,0},{16,24},{24,16},{32,40},{40,32},{48,56},{56,48},{64,72... | collective-permute-start | bytes 2211848 | tf_op jit(solution)/shard_map/ppermute | solution.py:387
  56.5 4.0 %collective-permute-start.11 = (bf16[576,640]{1,0:T(8,128)(2,1)S(1)}, bf16[576,640]{1,0:T(8,128)(2,1)S(1)}, u32[]{:S(2)}, u32[]{:S(2)}) collective-permute-start(bf16[576,640]{1,0:T(8,128)(2,1)S(1)} %collective-permute-done.8.refs_4_), channel_id=1, source_target_pairs={{0,8},{8,0},{16,24},{24,16},{32,40},{40,32},{48,56},{56,48},{64,72... | collective-permute-start | bytes 2211848 | tf_op jit(solution)/shard_map/ppermute | solution.py:387
  56.6 8.9 %collective-permute-start.15 = (bf16[192,640]{1,0:T(8,128)(2,1)S(1)}, bf16[192,640]{1,0:T(8,128)(2,1)S(1)}, u32[]{:S(2)}, u32[]{:S(2)}) collective-permute-start(bf16[192,640]{1,0:T(8,128)(2,1)S(1)} %slice.15), channel_id=1, source_target_pairs={{0,3},{1,0},{2,1},{3,2},{4,7},{5,4},{6,5},{7,6},{8,11},{9,8},{10,9... | collective-permute-start | bytes 737288 | tf_op jit(solution)/shard_map/ppermute | solution.py:388
  59.7 9.3 %collective-permute-start.13 = (bf16[192,640]{1,0:T(8,128)(2,1)S(1)}, bf16[192,640]{1,0:T(8,128)(2,1)S(1)}, u32[]{:S(2)}, u32[]{:S(2)}) collective-permute-start(bf16[192,640]{1,0:T(8,128)(2,1)S(1)} %slice.14), channel_id=1, source_target_pairs={{0,1},{1,2},{2,3},{3,0},{4,5},{5,6},{6,7},{7,4},{8,9},{9,10},{10,1... | collective-permute-start | bytes 737288 | tf_op jit(solution)/shard_map/ppermute | solution.py:388
  60.7 8.3 %collective-permute-start.21 = (bf16[288,384]{1,0:T(8,128)(2,1)S(1)}, bf16[288,384]{1,0:T(8,128)(2,1)S(1)}, u32[]{:S(2)}, u32[]{:S(2)}) collective-permute-start(bf16[288,384]{1,0:T(8,128)(2,1)S(1)} %get-tuple-element.76), channel_id=1, source_target_pairs={{0,64},{8,72},{16,80},{24,88},{32,96},{40,104},{48,112},{56,120},{... | collective-permute-start | bytes 663560 | tf_op jit(solution)/shard_map/ppermute | solution.py:393
  62.3 10.7 %collective-permute-start.12 = (bf16[288,384]{1,0:T(8,128)(2,1)S(1)}, bf16[288,384]{1,0:T(8,128)(2,1)S(1)}, u32[]{:S(2)}, u32[]{:S(2)}) collective-permute-start(bf16[288,384]{1,0:T(8,128)(2,1)S(1)} %get-tuple-element.65), channel_id=1, source_target_pairs={{0,64},{8,72},{16,80},{24,88},{32,96},{40,104},{48,112},{56,120},{... | collective-permute-start | bytes 663560 | tf_op jit(solution)/shard_map/ppermute | solution.py:394
  65.5 9.3 %collective-permute-start.16 = (bf16[192,640]{1,0:T(8,128)(2,1)S(1)}, bf16[192,640]{1,0:T(8,128)(2,1)S(1)}, u32[]{:S(2)}, u32[]{:S(2)}) collective-permute-start(bf16[192,640]{1,0:T(8,128)(2,1)S(1)} %collective-permute-done.15.refs_3_), channel_id=1, source_target_pairs={{0,8},{8,0},{16,24},{24,16},{32,40},{40,32},{48,56},{56,48},{64,72... | collective-permute-start | bytes 737288 | tf_op jit(solution)/shard_map/ppermute | solution.py:395
  69.0 5.8 %collective-permute-start.14 = (bf16[192,640]{1,0:T(8,128)(2,1)S(1)}, bf16[192,640]{1,0:T(8,128)(2,1)S(1)}, u32[]{:S(2)}, u32[]{:S(2)}) collective-permute-start(bf16[192,640]{1,0:T(8,128)(2,1)S(1)} %collective-permute-done.13.refs_2_), channel_id=1, source_target_pairs={{0,8},{8,0},{16,24},{24,16},{32,40},{40,32},{48,56},{56,48},{64,72... | collective-permute-start | bytes 737288 | tf_op jit(solution)/shard_map/ppermute | solution.py:395
  69.3 9.3 %collective-permute-start.24 = (bf16[256,384]{1,0:T(8,128)(2,1)S(1)}, bf16[256,384]{1,0:T(8,128)(2,1)S(1)}, u32[]{:S(2)}, u32[]{:S(2)}) collective-permute-start(bf16[256,384]{1,0:T(8,128)(2,1)S(1)} %combine_x.3.a0), channel_id=1, source_target_pairs={{0,3},{1,0},{2,1},{3,2},{4,7},{5,4},{6,5},{7,6},{8,11},{9,8},{10,9... | collective-permute-start | bytes 589832 | tf_op jit(solution)/shard_map/ppermute | solution.py:403
  72.3 9.3 %collective-permute-start.23 = (bf16[256,384]{1,0:T(8,128)(2,1)S(1)}, bf16[256,384]{1,0:T(8,128)(2,1)S(1)}, u32[]{:S(2)}, u32[]{:S(2)}) collective-permute-start(bf16[256,384]{1,0:T(8,128)(2,1)S(1)} %combine_x.3.a0), channel_id=1, source_target_pairs={{0,2},{1,3},{2,0},{3,1},{4,6},{5,7},{6,4},{7,5},{8,10},{9,11},{10,... | collective-permute-start | bytes 589832 | tf_op jit(solution)/shard_map/ppermute | solution.py:403
  73.0 13.3 %collective-permute-start.22 = (bf16[256,384]{1,0:T(8,128)(2,1)S(1)}, bf16[256,384]{1,0:T(8,128)(2,1)S(1)}, u32[]{:S(2)}, u32[]{:S(2)}) collective-permute-start(bf16[256,384]{1,0:T(8,128)(2,1)S(1)} %combine_x.3.a0), channel_id=1, source_target_pairs={{0,1},{1,2},{2,3},{3,0},{4,5},{5,6},{6,7},{7,4},{8,9},{9,10},{10,1... | collective-permute-start | bytes 589832 | tf_op jit(solution)/shard_map/ppermute | solution.py:403
  74.8 15.8 %collective-permute-start.19 = (bf16[256,384]{1,0:T(8,128)(2,1)S(1)}, bf16[256,384]{1,0:T(8,128)(2,1)S(1)}, u32[]{:S(2)}, u32[]{:S(2)}) collective-permute-start(bf16[256,384]{1,0:T(8,128)(2,1)S(1)} %combine_x.2.a0), channel_id=1, source_target_pairs={{0,3},{1,0},{2,1},{3,2},{4,7},{5,4},{6,5},{7,6},{8,11},{9,8},{10,9... | collective-permute-start | bytes 589832 | tf_op jit(solution)/shard_map/ppermute | solution.py:403
  76.5 14.1 %collective-permute-start.18 = (bf16[256,384]{1,0:T(8,128)(2,1)S(1)}, bf16[256,384]{1,0:T(8,128)(2,1)S(1)}, u32[]{:S(2)}, u32[]{:S(2)}) collective-permute-start(bf16[256,384]{1,0:T(8,128)(2,1)S(1)} %combine_x.2.a0), channel_id=1, source_target_pairs={{0,2},{1,3},{2,0},{3,1},{4,6},{5,7},{6,4},{7,5},{8,10},{9,11},{10,... | collective-permute-start | bytes 589832 | tf_op jit(solution)/shard_map/ppermute | solution.py:403
  78.5 13.0 %collective-permute-start.17 = (bf16[256,384]{1,0:T(8,128)(2,1)S(1)}, bf16[256,384]{1,0:T(8,128)(2,1)S(1)}, u32[]{:S(2)}, u32[]{:S(2)}) collective-permute-start(bf16[256,384]{1,0:T(8,128)(2,1)S(1)} %combine_x.2.a0), channel_id=1, source_target_pairs={{0,1},{1,2},{2,3},{3,0},{4,5},{5,6},{6,7},{7,4},{8,9},{9,10},{10,1... | collective-permute-start | bytes 589832 | tf_op jit(solution)/shard_map/ppermute | solution.py:403
  87.5 8.7 %collective-permute-start.25 = (bf16[256,640]{1,0:T(8,128)(2,1)S(1)}, bf16[256,640]{1,0:T(8,128)(2,1)S(1)}, u32[]{:S(2)}, u32[]{:S(2)}) collective-permute-start(bf16[256,640]{1,0:T(8,128)(2,1)S(1)} %get-tuple-element.78), channel_id=1, source_target_pairs={{0,4},{1,5},{2,6},{3,7},{4,0},{5,1},{6,2},{7,3},{8,12},{9,13},{10,... | collective-permute-start | bytes 983048 | tf_op jit(solution)/shard_map/ppermute | solution.py:405
  92.7 10.5 %collective-permute-start.20 = (bf16[256,640]{1,0:T(8,128)(2,1)S(1)}, bf16[256,640]{1,0:T(8,128)(2,1)S(1)}, u32[]{:S(2)}, u32[]{:S(2)}) collective-permute-start(bf16[256,640]{1,0:T(8,128)(2,1)S(1)} %get-tuple-element.74), channel_id=1, source_target_pairs={{0,4},{1,5},{2,6},{3,7},{4,0},{5,1},{6,2},{7,3},{8,12},{9,13},{10,... | collective-permute-start | bytes 983048 | tf_op jit(solution)/shard_map/ppermute | solution.py:405

commit v7 on v5

--- a/solution.py
+++ b/solution.py
@@ -240,11 +240,11 @@
             for half, (own, near, cross) in enumerate(((own0, near0, cross0), (own1, near1, cross1))):
                 rows = acc[half * HALF : (half + 1) * HALF]
                 base = (2 * half + i // 2) * PACK
-                quarter = slice(i * PACK, (i + 1) * PACK)
-                if i < 3:
+                quarter = slice((i % 2) * PACK, (i % 2 + 1) * PACK)
+                if i < 2:
                     old = own[quarter, col].astype(F32) + near[quarter, col].astype(F32)
                 else:
-                    old = cross[:, col].astype(F32)
+                    old = cross[quarter, col].astype(F32)
                 out[base : base + HALF, col] = (rows[:, :HD] + old[:HALF]).astype(BF16)
                 for p in range(HALF // 128):
                     t = jnp.transpose(rows[p * 128 : (p + 1) * 128, HD:])[:16]
@@ -375,13 +375,13 @@
     up = lax.ppermute(up, "head", Y_STEP[1])
     down = lax.ppermute(down, "head", Y_STEP[3])
     q_xc = lax.ppermute(q_x, "seq", SWAP_CORE)
-    parts_own = attend_part((q, q_core, q_x), (kv,))
+    parts_own = attend_part((q, q_core), (kv,))
     below, above, *parts_own = lax.optimization_barrier((below, above, *parts_own))
     far_a = lax.ppermute(below[:256], "seq", Z_UP)
     far_b = lax.ppermute(above[256:], "seq", Z_DOWN)
     qs = (q, q_core, q_x, q_xc)
-    parts_near = attend_part(qs[:3], (below, above))
-    parts_cross = attend_part(qs[3:], (kv, below, above))
+    parts_near = attend_part(qs[:2], (below, above))
+    parts_cross = attend_part(qs[2:], (kv, below, above))
     part, up, down = lax.optimization_barrier((parts_near[0], up, down))
     parts = (*parts_own, part, parts_near[1], *parts_cross)
     second = [lax.ppermute(w, "seq", SWAP_CORE) for w in (up, down)]

time: 104 us -> 105 us (level)
  no operation moved by 1% of the time
where the time goes in v7:
time: 105 us
  Pallas kernels  41.6 us (40%)
  starting transfers between devices  34.5 us (33%)
  waiting for transfers between devices  27.6 us (26%)
    pallas_call x3, Pallas kernels, attend_part(): pl.pallas_call(functools.partial(part_kernel, len(qs), len(kvs)), grid=(G...  15.2 us
    pallas_call x1, Pallas kernels, project(): pl.pallas_call(qkv_kernel, in_specs=[hbm] * 8, out_specs=[vmem, vmem], ou...  14.3 us
    ppermute x6, starting transfers between devices, shards(): attended = [att] + [lax.ppermute(att, 'head', Y_STEP[r]) for r in (1, 2, 3)]  9.23 us
    ppermute x6, waiting for transfers between devices, shards(): attended = [att] + [lax.ppermute(att, 'head', Y_STEP[r]) for r in (1, 2, 3)]  8.89 us
    ppermute x2, starting transfers between devices, shards(): out = finish(half, kept, lax.ppermute(sent, 'head', SWAP_XHI), out)  6.2 us
    ppermute x2, waiting for transfers between devices, shards(): out = finish(half, kept, lax.ppermute(sent, 'head', SWAP_XHI), out)  5.51 us
    ppermute x1, waiting for transfers between devices, shards(): recv0 = lax.ppermute(away0, 'seq', SWAP_X)  4.57 us
    ppermute x1, starting transfers between devices, shards(): above = lax.ppermute(kv, 'seq', Z_DOWN)  4.19 us
  transfers between devices with their start and end apart: 26, of which 10 were waited for; matrix products, arithmetic and copies ran while one was open for 1% of the time, Pallas kernels for 22%

profile of v7, /device:TPU:0, one launch (start us, length us, event | category | flops | bytes accessed | tf_op | source)
XLA Modules:
  0.0 104.7 jit_solution(8810973947165290539)
XLA Ops:
  0.0 14.3 %project.1 = (bf16[512,384]{1,0:T(8,128)(2,1)}, bf16[512,768]{1,0:T(8,128)(2,1)}) custom-call(bf16[512,5120]{1,0:T(8,128)(2,1)} %tok.1, f32[1,5120]{1,0:T(1,128)} %bitcast.8, f32[1,5120]{1,0:T(1,128)} %bitcast.9, bf16[5120,384]{1,0:T(8,128)(2,1)} %wq.1, bf16[5120,384]{1,0:T(8,128)(2,1)} %wk.1, bf16[5120,384]{1,0:T(8,128)(2,1)} %wv.1, f32[384]{0:T(512)} %gq_h.1, ...), custom_call_target="tpu_custom_call" | custom-call | flops 6039797760 | bytes 18000000 | tf_op jit(solution)/shard_map/project/pallas_call | solution.py:131
  14.3 4.2 %collective-permute-start.4 = (bf16[512,768]{1,0:T(8,128)(2,1)}, bf16[512,768]{1,0:T(8,128)(2,1)S(1)}, u32[]{:S(2)}, u32[]{:S(2)}) collective-permute-start(bf16[512,768]{1,0:T(8,128)(2,1)} %get-tuple-element.44.refs_2_), channel_id=1, source_target_pairs={{0,48},{8,56},{16,0},{24,8},{32,16},{40,24},{48,32},{56,40},{64,11... | collective-permute-start | bytes 2359304 | tf_op jit(solution)/shard_map/ppermute | solution.py:365
  18.5 0.0 collective-permute-start.3
  18.5 0.0 collective-permute-start
  18.5 1.5 %collective-permute-start.1 = (bf16[512,384]{1,0:T(8,128)(2,1)}, bf16[512,384]{1,0:T(8,128)(2,1)S(1)}, u32[]{:S(2)}, u32[]{:S(2)}) collective-permute-start(bf16[512,384]{1,0:T(8,128)(2,1)} %get-tuple-element.42.refs_0_.q0), channel_id=1, source_target_pairs={{0,64},{8,72},{16,80},{24,88},{32,96},{40,104},{48,112},{56,120},{... | collective-permute-start | bytes 1179656 | tf_op jit(solution)/shard_map/ppermute | solution.py:372
  20.0 0.7 stack.23.cols
  20.7 0.0 collective-permute-done.refs_1_.q1
  20.7 3.8 %take_blocks.1 = (bf16[384,640]{1,0:T(8,128)(2,1)}, bf16[576,640]{1,0:T(8,128)(2,1)}, bf16[576,640]{1,0:T(8,128)(2,1)}, bf16[384,640]{1,0:T(8,128)(2,1)}) custom-call(s32[5]{0:T(128)} %stack.23.cols, bf16[384,5120]{1,0:T(8,128)(2,1)} %wo.1), custom_call_target="tpu_custom_call" | custom-call | flops 1000000 | bytes 6000000 | tf_op jit(solution)/shard_map/take_blocks/pallas_call | solution.py:179
  24.5 1.6 %collective-permute-start.7 = (bf16[576,640]{1,0:T(8,128)(2,1)}, bf16[576,640]{1,0:T(8,128)(2,1)S(1)}, u32[]{:S(2)}, u32[]{:S(2)}) collective-permute-start(bf16[576,640]{1,0:T(8,128)(2,1)} %get-tuple-element.53), channel_id=1, source_target_pairs={{0,1},{1,2},{2,3},{3,0},{4,5},{5,6},{6,7},{7,4},{8,9},{9,10},{10,1... | collective-permute-start | bytes 2211848 | tf_op jit(solution)/shard_map/ppermute | solution.py:375
  26.2 1.7 %collective-permute-start.8 = (bf16[576,640]{1,0:T(8,128)(2,1)}, bf16[576,640]{1,0:T(8,128)(2,1)S(1)}, u32[]{:S(2)}, u32[]{:S(2)}) collective-permute-start(bf16[576,640]{1,0:T(8,128)(2,1)} %get-tuple-element.54), channel_id=1, source_target_pairs={{0,3},{1,0},{2,1},{3,2},{4,7},{5,4},{6,5},{7,6},{8,11},{9,8},{10,9... | collective-permute-start | bytes 2211848 | tf_op jit(solution)/shard_map/ppermute | solution.py:376
  27.8 2.4 %collective-permute-done.1.refs_0_.q2 = bf16[512,384]{1,0:T(8,128)(2,1)S(1)} collective-permute-done((bf16[512,384]{1,0:T(8,128)(2,1)}, bf16[512,384]{1,0:T(8,128)(2,1)S(1)}, u32[]{:S(2)}, u32[]{:S(2)}) %collective-permute-start.1) | collective-permute-done | bytes 393248 | tf_op jit(solution)/shard_map/ppermute | solution.py:372
  30.3 0.0 collective-permute-start.2
  30.3 3.4 %attend_part.3 = (bf16[576,384]{1,0:T(8,128)(2,1)S(1)}, bf16[576,384]{1,0:T(8,128)(2,1)S(1)}) custom-call(bf16[512,384]{1,0:T(8,128)(2,1)S(1)} %copy-done.3, bf16[512,384]{1,0:T(8,128)(2,1)S(1)} %collective-permute-done.refs_1_.q1, bf16[512,768]{1,0:T(8,128)(2,1)S(1)} %copy-done.2), custom_call_target="tpu_custom_call" | custom-call | flops 402653184 | bytes 1000000 | tf_op jit(solution)/shard_map/attend_part/pallas_call | solution.py:222
  33.7 2.0 %collective-permute-done.4.refs_3_.refs_4_ = bf16[512,768]{1,0:T(8,128)(2,1)S(1)} collective-permute-done((bf16[512,768]{1,0:T(8,128)(2,1)}, bf16[512,768]{1,0:T(8,128)(2,1)S(1)}, u32[]{:S(2)}, u32[]{:S(2)}) %collective-permute-start.4) | collective-permute-done | bytes 786464 | tf_op jit(solution)/shard_map/ppermute | solution.py:365
  35.6 3.3 %collective-permute-done.3.refs_2_.refs_3_ = bf16[512,768]{1,0:T(8,128)(2,1)S(1)} collective-permute-done((bf16[512,768]{1,0:T(8,128)(2,1)}, bf16[512,768]{1,0:T(8,128)(2,1)S(1)}, u32[]{:S(2)}, u32[]{:S(2)}) %collective-permute-start.3) | collective-permute-done | bytes 786464 | tf_op jit(solution)/shard_map/ppermute | solution.py:364
  39.0 0.4 collective-permute-start.6
  39.4 1.7 %collective-permute-start.5 = (bf16[256,768]{1,0:T(8,128)(2,1)S(1)}, bf16[256,768]{1,0:T(8,128)(2,1)S(1)}, u32[]{:S(2)}, u32[]{:S(2)}) collective-permute-start(bf16[256,768]{1,0:T(8,128)(2,1)S(1)} %slice.12), channel_id=1, source_target_pairs={{0,16},{8,24},{16,32},{24,40},{32,48},{40,56},{48,0},{56,8},{64,80... | collective-permute-start | bytes 1179656 | tf_op jit(solution)/shard_map/ppermute | solution.py:380
  41.1 5.1 %attend_part.4 = (bf16[576,384]{1,0:T(8,128)(2,1)S(1)}, bf16[576,384]{1,0:T(8,128)(2,1)S(1)}) custom-call(bf16[512,384]{1,0:T(8,128)(2,1)S(1)} %copy-done.3, bf16[512,384]{1,0:T(8,128)(2,1)S(1)} %collective-permute-done.refs_1_.q1, bf16[512,768]{1,0:T(8,128)(2,1)S(1)} %collective-permute-done.3.refs_2_.refs_3_, ...), custom_call_target="tpu_custom_call" | custom-call | flops 805306368 | bytes 1000000 | tf_op jit(solution)/shard_map/attend_part/pallas_call | solution.py:222
  46.2 0.0 collective-permute-done.2.refs_1_.q3
  46.2 6.8 %attend_part.5 = (bf16[576,384]{1,0:T(8,128)(2,1)S(1)}, bf16[576,384]{1,0:T(8,128)(2,1)S(1)}) custom-call(bf16[512,384]{1,0:T(8,128)(2,1)S(1)} %collective-permute-done.1.refs_0_.q2, bf16[512,384]{1,0:T(8,128)(2,1)S(1)} %collective-permute-done.2.refs_1_.q3, bf16[512,768]{1,0:T(8,128)(2,1)S(1)} %copy-done.2, ...), custom_call_target="tpu_custom_call" | custom-call | flops 1207959552 | bytes 1000000 | tf_op jit(solution)/shard_map/attend_part/pallas_call | solution.py:222
  52.9 0.0 collective-permute-done.7.refs_1_
  53.0 0.0 collective-permute-done.8.refs_4_
  53.0 0.0 collective-permute-done.6.k1
  53.0 0.0 collective-permute-done.5.k0
  53.0 3.7 %attend_last.1 = (bf16[1152,384]{1,0:T(8,128)(2,1)S(1)}, bf16[1152,384]{1,0:T(8,128)(2,1)S(1)}) custom-call(bf16[512,384]{1,0:T(8,128)(2,1)S(1)} %copy-done.3, bf16[512,384]{1,0:T(8,128)(2,1)S(1)} %collective-permute-done.refs_1_.q1, bf16[512,384]{1,0:T(8,128)(2,1)S(1)} %collective-permute-done.1.refs_0_.q2, ...), custom_call_target="tpu_custom_call" | custom-call | flops 3221225472 | bytes 8000000 | tf_op jit(solution)/shard_map/attend_last/pallas_call | solution.py:257
  56.7 0.1 collective-permute-start.9
  56.8 0.5 collective-permute-start.10
  57.3 0.1 collective-permute-start.11
  57.4 3.1 %collective-permute-start.14 = (bf16[192,640]{1,0:T(8,128)(2,1)S(1)}, bf16[192,640]{1,0:T(8,128)(2,1)S(1)}, u32[]{:S(2)}, u32[]{:S(2)}) collective-permute-start(bf16[192,640]{1,0:T(8,128)(2,1)S(1)} %slice.15), channel_id=1, source_target_pairs={{0,3},{1,0},{2,1},{3,2},{4,7},{5,4},{6,5},{7,6},{8,11},{9,8},{10,9... | collective-permute-start | bytes 737288 | tf_op jit(solution)/shard_map/ppermute | solution.py:388
  60.5 0.0 collective-permute-done.10.refs_6_
  60.5 0.8 collective-permute-done.11.refs_9_
  61.3 0.0 collective-permute-done.9.recv
  61.4 0.2 combine_core.1
  61.6 1.6 %collective-permute-start.21 = (bf16[288,384]{1,0:T(8,128)(2,1)S(1)}, bf16[288,384]{1,0:T(8,128)(2,1)S(1)}, u32[]{:S(2)}, u32[]{:S(2)}) collective-permute-start(bf16[288,384]{1,0:T(8,128)(2,1)S(1)} %get-tuple-element.76), channel_id=1, source_target_pairs={{0,64},{8,72},{16,80},{24,88},{32,96},{40,104},{48,112},{56,120},{... | collective-permute-start | bytes 663560 | tf_op jit(solution)/shard_map/ppermute | solution.py:393
  63.2 1.6 %collective-permute-start.13 = (bf16[192,640]{1,0:T(8,128)(2,1)S(1)}, bf16[192,640]{1,0:T(8,128)(2,1)S(1)}, u32[]{:S(2)}, u32[]{:S(2)}) collective-permute-start(bf16[192,640]{1,0:T(8,128)(2,1)S(1)} %slice.14), channel_id=1, source_target_pairs={{0,1},{1,2},{2,3},{3,0},{4,5},{5,6},{6,7},{7,4},{8,9},{9,10},{10,1... | collective-permute-start | bytes 737288 | tf_op jit(solution)/shard_map/ppermute | solution.py:388
  64.8 0.5 collective-permute-start.12
  65.3 4.6 %collective-permute-done.21.recv = bf16[288,384]{1,0:T(8,128)(2,1)S(1)} collective-permute-done((bf16[288,384]{1,0:T(8,128)(2,1)S(1)}, bf16[288,384]{1,0:T(8,128)(2,1)S(1)}, u32[]{:S(2)}, u32[]{:S(2)}) %collective-permute-start.21) | collective-permute-done | bytes 221216 | tf_op jit(solution)/shard_map/ppermute | solution.py:393
  69.9 0.2 combine_x.3.a0
  70.1 3.1 %collective-permute-start.24 = (bf16[256,384]{1,0:T(8,128)(2,1)S(1)}, bf16[256,384]{1,0:T(8,128)(2,1)S(1)}, u32[]{:S(2)}, u32[]{:S(2)}) collective-permute-start(bf16[256,384]{1,0:T(8,128)(2,1)S(1)} %combine_x.3.a0), channel_id=1, source_target_pairs={{0,3},{1,0},{2,1},{3,2},{4,7},{5,4},{6,5},{7,6},{8,11},{9,8},{10,9... | collective-permute-start | bytes 589832 | tf_op jit(solution)/shard_map/ppermute | solution.py:402
  73.2 0.6 collective-permute-start.23
  73.8 0.0 collective-permute-done.14.refs_3_
  73.8 1.0 collective-permute-start.22
  74.8 0.0 collective-permute-done.13.refs_2_
  74.8 0.0 collective-permute-done.12.recv
  74.8 0.5 collective-permute-start.19
  75.3 0.2 combine_x.2.a0
  75.5 4.7 %collective-permute-done.24.a3 = bf16[256,384]{1,0:T(8,128)(2,1)S(1)} collective-permute-done((bf16[256,384]{1,0:T(8,128)(2,1)S(1)}, bf16[256,384]{1,0:T(8,128)(2,1)S(1)}, u32[]{:S(2)}, u32[]{:S(2)}) %collective-permute-start.24) | collective-permute-done | bytes 196640 | tf_op jit(solution)/shard_map/ppermute | solution.py:402
  80.2 3.7 %collective-permute-start.17 = (bf16[256,384]{1,0:T(8,128)(2,1)S(1)}, bf16[256,384]{1,0:T(8,128)(2,1)S(1)}, u32[]{:S(2)}, u32[]{:S(2)}) collective-permute-start(bf16[256,384]{1,0:T(8,128)(2,1)S(1)} %combine_x.2.a0), channel_id=1, source_target_pairs={{0,3},{1,0},{2,1},{3,2},{4,7},{5,4},{6,5},{7,6},{8,11},{9,8},{10,9... | collective-permute-start | bytes 589832 | tf_op jit(solution)/shard_map/ppermute | solution.py:402
  83.9 0.0 collective-permute-done.23.a2
  83.9 0.0 collective-permute-start.16
  83.9 0.0 collective-permute-done.22.a1
  83.9 0.9 collective-permute-start.15
  84.8 0.0 collective-permute-done.18.refs_7_
  84.8 0.0 collective-permute-done.19.refs_8_
  84.8 1.2 %out_project.3 = (bf16[256,640]{1,0:T(8,128)(2,1)S(1)}, bf16[256,640]{1,0:T(8,128)(2,1)S(1)}) custom-call(s32[1]{0:T(128)} %bitcast.core, bf16[256,384]{1,0:T(8,128)(2,1)S(1)} %combine_x.3.a0, bf16[256,384]{1,0:T(8,128)(2,1)S(1)} %collective-permute-done.22.a1, bf16[256,384]{1,0:T(8,128)(2,1)S(1)} %collective-permute-done.23.a2, ...), custom_call_target="tpu_custom_call" | custom-call | flops 1006632960 | bytes 6000000 | tf_op jit(solution)/shard_map/out_project/pallas_call | solution.py:327
  86.0 3.1 %collective-permute-start.25 = (bf16[256,640]{1,0:T(8,128)(2,1)S(1)}, bf16[256,640]{1,0:T(8,128)(2,1)S(1)}, u32[]{:S(2)}, u32[]{:S(2)}) collective-permute-start(bf16[256,640]{1,0:T(8,128)(2,1)S(1)} %get-tuple-element.78), channel_id=1, source_target_pairs={{0,4},{1,5},{2,6},{3,7},{4,0},{5,1},{6,2},{7,3},{8,12},{9,13},{10,... | collective-permute-start | bytes 983048 | tf_op jit(solution)/shard_map/ppermute | solution.py:404
  89.1 0.1 collective-permute-done.17.a3
  89.2 2.0 %collective-permute-done.16.a2 = bf16[256,384]{1,0:T(8,128)(2,1)S(1)} collective-permute-done((bf16[256,384]{1,0:T(8,128)(2,1)S(1)}, bf16[256,384]{1,0:T(8,128)(2,1)S(1)}, u32[]{:S(2)}, u32[]{:S(2)}) %collective-permute-start.16) | collective-permute-done | bytes 196640 | tf_op jit(solution)/shard_map/ppermute | solution.py:402
  91.2 2.1 %collective-permute-done.15.a1 = bf16[256,384]{1,0:T(8,128)(2,1)S(1)} collective-permute-done((bf16[256,384]{1,0:T(8,128)(2,1)S(1)}, bf16[256,384]{1,0:T(8,128)(2,1)S(1)}, u32[]{:S(2)}, u32[]{:S(2)}) %collective-permute-start.15) | collective-permute-done | bytes 196640 | tf_op jit(solution)/shard_map/ppermute | solution.py:402
  93.3 1.2 %out_project.2 = (bf16[256,640]{1,0:T(8,128)(2,1)S(1)}, bf16[256,640]{1,0:T(8,128)(2,1)S(1)}) custom-call(s32[1]{0:T(128)} %bitcast.core, bf16[256,384]{1,0:T(8,128)(2,1)S(1)} %combine_x.2.a0, bf16[256,384]{1,0:T(8,128)(2,1)S(1)} %collective-permute-done.15.a1, bf16[256,384]{1,0:T(8,128)(2,1)S(1)} %collective-permute-done.16.a2, ...), custom_call_target="tpu_custom_call" | custom-call | flops 1006632960 | bytes 6000000 | tf_op jit(solution)/shard_map/out_project/pallas_call | solution.py:327
  94.5 3.1 %collective-permute-start.20 = (bf16[256,640]{1,0:T(8,128)(2,1)S(1)}, bf16[256,640]{1,0:T(8,128)(2,1)S(1)}, u32[]{:S(2)}, u32[]{:S(2)}) collective-permute-start(bf16[256,640]{1,0:T(8,128)(2,1)S(1)} %get-tuple-element.74), channel_id=1, source_target_pairs={{0,4},{1,5},{2,6},{3,7},{4,0},{5,1},{6,2},{7,3},{8,12},{9,13},{10,... | collective-permute-start | bytes 983048 | tf_op jit(solution)/shard_map/ppermute | solution.py:404
  97.6 0.8 finish.2.rest_0_
  98.4 5.5 %collective-permute-done.20.recv = bf16[256,640]{1,0:T(8,128)(2,1)S(1)} collective-permute-done((bf16[256,640]{1,0:T(8,128)(2,1)S(1)}, bf16[256,640]{1,0:T(8,128)(2,1)S(1)}, u32[]{:S(2)}, u32[]{:S(2)}) %collective-permute-start.20) | collective-permute-done | bytes 327712 | tf_op jit(solution)/shard_map/ppermute | solution.py:404
  103.9 0.8 finish.3
  (14 shorter events, 0.1 us)
Async XLA Ops:
  14.3 16.0 %copy-start.2 = (bf16[512,768]{1,0:T(8,128)(2,1)S(1)}, bf16[512,768]{1,0:T(8,128)(2,1)}, u32[]{:S(2)}) copy-start(bf16[512,768]{1,0:T(8,128)(2,1)} %get-tuple-element.44.refs_2_) | copy-start | bytes 2359300
  14.3 16.0 %copy-start.3 = (bf16[512,384]{1,0:T(8,128)(2,1)S(1)}, bf16[512,384]{1,0:T(8,128)(2,1)}, u32[]{:S(2)}) copy-start(bf16[512,384]{1,0:T(8,128)(2,1)} %get-tuple-element.42.refs_0_.q0) | copy-start | bytes 1179652
  14.3 21.3 %collective-permute-start.4 = (bf16[512,768]{1,0:T(8,128)(2,1)}, bf16[512,768]{1,0:T(8,128)(2,1)S(1)}, u32[]{:S(2)}, u32[]{:S(2)}) collective-permute-start(bf16[512,768]{1,0:T(8,128)(2,1)} %get-tuple-element.44.refs_2_), channel_id=1, source_target_pairs={{0,48},{8,56},{16,0},{24,8},{32,16},{40,24},{48,32},{56,40},{64,11... | collective-permute-start | bytes 2359304 | tf_op jit(solution)/shard_map/ppermute | solution.py:365
  18.5 20.4 %collective-permute-start.3 = (bf16[512,768]{1,0:T(8,128)(2,1)}, bf16[512,768]{1,0:T(8,128)(2,1)S(1)}, u32[]{:S(2)}, u32[]{:S(2)}) collective-permute-start(bf16[512,768]{1,0:T(8,128)(2,1)} %get-tuple-element.44.refs_2_), channel_id=1, source_target_pairs={{0,16},{8,24},{16,32},{24,40},{32,48},{40,56},{48,0},{56,8},{64,80... | collective-permute-start | bytes 2359304 | tf_op jit(solution)/shard_map/ppermute | solution.py:364
  18.5 2.2 %collective-permute-start = (bf16[512,384]{1,0:T(8,128)(2,1)}, bf16[512,384]{1,0:T(8,128)(2,1)S(1)}, u32[]{:S(2)}, u32[]{:S(2)}) collective-permute-start(bf16[512,384]{1,0:T(8,128)(2,1)} %get-tuple-element.42.refs_0_.q0), channel_id=1, source_target_pairs={{0,8},{8,0},{16,24},{24,16},{32,40},{40,32},{48,56},{56,48},{64,72... | collective-permute-start | bytes 1179656 | tf_op jit(solution)/shard_map/ppermute | solution.py:371
  18.5 11.7 %collective-permute-start.1 = (bf16[512,384]{1,0:T(8,128)(2,1)}, bf16[512,384]{1,0:T(8,128)(2,1)S(1)}, u32[]{:S(2)}, u32[]{:S(2)}) collective-permute-start(bf16[512,384]{1,0:T(8,128)(2,1)} %get-tuple-element.42.refs_0_.q0), channel_id=1, source_target_pairs={{0,64},{8,72},{16,80},{24,88},{32,96},{40,104},{48,112},{56,120},{... | collective-permute-start | bytes 1179656 | tf_op jit(solution)/shard_map/ppermute | solution.py:372
  24.5 28.4 %collective-permute-start.7 = (bf16[576,640]{1,0:T(8,128)(2,1)}, bf16[576,640]{1,0:T(8,128)(2,1)S(1)}, u32[]{:S(2)}, u32[]{:S(2)}) collective-permute-start(bf16[576,640]{1,0:T(8,128)(2,1)} %get-tuple-element.53), channel_id=1, source_target_pairs={{0,1},{1,2},{2,3},{3,0},{4,5},{5,6},{6,7},{7,4},{8,9},{9,10},{10,1... | collective-permute-start | bytes 2211848 | tf_op jit(solution)/shard_map/ppermute | solution.py:375
  26.2 26.8 %collective-permute-start.8 = (bf16[576,640]{1,0:T(8,128)(2,1)}, bf16[576,640]{1,0:T(8,128)(2,1)S(1)}, u32[]{:S(2)}, u32[]{:S(2)}) collective-permute-start(bf16[576,640]{1,0:T(8,128)(2,1)} %get-tuple-element.54), channel_id=1, source_target_pairs={{0,3},{1,0},{2,1},{3,2},{4,7},{5,4},{6,5},{7,6},{8,11},{9,8},{10,9... | collective-permute-start | bytes 2211848 | tf_op jit(solution)/shard_map/ppermute | solution.py:376
  30.3 15.9 %collective-permute-start.2 = (bf16[512,384]{1,0:T(8,128)(2,1)S(1)}, bf16[512,384]{1,0:T(8,128)(2,1)S(1)}, u32[]{:S(2)}, u32[]{:S(2)}) collective-permute-start(bf16[512,384]{1,0:T(8,128)(2,1)S(1)} %collective-permute-done.1.refs_0_.q2), channel_id=1, source_target_pairs={{0,8},{8,0},{16,24},{24,16},{32,40},{40,32},{48,56},{56,48},{64,72... | collective-permute-start | bytes 1179656 | tf_op jit(solution)/shard_map/ppermute | solution.py:377
  39.0 14.0 %collective-permute-start.6 = (bf16[256,768]{1,0:T(8,128)(2,1)S(1)}, bf16[256,768]{1,0:T(8,128)(2,1)S(1)}, u32[]{:S(2)}, u32[]{:S(2)}) collective-permute-start(bf16[256,768]{1,0:T(8,128)(2,1)S(1)} %slice.13), channel_id=1, source_target_pairs={{0,48},{8,56},{16,0},{24,8},{32,16},{40,24},{48,32},{56,40},{64,11... | collective-permute-start | bytes 1179656 | tf_op jit(solution)/shard_map/ppermute | solution.py:381
  39.4 13.6 %collective-permute-start.5 = (bf16[256,768]{1,0:T(8,128)(2,1)S(1)}, bf16[256,768]{1,0:T(8,128)(2,1)S(1)}, u32[]{:S(2)}, u32[]{:S(2)}) collective-permute-start(bf16[256,768]{1,0:T(8,128)(2,1)S(1)} %slice.12), channel_id=1, source_target_pairs={{0,16},{8,24},{16,32},{24,40},{32,48},{40,56},{48,0},{56,8},{64,80... | collective-permute-start | bytes 1179656 | tf_op jit(solution)/shard_map/ppermute | solution.py:380
  56.7 28.1 %copy-start = (bf16[384,640]{1,0:T(8,128)(2,1)S(1)}, bf16[384,640]{1,0:T(8,128)(2,1)}, u32[]{:S(2)}) copy-start(bf16[384,640]{1,0:T(8,128)(2,1)} %get-tuple-element.67.refs_0_) | copy-start | bytes 1474564
  56.7 28.1 %copy-start.1 = (bf16[384,640]{1,0:T(8,128)(2,1)S(1)}, bf16[384,640]{1,0:T(8,128)(2,1)}, u32[]{:S(2)}) copy-start(bf16[384,640]{1,0:T(8,128)(2,1)} %get-tuple-element.70.refs_5_) | copy-start | bytes 1474564
  56.7 4.6 %collective-permute-start.9 = (bf16[1152,384]{1,0:T(8,128)(2,1)S(1)}, bf16[1152,384]{1,0:T(8,128)(2,1)S(1)}, u32[]{:S(2)}, u32[]{:S(2)}) collective-permute-start(bf16[1152,384]{1,0:T(8,128)(2,1)S(1)} %get-tuple-element.60), channel_id=1, source_target_pairs={{0,8},{8,0},{16,24},{24,16},{32,40},{40,32},{48,56},{56,48},{64,72... | collective-permute-start | bytes 2654216 | tf_op jit(solution)/shard_map/ppermute | solution.py:391
  56.8 3.7 %collective-permute-start.10 = (bf16[576,640]{1,0:T(8,128)(2,1)S(1)}, bf16[576,640]{1,0:T(8,128)(2,1)S(1)}, u32[]{:S(2)}, u32[]{:S(2)}) collective-permute-start(bf16[576,640]{1,0:T(8,128)(2,1)S(1)} %collective-permute-done.7.refs_1_), channel_id=1, source_target_pairs={{0,8},{8,0},{16,24},{24,16},{32,40},{40,32},{48,56},{56,48},{64,72... | collective-permute-start | bytes 2211848 | tf_op jit(solution)/shard_map/ppermute | solution.py:387
  57.3 4.0 %collective-permute-start.11 = (bf16[576,640]{1,0:T(8,128)(2,1)S(1)}, bf16[576,640]{1,0:T(8,128)(2,1)S(1)}, u32[]{:S(2)}, u32[]{:S(2)}) collective-permute-start(bf16[576,640]{1,0:T(8,128)(2,1)S(1)} %collective-permute-done.8.refs_4_), channel_id=1, source_target_pairs={{0,8},{8,0},{16,24},{24,16},{32,40},{40,32},{48,56},{56,48},{64,72... | collective-permute-start | bytes 2211848 | tf_op jit(solution)/shard_map/ppermute | solution.py:387
  57.4 16.4 %collective-permute-start.14 = (bf16[192,640]{1,0:T(8,128)(2,1)S(1)}, bf16[192,640]{1,0:T(8,128)(2,1)S(1)}, u32[]{:S(2)}, u32[]{:S(2)}) collective-permute-start(bf16[192,640]{1,0:T(8,128)(2,1)S(1)} %slice.15), channel_id=1, source_target_pairs={{0,3},{1,0},{2,1},{3,2},{4,7},{5,4},{6,5},{7,6},{8,11},{9,8},{10,9... | collective-permute-start | bytes 737288 | tf_op jit(solution)/shard_map/ppermute | solution.py:388
  61.6 8.3 %collective-permute-start.21 = (bf16[288,384]{1,0:T(8,128)(2,1)S(1)}, bf16[288,384]{1,0:T(8,128)(2,1)S(1)}, u32[]{:S(2)}, u32[]{:S(2)}) collective-permute-start(bf16[288,384]{1,0:T(8,128)(2,1)S(1)} %get-tuple-element.76), channel_id=1, source_target_pairs={{0,64},{8,72},{16,80},{24,88},{32,96},{40,104},{48,112},{56,120},{... | collective-permute-start | bytes 663560 | tf_op jit(solution)/shard_map/ppermute | solution.py:393
  63.2 11.6 %collective-permute-start.13 = (bf16[192,640]{1,0:T(8,128)(2,1)S(1)}, bf16[192,640]{1,0:T(8,128)(2,1)S(1)}, u32[]{:S(2)}, u32[]{:S(2)}) collective-permute-start(bf16[192,640]{1,0:T(8,128)(2,1)S(1)} %slice.14), channel_id=1, source_target_pairs={{0,1},{1,2},{2,3},{3,0},{4,5},{5,6},{6,7},{7,4},{8,9},{9,10},{10,1... | collective-permute-start | bytes 737288 | tf_op jit(solution)/shard_map/ppermute | solution.py:388
  64.8 10.0 %collective-permute-start.12 = (bf16[288,384]{1,0:T(8,128)(2,1)S(1)}, bf16[288,384]{1,0:T(8,128)(2,1)S(1)}, u32[]{:S(2)}, u32[]{:S(2)}) collective-permute-start(bf16[288,384]{1,0:T(8,128)(2,1)S(1)} %get-tuple-element.65), channel_id=1, source_target_pairs={{0,64},{8,72},{16,80},{24,88},{32,96},{40,104},{48,112},{56,120},{... | collective-permute-start | bytes 663560 | tf_op jit(solution)/shard_map/ppermute | solution.py:394
  70.1 10.1 %collective-permute-start.24 = (bf16[256,384]{1,0:T(8,128)(2,1)S(1)}, bf16[256,384]{1,0:T(8,128)(2,1)S(1)}, u32[]{:S(2)}, u32[]{:S(2)}) collective-permute-start(bf16[256,384]{1,0:T(8,128)(2,1)S(1)} %combine_x.3.a0), channel_id=1, source_target_pairs={{0,3},{1,0},{2,1},{3,2},{4,7},{5,4},{6,5},{7,6},{8,11},{9,8},{10,9... | collective-permute-start | bytes 589832 | tf_op jit(solution)/shard_map/ppermute | solution.py:402
  73.2 10.7 %collective-permute-start.23 = (bf16[256,384]{1,0:T(8,128)(2,1)S(1)}, bf16[256,384]{1,0:T(8,128)(2,1)S(1)}, u32[]{:S(2)}, u32[]{:S(2)}) collective-permute-start(bf16[256,384]{1,0:T(8,128)(2,1)S(1)} %combine_x.3.a0), channel_id=1, source_target_pairs={{0,2},{1,3},{2,0},{3,1},{4,6},{5,7},{6,4},{7,5},{8,10},{9,11},{10,... | collective-permute-start | bytes 589832 | tf_op jit(solution)/shard_map/ppermute | solution.py:402
  73.8 10.1 %collective-permute-start.22 = (bf16[256,384]{1,0:T(8,128)(2,1)S(1)}, bf16[256,384]{1,0:T(8,128)(2,1)S(1)}, u32[]{:S(2)}, u32[]{:S(2)}) collective-permute-start(bf16[256,384]{1,0:T(8,128)(2,1)S(1)} %combine_x.3.a0), channel_id=1, source_target_pairs={{0,1},{1,2},{2,3},{3,0},{4,5},{5,6},{6,7},{7,4},{8,9},{9,10},{10,1... | collective-permute-start | bytes 589832 | tf_op jit(solution)/shard_map/ppermute | solution.py:402
  74.8 10.0 %collective-permute-start.18 = (bf16[192,640]{1,0:T(8,128)(2,1)S(1)}, bf16[192,640]{1,0:T(8,128)(2,1)S(1)}, u32[]{:S(2)}, u32[]{:S(2)}) collective-permute-start(bf16[192,640]{1,0:T(8,128)(2,1)S(1)} %collective-permute-done.13.refs_2_), channel_id=1, source_target_pairs={{0,8},{8,0},{16,24},{24,16},{32,40},{40,32},{48,56},{56,48},{64,72... | collective-permute-start | bytes 737288 | tf_op jit(solution)/shard_map/ppermute | solution.py:396
  74.8 10.0 %collective-permute-start.19 = (bf16[192,640]{1,0:T(8,128)(2,1)S(1)}, bf16[192,640]{1,0:T(8,128)(2,1)S(1)}, u32[]{:S(2)}, u32[]{:S(2)}) collective-permute-start(bf16[192,640]{1,0:T(8,128)(2,1)S(1)} %collective-permute-done.14.refs_3_), channel_id=1, source_target_pairs={{0,8},{8,0},{16,24},{24,16},{32,40},{40,32},{48,56},{56,48},{64,72... | collective-permute-start | bytes 737288 | tf_op jit(solution)/shard_map/ppermute | solution.py:396
  80.2 9.0 %collective-permute-start.17 = (bf16[256,384]{1,0:T(8,128)(2,1)S(1)}, bf16[256,384]{1,0:T(8,128)(2,1)S(1)}, u32[]{:S(2)}, u32[]{:S(2)}) collective-permute-start(bf16[256,384]{1,0:T(8,128)(2,1)S(1)} %combine_x.2.a0), channel_id=1, source_target_pairs={{0,3},{1,0},{2,1},{3,2},{4,7},{5,4},{6,5},{7,6},{8,11},{9,8},{10,9... | collective-permute-start | bytes 589832 | tf_op jit(solution)/shard_map/ppermute | solution.py:402
  83.9 7.3 %collective-permute-start.16 = (bf16[256,384]{1,0:T(8,128)(2,1)S(1)}, bf16[256,384]{1,0:T(8,128)(2,1)S(1)}, u32[]{:S(2)}, u32[]{:S(2)}) collective-permute-start(bf16[256,384]{1,0:T(8,128)(2,1)S(1)} %combine_x.2.a0), channel_id=1, source_target_pairs={{0,2},{1,3},{2,0},{3,1},{4,6},{5,7},{6,4},{7,5},{8,10},{9,11},{10,... | collective-permute-start | bytes 589832 | tf_op jit(solution)/shard_map/ppermute | solution.py:402
  83.9 9.3 %collective-permute-start.15 = (bf16[256,384]{1,0:T(8,128)(2,1)S(1)}, bf16[256,384]{1,0:T(8,128)(2,1)S(1)}, u32[]{:S(2)}, u32[]{:S(2)}) collective-permute-start(bf16[256,384]{1,0:T(8,128)(2,1)S(1)} %combine_x.2.a0), channel_id=1, source_target_pairs={{0,1},{1,2},{2,3},{3,0},{4,5},{5,6},{6,7},{7,4},{8,9},{9,10},{10,1... | collective-permute-start | bytes 589832 | tf_op jit(solution)/shard_map/ppermute | solution.py:402
  86.0 11.5 %collective-permute-start.25 = (bf16[256,640]{1,0:T(8,128)(2,1)S(1)}, bf16[256,640]{1,0:T(8,128)(2,1)S(1)}, u32[]{:S(2)}, u32[]{:S(2)}) collective-permute-start(bf16[256,640]{1,0:T(8,128)(2,1)S(1)} %get-tuple-element.78), channel_id=1, source_target_pairs={{0,4},{1,5},{2,6},{3,7},{4,0},{5,1},{6,2},{7,3},{8,12},{9,13},{10,... | collective-permute-start | bytes 983048 | tf_op jit(solution)/shard_map/ppermute | solution.py:404
  94.5 9.4 %collective-permute-start.20 = (bf16[256,640]{1,0:T(8,128)(2,1)S(1)}, bf16[256,640]{1,0:T(8,128)(2,1)S(1)}, u32[]{:S(2)}, u32[]{:S(2)}) collective-permute-start(bf16[256,640]{1,0:T(8,128)(2,1)S(1)} %get-tuple-element.74), channel_id=1, source_target_pairs={{0,4},{1,5},{2,6},{3,7},{4,0},{5,1},{6,2},{7,3},{8,12},{9,13},{10,... | collective-permute-start | bytes 983048 | tf_op jit(solution)/shard_map/ppermute | solution.py:404

commit v8 on v5

--- a/solution.py
+++ b/solution.py
@@ -231,20 +231,17 @@
     )(*qs, *kvs)
 
 
-def last_kernel(q0, q1, q2, q3, k0, k1, own0, own1, near0, near1, cross0, cross1, keep, send):
+def last_kernel(q0, q1, q2, q3, k0, k1, own0, own1, near0, near1, keep, send):
     for h in range(GROUP_HEADS):
         col = slice(h * HD, (h + 1) * HD)
         wide = slice(2 * h * HD, 2 * (h + 1) * HD)
         for i, (q, out) in enumerate(((q0, keep), (q1, send), (q2, keep), (q3, send))):
             acc = mix(q[:, col], (k0[:, wide], k1[:, wide]), 256)
-            for half, (own, near, cross) in enumerate(((own0, near0, cross0), (own1, near1, cross1))):
+            for half, (own, near) in enumerate(((own0, near0), (own1, near1))):
                 rows = acc[half * HALF : (half + 1) * HALF]
                 base = (2 * half + i // 2) * PACK
                 quarter = slice(i * PACK, (i + 1) * PACK)
-                if i < 3:
-                    old = own[quarter, col].astype(F32) + near[quarter, col].astype(F32)
-                else:
-                    old = cross[:, col].astype(F32)
+                old = own[quarter, col].astype(F32) + near[quarter, col].astype(F32)
                 out[base : base + HALF, col] = (rows[:, :HD] + old[:HALF]).astype(BF16)
                 for p in range(HALF // 128):
                     t = jnp.transpose(rows[p * 128 : (p + 1) * 128, HD:])[:16]
@@ -375,15 +372,14 @@
     up = lax.ppermute(up, "head", Y_STEP[1])
     down = lax.ppermute(down, "head", Y_STEP[3])
     q_xc = lax.ppermute(q_x, "seq", SWAP_CORE)
-    parts_own = attend_part((q, q_core, q_x), (kv,))
+    parts_own = attend_part((q, q_core, q_x, q_xc), (kv,))
     below, above, *parts_own = lax.optimization_barrier((below, above, *parts_own))
     far_a = lax.ppermute(below[:256], "seq", Z_UP)
     far_b = lax.ppermute(above[256:], "seq", Z_DOWN)
     qs = (q, q_core, q_x, q_xc)
-    parts_near = attend_part(qs[:3], (below, above))
-    parts_cross = attend_part(qs[3:], (kv, below, above))
+    parts_near = attend_part(qs, (below, above))
     part, up, down = lax.optimization_barrier((parts_near[0], up, down))
-    parts = (*parts_own, part, parts_near[1], *parts_cross)
+    parts = (*parts_own, part, parts_near[1])
     second = [lax.ppermute(w, "seq", SWAP_CORE) for w in (up, down)]
     far = [lax.ppermute(up[WIDE:], "head", Y_STEP[1]), lax.ppermute(down[WIDE:], "head", Y_STEP[3])]
 

time: 104 us -> 108 us (1.038)
  waiting for transfers between devices: 26.6 us -> 32.8 us
  starting transfers between devices: 34.5 us -> 31.9 us
    ppermute x1, starting transfers between devices: 0.35 us -> 3.28 us  [shards(): far_b = lax.ppermute(above[256:], 'seq', Z_DOWN)]
    ppermute x1, waiting for transfers between devices: 2.44 us -> 5.28 us  [shards(): q_x = lax.ppermute(q, 'seq', SWAP_X)]
    ppermute x1, waiting for transfers between devices: 0.01 us -> 2.72 us  [shards(): far_a = lax.ppermute(below[:256], 'seq', Z_UP)]
    ppermute x1, waiting for transfers between devices: 3.31 us -> 0.99 us  [shards(): below = lax.ppermute(kv, 'seq', Z_UP)]
    ppermute x1, starting transfers between devices: 1.74 us -> 0.01 us  [shards(): far_a = lax.ppermute(below[:256], 'seq', Z_UP)]
    ppermute x1, starting transfers between devices: 3.08 us -> 1.73 us  [shards(): lax.ppermute(down[WIDE:], 'head', Y_STEP[3])]
    ppermute x2, waiting for transfers between devices: 0.82 us -> 2.17 us  [shards(): second = [lax.ppermute(w, 'seq', SWAP_CORE) for w in (up, down)]]
    ppermute x1, starting transfers between devices: 1.65 us -> 0.3 us  [shards(): lax.ppermute(up[WIDE:], 'head', Y_STEP[1])]
  transfers between devices with their start and end apart: 26 -> 26, of which waited for: 10 -> 12; matrix products, arithmetic and copies ran while one was open for 1% -> 1% of each run, Pallas kernels for 22% -> 21%
where the time goes in v8:
time: 108 us
  Pallas kernels  42.6 us (39%)
  waiting for transfers between devices  32.8 us (30%)
  starting transfers between devices  31.9 us (30%)
    pallas_call x2, Pallas kernels, attend_part(): pl.pallas_call(functools.partial(part_kernel, len(qs), len(kvs)), grid=(G...  15.2 us
    pallas_call x1, Pallas kernels, project(): pl.pallas_call(qkv_kernel, in_specs=[hbm] * 8, out_specs=[vmem, vmem], ou...  14.3 us
    ppermute x6, waiting for transfers between devices, shards(): attended = [att] + [lax.ppermute(att, 'head', Y_STEP[r]) for r in (1, 2, 3)]  8.79 us
    ppermute x6, starting transfers between devices, shards(): attended = [att] + [lax.ppermute(att, 'head', Y_STEP[r]) for r in (1, 2, 3)]  8.01 us
    ppermute x2, waiting for transfers between devices, shards(): out = finish(half, kept, lax.ppermute(sent, 'head', SWAP_XHI), out)  6.46 us
    ppermute x2, starting transfers between devices, shards(): out = finish(half, kept, lax.ppermute(sent, 'head', SWAP_XHI), out)  6.21 us
    ppermute x1, waiting for transfers between devices, shards(): recv0 = lax.ppermute(away0, 'seq', SWAP_X)  5.92 us
    ppermute x1, waiting for transfers between devices, shards(): q_x = lax.ppermute(q, 'seq', SWAP_X)  5.28 us
  transfers between devices with their start and end apart: 26, of which 12 were waited for; matrix products, arithmetic and copies ran while one was open for 1% of the time, Pallas kernels for 21%

profile of v8, /device:TPU:0, one launch (start us, length us, event | category | flops | bytes accessed | tf_op | source)
XLA Modules:
  0.0 108.3 jit_solution(14617711103919186599)
XLA Ops:
  0.0 14.3 %project.1 = (bf16[512,384]{1,0:T(8,128)(2,1)}, bf16[512,768]{1,0:T(8,128)(2,1)}) custom-call(bf16[512,5120]{1,0:T(8,128)(2,1)} %tok.1, f32[1,5120]{1,0:T(1,128)} %bitcast.8, f32[1,5120]{1,0:T(1,128)} %bitcast.9, bf16[5120,384]{1,0:T(8,128)(2,1)} %wq.1, bf16[5120,384]{1,0:T(8,128)(2,1)} %wk.1, bf16[5120,384]{1,0:T(8,128)(2,1)} %wv.1, f32[384]{0:T(512)} %gq_h.1, ...), custom_call_target="tpu_custom_call" | custom-call | flops 6039797760 | bytes 18000000 | tf_op jit(solution)/shard_map/project/pallas_call | solution.py:131
  14.3 1.7 %collective-permute-start.1 = (bf16[512,384]{1,0:T(8,128)(2,1)}, bf16[512,384]{1,0:T(8,128)(2,1)S(1)}, u32[]{:S(2)}, u32[]{:S(2)}) collective-permute-start(bf16[512,384]{1,0:T(8,128)(2,1)} %get-tuple-element.40.refs_0_.q0), channel_id=1, source_target_pairs={{0,64},{8,72},{16,80},{24,88},{32,96},{40,104},{48,112},{56,120},{... | collective-permute-start | bytes 1179656 | tf_op jit(solution)/shard_map/ppermute | solution.py:369
  16.0 4.0 %collective-permute-start.4 = (bf16[512,768]{1,0:T(8,128)(2,1)}, bf16[512,768]{1,0:T(8,128)(2,1)S(1)}, u32[]{:S(2)}, u32[]{:S(2)}) collective-permute-start(bf16[512,768]{1,0:T(8,128)(2,1)} %get-tuple-element.42.refs_4_), channel_id=1, source_target_pairs={{0,48},{8,56},{16,0},{24,8},{32,16},{40,24},{48,32},{56,40},{64,11... | collective-permute-start | bytes 2359304 | tf_op jit(solution)/shard_map/ppermute | solution.py:362
  20.0 0.0 collective-permute-start.3
  20.0 0.0 collective-permute-start
  20.0 5.3 %collective-permute-done.1.refs_2_.q2 = bf16[512,384]{1,0:T(8,128)(2,1)S(1)} collective-permute-done((bf16[512,384]{1,0:T(8,128)(2,1)}, bf16[512,384]{1,0:T(8,128)(2,1)S(1)}, u32[]{:S(2)}, u32[]{:S(2)}) %collective-permute-start.1) | collective-permute-done | bytes 393248 | tf_op jit(solution)/shard_map/ppermute | solution.py:369
  25.3 0.0 collective-permute-start.2
  25.3 0.6 stack.23.cols
  25.9 0.0 collective-permute-done.refs_1_.q1
  25.9 3.8 %take_blocks.1 = (bf16[384,640]{1,0:T(8,128)(2,1)}, bf16[576,640]{1,0:T(8,128)(2,1)}, bf16[576,640]{1,0:T(8,128)(2,1)}, bf16[384,640]{1,0:T(8,128)(2,1)}) custom-call(s32[5]{0:T(128)} %stack.23.cols, bf16[384,5120]{1,0:T(8,128)(2,1)} %wo.1), custom_call_target="tpu_custom_call" | custom-call | flops 1000000 | bytes 6000000 | tf_op jit(solution)/shard_map/take_blocks/pallas_call | solution.py:179
  29.8 1.9 %collective-permute-start.7 = (bf16[576,640]{1,0:T(8,128)(2,1)}, bf16[576,640]{1,0:T(8,128)(2,1)S(1)}, u32[]{:S(2)}, u32[]{:S(2)}) collective-permute-start(bf16[576,640]{1,0:T(8,128)(2,1)} %get-tuple-element.51), channel_id=1, source_target_pairs={{0,1},{1,2},{2,3},{3,0},{4,5},{5,6},{6,7},{7,4},{8,9},{9,10},{10,1... | collective-permute-start | bytes 2211848 | tf_op jit(solution)/shard_map/ppermute | solution.py:372
  31.7 1.5 %collective-permute-start.8 = (bf16[576,640]{1,0:T(8,128)(2,1)}, bf16[576,640]{1,0:T(8,128)(2,1)S(1)}, u32[]{:S(2)}, u32[]{:S(2)}) collective-permute-start(bf16[576,640]{1,0:T(8,128)(2,1)} %get-tuple-element.52), channel_id=1, source_target_pairs={{0,3},{1,0},{2,1},{3,2},{4,7},{5,4},{6,5},{7,6},{8,11},{9,8},{10,9... | collective-permute-start | bytes 2211848 | tf_op jit(solution)/shard_map/ppermute | solution.py:373
  33.2 0.0 collective-permute-done.2.refs_3_.q3
  33.2 6.0 %attend_part.2 = (bf16[1152,384]{1,0:T(8,128)(2,1)S(1)}, bf16[1152,384]{1,0:T(8,128)(2,1)S(1)}) custom-call(bf16[512,384]{1,0:T(8,128)(2,1)S(1)} %copy-done.3, bf16[512,384]{1,0:T(8,128)(2,1)S(1)} %collective-permute-done.refs_1_.q1, bf16[512,384]{1,0:T(8,128)(2,1)S(1)} %collective-permute-done.1.refs_2_.q2, ...), custom_call_target="tpu_custom_call" | custom-call | flops 805306368 | bytes 1000000 | tf_op jit(solution)/shard_map/attend_part/pallas_call | solution.py:222
  39.2 0.0 collective-permute-done.4.refs_5_
  39.2 1.0 collective-permute-done.3.refs_4_
  40.2 3.3 %collective-permute-start.6 = (bf16[256,768]{1,0:T(8,128)(2,1)S(1)}, bf16[256,768]{1,0:T(8,128)(2,1)S(1)}, u32[]{:S(2)}, u32[]{:S(2)}) collective-permute-start(bf16[256,768]{1,0:T(8,128)(2,1)S(1)} %slice.13), channel_id=1, source_target_pairs={{0,48},{8,56},{16,0},{24,8},{32,16},{40,24},{48,32},{56,40},{64,11... | collective-permute-start | bytes 1179656 | tf_op jit(solution)/shard_map/ppermute | solution.py:378
  43.5 0.0 collective-permute-start.5
  43.5 9.3 %attend_part.3 = (bf16[1152,384]{1,0:T(8,128)(2,1)S(1)}, bf16[1152,384]{1,0:T(8,128)(2,1)S(1)}) custom-call(bf16[512,384]{1,0:T(8,128)(2,1)S(1)} %copy-done.3, bf16[512,384]{1,0:T(8,128)(2,1)S(1)} %collective-permute-done.refs_1_.q1, bf16[512,384]{1,0:T(8,128)(2,1)S(1)} %collective-permute-done.1.refs_2_.q2, ...), custom_call_target="tpu_custom_call" | custom-call | flops 1610612736 | bytes 1000000 | tf_op jit(solution)/shard_map/attend_part/pallas_call | solution.py:222
  52.8 0.0 collective-permute-done.7.refs_1_
  52.8 0.0 collective-permute-done.8.refs_4_
  52.8 0.0 collective-permute-done.6.k1
  52.8 2.7 %collective-permute-done.5.k0 = bf16[256,768]{1,0:T(8,128)(2,1)S(1)} collective-permute-done((bf16[256,768]{1,0:T(8,128)(2,1)S(1)}, bf16[256,768]{1,0:T(8,128)(2,1)S(1)}, u32[]{:S(2)}, u32[]{:S(2)}) %collective-permute-start.5) | collective-permute-done | bytes 393248 | tf_op jit(solution)/shard_map/ppermute | solution.py:377
  55.5 4.7 %attend_last.1 = (bf16[1152,384]{1,0:T(8,128)(2,1)S(1)}, bf16[1152,384]{1,0:T(8,128)(2,1)S(1)}) custom-call(bf16[512,384]{1,0:T(8,128)(2,1)S(1)} %copy-done.3, bf16[512,384]{1,0:T(8,128)(2,1)S(1)} %collective-permute-done.refs_1_.q1, bf16[512,384]{1,0:T(8,128)(2,1)S(1)} %collective-permute-done.1.refs_2_.q2, ...), custom_call_target="tpu_custom_call" | custom-call | flops 3221225472 | bytes 8000000 | tf_op jit(solution)/shard_map/attend_last/pallas_call | solution.py:254
  60.3 0.1 collective-permute-start.9
  60.4 0.5 collective-permute-start.10
  60.9 0.1 collective-permute-start.11
  61.0 1.7 %collective-permute-start.14 = (bf16[192,640]{1,0:T(8,128)(2,1)S(1)}, bf16[192,640]{1,0:T(8,128)(2,1)S(1)}, u32[]{:S(2)}, u32[]{:S(2)}) collective-permute-start(bf16[192,640]{1,0:T(8,128)(2,1)S(1)} %slice.15), channel_id=1, source_target_pairs={{0,3},{1,0},{2,1},{3,2},{4,7},{5,4},{6,5},{7,6},{8,11},{9,8},{10,9... | collective-permute-start | bytes 737288 | tf_op jit(solution)/shard_map/ppermute | solution.py:384
  62.7 1.1 %collective-permute-done.10.refs_6_ = bf16[576,640]{1,0:T(8,128)(2,1)S(1)} collective-permute-done((bf16[576,640]{1,0:T(8,128)(2,1)S(1)}, bf16[576,640]{1,0:T(8,128)(2,1)S(1)}, u32[]{:S(2)}, u32[]{:S(2)}) %collective-permute-start.10) | collective-permute-done | bytes 737312 | tf_op jit(solution)/shard_map/ppermute | solution.py:383
  63.8 1.1 collective-permute-done.11.refs_9_
  64.9 0.0 collective-permute-done.9.recv
  64.9 0.2 combine_core.1
  65.1 1.6 %collective-permute-start.21 = (bf16[288,384]{1,0:T(8,128)(2,1)S(1)}, bf16[288,384]{1,0:T(8,128)(2,1)S(1)}, u32[]{:S(2)}, u32[]{:S(2)}) collective-permute-start(bf16[288,384]{1,0:T(8,128)(2,1)S(1)} %get-tuple-element.72), channel_id=1, source_target_pairs={{0,64},{8,72},{16,80},{24,88},{32,96},{40,104},{48,112},{56,120},{... | collective-permute-start | bytes 663560 | tf_op jit(solution)/shard_map/ppermute | solution.py:389
  66.7 0.3 collective-permute-start.13
  67.0 0.5 collective-permute-start.12
  67.5 5.9 %collective-permute-done.21.recv = bf16[288,384]{1,0:T(8,128)(2,1)S(1)} collective-permute-done((bf16[288,384]{1,0:T(8,128)(2,1)S(1)}, bf16[288,384]{1,0:T(8,128)(2,1)S(1)}, u32[]{:S(2)}, u32[]{:S(2)}) %collective-permute-start.21) | collective-permute-done | bytes 221216 | tf_op jit(solution)/shard_map/ppermute | solution.py:389
  73.5 0.2 combine_x.3.a0
  73.6 1.7 %collective-permute-start.24 = (bf16[256,384]{1,0:T(8,128)(2,1)S(1)}, bf16[256,384]{1,0:T(8,128)(2,1)S(1)}, u32[]{:S(2)}, u32[]{:S(2)}) collective-permute-start(bf16[256,384]{1,0:T(8,128)(2,1)S(1)} %combine_x.3.a0), channel_id=1, source_target_pairs={{0,3},{1,0},{2,1},{3,2},{4,7},{5,4},{6,5},{7,6},{8,11},{9,8},{10,9... | collective-permute-start | bytes 589832 | tf_op jit(solution)/shard_map/ppermute | solution.py:398
  75.4 0.6 collective-permute-start.23
  76.0 0.0 collective-permute-done.14.refs_3_
  76.0 1.0 collective-permute-start.22
  77.0 0.0 collective-permute-done.13.refs_2_
  77.0 0.4 collective-permute-done.12.recv
  77.4 0.0 collective-permute-start.18
  77.4 0.5 collective-permute-start.19
  77.9 0.2 combine_x.2.a0
  78.1 3.3 %collective-permute-done.24.a3 = bf16[256,384]{1,0:T(8,128)(2,1)S(1)} collective-permute-done((bf16[256,384]{1,0:T(8,128)(2,1)S(1)}, bf16[256,384]{1,0:T(8,128)(2,1)S(1)}, u32[]{:S(2)}, u32[]{:S(2)}) %collective-permute-start.24) | collective-permute-done | bytes 196640 | tf_op jit(solution)/shard_map/ppermute | solution.py:398
  81.4 2.6 %collective-permute-start.17 = (bf16[256,384]{1,0:T(8,128)(2,1)S(1)}, bf16[256,384]{1,0:T(8,128)(2,1)S(1)}, u32[]{:S(2)}, u32[]{:S(2)}) collective-permute-start(bf16[256,384]{1,0:T(8,128)(2,1)S(1)} %combine_x.2.a0), channel_id=1, source_target_pairs={{0,3},{1,0},{2,1},{3,2},{4,7},{5,4},{6,5},{7,6},{8,11},{9,8},{10,9... | collective-permute-start | bytes 589832 | tf_op jit(solution)/shard_map/ppermute | solution.py:398
  84.0 0.1 collective-permute-done.23.a2
  84.1 0.6 collective-permute-start.16
  84.8 3.0 %collective-permute-done.22.a1 = bf16[256,384]{1,0:T(8,128)(2,1)S(1)} collective-permute-done((bf16[256,384]{1,0:T(8,128)(2,1)S(1)}, bf16[256,384]{1,0:T(8,128)(2,1)S(1)}, u32[]{:S(2)}, u32[]{:S(2)}) %collective-permute-start.22) | collective-permute-done | bytes 196640 | tf_op jit(solution)/shard_map/ppermute | solution.py:398
  87.8 1.4 %collective-permute-start.15 = (bf16[256,384]{1,0:T(8,128)(2,1)S(1)}, bf16[256,384]{1,0:T(8,128)(2,1)S(1)}, u32[]{:S(2)}, u32[]{:S(2)}) collective-permute-start(bf16[256,384]{1,0:T(8,128)(2,1)S(1)} %combine_x.2.a0), channel_id=1, source_target_pairs={{0,1},{1,2},{2,3},{3,0},{4,5},{5,6},{6,7},{7,4},{8,9},{9,10},{10,1... | collective-permute-start | bytes 589832 | tf_op jit(solution)/shard_map/ppermute | solution.py:398
  89.2 0.0 collective-permute-done.18.refs_7_
  89.2 0.0 collective-permute-done.19.refs_8_
  89.2 1.2 %out_project.3 = (bf16[256,640]{1,0:T(8,128)(2,1)S(1)}, bf16[256,640]{1,0:T(8,128)(2,1)S(1)}) custom-call(s32[1]{0:T(128)} %bitcast.core, bf16[256,384]{1,0:T(8,128)(2,1)S(1)} %combine_x.3.a0, bf16[256,384]{1,0:T(8,128)(2,1)S(1)} %collective-permute-done.22.a1, bf16[256,384]{1,0:T(8,128)(2,1)S(1)} %collective-permute-done.23.a2, ...), custom_call_target="tpu_custom_call" | custom-call | flops 1006632960 | bytes 6000000 | tf_op jit(solution)/shard_map/out_project/pallas_call | solution.py:324
  90.4 3.1 %collective-permute-start.25 = (bf16[256,640]{1,0:T(8,128)(2,1)S(1)}, bf16[256,640]{1,0:T(8,128)(2,1)S(1)}, u32[]{:S(2)}, u32[]{:S(2)}) collective-permute-start(bf16[256,640]{1,0:T(8,128)(2,1)S(1)} %get-tuple-element.74), channel_id=1, source_target_pairs={{0,4},{1,5},{2,6},{3,7},{4,0},{5,1},{6,2},{7,3},{8,12},{9,13},{10,... | collective-permute-start | bytes 983048 | tf_op jit(solution)/shard_map/ppermute | solution.py:400
  93.6 0.0 collective-permute-done.17.a3
  93.6 0.0 collective-permute-done.16.a2
  93.6 2.3 %collective-permute-done.15.a1 = bf16[256,384]{1,0:T(8,128)(2,1)S(1)} collective-permute-done((bf16[256,384]{1,0:T(8,128)(2,1)S(1)}, bf16[256,384]{1,0:T(8,128)(2,1)S(1)}, u32[]{:S(2)}, u32[]{:S(2)}) %collective-permute-start.15) | collective-permute-done | bytes 196640 | tf_op jit(solution)/shard_map/ppermute | solution.py:398
  95.9 1.2 %out_project.2 = (bf16[256,640]{1,0:T(8,128)(2,1)S(1)}, bf16[256,640]{1,0:T(8,128)(2,1)S(1)}) custom-call(s32[1]{0:T(128)} %bitcast.core, bf16[256,384]{1,0:T(8,128)(2,1)S(1)} %combine_x.2.a0, bf16[256,384]{1,0:T(8,128)(2,1)S(1)} %collective-permute-done.15.a1, bf16[256,384]{1,0:T(8,128)(2,1)S(1)} %collective-permute-done.16.a2, ...), custom_call_target="tpu_custom_call" | custom-call | flops 1006632960 | bytes 6000000 | tf_op jit(solution)/shard_map/out_project/pallas_call | solution.py:324
  97.1 3.1 %collective-permute-start.20 = (bf16[256,640]{1,0:T(8,128)(2,1)S(1)}, bf16[256,640]{1,0:T(8,128)(2,1)S(1)}, u32[]{:S(2)}, u32[]{:S(2)}) collective-permute-start(bf16[256,640]{1,0:T(8,128)(2,1)S(1)} %get-tuple-element.70), channel_id=1, source_target_pairs={{0,4},{1,5},{2,6},{3,7},{4,0},{5,1},{6,2},{7,3},{8,12},{9,13},{10,... | collective-permute-start | bytes 983048 | tf_op jit(solution)/shard_map/ppermute | solution.py:400
  100.2 0.8 finish.2.rest_0_
  101.0 6.5 %collective-permute-done.20.recv = bf16[256,640]{1,0:T(8,128)(2,1)S(1)} collective-permute-done((bf16[256,640]{1,0:T(8,128)(2,1)S(1)}, bf16[256,640]{1,0:T(8,128)(2,1)S(1)}, u32[]{:S(2)}, u32[]{:S(2)}) %collective-permute-start.20) | collective-permute-done | bytes 327712 | tf_op jit(solution)/shard_map/ppermute | solution.py:400
  107.5 0.8 finish.3
  (13 shorter events, 0.1 us)
Async XLA Ops:
  14.3 18.9 %copy-start.2 = (bf16[512,768]{1,0:T(8,128)(2,1)S(1)}, bf16[512,768]{1,0:T(8,128)(2,1)}, u32[]{:S(2)}) copy-start(bf16[512,768]{1,0:T(8,128)(2,1)} %get-tuple-element.42.refs_4_) | copy-start | bytes 2359300
  14.3 18.9 %copy-start.3 = (bf16[512,384]{1,0:T(8,128)(2,1)S(1)}, bf16[512,384]{1,0:T(8,128)(2,1)}, u32[]{:S(2)}) copy-start(bf16[512,384]{1,0:T(8,128)(2,1)} %get-tuple-element.40.refs_0_.q0) | copy-start | bytes 1179652
  14.3 11.0 %collective-permute-start.1 = (bf16[512,384]{1,0:T(8,128)(2,1)}, bf16[512,384]{1,0:T(8,128)(2,1)S(1)}, u32[]{:S(2)}, u32[]{:S(2)}) collective-permute-start(bf16[512,384]{1,0:T(8,128)(2,1)} %get-tuple-element.40.refs_0_.q0), channel_id=1, source_target_pairs={{0,64},{8,72},{16,80},{24,88},{32,96},{40,104},{48,112},{56,120},{... | collective-permute-start | bytes 1179656 | tf_op jit(solution)/shard_map/ppermute | solution.py:369
  16.0 23.2 %collective-permute-start.4 = (bf16[512,768]{1,0:T(8,128)(2,1)}, bf16[512,768]{1,0:T(8,128)(2,1)S(1)}, u32[]{:S(2)}, u32[]{:S(2)}) collective-permute-start(bf16[512,768]{1,0:T(8,128)(2,1)} %get-tuple-element.42.refs_4_), channel_id=1, source_target_pairs={{0,48},{8,56},{16,0},{24,8},{32,16},{40,24},{48,32},{56,40},{64,11... | collective-permute-start | bytes 2359304 | tf_op jit(solution)/shard_map/ppermute | solution.py:362
  20.0 20.1 %collective-permute-start.3 = (bf16[512,768]{1,0:T(8,128)(2,1)}, bf16[512,768]{1,0:T(8,128)(2,1)S(1)}, u32[]{:S(2)}, u32[]{:S(2)}) collective-permute-start(bf16[512,768]{1,0:T(8,128)(2,1)} %get-tuple-element.42.refs_4_), channel_id=1, source_target_pairs={{0,16},{8,24},{16,32},{24,40},{32,48},{40,56},{48,0},{56,8},{64,80... | collective-permute-start | bytes 2359304 | tf_op jit(solution)/shard_map/ppermute | solution.py:361
  20.0 5.9 %collective-permute-start = (bf16[512,384]{1,0:T(8,128)(2,1)}, bf16[512,384]{1,0:T(8,128)(2,1)S(1)}, u32[]{:S(2)}, u32[]{:S(2)}) collective-permute-start(bf16[512,384]{1,0:T(8,128)(2,1)} %get-tuple-element.40.refs_0_.q0), channel_id=1, source_target_pairs={{0,8},{8,0},{16,24},{24,16},{32,40},{40,32},{48,56},{56,48},{64,72... | collective-permute-start | bytes 1179656 | tf_op jit(solution)/shard_map/ppermute | solution.py:368
  25.3 7.9 %collective-permute-start.2 = (bf16[512,384]{1,0:T(8,128)(2,1)S(1)}, bf16[512,384]{1,0:T(8,128)(2,1)}, u32[]{:S(2)}, u32[]{:S(2)}) collective-permute-start(bf16[512,384]{1,0:T(8,128)(2,1)S(1)} %collective-permute-done.1.refs_2_.q2), channel_id=1, source_target_pairs={{0,8},{8,0},{16,24},{24,16},{32,40},{40,32},{48,56},{56,48},{64,72... | collective-permute-start | bytes 1179656 | tf_op jit(solution)/shard_map/ppermute | solution.py:374
  29.8 23.0 %collective-permute-start.7 = (bf16[576,640]{1,0:T(8,128)(2,1)}, bf16[576,640]{1,0:T(8,128)(2,1)S(1)}, u32[]{:S(2)}, u32[]{:S(2)}) collective-permute-start(bf16[576,640]{1,0:T(8,128)(2,1)} %get-tuple-element.51), channel_id=1, source_target_pairs={{0,1},{1,2},{2,3},{3,0},{4,5},{5,6},{6,7},{7,4},{8,9},{9,10},{10,1... | collective-permute-start | bytes 2211848 | tf_op jit(solution)/shard_map/ppermute | solution.py:372
  31.7 21.1 %collective-permute-start.8 = (bf16[576,640]{1,0:T(8,128)(2,1)}, bf16[576,640]{1,0:T(8,128)(2,1)S(1)}, u32[]{:S(2)}, u32[]{:S(2)}) collective-permute-start(bf16[576,640]{1,0:T(8,128)(2,1)} %get-tuple-element.52), channel_id=1, source_target_pairs={{0,3},{1,0},{2,1},{3,2},{4,7},{5,4},{6,5},{7,6},{8,11},{9,8},{10,9... | collective-permute-start | bytes 2211848 | tf_op jit(solution)/shard_map/ppermute | solution.py:373
  40.2 12.6 %collective-permute-start.6 = (bf16[256,768]{1,0:T(8,128)(2,1)S(1)}, bf16[256,768]{1,0:T(8,128)(2,1)S(1)}, u32[]{:S(2)}, u32[]{:S(2)}) collective-permute-start(bf16[256,768]{1,0:T(8,128)(2,1)S(1)} %slice.13), channel_id=1, source_target_pairs={{0,48},{8,56},{16,0},{24,8},{32,16},{40,24},{48,32},{56,40},{64,11... | collective-permute-start | bytes 1179656 | tf_op jit(solution)/shard_map/ppermute | solution.py:378
  43.5 12.0 %collective-permute-start.5 = (bf16[256,768]{1,0:T(8,128)(2,1)S(1)}, bf16[256,768]{1,0:T(8,128)(2,1)S(1)}, u32[]{:S(2)}, u32[]{:S(2)}) collective-permute-start(bf16[256,768]{1,0:T(8,128)(2,1)S(1)} %slice.12), channel_id=1, source_target_pairs={{0,16},{8,24},{16,32},{24,40},{32,48},{40,56},{48,0},{56,8},{64,80... | collective-permute-start | bytes 1179656 | tf_op jit(solution)/shard_map/ppermute | solution.py:377
  60.3 29.0 %copy-start = (bf16[384,640]{1,0:T(8,128)(2,1)S(1)}, bf16[384,640]{1,0:T(8,128)(2,1)}, u32[]{:S(2)}) copy-start(bf16[384,640]{1,0:T(8,128)(2,1)} %get-tuple-element.63.refs_0_) | copy-start | bytes 1474564
  60.3 29.0 %copy-start.1 = (bf16[384,640]{1,0:T(8,128)(2,1)S(1)}, bf16[384,640]{1,0:T(8,128)(2,1)}, u32[]{:S(2)}) copy-start(bf16[384,640]{1,0:T(8,128)(2,1)} %get-tuple-element.66.refs_5_) | copy-start | bytes 1474564
  60.3 4.6 %collective-permute-start.9 = (bf16[1152,384]{1,0:T(8,128)(2,1)S(1)}, bf16[1152,384]{1,0:T(8,128)(2,1)S(1)}, u32[]{:S(2)}, u32[]{:S(2)}) collective-permute-start(bf16[1152,384]{1,0:T(8,128)(2,1)S(1)} %get-tuple-element.56), channel_id=1, source_target_pairs={{0,8},{8,0},{16,24},{24,16},{32,40},{40,32},{48,56},{56,48},{64,72... | collective-permute-start | bytes 2654216 | tf_op jit(solution)/shard_map/ppermute | solution.py:387
  60.4 3.5 %collective-permute-start.10 = (bf16[576,640]{1,0:T(8,128)(2,1)S(1)}, bf16[576,640]{1,0:T(8,128)(2,1)S(1)}, u32[]{:S(2)}, u32[]{:S(2)}) collective-permute-start(bf16[576,640]{1,0:T(8,128)(2,1)S(1)} %collective-permute-done.7.refs_1_), channel_id=1, source_target_pairs={{0,8},{8,0},{16,24},{24,16},{32,40},{40,32},{48,56},{56,48},{64,72... | collective-permute-start | bytes 2211848 | tf_op jit(solution)/shard_map/ppermute | solution.py:383
  60.9 4.0 %collective-permute-start.11 = (bf16[576,640]{1,0:T(8,128)(2,1)S(1)}, bf16[576,640]{1,0:T(8,128)(2,1)S(1)}, u32[]{:S(2)}, u32[]{:S(2)}) collective-permute-start(bf16[576,640]{1,0:T(8,128)(2,1)S(1)} %collective-permute-done.8.refs_4_), channel_id=1, source_target_pairs={{0,8},{8,0},{16,24},{24,16},{32,40},{40,32},{48,56},{56,48},{64,72... | collective-permute-start | bytes 2211848 | tf_op jit(solution)/shard_map/ppermute | solution.py:383
  61.0 15.0 %collective-permute-start.14 = (bf16[192,640]{1,0:T(8,128)(2,1)S(1)}, bf16[192,640]{1,0:T(8,128)(2,1)S(1)}, u32[]{:S(2)}, u32[]{:S(2)}) collective-permute-start(bf16[192,640]{1,0:T(8,128)(2,1)S(1)} %slice.15), channel_id=1, source_target_pairs={{0,3},{1,0},{2,1},{3,2},{4,7},{5,4},{6,5},{7,6},{8,11},{9,8},{10,9... | collective-permute-start | bytes 737288 | tf_op jit(solution)/shard_map/ppermute | solution.py:384
  65.1 8.3 %collective-permute-start.21 = (bf16[288,384]{1,0:T(8,128)(2,1)S(1)}, bf16[288,384]{1,0:T(8,128)(2,1)S(1)}, u32[]{:S(2)}, u32[]{:S(2)}) collective-permute-start(bf16[288,384]{1,0:T(8,128)(2,1)S(1)} %get-tuple-element.72), channel_id=1, source_target_pairs={{0,64},{8,72},{16,80},{24,88},{32,96},{40,104},{48,112},{56,120},{... | collective-permute-start | bytes 663560 | tf_op jit(solution)/shard_map/ppermute | solution.py:389
  66.7 10.3 %collective-permute-start.13 = (bf16[192,640]{1,0:T(8,128)(2,1)S(1)}, bf16[192,640]{1,0:T(8,128)(2,1)S(1)}, u32[]{:S(2)}, u32[]{:S(2)}) collective-permute-start(bf16[192,640]{1,0:T(8,128)(2,1)S(1)} %slice.14), channel_id=1, source_target_pairs={{0,1},{1,2},{2,3},{3,0},{4,5},{5,6},{6,7},{7,4},{8,9},{9,10},{10,1... | collective-permute-start | bytes 737288 | tf_op jit(solution)/shard_map/ppermute | solution.py:384
  67.0 10.4 %collective-permute-start.12 = (bf16[288,384]{1,0:T(8,128)(2,1)S(1)}, bf16[288,384]{1,0:T(8,128)(2,1)S(1)}, u32[]{:S(2)}, u32[]{:S(2)}) collective-permute-start(bf16[288,384]{1,0:T(8,128)(2,1)S(1)} %get-tuple-element.61), channel_id=1, source_target_pairs={{0,64},{8,72},{16,80},{24,88},{32,96},{40,104},{48,112},{56,120},{... | collective-permute-start | bytes 663560 | tf_op jit(solution)/shard_map/ppermute | solution.py:390
  73.6 7.8 %collective-permute-start.24 = (bf16[256,384]{1,0:T(8,128)(2,1)S(1)}, bf16[256,384]{1,0:T(8,128)(2,1)S(1)}, u32[]{:S(2)}, u32[]{:S(2)}) collective-permute-start(bf16[256,384]{1,0:T(8,128)(2,1)S(1)} %combine_x.3.a0), channel_id=1, source_target_pairs={{0,3},{1,0},{2,1},{3,2},{4,7},{5,4},{6,5},{7,6},{8,11},{9,8},{10,9... | collective-permute-start | bytes 589832 | tf_op jit(solution)/shard_map/ppermute | solution.py:398
  75.4 8.7 %collective-permute-start.23 = (bf16[256,384]{1,0:T(8,128)(2,1)S(1)}, bf16[256,384]{1,0:T(8,128)(2,1)S(1)}, u32[]{:S(2)}, u32[]{:S(2)}) collective-permute-start(bf16[256,384]{1,0:T(8,128)(2,1)S(1)} %combine_x.3.a0), channel_id=1, source_target_pairs={{0,2},{1,3},{2,0},{3,1},{4,6},{5,7},{6,4},{7,5},{8,10},{9,11},{10,... | collective-permute-start | bytes 589832 | tf_op jit(solution)/shard_map/ppermute | solution.py:398
  76.0 11.8 %collective-permute-start.22 = (bf16[256,384]{1,0:T(8,128)(2,1)S(1)}, bf16[256,384]{1,0:T(8,128)(2,1)S(1)}, u32[]{:S(2)}, u32[]{:S(2)}) collective-permute-start(bf16[256,384]{1,0:T(8,128)(2,1)S(1)} %combine_x.3.a0), channel_id=1, source_target_pairs={{0,1},{1,2},{2,3},{3,0},{4,5},{5,6},{6,7},{7,4},{8,9},{9,10},{10,1... | collective-permute-start | bytes 589832 | tf_op jit(solution)/shard_map/ppermute | solution.py:398
  77.4 11.8 %collective-permute-start.18 = (bf16[192,640]{1,0:T(8,128)(2,1)S(1)}, bf16[192,640]{1,0:T(8,128)(2,1)S(1)}, u32[]{:S(2)}, u32[]{:S(2)}) collective-permute-start(bf16[192,640]{1,0:T(8,128)(2,1)S(1)} %collective-permute-done.13.refs_2_), channel_id=1, source_target_pairs={{0,8},{8,0},{16,24},{24,16},{32,40},{40,32},{48,56},{56,48},{64,72... | collective-permute-start | bytes 737288 | tf_op jit(solution)/shard_map/ppermute | solution.py:392
  77.4 11.8 %collective-permute-start.19 = (bf16[192,640]{1,0:T(8,128)(2,1)S(1)}, bf16[192,640]{1,0:T(8,128)(2,1)S(1)}, u32[]{:S(2)}, u32[]{:S(2)}) collective-permute-start(bf16[192,640]{1,0:T(8,128)(2,1)S(1)} %collective-permute-done.14.refs_3_), channel_id=1, source_target_pairs={{0,8},{8,0},{16,24},{24,16},{32,40},{40,32},{48,56},{56,48},{64,72... | collective-permute-start | bytes 737288 | tf_op jit(solution)/shard_map/ppermute | solution.py:392
  81.4 12.1 %collective-permute-start.17 = (bf16[256,384]{1,0:T(8,128)(2,1)S(1)}, bf16[256,384]{1,0:T(8,128)(2,1)S(1)}, u32[]{:S(2)}, u32[]{:S(2)}) collective-permute-start(bf16[256,384]{1,0:T(8,128)(2,1)S(1)} %combine_x.2.a0), channel_id=1, source_target_pairs={{0,3},{1,0},{2,1},{3,2},{4,7},{5,4},{6,5},{7,6},{8,11},{9,8},{10,9... | collective-permute-start | bytes 589832 | tf_op jit(solution)/shard_map/ppermute | solution.py:398
  84.1 9.4 %collective-permute-start.16 = (bf16[256,384]{1,0:T(8,128)(2,1)S(1)}, bf16[256,384]{1,0:T(8,128)(2,1)S(1)}, u32[]{:S(2)}, u32[]{:S(2)}) collective-permute-start(bf16[256,384]{1,0:T(8,128)(2,1)S(1)} %combine_x.2.a0), channel_id=1, source_target_pairs={{0,2},{1,3},{2,0},{3,1},{4,6},{5,7},{6,4},{7,5},{8,10},{9,11},{10,... | collective-permute-start | bytes 589832 | tf_op jit(solution)/shard_map/ppermute | solution.py:398
  87.8 8.1 %collective-permute-start.15 = (bf16[256,384]{1,0:T(8,128)(2,1)S(1)}, bf16[256,384]{1,0:T(8,128)(2,1)S(1)}, u32[]{:S(2)}, u32[]{:S(2)}) collective-permute-start(bf16[256,384]{1,0:T(8,128)(2,1)S(1)} %combine_x.2.a0), channel_id=1, source_target_pairs={{0,1},{1,2},{2,3},{3,0},{4,5},{5,6},{6,7},{7,4},{8,9},{9,10},{10,1... | collective-permute-start | bytes 589832 | tf_op jit(solution)/shard_map/ppermute | solution.py:398
  90.4 9.7 %collective-permute-start.25 = (bf16[256,640]{1,0:T(8,128)(2,1)S(1)}, bf16[256,640]{1,0:T(8,128)(2,1)S(1)}, u32[]{:S(2)}, u32[]{:S(2)}) collective-permute-start(bf16[256,640]{1,0:T(8,128)(2,1)S(1)} %get-tuple-element.74), channel_id=1, source_target_pairs={{0,4},{1,5},{2,6},{3,7},{4,0},{5,1},{6,2},{7,3},{8,12},{9,13},{10,... | collective-permute-start | bytes 983048 | tf_op jit(solution)/shard_map/ppermute | solution.py:400
  97.1 10.4 %collective-permute-start.20 = (bf16[256,640]{1,0:T(8,128)(2,1)S(1)}, bf16[256,640]{1,0:T(8,128)(2,1)S(1)}, u32[]{:S(2)}, u32[]{:S(2)}) collective-permute-start(bf16[256,640]{1,0:T(8,128)(2,1)S(1)} %get-tuple-element.70), channel_id=1, source_target_pairs={{0,4},{1,5},{2,6},{3,7},{4,0},{5,1},{6,2},{7,3},{8,12},{9,13},{10,... | collective-permute-start | bytes 983048 | tf_op jit(solution)/shard_map/ppermute | solution.py:400
